TPU v7x, 32 devices: a whole 2x2x4 slice. The times are simulated.
32 devices in a mesh: dp: 8 (over y, x, core), space: 4 (over z).
Axes of the slice: x: 2, y: 2, z: 4, core: 2. Of those that a mesh axis runs over, the one named last changes fastest.
Arguments:
- features: bfloat16 [8192, 256], P(('dp', 'space')), may hold values from -6 to 6
- weights: bfloat16 [27, 256, 256], replicated, may hold values from -0.125 to 0.125
- cotangent: bfloat16 [8192, 256], P(('dp', 'space')), may hold values from -6 to 6
- kernel_map: int32 [27, 8192], P(None, ('dp', 'space')), may hold values from 0 to 384, as said below
- live: int32 [32], P(('dp', 'space')), may hold values from 64 to 256, as said below
- send_up: int32 [32, 64], P(('dp', 'space')), may hold values from 0 to 255, as said below
- send_down: int32 [32, 64], P(('dp', 'space')), may hold values from 0 to 255, as said below
Outputs:
- out_features: bfloat16 [8192, 256], P(('dp', 'space'))
- grad_features: bfloat16 [8192, 256], P(('dp', 'space'))
- grad_weights: bfloat16 [27, 256, 256], replicated
Inputs may be any that keep to these rules, and one draw needn't show every extreme that they name: In each group of 4 devices along space at least one device has all 256 slots live. `send_up`: each entry is a live row of its own device. `send_down`: each entry is a live row of its own device. `kernel_map`: at offset 27 // 2 a live row maps to itself. Rows that are not live map to slot 384 at every offset. Otherwise an entry is a live row of the same device, a slot from 256 to 383, or the zero slot 384.
All inputs are finite; a program needn't handle non-finite values.
Results may differ from a plain program's by a relative error of at most 0.001.
Values may be sent and summed in bfloat16 or wider, within the bound.
No kernel may reach another device: no remote copies, remote signals or barrier semaphores. Data moves between devices by JAX's collectives and lax.ppermute only.
A program may use at most 128 MiB of HBM per device.

v0:
```python
import math

import jax
import jax.numpy as jnp
from jax import lax
from jax.sharding import PartitionSpec as P


def passed_along(value, axis, steps):
    count = lax.axis_size(axis)
    initial, last = (max(0, -steps), min(count, count - steps))
    return lax.ppermute(value, axis, [(source, source + steps) for source in range(initial, last)])


def shards(features, weights, cotangent, kernel_map, live, send_up, send_down):
    rows, width = features.shape
    halo_rows = send_up.shape[1]
    live_count = live[0]
    live_mask = (jnp.arange(rows, dtype=jnp.int32) < live_count)[:, None]
    feat_live = jnp.where(live_mask, features, jnp.zeros((), features.dtype))
    cot_live = jnp.where(live_mask, cotangent, jnp.zeros((), cotangent.dtype))
    up_rows = send_up[0]
    down_rows = send_down[0]
    rows_lower = passed_along(feat_live[up_rows], "space", 1)
    rows_upper = passed_along(feat_live[down_rows], "space", -1)
    row_table = jnp.concatenate(
        [feat_live, rows_lower, rows_upper, jnp.zeros((1, width), features.dtype)], axis=0
    )
    table_rows = row_table.shape[0]
    out_init = jnp.zeros((rows, width), jnp.float32)
    grad_init = jnp.zeros((table_rows, width), jnp.float32)
    contract_out = (((1,), (1,)), ((), ()))
    contract_rows = (((0,), (0,)), ((), ()))

    def per_offset(carry, inputs):
        weight_k, map_k = inputs
        out_acc, grad_acc = carry
        picked = row_table[map_k]
        out_acc = out_acc + jnp.dot(picked, weight_k, preferred_element_type=jnp.float32)
        back = lax.dot_general(cot_live, weight_k, contract_out, preferred_element_type=jnp.float32)
        grad_acc = grad_acc.at[map_k].add(back)
        w_acc = lax.dot_general(picked, cot_live, contract_rows, preferred_element_type=jnp.float32)
        return ((out_acc, grad_acc), w_acc)

    (out_acc, grad_acc), wgrads = lax.scan(per_offset, (out_init, grad_init), (weights, kernel_map))
    out_features = jnp.where(live_mask, out_acc, 0.0).astype(jnp.bfloat16)
    lower_slots = grad_acc[rows : rows + halo_rows]
    upper_slots = grad_acc[rows + halo_rows : rows + 2 * halo_rows]
    back_up = passed_along(lower_slots, "space", -1)
    back_down = passed_along(upper_slots, "space", 1)
    grad_in = grad_acc[:rows].at[up_rows].add(back_up).at[down_rows].add(back_down)
    grad_features = jnp.where(live_mask, grad_in, 0.0).astype(jnp.bfloat16)
    grad_scale = 1.0 / math.sqrt(rows * lax.axis_size("dp") * lax.axis_size("space"))
    weight_sum = lax.psum(wgrads, ("dp", "space"))
    grad_weights = (weight_sum * grad_scale).astype(jnp.bfloat16)
    return (out_features, grad_features, grad_weights)


def solution(mesh):
    placed = (
        P(("dp", "space"), None),
        P(),
        P(("dp", "space"), None),
        P(None, ("dp", "space")),
        P(("dp", "space")),
        P(("dp", "space"), None),
        P(("dp", "space"), None),
    )
    return jax.shard_map(
        shards,
        mesh=mesh,
        in_specs=placed,
        out_specs=(P(("dp", "space"), None), P(("dp", "space"), None), P()),
        check_vma=False,
    )
```

profile of v0, /device:TPU:0, one launch (start us, length us, event | category | flops | bytes accessed | tf_op | source)
XLA Modules:
  0.0 404.7 jit_solution(13033189709039551600)
XLA Ops:
  10.3 4.9 %collective-permute-start = (bf16[64,256]{1,0:T(8,128)(2,1)S(1)}, bf16[64,256]{1,0:T(8,128)(2,1)S(1)}, u32[]{:S(2)}, u32[]{:S(2)}) collective-permute-start(bf16[64,256]{1,0:T(8,128)(2,1)S(1)} %gather_fusion.1), channel_id=1, source_target_pairs={{0,1},{1,2},{2,3},{4,5},{5,6},{6,7},{8,9},{9,10},{10,11},{12,13},{... | collective-permute-start | bytes 98312 | tf_op jit(solution)/shard_map/ppermute | solution.py:12
  16.6 1.3 collective-permute-start.1
  18.0 4.5 %collective-permute-done.1 = bf16[64,256]{1,0:T(8,128)(2,1)S(1)} collective-permute-done((bf16[64,256]{1,0:T(8,128)(2,1)S(1)}, bf16[64,256]{1,0:T(8,128)(2,1)S(1)}, u32[]{:S(2)}, u32[]{:S(2)}) %collective-permute-start.1) | collective-permute-done | bytes 32800 | tf_op jit(solution)/shard_map/ppermute | solution.py:12
  22.6 198.9 %while.15 = (s32[]{:T(128)}, f32[256,256]{1,0:T(8,128)S(1)}, f32[385,256]{1,0:T(8,128)S(1)}, f32[27,256,256]{2,1,0:T(8,128)}, s32[27,256]{1,0:T(8,128)}, /*index...) while((s32[]{:T(128)}, f32[256,256]{1,0:T(8,128)S(1)}, ...), condition=%wide.region_2.3_spmd.clone, body=%wide.region_0.2_spmd.clone.sunk | while | flops 100861696 | bytes 3417223 | solution.py:45
  23.3 1.2 gather_fusion
  26.9 2.1 scatter_fusion
  30.7 1.2 gather_fusion
  34.2 2.1 scatter_fusion
  38.0 1.2 gather_fusion
  41.6 2.1 scatter_fusion
  45.4 1.2 gather_fusion
  48.9 2.1 scatter_fusion
  52.7 1.2 gather_fusion
  56.3 2.1 scatter_fusion
  60.1 1.2 gather_fusion
  63.7 2.1 scatter_fusion
  67.5 1.2 gather_fusion
  71.0 2.1 scatter_fusion
  74.8 1.2 gather_fusion
  78.4 2.1 scatter_fusion
  85.8 2.1 scatter_fusion
  93.2 2.1 scatter_fusion
  100.5 2.1 scatter_fusion
  107.9 2.1 scatter_fusion
  111.7 1.2 gather_fusion
  115.3 2.2 scatter_fusion
  119.1 1.2 gather_fusion
  122.6 2.1 scatter_fusion
  126.5 1.2 gather_fusion
  130.0 2.1 scatter_fusion
  137.4 2.1 scatter_fusion
  144.8 2.1 scatter_fusion
  148.6 1.2 gather_fusion
  152.1 2.1 scatter_fusion
  159.5 2.1 scatter_fusion
  166.8 2.1 scatter_fusion
  170.6 1.2 gather_fusion
  174.2 2.1 scatter_fusion
  181.6 2.1 scatter_fusion
  188.9 2.1 scatter_fusion
  196.3 2.1 scatter_fusion
  203.7 2.1 scatter_fusion
  211.0 2.1 scatter_fusion
  218.4 2.1 scatter_fusion
  221.5 1.3 collective-permute-start.2
  222.8 4.5 %collective-permute-start.3 = (f32[64,256]{1,0:T(8,128)S(1)}, f32[64,256]{1,0:T(8,128)S(1)}, u32[]{:S(2)}, u32[]{:S(2)}) collective-permute-start(f32[64,256]{1,0:T(8,128)S(1)} %get-tuple-element.93), channel_id=1, source_target_pairs={{0,1},{1,2},{2,3},{4,5},{5,6},{6,7},{8,9},{9,10},{10,11},{12,13},{... | collective-permute-start | bytes 196616 | tf_op jit(solution)/shard_map/ppermute | solution.py:12
  231.1 161.0 %all-reduce.2.cloned.1.call-done = f32[27,256,256]{2,1,0:T(8,128)} async-done(((f32[27,256,256]{2,1,0:T(8,128)}), f32[27,256,256]{2,1,0:T(8,128)}) %all-reduce.2.cloned.1.call-update) | async-done | bytes 7077904 | tf_op jit(solution)/shard_map/psum | solution.py:54
  392.1 5.7 %multiply_convert_fusion = bf16[27,256,256]{2,1,0:T(8,128)(2,1)} fusion(f32[27,256,256]{2,1,0:T(8,128)} %all-reduce.2.cloned.1.call-done), kind=kLoop, calls=%fused_computation.18 | loop fusion | flops 3538944 | bytes 10616832 | tf_op jit(solution)/shard_map/convert_element_type | solution.py:55
  (199 shorter events, 132.8 us)
Async XLA Ops:
  7.2 384.9 %all-reduce.2.cloned.1.call-start = ((), (), s32[]{:S(2)}) async-start(), calls=%async_computation | async-start | bytes 14155776 | tf_op jit(solution)/shard_map/psum | solution.py:54
  10.3 7.6 %collective-permute-start = (bf16[64,256]{1,0:T(8,128)(2,1)S(1)}, bf16[64,256]{1,0:T(8,128)(2,1)S(1)}, u32[]{:S(2)}, u32[]{:S(2)}) collective-permute-start(bf16[64,256]{1,0:T(8,128)(2,1)S(1)} %gather_fusion.1), channel_id=1, source_target_pairs={{0,1},{1,2},{2,3},{4,5},{5,6},{6,7},{8,9},{9,10},{10,11},{12,13},{... | collective-permute-start | bytes 98312 | tf_op jit(solution)/shard_map/ppermute | solution.py:12
  16.6 5.8 %collective-permute-start.1 = (bf16[64,256]{1,0:T(8,128)(2,1)S(1)}, bf16[64,256]{1,0:T(8,128)(2,1)S(1)}, u32[]{:S(2)}, u32[]{:S(2)}) collective-permute-start(bf16[64,256]{1,0:T(8,128)(2,1)S(1)} %gather_fusion.2), channel_id=1, source_target_pairs={{1,0},{2,1},{3,2},{5,4},{6,5},{7,6},{9,8},{10,9},{11,10},{13,12},{... | collective-permute-start | bytes 98312 | tf_op jit(solution)/shard_map/ppermute | solution.py:12
  221.5 6.2 %collective-permute-start.2 = (f32[64,256]{1,0:T(8,128)S(1)}, f32[64,256]{1,0:T(8,128)S(1)}, u32[]{:S(2)}, u32[]{:S(2)}) collective-permute-start(f32[64,256]{1,0:T(8,128)S(1)} %get-tuple-element.94), channel_id=1, source_target_pairs={{1,0},{2,1},{3,2},{5,4},{6,5},{7,6},{9,8},{10,9},{11,10},{13,12},{... | collective-permute-start | bytes 196616 | tf_op jit(solution)/shard_map/ppermute | solution.py:12
  222.8 6.4 %collective-permute-start.3 = (f32[64,256]{1,0:T(8,128)S(1)}, f32[64,256]{1,0:T(8,128)S(1)}, u32[]{:S(2)}, u32[]{:S(2)}) collective-permute-start(f32[64,256]{1,0:T(8,128)S(1)} %get-tuple-element.93), channel_id=1, source_target_pairs={{0,1},{1,2},{2,3},{4,5},{5,6},{6,7},{8,9},{9,10},{10,11},{12,13},{... | collective-permute-start | bytes 196616 | tf_op jit(solution)/shard_map/ppermute | solution.py:12
Sparse Core Ops, SparseCore 0:
  221.6 170.4 all-reduce.1
where the time goes:
time: 407 us; the launch traced here: 405 us
  waiting for transfers between devices  166 us (41%)
  other arithmetic  88.3 us (22%)
  matrix products  86.3 us (21%)
  local copies, waits for them, and re-layouts  36 us (9%)
  between operations  14.8 us (4%)
  starting transfers between devices  12.1 us (3%)
    psum x1, waiting for transfers between devices, shards(): weight_sum = lax.psum(wgrads, ('dp', 'space'))  161 us
    scatter-add x27, other arithmetic, per_offset(): grad_acc = grad_acc.at[map_k].add(back)  57.9 us
    gather x27, local copies, waits for them, and re-layouts, per_offset(): picked = row_table[map_k]  31.1 us
    dot_general x27, matrix products, per_offset(): jnp.dot(picked, weight_k, preferred_element_type=jnp.float32)  30.5 us
    dot_general x27, matrix products, per_offset(): lax.dot_general(cot_live, weight_k, contract_out, preferred_element_type=...  30.3 us
    dot_general x27, matrix products, per_offset(): lax.dot_general(picked, cot_live, contract_rows, preferred_element_type=j...  25.5 us
    select_n x27, other arithmetic, per_offset(): picked = row_table[map_k]  19 us
    ppermute x4, starting transfers between devices, passed_along(): lax.ppermute(value, axis, [(source, source + steps) for source in range(i...  12.1 us
  transfers between devices with their start and end apart: 5, of which 4 were waited for; matrix products, arithmetic and copies ran while one was open for 1% of the time, Pallas kernels for 0%

commit v1 on v0

v1 whole, which is shorter than its diff:
```python
import functools
import math

import jax
import jax.numpy as jnp
from jax import lax
from jax.experimental import pallas as pl
from jax.experimental.pallas import tpu as pltpu
from jax.sharding import PartitionSpec as P

BF = jnp.bfloat16
F32 = jnp.float32
VMEM_LIMIT = 48 * 1024 * 1024
VMEM = pl.BlockSpec(memory_space=pltpu.VMEM)
SMEM = pl.BlockSpec(memory_space=pltpu.SMEM)


def params():
    return pltpu.CompilerParams(vmem_limit_bytes=VMEM_LIMIT)


def dot(a, b):
    return jnp.dot(a, b, preferred_element_type=F32)


def split(value, terms):
    parts = []
    for _ in range(terms):
        part = value.astype(BF)
        parts.append(part)
        value = value - part.astype(F32)
    return parts


def prep_kernel(live_ref, x_ref, dy_ref, map_ref, up_ref, down_ref, pack_ref, up_rows_ref, down_rows_ref, map_scr):
    rows, width = x_ref.shape
    halo = up_ref.shape[1]
    keep = lax.broadcasted_iota(jnp.int32, (rows, width), 0) < live_ref[0]
    x_live = jnp.where(keep, x_ref[...].astype(F32), 0.0).astype(BF)
    pack_ref[0:rows] = x_live
    pack_ref[rows : 2 * rows] = jnp.where(keep, dy_ref[...].astype(F32), 0.0).astype(BF)
    map_scr[...] = jnp.full(map_scr.shape, rows + 2 * halo, jnp.int32)
    map_scr[0 : map_ref.shape[0]] = map_ref[...]
    slots = map_scr[...]
    pack_ref[2 * rows :] = jnp.where(slots > 256, 256 - slots, slots).astype(F32).astype(BF)
    iota = lax.broadcasted_iota(jnp.int32, (rows, halo), 0)
    for index_ref, picked_ref in ((up_ref, up_rows_ref), (down_ref, down_rows_ref)):
        chosen = (iota == index_ref[...]).astype(F32).astype(BF)
        picked_ref[...] = lax.dot_general(chosen, x_live, (((0,), (0,)), ((), ())), preferred_element_type=F32).astype(BF)


def prep(live, features, cotangent, kernel_map, send_up, send_down, map_rows):
    rows, width = features.shape
    halo = send_up.shape[1]
    return pl.pallas_call(
        prep_kernel,
        out_shape=(
            jax.ShapeDtypeStruct((2 * rows + map_rows, width), BF),
            jax.ShapeDtypeStruct((halo, width), BF),
            jax.ShapeDtypeStruct((halo, width), BF),
        ),
        in_specs=[SMEM] + [VMEM] * 5,
        out_specs=(VMEM,) * 3,
        scratch_shapes=[pltpu.VMEM((map_rows, rows), jnp.int32)],
        compiler_params=params(),
        name="prep",
    )(live, features, cotangent, kernel_map, send_up, send_down)


def own_kernel(live_ref, pack_ref, lower_ref, upper_ref, map_ref, w_ref, out_ref, own_ref, low_ref, high_ref, table, out_acc, grad_acc):
    step = pl.program_id(0)
    offsets = w_ref.shape[0]
    halo, width = lower_ref.shape
    rows = out_ref.shape[0]
    slots = table.shape[0]

    @pl.when(step == 0)
    def _():
        table[0:rows] = pack_ref[0:rows]
        table[rows : rows + halo] = lower_ref[...]
        table[rows + halo :] = upper_ref[...]
        out_acc[...] = jnp.zeros_like(out_acc)
        grad_acc[...] = jnp.zeros_like(grad_acc)

    dy = pack_ref[rows : 2 * rows]
    slot_down = lax.broadcasted_iota(jnp.int32, (slots, rows), 0)
    slot_along = lax.broadcasted_iota(jnp.int32, (rows, 128), 1)
    out_sum = out_acc[...]
    grad_sum = grad_acc[...]
    for i in range(offsets):
        row = map_ref[pl.ds(step * offsets + i, 1), :]
        scatter = (slot_down == row).astype(F32).astype(BF)
        column = jnp.transpose(jnp.broadcast_to(row, (128, rows)))
        gather = jnp.concatenate(
            [(slot_along + 128 * b == column).astype(F32).astype(BF) for b in range(slots // 128)], axis=1
        )
        weight = w_ref[i]
        out_sum = out_sum + dot(dot(gather, table[...]).astype(BF), weight)
        back = lax.dot_general(dy, weight, (((1,), (1,)), ((), ())), preferred_element_type=F32)
        for part in split(back, 2):
            grad_sum = grad_sum + dot(scatter, part)
    out_acc[...] = out_sum
    grad_acc[...] = grad_sum

    @pl.when(step == pl.num_programs(0) - 1)
    def _():
        keep = lax.broadcasted_iota(jnp.int32, (rows, width), 0) < live_ref[0]
        out_ref[...] = jnp.where(keep, out_acc[...], 0.0).astype(BF)
        own_ref[...] = grad_acc[0:rows]
        low_ref[...] = grad_acc[rows : rows + halo]
        high_ref[...] = grad_acc[rows + halo :]


def own(live, pack, lower, upper, kernel_map, weights):
    offsets, width, _ = weights.shape
    halo = lower.shape[0]
    rows = kernel_map.shape[1]
    slots = rows + 2 * halo
    per_step = 3 if offsets % 3 == 0 else 1
    whole = lambda shape: pl.BlockSpec(shape, lambda k: (0,) * len(shape))
    return pl.pallas_call(
        own_kernel,
        grid=(offsets // per_step,),
        out_shape=(
            jax.ShapeDtypeStruct((rows, width), BF),
            jax.ShapeDtypeStruct((rows, width), F32),
            jax.ShapeDtypeStruct((halo, width), F32),
            jax.ShapeDtypeStruct((halo, width), F32),
        ),
        in_specs=[
            SMEM,
            whole(pack.shape),
            whole(lower.shape),
            whole(upper.shape),
            whole(kernel_map.shape),
            pl.BlockSpec((per_step, width, width), lambda k: (k, 0, 0)),
        ],
        out_specs=(whole((rows, width)), whole((rows, width)), whole((halo, width)), whole((halo, width))),
        scratch_shapes=[pltpu.VMEM((slots, width), BF), pltpu.VMEM((rows, width), F32), pltpu.VMEM((slots, width), F32)],
        compiler_params=params(),
        cost_estimate=pl.CostEstimate(flops=12_000_000_000, bytes_accessed=4_500_000, transcendentals=0),
        name="own",
    )(live, pack, lower, upper, kernel_map, weights)


def wgrad_kernel(sources, place_ref, *refs):
    packs, lowers, uppers = refs[:sources], refs[sources : 2 * sources], refs[2 * sources : 3 * sources]
    keep_ref, send_ref, table_t, dys, maps, picked = refs[3 * sources :]
    count, half, width = keep_ref.shape
    halo = lowers[0].shape[0]
    rows = dys.shape[0] // sources
    slots = rows + 2 * halo
    for s in range(sources):
        table_t[:, s * slots : s * slots + rows] = jnp.transpose(packs[s][0:rows])
        table_t[:, s * slots + rows : (s + 1) * slots] = jnp.transpose(
            jnp.concatenate([lowers[s][...], uppers[s][...]], axis=0)
        )
        dys[s * rows : (s + 1) * rows] = packs[s][rows : 2 * rows]
        code = packs[s][2 * rows :].astype(F32).astype(jnp.int32)
        maps[s] = jnp.where(code < 0, 256 - code, code)
    first = place_ref[0] * count
    core = place_ref[1]
    slot_down = lax.broadcasted_iota(jnp.int32, (slots, rows), 0)

    def offset(j, carry):
        for s in range(sources):
            row = maps[s, pl.ds(first + j, 1), :]
            chosen = (slot_down == row).astype(F32).astype(BF)
            picked[:, s * rows : (s + 1) * rows] = dot(table_t[:, s * slots : (s + 1) * slots], chosen).astype(BF)
        send_ref[j] = dot(picked[pl.ds(pl.multiple_of((1 - core) * half, half), half), :], dys[...])
        keep_ref[j] = dot(picked[pl.ds(pl.multiple_of(core * half, half), half), :], dys[...])
        return carry

    lax.fori_loop(0, count, offset, 0)


def wgrad(place, packs, lowers, uppers, count, rows):
    sources = len(packs)
    width = packs[0].shape[1]
    halo = lowers[0].shape[0]
    slots = rows + 2 * halo
    shape = jax.ShapeDtypeStruct((count, width // 2, width), F32)
    return pl.pallas_call(
        functools.partial(wgrad_kernel, sources),
        out_shape=(shape, shape),
        in_specs=[SMEM] + [VMEM] * (3 * sources),
        out_specs=(VMEM, VMEM),
        scratch_shapes=[
            pltpu.VMEM((width, sources * slots), BF),
            pltpu.VMEM((sources * rows, width), BF),
            pltpu.VMEM((sources, packs[0].shape[0] - 2 * rows, rows), jnp.int32),
            pltpu.VMEM((width, sources * rows), BF),
        ],
        compiler_params=params(),
        cost_estimate=pl.CostEstimate(flops=4_000_000_000, bytes_accessed=4_500_000, transcendentals=0),
        name="wgrad",
    )(place, *packs, *lowers, *uppers)


def blocks_kernel(place_ref, keep_ref, got_ref, *block_refs):
    block = block_refs[0].shape[1]
    for m, block_ref in enumerate(block_refs):
        at = pl.ds(pl.multiple_of((place_ref[2] ^ m) * block, block), block)
        block_ref[...] = keep_ref[:, at, :] + got_ref[:, at, :]


def blocks(place, keep, got, parts):
    count, half, width = keep.shape
    shape = jax.ShapeDtypeStruct((count, half // parts, width), F32)
    return pl.pallas_call(
        blocks_kernel,
        out_shape=(shape,) * parts,
        in_specs=[SMEM, VMEM, VMEM],
        out_specs=(VMEM,) * parts,
        compiler_params=params(),
        name="blocks",
    )(place, keep, got)


def final_kernel(live_ref, own_ref, back_up_ref, back_down_ref, up_ref, down_ref, out_ref):
    rows, width = own_ref.shape
    halo = up_ref.shape[1]
    total = own_ref[...]
    iota = lax.broadcasted_iota(jnp.int32, (rows, halo), 0)
    for index_ref, back_ref in ((up_ref, back_up_ref), (down_ref, back_down_ref)):
        chosen = (iota == index_ref[...]).astype(F32).astype(BF)
        for part in split(back_ref[...], 3):
            total = total + dot(chosen, part)
    keep = lax.broadcasted_iota(jnp.int32, (rows, width), 0) < live_ref[0]
    out_ref[...] = jnp.where(keep, total, 0.0).astype(BF)


def final(live, own_grad, back_up, back_down, send_up, send_down):
    return pl.pallas_call(
        final_kernel,
        out_shape=jax.ShapeDtypeStruct(own_grad.shape, BF),
        in_specs=[SMEM] + [VMEM] * 5,
        out_specs=VMEM,
        compiler_params=params(),
        name="final",
    )(live, own_grad, back_up, back_down, send_up, send_down)


def assemble_kernel(groups, place_ref, *refs):
    sources, out_ref, sems = refs[: 2 * groups], refs[2 * groups], refs[2 * groups + 1]
    offsets = out_ref.shape[0]
    parts, count, block, _ = sources[0].shape
    short = offsets - (groups - 1) * count

    def copies(index, part):
        m, o = index // 2, index % 2
        group = place_ref[0] ^ m
        row = ((place_ref[1] ^ o) * parts + (place_ref[2] ^ part)) * block
        row = pl.ds(pl.multiple_of(row, block), block)
        source = sources[index].at[part]
        sem = sems.at[index, part]
        yield group == group, pltpu.make_async_copy(
            source.at[0:short], out_ref.at[pl.ds(group * count, short), row], sem.at[0]
        )
        if short < count:
            yield group < groups - 1, pltpu.make_async_copy(
                source.at[short:count], out_ref.at[pl.ds(group * count + short, count - short), row], sem.at[1]
            )

    for act in ("start", "wait"):
        for index in range(2 * groups):
            for part in range(parts):
                for n, (wanted, copy) in enumerate(copies(index, part)):
                    if n == 0:
                        getattr(copy, act)()
                    else:
                        pl.when(wanted)(getattr(copy, act))


def assemble(place, pieces, offsets, width):
    parts = pieces[0].shape[0]
    return pl.pallas_call(
        functools.partial(assemble_kernel, len(pieces) // 2),
        out_shape=jax.ShapeDtypeStruct((offsets, width, width), BF),
        in_specs=[SMEM] + [pl.BlockSpec(memory_space=pl.ANY)] * len(pieces),
        out_specs=pl.BlockSpec(memory_space=pl.ANY),
        scratch_shapes=[pltpu.SemaphoreType.DMA((len(pieces), parts, 2))],
        compiler_params=params(),
        name="assemble",
    )(place, *pieces)


def assemble_plain(place, pieces, offsets, width):
    parts, count, block, _ = pieces[0].shape
    groups = len(pieces) // 2
    whole = jnp.zeros((groups * count, width, width), BF)
    for index, piece in enumerate(pieces):
        for part in range(parts):
            row = ((place[1] ^ (index % 2)) * parts + (place[2] ^ part)) * block
            whole = lax.dynamic_update_slice(whole, piece[part], ((place[0] ^ (index // 2)) * count, row, 0))
    return whole[:offsets]


def swap(value, axis, mask):
    return lax.ppermute(value, axis, [(i, i ^ mask) for i in range(lax.axis_size(axis))])


def passed_along(value, axis, steps):
    count = lax.axis_size(axis)
    return lax.ppermute(value, axis, [(i, i + steps) for i in range(max(0, -steps), min(count, count - steps))])


def shards(features, weights, cotangent, kernel_map, live, send_up, send_down):
    rows, width = features.shape
    offsets = weights.shape[0]
    groups = lax.axis_size("dp") // 2
    parts = lax.axis_size("space")
    count = -(-offsets // groups)
    map_rows = -(-(groups * count) // 16) * 16
    dp, space = lax.axis_index("dp"), lax.axis_index("space")
    place = jnp.stack([dp // 2, dp % 2, space]).astype(jnp.int32)

    pack, up_rows, down_rows = prep(live, features, cotangent, kernel_map, send_up, send_down, map_rows)
    lower = passed_along(up_rows, "space", 1)
    upper = passed_along(down_rows, "space", -1)
    packs = [pack] + [swap(pack, "dp", 2 * m) for m in range(1, groups)]
    lowers = [lower] + [swap(lower, "dp", 2 * m) for m in range(1, groups)]
    uppers = [upper] + [swap(upper, "dp", 2 * m) for m in range(1, groups)]

    out_features, own_grad, low_grad, high_grad = own(live, pack, lower, upper, kernel_map, weights)
    back_up = passed_along(low_grad, "space", -1)
    back_down = passed_along(high_grad, "space", 1)
    grad_features = final(live, own_grad, back_up, back_down, send_up, send_down)

    keep, send = wgrad(place, packs, lowers, uppers, count, rows)
    mine = blocks(place, keep, swap(send, "dp", 1), parts)
    total = mine[0]
    for m in range(1, parts):
        total = total + swap(mine[m], "space", m)
    scale = 1.0 / math.sqrt(rows * lax.axis_size("dp") * parts)
    rounded = (total * scale).astype(BF)
    line = jnp.stack([rounded] + [swap(rounded, "space", m) for m in range(1, parts)])
    pieces = []
    for m in range(groups):
        piece = swap(line, "dp", 2 * m) if m else line
        pieces += [piece, swap(piece, "dp", 1)]
    put = assemble if rounded.shape[1] % 16 == 0 else assemble_plain
    grad_weights = put(place, pieces, offsets, width)
    return (out_features, grad_features, grad_weights)


def solution(mesh):
    placed = (
        P(("dp", "space"), None),
        P(),
        P(("dp", "space"), None),
        P(None, ("dp", "space")),
        P(("dp", "space")),
        P(("dp", "space"), None),
        P(("dp", "space"), None),
    )
    return jax.shard_map(
        shards,
        mesh=mesh,
        in_specs=placed,
        out_specs=(P(("dp", "space"), None), P(("dp", "space"), None), P()),
        check_vma=False,
    )
```

time: 407 us -> 130 us (0.32)
  waiting for transfers between devices: 166 us -> 57.4 us
  other arithmetic: 88.3 us -> 0.21 us
  matrix products: 86.3 us -> 0 us
  local copies, waits for them, and re-layouts: 36 us -> 3.89 us
  starting transfers between devices: 12.1 us -> 40 us
  Pallas kernels: 0 us -> 26.4 us
  between operations: 14.8 us -> 1.44 us
    psum x1 -> x0, waiting for transfers between devices: 161 us -> none  [shards(): weight_sum = lax.psum(wgrads, ('dp', 'space'))]
    dot_general x81 -> x0, matrix products: 86.3 us -> none  [the longest x27 30.5 us: per_offset(): jnp.dot(picked, weight_k, preferred_element_type=jnp.float32)]
    scatter-add x29 -> x0, other arithmetic: 60 us -> none  [the longest x27 57.9 us: per_offset(): grad_acc = grad_acc.at[map_k].add(back)]
    ppermute x4 -> x27, waiting for transfers between devices: 5.27 us -> 57.4 us  [the longest x23 48.6 us: swap(): lax.ppermute(value, axis, [(i, i ^ mask) for i in range(lax.axis_size(axi...]
    gather x29 -> x0, local copies, waits for them, and re-layouts: 32.5 us -> none  [the longest x27 31.1 us: per_offset(): picked = row_table[map_k]]
    ppermute x4 -> x27, starting transfers between devices: 12.1 us -> 40 us  [the longest x23 29.8 us: swap(): lax.ppermute(value, axis, [(i, i ^ mask) for i in range(lax.axis_size(axi...]
    pallas_call x0 -> x6, Pallas kernels: none -> 26.4 us  [the longest x1 15.8 us: own(): pl.pallas_call(own_kernel, grid=(offsets // per_step,), out_shape=(jax.Sh...]
    select_n x30 -> x0, other arithmetic: 21.4 us -> none  [the longest x27 19 us: per_offset(): picked = row_table[map_k]]
  transfers between devices with their start and end apart: 5 -> 27, of which waited for: 4 -> 15; matrix products, arithmetic and copies ran while one was open for 1% -> 0% of each run, Pallas kernels for 0% -> 13%
where the time goes in v1:
time: 130 us; the launch traced here: 129 us
  waiting for transfers between devices  57.4 us (44%)
  starting transfers between devices  40 us (31%)
  Pallas kernels  26.4 us (20%)
  local copies, waits for them, and re-layouts  3.89 us (3%)
  between operations  1.44 us (1%)
    ppermute x23, waiting for transfers between devices, swap(): lax.ppermute(value, axis, [(i, i ^ mask) for i in range(lax.axis_size(axi...  48.6 us
    ppermute x23, starting transfers between devices, swap(): lax.ppermute(value, axis, [(i, i ^ mask) for i in range(lax.axis_size(axi...  29.8 us
    pallas_call x1, Pallas kernels, own(): pl.pallas_call(own_kernel, grid=(offsets // per_step,), out_shape=(jax.Sh...  15.8 us
    ppermute x4, starting transfers between devices, passed_along(): lax.ppermute(value, axis, [(i, i + steps) for i in range(max(0, -steps),...  10.3 us
    ppermute x4, waiting for transfers between devices, passed_along(): lax.ppermute(value, axis, [(i, i + steps) for i in range(max(0, -steps),...  8.81 us
    pallas_call x1, Pallas kernels, wgrad(): pl.pallas_call(functools.partial(wgrad_kernel, sources), out_shape=(shape...  5.84 us
    unnamed x18, local copies, waits for them, and re-layouts  3.89 us
    pallas_call x1, Pallas kernels, assemble(): pl.pallas_call(functools.partial(assemble_kernel, len(pieces) // 2), out_...  2.89 us
  transfers between devices with their start and end apart: 27, of which 15 were waited for; matrix products, arithmetic and copies ran while one was open for 0% of the time, Pallas kernels for 13%

profile of v1, /device:TPU:0, one launch (start us, length us, event | category | flops | bytes accessed | tf_op | source)
XLA Modules:
  0.0 129.4 jit_solution(15669478073063661633)
XLA Ops:
  1.3 0.9 copy-done
  2.2 0.9 copy-done.1
  3.1 0.8 copy-done.2
  3.8 0.7 copy-done.4
  4.5 0.7 copy-done.6
  5.2 0.2 prep.1
  5.4 4.0 %collective-permute-start.6 = (bf16[544,256]{1,0:T(8,128)(2,1)S(1)}, bf16[544,256]{1,0:T(8,128)(2,1)S(1)}, u32[]{:S(2)}, u32[]{:S(2)}) collective-permute-start(bf16[544,256]{1,0:T(8,128)(2,1)S(1)} %get-tuple-element.16.pack_ref.refs_0_), channel_id=1, source_target_pairs={{0,24},{4,28},{8,16},{12,20},{16,8},{20,12},{24,0},{28,4},{1,25},{... | collective-permute-start | bytes 835592 | tf_op jit(solution)/shard_map/ppermute | solution.py:300
  9.3 0.5 collective-permute-start.5
  9.8 0.1 collective-permute-start.4
  10.0 3.9 %collective-permute-start = (bf16[64,256]{1,0:T(8,128)(2,1)S(1)}, bf16[64,256]{1,0:T(8,128)(2,1)S(1)}, u32[]{:S(2)}, u32[]{:S(2)}) collective-permute-start(bf16[64,256]{1,0:T(8,128)(2,1)S(1)} %get-tuple-element.17), channel_id=1, source_target_pairs={{0,1},{1,2},{2,3},{4,5},{5,6},{6,7},{8,9},{9,10},{10,11},{12,13},{... | collective-permute-start | bytes 98312 | tf_op jit(solution)/shard_map/ppermute | solution.py:305
  13.9 1.3 collective-permute-start.1
  15.2 0.3 collective-permute-done.lower_ref.refs_4_
  15.4 2.4 %collective-permute-start.9 = (bf16[64,256]{1,0:T(8,128)(2,1)S(1)}, bf16[64,256]{1,0:T(8,128)(2,1)S(1)}, u32[]{:S(2)}, u32[]{:S(2)}) collective-permute-start(bf16[64,256]{1,0:T(8,128)(2,1)S(1)} %collective-permute-done.lower_ref.refs_4_), channel_id=1, source_target_pairs={{0,24},{4,28},{8,16},{12,20},{16,8},{20,12},{24,0},{28,4},{1,25},{... | collective-permute-start | bytes 98312 | tf_op jit(solution)/shard_map/ppermute | solution.py:300
  17.9 1.8 %collective-permute-done.1.upper_ref.refs_8_ = bf16[64,256]{1,0:T(8,128)(2,1)S(1)} collective-permute-done((bf16[64,256]{1,0:T(8,128)(2,1)S(1)}, bf16[64,256]{1,0:T(8,128)(2,1)S(1)}, u32[]{:S(2)}, u32[]{:S(2)}) %collective-permute-start.1) | collective-permute-done | bytes 32800 | tf_op jit(solution)/shard_map/ppermute | solution.py:305
  19.7 1.5 %collective-permute-start.8 = (bf16[64,256]{1,0:T(8,128)(2,1)S(1)}, bf16[64,256]{1,0:T(8,128)(2,1)S(1)}, u32[]{:S(2)}, u32[]{:S(2)}) collective-permute-start(bf16[64,256]{1,0:T(8,128)(2,1)S(1)} %collective-permute-done.lower_ref.refs_4_), channel_id=1, source_target_pairs={{0,16},{4,20},{8,24},{12,28},{16,0},{20,4},{24,8},{28,12},{1,17},{... | collective-permute-start | bytes 98312 | tf_op jit(solution)/shard_map/ppermute | solution.py:300
  21.2 1.6 %collective-permute-done.9.refs_7_ = bf16[64,256]{1,0:T(8,128)(2,1)S(1)} collective-permute-done((bf16[64,256]{1,0:T(8,128)(2,1)S(1)}, bf16[64,256]{1,0:T(8,128)(2,1)S(1)}, u32[]{:S(2)}, u32[]{:S(2)}) %collective-permute-start.9) | collective-permute-done | bytes 32800 | tf_op jit(solution)/shard_map/ppermute | solution.py:300
  22.8 1.7 %collective-permute-start.7 = (bf16[64,256]{1,0:T(8,128)(2,1)S(1)}, bf16[64,256]{1,0:T(8,128)(2,1)S(1)}, u32[]{:S(2)}, u32[]{:S(2)}) collective-permute-start(bf16[64,256]{1,0:T(8,128)(2,1)S(1)} %collective-permute-done.lower_ref.refs_4_), channel_id=1, source_target_pairs={{0,8},{4,12},{8,0},{12,4},{16,24},{20,28},{24,16},{28,20},{1,9},{5... | collective-permute-start | bytes 98312 | tf_op jit(solution)/shard_map/ppermute | solution.py:300
  24.5 1.5 %collective-permute-start.12 = (bf16[64,256]{1,0:T(8,128)(2,1)S(1)}, bf16[64,256]{1,0:T(8,128)(2,1)S(1)}, u32[]{:S(2)}, u32[]{:S(2)}) collective-permute-start(bf16[64,256]{1,0:T(8,128)(2,1)S(1)} %collective-permute-done.1.upper_ref.refs_8_), channel_id=1, source_target_pairs={{0,24},{4,28},{8,16},{12,20},{16,8},{20,12},{24,0},{28,4},{1,25},{... | collective-permute-start | bytes 98312 | tf_op jit(solution)/shard_map/ppermute | solution.py:300
  26.0 0.8 collective-permute-done.7.refs_5_
  26.9 1.6 %collective-permute-start.11 = (bf16[64,256]{1,0:T(8,128)(2,1)S(1)}, bf16[64,256]{1,0:T(8,128)(2,1)S(1)}, u32[]{:S(2)}, u32[]{:S(2)}) collective-permute-start(bf16[64,256]{1,0:T(8,128)(2,1)S(1)} %collective-permute-done.1.upper_ref.refs_8_), channel_id=1, source_target_pairs={{0,16},{4,20},{8,24},{12,28},{16,0},{20,4},{24,8},{28,12},{1,17},{... | collective-permute-start | bytes 98312 | tf_op jit(solution)/shard_map/ppermute | solution.py:300
  28.4 0.9 collective-permute-done.12.refs_11_
  29.3 0.6 collective-permute-start.10
  30.0 0.8 collective-permute-done.11.refs_10_
  30.8 2.4 %collective-permute-done.10.refs_9_ = bf16[64,256]{1,0:T(8,128)(2,1)S(1)} collective-permute-done((bf16[64,256]{1,0:T(8,128)(2,1)S(1)}, bf16[64,256]{1,0:T(8,128)(2,1)S(1)}, u32[]{:S(2)}, u32[]{:S(2)}) %collective-permute-start.10) | collective-permute-done | bytes 32800 | tf_op jit(solution)/shard_map/ppermute | solution.py:300
  33.2 5.8 %wgrad.1 = (f32[7,128,256]{2,1,0:T(8,128)S(1)}, f32[7,128,256]{2,1,0:T(8,128)S(1)}) custom-call(s32[3]{0:T(128)S(1)} %pad_add_fusion.place_ref, bf16[544,256]{1,0:T(8,128)(2,1)S(1)} %get-tuple-element.16.pack_ref.refs_0_, bf16[544,256]{1,0:T(8,128)(2,1)S(1)} %collective-permute-done.4.refs_1_, bf16[544,256]{1,0:T(8,128)(2,1)S(1)} %collective-permute-done.5.refs_2_, ...), custom_call_target="tpu_custom_call" | custom-call | flops 4000000000 | bytes 4500000 | tf_op jit(solution)/shard_map/wgrad/pallas_call | solution.py:183
  39.2 2.5 %collective-permute-done.13.got_ref = f32[7,128,256]{2,1,0:T(8,128)S(1)} collective-permute-done((f32[7,128,256]{2,1,0:T(8,128)S(1)}, f32[7,128,256]{2,1,0:T(8,128)S(1)}, u32[]{:S(2)}, u32[]{:S(2)}) %collective-permute-start.13) | collective-permute-done | bytes 917536 | tf_op jit(solution)/shard_map/ppermute | solution.py:300
  41.7 0.6 blocks.1
  42.3 1.6 %collective-permute-start.14 = (f32[7,32,256]{2,1,0:T(8,128)S(1)}, f32[7,32,256]{2,1,0:T(8,128)S(1)}, u32[]{:S(2)}, u32[]{:S(2)}) collective-permute-start(f32[7,32,256]{2,1,0:T(8,128)S(1)} %get-tuple-element.26), channel_id=1, source_target_pairs={{0,1},{1,0},{2,3},{3,2},{4,5},{5,4},{6,7},{7,6},{8,9},{9,8},{10,11... | collective-permute-start | bytes 688136 | tf_op jit(solution)/shard_map/ppermute | solution.py:300
  43.9 2.6 %collective-permute-start.15 = (f32[7,32,256]{2,1,0:T(8,128)S(1)}, f32[7,32,256]{2,1,0:T(8,128)S(1)}, u32[]{:S(2)}, u32[]{:S(2)}) collective-permute-start(f32[7,32,256]{2,1,0:T(8,128)S(1)} %get-tuple-element.27), channel_id=1, source_target_pairs={{0,2},{1,3},{2,0},{3,1},{4,6},{5,7},{6,4},{7,5},{8,10},{9,11},{10,... | collective-permute-start | bytes 688136 | tf_op jit(solution)/shard_map/ppermute | solution.py:300
  46.5 0.2 collective-permute-start.16
  46.8 7.6 %collective-permute-done.14 = f32[7,32,256]{2,1,0:T(8,128)S(1)} collective-permute-done((f32[7,32,256]{2,1,0:T(8,128)S(1)}, f32[7,32,256]{2,1,0:T(8,128)S(1)}, u32[]{:S(2)}, u32[]{:S(2)}) %collective-permute-start.14) | collective-permute-done | bytes 229408 | tf_op jit(solution)/shard_map/ppermute | solution.py:300
  54.3 8.8 %collective-permute-done.15 = f32[7,32,256]{2,1,0:T(8,128)S(1)} collective-permute-done((f32[7,32,256]{2,1,0:T(8,128)S(1)}, f32[7,32,256]{2,1,0:T(8,128)S(1)}, u32[]{:S(2)}, u32[]{:S(2)}) %collective-permute-start.15) | collective-permute-done | bytes 229408 | tf_op jit(solution)/shard_map/ppermute | solution.py:300
  63.2 2.5 %collective-permute-start.19 = (bf16[7,32,256]{2,1,0:T(8,128)(2,1)S(1)}, bf16[7,32,256]{2,1,0:T(8,128)(2,1)S(1)}, u32[]{:S(2)}, u32[]{:S(2)}) collective-permute-start(bf16[7,32,256]{2,1,0:T(8,128)(2,1)S(1)} %multiply_convert_fusion), channel_id=1, source_target_pairs={{0,3},{1,2},{2,1},{3,0},{4,7},{5,6},{6,5},{7,4},{8,11},{9,10},{10,... | collective-permute-start | bytes 344072 | tf_op jit(solution)/shard_map/ppermute | solution.py:300
  65.8 4.6 %collective-permute-start.18 = (bf16[7,32,256]{2,1,0:T(8,128)(2,1)S(1)}, bf16[7,32,256]{2,1,0:T(8,128)(2,1)S(1)}, u32[]{:S(2)}, u32[]{:S(2)}) collective-permute-start(bf16[7,32,256]{2,1,0:T(8,128)(2,1)S(1)} %multiply_convert_fusion), channel_id=1, source_target_pairs={{0,2},{1,3},{2,0},{3,1},{4,6},{5,7},{6,4},{7,5},{8,10},{9,11},{10,... | collective-permute-start | bytes 344072 | tf_op jit(solution)/shard_map/ppermute | solution.py:300
  70.5 6.9 %collective-permute-done.18 = bf16[7,32,256]{2,1,0:T(8,128)(2,1)S(1)} collective-permute-done((bf16[7,32,256]{2,1,0:T(8,128)(2,1)S(1)}, bf16[7,32,256]{2,1,0:T(8,128)(2,1)S(1)}, u32[]{:S(2)}, u32[]{:S(2)}) %collective-permute-start.18) | collective-permute-done | bytes 114720 | tf_op jit(solution)/shard_map/ppermute | solution.py:300
  77.4 1.6 %collective-permute-start.25 = (bf16[4,7,32,256]{3,2,1,0:T(8,128)(2,1)S(1)}, bf16[4,7,32,256]{3,2,1,0:T(8,128)(2,1)S(1)}, u32[]{:S(2)}, u32[]{:S(2)}) collective-permute-start(bf16[4,7,32,256]{3,2,1,0:T(8,128)(2,1)S(1)} %pad_maximum_fusion.refs_0_), channel_id=1, source_target_pairs={{0,24},{4,28},{8,16},{12,20},{16,8},{20,12},{24,0},{28,4},{1,25},{... | collective-permute-start | bytes 1376264 | tf_op jit(solution)/shard_map/ppermute | solution.py:300
  79.0 0.5 collective-permute-start.23
  79.6 1.4 %collective-permute-start.21 = (bf16[4,7,32,256]{3,2,1,0:T(8,128)(2,1)S(1)}, bf16[4,7,32,256]{3,2,1,0:T(8,128)(2,1)S(1)}, u32[]{:S(2)}, u32[]{:S(2)}) collective-permute-start(bf16[4,7,32,256]{3,2,1,0:T(8,128)(2,1)S(1)} %pad_maximum_fusion.refs_0_), channel_id=1, source_target_pairs={{0,8},{4,12},{8,0},{12,4},{16,24},{20,28},{24,16},{28,20},{1,9},{5... | collective-permute-start | bytes 1376264 | tf_op jit(solution)/shard_map/ppermute | solution.py:300
  81.0 10.9 %collective-permute-done.25.refs_6_ = bf16[4,7,32,256]{3,2,1,0:T(8,128)(2,1)S(1)} collective-permute-done((bf16[4,7,32,256]{3,2,1,0:T(8,128)(2,1)S(1)}, bf16[4,7,32,256]{3,2,1,0:T(8,128)(2,1)S(1)}, u32[]{:S(2)}, u32[]{:S(2)}) %collective-permute-start.25) | collective-permute-done | bytes 458784 | tf_op jit(solution)/shard_map/ppermute | solution.py:300
  91.9 5.4 %collective-permute-done.23.refs_4_ = bf16[4,7,32,256]{3,2,1,0:T(8,128)(2,1)S(1)} collective-permute-done((bf16[4,7,32,256]{3,2,1,0:T(8,128)(2,1)S(1)}, bf16[4,7,32,256]{3,2,1,0:T(8,128)(2,1)S(1)}, u32[]{:S(2)}, u32[]{:S(2)}) %collective-permute-start.23) | collective-permute-done | bytes 458784 | tf_op jit(solution)/shard_map/ppermute | solution.py:300
  97.3 0.5 collective-permute-start.22
  97.8 15.8 %own.1 = (bf16[256,256]{1,0:T(8,128)(2,1)}, f32[256,256]{1,0:T(8,128)S(1)}, f32[64,256]{1,0:T(8,128)S(1)}, f32[64,256]{1,0:T(8,128)S(1)}) custom-call(s32[1]{0:T(128)S(6)} %copy.10.live_ref, bf16[544,256]{1,0:T(8,128)(2,1)S(1)} %get-tuple-element.16.pack_ref.refs_0_, bf16[64,256]{1,0:T(8,128)(2,1)S(1)} %collective-permute-done.lower_ref.refs_4_, ...), custom_call_target="tpu_custom_call" | custom-call | flops 12000000000 | bytes 4500000 | tf_op jit(solution)/shard_map/own/pallas_call | solution.py:121
  113.6 1.3 collective-permute-start.2
  114.9 4.9 %collective-permute-done.2.back_up_ref = f32[64,256]{1,0:T(8,128)S(1)} collective-permute-done((f32[64,256]{1,0:T(8,128)S(1)}, f32[64,256]{1,0:T(8,128)S(1)}, u32[]{:S(2)}, u32[]{:S(2)}) %collective-permute-start.2) | collective-permute-done | bytes 65568 | tf_op jit(solution)/shard_map/ppermute | solution.py:305
  119.8 3.8 %collective-permute-start.3 = (f32[64,256]{1,0:T(8,128)S(1)}, f32[64,256]{1,0:T(8,128)S(1)}, u32[]{:S(2)}, u32[]{:S(2)}) collective-permute-start(f32[64,256]{1,0:T(8,128)S(1)} %get-tuple-element.22), channel_id=1, source_target_pairs={{0,1},{1,2},{2,3},{4,5},{5,6},{6,7},{8,9},{9,10},{10,11},{12,13},{... | collective-permute-start | bytes 196616 | tf_op jit(solution)/shard_map/ppermute | solution.py:305
  123.6 1.9 %collective-permute-done.3.back_down_ref = f32[64,256]{1,0:T(8,128)S(1)} collective-permute-done((f32[64,256]{1,0:T(8,128)S(1)}, f32[64,256]{1,0:T(8,128)S(1)}, u32[]{:S(2)}, u32[]{:S(2)}) %collective-permute-start.3) | collective-permute-done | bytes 65568 | tf_op jit(solution)/shard_map/ppermute | solution.py:305
  125.5 1.0 final.1
  126.5 2.9 %assemble.1 = bf16[27,256,256]{2,1,0:T(8,128)(2,1)} custom-call(s32[3]{0:T(128)S(1)} %pad_add_fusion.place_ref, bf16[4,7,32,256]{3,2,1,0:T(8,128)(2,1)S(1)} %pad_maximum_fusion.refs_0_, bf16[4,7,32,256]{3,2,1,0:T(8,128)(2,1)S(1)} %collective-permute-done.20.refs_1_, bf16[4,7,32,256]{3,2,1,0:T(8,128)(2,1)S(1)} %collective-permute-done.21.refs_2_, ...), custom_call_target="tpu_custom_call" | custom-call | tf_op jit(solution)/shard_map/assemble/pallas_call | solution.py:277
  (33 shorter events, 0.5 us)
Async XLA Ops:
  1.3 0.9 copy-start
  2.2 0.9 copy-start.1
  3.1 0.8 copy-start.2
  3.8 0.7 copy-start.4
  4.5 0.7 copy-start.6
  5.4 27.9 %collective-permute-start.6 = (bf16[544,256]{1,0:T(8,128)(2,1)S(1)}, bf16[544,256]{1,0:T(8,128)(2,1)S(1)}, u32[]{:S(2)}, u32[]{:S(2)}) collective-permute-start(bf16[544,256]{1,0:T(8,128)(2,1)S(1)} %get-tuple-element.16.pack_ref.refs_0_), channel_id=1, source_target_pairs={{0,24},{4,28},{8,16},{12,20},{16,8},{20,12},{24,0},{28,4},{1,25},{... | collective-permute-start | bytes 835592 | tf_op jit(solution)/shard_map/ppermute | solution.py:300
  9.3 23.9 %collective-permute-start.5 = (bf16[544,256]{1,0:T(8,128)(2,1)S(1)}, bf16[544,256]{1,0:T(8,128)(2,1)S(1)}, u32[]{:S(2)}, u32[]{:S(2)}) collective-permute-start(bf16[544,256]{1,0:T(8,128)(2,1)S(1)} %get-tuple-element.16.pack_ref.refs_0_), channel_id=1, source_target_pairs={{0,16},{4,20},{8,24},{12,28},{16,0},{20,4},{24,8},{28,12},{1,17},{... | collective-permute-start | bytes 835592 | tf_op jit(solution)/shard_map/ppermute | solution.py:300
  9.8 23.4 %collective-permute-start.4 = (bf16[544,256]{1,0:T(8,128)(2,1)S(1)}, bf16[544,256]{1,0:T(8,128)(2,1)S(1)}, u32[]{:S(2)}, u32[]{:S(2)}) collective-permute-start(bf16[544,256]{1,0:T(8,128)(2,1)S(1)} %get-tuple-element.16.pack_ref.refs_0_), channel_id=1, source_target_pairs={{0,8},{4,12},{8,0},{12,4},{16,24},{20,28},{24,16},{28,20},{1,9},{5... | collective-permute-start | bytes 835592 | tf_op jit(solution)/shard_map/ppermute | solution.py:300
  10.0 5.5 %collective-permute-start = (bf16[64,256]{1,0:T(8,128)(2,1)S(1)}, bf16[64,256]{1,0:T(8,128)(2,1)S(1)}, u32[]{:S(2)}, u32[]{:S(2)}) collective-permute-start(bf16[64,256]{1,0:T(8,128)(2,1)S(1)} %get-tuple-element.17), channel_id=1, source_target_pairs={{0,1},{1,2},{2,3},{4,5},{5,6},{6,7},{8,9},{9,10},{10,11},{12,13},{... | collective-permute-start | bytes 98312 | tf_op jit(solution)/shard_map/ppermute | solution.py:305
  13.9 5.8 %collective-permute-start.1 = (bf16[64,256]{1,0:T(8,128)(2,1)S(1)}, bf16[64,256]{1,0:T(8,128)(2,1)S(1)}, u32[]{:S(2)}, u32[]{:S(2)}) collective-permute-start(bf16[64,256]{1,0:T(8,128)(2,1)S(1)} %get-tuple-element.18), channel_id=1, source_target_pairs={{1,0},{2,1},{3,2},{5,4},{6,5},{7,6},{9,8},{10,9},{11,10},{13,12},{... | collective-permute-start | bytes 98312 | tf_op jit(solution)/shard_map/ppermute | solution.py:305
  15.4 7.4 %collective-permute-start.9 = (bf16[64,256]{1,0:T(8,128)(2,1)S(1)}, bf16[64,256]{1,0:T(8,128)(2,1)S(1)}, u32[]{:S(2)}, u32[]{:S(2)}) collective-permute-start(bf16[64,256]{1,0:T(8,128)(2,1)S(1)} %collective-permute-done.lower_ref.refs_4_), channel_id=1, source_target_pairs={{0,24},{4,28},{8,16},{12,20},{16,8},{20,12},{24,0},{28,4},{1,25},{... | collective-permute-start | bytes 98312 | tf_op jit(solution)/shard_map/ppermute | solution.py:300
  19.7 4.8 %collective-permute-start.8 = (bf16[64,256]{1,0:T(8,128)(2,1)S(1)}, bf16[64,256]{1,0:T(8,128)(2,1)S(1)}, u32[]{:S(2)}, u32[]{:S(2)}) collective-permute-start(bf16[64,256]{1,0:T(8,128)(2,1)S(1)} %collective-permute-done.lower_ref.refs_4_), channel_id=1, source_target_pairs={{0,16},{4,20},{8,24},{12,28},{16,0},{20,4},{24,8},{28,12},{1,17},{... | collective-permute-start | bytes 98312 | tf_op jit(solution)/shard_map/ppermute | solution.py:300
  22.8 4.1 %collective-permute-start.7 = (bf16[64,256]{1,0:T(8,128)(2,1)S(1)}, bf16[64,256]{1,0:T(8,128)(2,1)S(1)}, u32[]{:S(2)}, u32[]{:S(2)}) collective-permute-start(bf16[64,256]{1,0:T(8,128)(2,1)S(1)} %collective-permute-done.lower_ref.refs_4_), channel_id=1, source_target_pairs={{0,8},{4,12},{8,0},{12,4},{16,24},{20,28},{24,16},{28,20},{1,9},{5... | collective-permute-start | bytes 98312 | tf_op jit(solution)/shard_map/ppermute | solution.py:300
  24.5 4.8 %collective-permute-start.12 = (bf16[64,256]{1,0:T(8,128)(2,1)S(1)}, bf16[64,256]{1,0:T(8,128)(2,1)S(1)}, u32[]{:S(2)}, u32[]{:S(2)}) collective-permute-start(bf16[64,256]{1,0:T(8,128)(2,1)S(1)} %collective-permute-done.1.upper_ref.refs_8_), channel_id=1, source_target_pairs={{0,24},{4,28},{8,16},{12,20},{16,8},{20,12},{24,0},{28,4},{1,25},{... | collective-permute-start | bytes 98312 | tf_op jit(solution)/shard_map/ppermute | solution.py:300
  26.9 3.9 %collective-permute-start.11 = (bf16[64,256]{1,0:T(8,128)(2,1)S(1)}, bf16[64,256]{1,0:T(8,128)(2,1)S(1)}, u32[]{:S(2)}, u32[]{:S(2)}) collective-permute-start(bf16[64,256]{1,0:T(8,128)(2,1)S(1)} %collective-permute-done.1.upper_ref.refs_8_), channel_id=1, source_target_pairs={{0,16},{4,20},{8,24},{12,28},{16,0},{20,4},{24,8},{28,12},{1,17},{... | collective-permute-start | bytes 98312 | tf_op jit(solution)/shard_map/ppermute | solution.py:300
  29.3 3.9 %collective-permute-start.10 = (bf16[64,256]{1,0:T(8,128)(2,1)S(1)}, bf16[64,256]{1,0:T(8,128)(2,1)S(1)}, u32[]{:S(2)}, u32[]{:S(2)}) collective-permute-start(bf16[64,256]{1,0:T(8,128)(2,1)S(1)} %collective-permute-done.1.upper_ref.refs_8_), channel_id=1, source_target_pairs={{0,8},{4,12},{8,0},{12,4},{16,24},{20,28},{24,16},{28,20},{1,9},{5... | collective-permute-start | bytes 98312 | tf_op jit(solution)/shard_map/ppermute | solution.py:300
  39.1 58.7 %copy-start.3 = (s32[27,256]{1,0:T(8,128)S(1)}, s32[27,256]{1,0:T(8,128)}, u32[]{:S(2)}) copy-start(s32[27,256]{1,0:T(8,128)} %map_ref.3) | copy-start | bytes 82948
  39.1 58.7 %copy-start.8 = (bf16[27,256,256]{2,1,0:T(8,128)(2,1)S(1)}, bf16[27,256,256]{2,1,0:T(8,128)(2,1)}, u32[]{:S(2)}) copy-start(bf16[27,256,256]{2,1,0:T(8,128)(2,1)} %w_ref.1) | copy-start | bytes 10616836
  39.1 2.5 %collective-permute-start.13 = (f32[7,128,256]{2,1,0:T(8,128)S(1)}, f32[7,128,256]{2,1,0:T(8,128)S(1)}, u32[]{:S(2)}, u32[]{:S(2)}) collective-permute-start(f32[7,128,256]{2,1,0:T(8,128)S(1)} %get-tuple-element.24), channel_id=1, source_target_pairs={{0,4},{4,0},{8,12},{12,8},{16,20},{20,16},{24,28},{28,24},{1,5},{5... | collective-permute-start | bytes 2752520 | tf_op jit(solution)/shard_map/ppermute | solution.py:300
  42.3 12.0 %collective-permute-start.14 = (f32[7,32,256]{2,1,0:T(8,128)S(1)}, f32[7,32,256]{2,1,0:T(8,128)S(1)}, u32[]{:S(2)}, u32[]{:S(2)}) collective-permute-start(f32[7,32,256]{2,1,0:T(8,128)S(1)} %get-tuple-element.26), channel_id=1, source_target_pairs={{0,1},{1,0},{2,3},{3,2},{4,5},{5,4},{6,7},{7,6},{8,9},{9,8},{10,11... | collective-permute-start | bytes 688136 | tf_op jit(solution)/shard_map/ppermute | solution.py:300
  43.9 19.2 %collective-permute-start.15 = (f32[7,32,256]{2,1,0:T(8,128)S(1)}, f32[7,32,256]{2,1,0:T(8,128)S(1)}, u32[]{:S(2)}, u32[]{:S(2)}) collective-permute-start(f32[7,32,256]{2,1,0:T(8,128)S(1)} %get-tuple-element.27), channel_id=1, source_target_pairs={{0,2},{1,3},{2,0},{3,1},{4,6},{5,7},{6,4},{7,5},{8,10},{9,11},{10,... | collective-permute-start | bytes 688136 | tf_op jit(solution)/shard_map/ppermute | solution.py:300
  46.5 16.6 %collective-permute-start.16 = (f32[7,32,256]{2,1,0:T(8,128)S(1)}, f32[7,32,256]{2,1,0:T(8,128)S(1)}, u32[]{:S(2)}, u32[]{:S(2)}) collective-permute-start(f32[7,32,256]{2,1,0:T(8,128)S(1)} %get-tuple-element.28), channel_id=1, source_target_pairs={{0,3},{1,2},{2,1},{3,0},{4,7},{5,6},{6,5},{7,4},{8,11},{9,10},{10,... | collective-permute-start | bytes 688136 | tf_op jit(solution)/shard_map/ppermute | solution.py:300
  63.2 7.3 %collective-permute-start.19 = (bf16[7,32,256]{2,1,0:T(8,128)(2,1)S(1)}, bf16[7,32,256]{2,1,0:T(8,128)(2,1)S(1)}, u32[]{:S(2)}, u32[]{:S(2)}) collective-permute-start(bf16[7,32,256]{2,1,0:T(8,128)(2,1)S(1)} %multiply_convert_fusion), channel_id=1, source_target_pairs={{0,3},{1,2},{2,1},{3,0},{4,7},{5,6},{6,5},{7,4},{8,11},{9,10},{10,... | collective-permute-start | bytes 344072 | tf_op jit(solution)/shard_map/ppermute | solution.py:300
  65.8 11.6 %collective-permute-start.18 = (bf16[7,32,256]{2,1,0:T(8,128)(2,1)S(1)}, bf16[7,32,256]{2,1,0:T(8,128)(2,1)S(1)}, u32[]{:S(2)}, u32[]{:S(2)}) collective-permute-start(bf16[7,32,256]{2,1,0:T(8,128)(2,1)S(1)} %multiply_convert_fusion), channel_id=1, source_target_pairs={{0,2},{1,3},{2,0},{3,1},{4,6},{5,7},{6,4},{7,5},{8,10},{9,11},{10,... | collective-permute-start | bytes 344072 | tf_op jit(solution)/shard_map/ppermute | solution.py:300
  70.4 7.0 %collective-permute-start.17 = (bf16[7,32,256]{2,1,0:T(8,128)(2,1)S(1)}, bf16[7,32,256]{2,1,0:T(8,128)(2,1)S(1)}, u32[]{:S(2)}, u32[]{:S(2)}) collective-permute-start(bf16[7,32,256]{2,1,0:T(8,128)(2,1)S(1)} %multiply_convert_fusion), channel_id=1, source_target_pairs={{0,1},{1,0},{2,3},{3,2},{4,5},{5,4},{6,7},{7,6},{8,9},{9,8},{10,11... | collective-permute-start | bytes 344072 | tf_op jit(solution)/shard_map/ppermute | solution.py:300
  77.4 48.1 %copy-start.5 = (s32[1,64]{1,0:T(1,128)S(1)}, s32[1,64]{1,0:T(1,128)}, u32[]{:S(2)}) copy-start(s32[1,64]{1,0:T(1,128)} %up_ref.3) | copy-start | bytes 772
  77.4 48.1 %copy-start.7 = (s32[1,64]{1,0:T(1,128)S(1)}, s32[1,64]{1,0:T(1,128)}, u32[]{:S(2)}) copy-start(s32[1,64]{1,0:T(1,128)} %down_ref.3) | copy-start | bytes 772
  77.4 14.4 %collective-permute-start.25 = (bf16[4,7,32,256]{3,2,1,0:T(8,128)(2,1)S(1)}, bf16[4,7,32,256]{3,2,1,0:T(8,128)(2,1)S(1)}, u32[]{:S(2)}, u32[]{:S(2)}) collective-permute-start(bf16[4,7,32,256]{3,2,1,0:T(8,128)(2,1)S(1)} %pad_maximum_fusion.refs_0_), channel_id=1, source_target_pairs={{0,24},{4,28},{8,16},{12,20},{16,8},{20,12},{24,0},{28,4},{1,25},{... | collective-permute-start | bytes 1376264 | tf_op jit(solution)/shard_map/ppermute | solution.py:300
  79.0 18.2 %collective-permute-start.23 = (bf16[4,7,32,256]{3,2,1,0:T(8,128)(2,1)S(1)}, bf16[4,7,32,256]{3,2,1,0:T(8,128)(2,1)S(1)}, u32[]{:S(2)}, u32[]{:S(2)}) collective-permute-start(bf16[4,7,32,256]{3,2,1,0:T(8,128)(2,1)S(1)} %pad_maximum_fusion.refs_0_), channel_id=1, source_target_pairs={{0,16},{4,20},{8,24},{12,28},{16,0},{20,4},{24,8},{28,12},{1,17},{... | collective-permute-start | bytes 1376264 | tf_op jit(solution)/shard_map/ppermute | solution.py:300
  79.6 17.7 %collective-permute-start.21 = (bf16[4,7,32,256]{3,2,1,0:T(8,128)(2,1)S(1)}, bf16[4,7,32,256]{3,2,1,0:T(8,128)(2,1)S(1)}, u32[]{:S(2)}, u32[]{:S(2)}) collective-permute-start(bf16[4,7,32,256]{3,2,1,0:T(8,128)(2,1)S(1)} %pad_maximum_fusion.refs_0_), channel_id=1, source_target_pairs={{0,8},{4,12},{8,0},{12,4},{16,24},{20,28},{24,16},{28,20},{1,9},{5... | collective-permute-start | bytes 1376264 | tf_op jit(solution)/shard_map/ppermute | solution.py:300
  81.0 45.5 %collective-permute-start.20 = (bf16[4,7,32,256]{3,2,1,0:T(8,128)(2,1)S(1)}, bf16[4,7,32,256]{3,2,1,0:T(8,128)(2,1)S(1)}, u32[]{:S(2)}, u32[]{:S(2)}) collective-permute-start(bf16[4,7,32,256]{3,2,1,0:T(8,128)(2,1)S(1)} %pad_maximum_fusion.refs_0_), channel_id=1, source_target_pairs={{0,4},{4,0},{8,12},{12,8},{16,20},{20,16},{24,28},{28,24},{1,5},{5... | collective-permute-start | bytes 1376264 | tf_op jit(solution)/shard_map/ppermute | solution.py:300
  91.9 34.6 %collective-permute-start.26 = (bf16[4,7,32,256]{3,2,1,0:T(8,128)(2,1)S(1)}, bf16[4,7,32,256]{3,2,1,0:T(8,128)(2,1)S(1)}, u32[]{:S(2)}, u32[]{:S(2)}) collective-permute-start(bf16[4,7,32,256]{3,2,1,0:T(8,128)(2,1)S(1)} %collective-permute-done.25.refs_6_), channel_id=1, source_target_pairs={{0,4},{4,0},{8,12},{12,8},{16,20},{20,16},{24,28},{28,24},{1,5},{5... | collective-permute-start | bytes 1376264 | tf_op jit(solution)/shard_map/ppermute | solution.py:300
  97.2 29.3 %collective-permute-start.24 = (bf16[4,7,32,256]{3,2,1,0:T(8,128)(2,1)S(1)}, bf16[4,7,32,256]{3,2,1,0:T(8,128)(2,1)S(1)}, u32[]{:S(2)}, u32[]{:S(2)}) collective-permute-start(bf16[4,7,32,256]{3,2,1,0:T(8,128)(2,1)S(1)} %collective-permute-done.23.refs_4_), channel_id=1, source_target_pairs={{0,4},{4,0},{8,12},{12,8},{16,20},{20,16},{24,28},{28,24},{1,5},{5... | collective-permute-start | bytes 1376264 | tf_op jit(solution)/shard_map/ppermute | solution.py:300
  97.3 29.2 %collective-permute-start.22 = (bf16[4,7,32,256]{3,2,1,0:T(8,128)(2,1)S(1)}, bf16[4,7,32,256]{3,2,1,0:T(8,128)(2,1)S(1)}, u32[]{:S(2)}, u32[]{:S(2)}) collective-permute-start(bf16[4,7,32,256]{3,2,1,0:T(8,128)(2,1)S(1)} %collective-permute-done.21.refs_2_), channel_id=1, source_target_pairs={{0,4},{4,0},{8,12},{12,8},{16,20},{20,16},{24,28},{28,24},{1,5},{5... | collective-permute-start | bytes 1376264 | tf_op jit(solution)/shard_map/ppermute | solution.py:300
  113.6 6.1 %collective-permute-start.2 = (f32[64,256]{1,0:T(8,128)S(1)}, f32[64,256]{1,0:T(8,128)S(1)}, u32[]{:S(2)}, u32[]{:S(2)}) collective-permute-start(f32[64,256]{1,0:T(8,128)S(1)} %get-tuple-element.21), channel_id=1, source_target_pairs={{1,0},{2,1},{3,2},{5,4},{6,5},{7,6},{9,8},{10,9},{11,10},{13,12},{... | collective-permute-start | bytes 196616 | tf_op jit(solution)/shard_map/ppermute | solution.py:305
  119.8 5.7 %collective-permute-start.3 = (f32[64,256]{1,0:T(8,128)S(1)}, f32[64,256]{1,0:T(8,128)S(1)}, u32[]{:S(2)}, u32[]{:S(2)}) collective-permute-start(f32[64,256]{1,0:T(8,128)S(1)} %get-tuple-element.22), channel_id=1, source_target_pairs={{0,1},{1,2},{2,3},{4,5},{5,6},{6,7},{8,9},{9,10},{10,11},{12,13},{... | collective-permute-start | bytes 196616 | tf_op jit(solution)/shard_map/ppermute | solution.py:305

commit v2 on v1

v2 whole, which is shorter than its diff:
```python
import functools
import math

import jax
import jax.numpy as jnp
from jax import lax
from jax.experimental import pallas as pl
from jax.experimental.pallas import tpu as pltpu
from jax.sharding import PartitionSpec as P

BF = jnp.bfloat16
F32 = jnp.float32
VMEM_LIMIT = 48 * 1024 * 1024
VMEM = pl.BlockSpec(memory_space=pltpu.VMEM)
SMEM = pl.BlockSpec(memory_space=pltpu.SMEM)
ANY = pl.BlockSpec(memory_space=pl.ANY)
HBM = pl.BlockSpec(memory_space=pltpu.HBM)
TOKEN = jax.ShapeDtypeStruct((8, 128), F32)


def params():
    return pltpu.CompilerParams(vmem_limit_bytes=VMEM_LIMIT)


def dot(a, b):
    return jnp.dot(a, b, preferred_element_type=F32)


def split(value, terms):
    parts = []
    for _ in range(terms):
        part = value.astype(BF)
        parts.append(part)
        value = value - part.astype(F32)
    return parts


def prep_kernel(live_ref, x_hbm, dy_hbm, map_hbm, up_hbm, down_hbm, pack_ref, up_rows_ref, down_rows_ref, *scratch):
    x_ref, dy_ref, map_ref, up_ref, down_ref, map_scr, sems = scratch
    sources = (x_hbm, up_hbm, down_hbm, dy_hbm, map_hbm)
    targets = (x_ref, up_ref, down_ref, dy_ref, map_ref)
    copies = [pltpu.make_async_copy(a, b, sems.at[i]) for i, (a, b) in enumerate(zip(sources, targets))]
    for copy in copies:
        copy.start()
    rows, width = x_ref.shape
    halo = up_ref.shape[1]
    keep = lax.broadcasted_iota(jnp.int32, (rows, width), 0) < live_ref[0]
    iota = lax.broadcasted_iota(jnp.int32, (rows, halo), 0)
    for copy in copies[:3]:
        copy.wait()
    x_live = jnp.where(keep, x_ref[...].astype(F32), 0.0).astype(BF)
    pack_ref[0:rows] = x_live
    for index_ref, picked_ref in ((up_ref, up_rows_ref), (down_ref, down_rows_ref)):
        chosen = (iota == index_ref[...]).astype(F32).astype(BF)
        picked_ref[...] = lax.dot_general(chosen, x_live, (((0,), (0,)), ((), ())), preferred_element_type=F32).astype(BF)
    for copy in copies[3:]:
        copy.wait()
    pack_ref[rows : 2 * rows] = jnp.where(keep, dy_ref[...].astype(F32), 0.0).astype(BF)
    map_scr[...] = jnp.full(map_scr.shape, rows + 2 * halo, jnp.int32)
    map_scr[0 : map_ref.shape[0]] = map_ref[...]
    slots = map_scr[...]
    pack_ref[2 * rows :] = jnp.where(slots > 256, 256 - slots, slots).astype(F32).astype(BF)


def prep(live, features, cotangent, kernel_map, send_up, send_down, map_rows):
    rows, width = features.shape
    halo = send_up.shape[1]
    return pl.pallas_call(
        prep_kernel,
        out_shape=(
            jax.ShapeDtypeStruct((2 * rows + map_rows, width), BF),
            jax.ShapeDtypeStruct((halo, width), BF),
            jax.ShapeDtypeStruct((halo, width), BF),
        ),
        in_specs=[SMEM] + [HBM] * 5,
        out_specs=(VMEM,) * 3,
        scratch_shapes=[
            pltpu.VMEM((rows, width), BF),
            pltpu.VMEM((rows, width), BF),
            pltpu.VMEM(kernel_map.shape, jnp.int32),
            pltpu.VMEM(send_up.shape, jnp.int32),
            pltpu.VMEM(send_down.shape, jnp.int32),
            pltpu.VMEM((map_rows, rows), jnp.int32),
            pltpu.SemaphoreType.DMA((5,)),
        ],
        compiler_params=params(),
        name="prep",
    )(live, features, cotangent, kernel_map, send_up, send_down)


def decoded(code):
    code = code.astype(F32).astype(jnp.int32)
    return jnp.where(code < 0, 256 - code, code)


def backward_kernel(pack_ref, w_ref, after_ref, own_ref, low_ref, high_ref, token_ref, maps, grad_acc, chosen, terms):
    step = pl.program_id(0)
    offsets = w_ref.shape[0]
    rows, width = own_ref.shape
    halo = low_ref.shape[0]
    slots = grad_acc.shape[0]

    @pl.when(step == 0)
    def _():
        maps[...] = decoded(pack_ref[2 * rows :])
        grad_acc[...] = jnp.zeros_like(grad_acc)

    dy = pack_ref[rows : 2 * rows]
    slot_down = lax.broadcasted_iota(jnp.int32, (slots, rows), 0)
    for i in range(offsets):
        row = maps[pl.ds(step * offsets + i, 1), :]
        chosen[:, i * rows : (i + 1) * rows] = (slot_down == row).astype(F32).astype(BF)
        back = lax.dot_general(dy, w_ref[i], (((1,), (1,)), ((), ())), preferred_element_type=F32)
        for t, part in enumerate(split(back, 2)):
            terms[t, i * rows : (i + 1) * rows] = part
    grad_acc[...] += dot(chosen[...], terms[0]) + dot(chosen[...], terms[1])

    @pl.when(step == pl.num_programs(0) - 1)
    def _():
        own_ref[...] = grad_acc[0:rows]
        low_ref[...] = grad_acc[rows : rows + halo]
        high_ref[...] = grad_acc[rows + halo :]
        token_ref[...] = jnp.zeros_like(token_ref)


def whole(shape):
    return pl.BlockSpec(shape, lambda k: (0,) * len(shape))


def backward(pack, weights, rows, halo, after):
    offsets, width, _ = weights.shape
    slots = rows + 2 * halo
    per_step = 3 if offsets % 3 == 0 else 1
    return pl.pallas_call(
        backward_kernel,
        grid=(offsets // per_step,),
        out_shape=(
            jax.ShapeDtypeStruct((rows, width), F32),
            jax.ShapeDtypeStruct((halo, width), F32),
            jax.ShapeDtypeStruct((halo, width), F32),
            TOKEN,
        ),
        in_specs=[whole(pack.shape), pl.BlockSpec((per_step, width, width), lambda k: (k, 0, 0)), ANY],
        out_specs=(whole((rows, width)), whole((halo, width)), whole((halo, width)), whole(TOKEN.shape)),
        scratch_shapes=[
            pltpu.VMEM((pack.shape[0] - 2 * rows, rows), jnp.int32),
            pltpu.VMEM((slots, width), F32),
            pltpu.VMEM((slots, per_step * rows), BF),
            pltpu.VMEM((2, per_step * rows, width), BF),
        ],
        compiler_params=params(),
        cost_estimate=pl.CostEstimate(flops=8_000_000_000, bytes_accessed=4_500_000, transcendentals=0),
        name="backward",
    )(pack, weights, after)


def forward_kernel(live_ref, pack_ref, halo_ref, w_ref, after_ref, out_ref, token_ref, table, maps, out_acc, picked):
    step = pl.program_id(0)
    offsets = w_ref.shape[0]
    rows, width = out_ref.shape
    slots = table.shape[0]

    @pl.when(step == 0)
    def _():
        maps[...] = decoded(pack_ref[2 * rows :])
        table[0:rows] = pack_ref[0:rows]
        table[rows:] = halo_ref[...]
        out_acc[...] = jnp.zeros_like(out_acc)

    along = lax.broadcasted_iota(jnp.int32, (rows, 128), 1)
    for i in range(offsets):
        row = maps[pl.ds(step * offsets + i, 1), :]
        column = jnp.transpose(jnp.broadcast_to(row, (128, rows)))
        chosen = jnp.concatenate(
            [(along + 128 * b == column).astype(F32).astype(BF) for b in range(slots // 128)], axis=1
        )
        picked[:, i * width : (i + 1) * width] = dot(chosen, table[...]).astype(BF)
    out_acc[...] += dot(picked[...], w_ref[...].reshape(offsets * width, width))

    @pl.when(step == pl.num_programs(0) - 1)
    def _():
        keep = lax.broadcasted_iota(jnp.int32, (rows, width), 0) < live_ref[0]
        out_ref[...] = jnp.where(keep, out_acc[...], 0.0).astype(BF)
        token_ref[...] = jnp.zeros_like(token_ref)


def forward(live, pack, halo_rows, weights, rows, after):
    offsets, width, _ = weights.shape
    slots = rows + halo_rows.shape[0]
    per_step = 3 if offsets % 3 == 0 else 1
    return pl.pallas_call(
        forward_kernel,
        grid=(offsets // per_step,),
        out_shape=(jax.ShapeDtypeStruct((rows, width), BF), TOKEN),
        in_specs=[
            SMEM,
            whole(pack.shape),
            whole(halo_rows.shape),
            pl.BlockSpec((per_step, width, width), lambda k: (k, 0, 0)),
            ANY,
        ],
        out_specs=(whole((rows, width)), whole(TOKEN.shape)),
        scratch_shapes=[
            pltpu.VMEM((slots, width), BF),
            pltpu.VMEM((pack.shape[0] - 2 * rows, rows), jnp.int32),
            pltpu.VMEM((rows, width), F32),
            pltpu.VMEM((rows, per_step * width), BF),
        ],
        compiler_params=params(),
        cost_estimate=pl.CostEstimate(flops=5_000_000_000, bytes_accessed=4_500_000, transcendentals=0),
        name="forward",
    )(live, pack, halo_rows, weights, after)


def wgrad_kernel(sources, place_ref, *refs):
    packs, halos = refs[:sources], refs[sources : 2 * sources]
    keep_ref, send_ref, table_t, dys, maps, picked = refs[2 * sources :]
    count, half, width = keep_ref.shape
    rows = dys.shape[0] // sources
    slots = rows + halos[0].shape[0]
    for s in range(sources):
        table_t[:, s * slots : s * slots + rows] = jnp.transpose(packs[s][0:rows])
        table_t[:, s * slots + rows : (s + 1) * slots] = jnp.transpose(halos[s][...])
        dys[s * rows : (s + 1) * rows] = packs[s][rows : 2 * rows]
        maps[s] = decoded(packs[s][2 * rows :])
    first = place_ref[0] * count
    core = place_ref[1]
    slot_down = lax.broadcasted_iota(jnp.int32, (slots, rows), 0)

    def offset(j, carry):
        for s in range(sources):
            row = maps[s, pl.ds(first + j, 1), :]
            chosen = (slot_down == row).astype(F32).astype(BF)
            picked[:, s * rows : (s + 1) * rows] = dot(table_t[:, s * slots : (s + 1) * slots], chosen).astype(BF)
        send_ref[j] = dot(picked[pl.ds(pl.multiple_of((1 - core) * half, half), half), :], dys[...])
        keep_ref[j] = dot(picked[pl.ds(pl.multiple_of(core * half, half), half), :], dys[...])
        return carry

    lax.fori_loop(0, count, offset, 0)


def wgrad(place, packs, halos, count, rows):
    sources = len(packs)
    width = packs[0].shape[1]
    slots = rows + halos[0].shape[0]
    shape = jax.ShapeDtypeStruct((count, width // 2, width), F32)
    return pl.pallas_call(
        functools.partial(wgrad_kernel, sources),
        out_shape=(shape, shape),
        in_specs=[SMEM] + [VMEM] * (2 * sources),
        out_specs=(VMEM, VMEM),
        scratch_shapes=[
            pltpu.VMEM((width, sources * slots), BF),
            pltpu.VMEM((sources * rows, width), BF),
            pltpu.VMEM((sources, packs[0].shape[0] - 2 * rows, rows), jnp.int32),
            pltpu.VMEM((width, sources * rows), BF),
        ],
        compiler_params=params(),
        cost_estimate=pl.CostEstimate(flops=4_000_000_000, bytes_accessed=4_500_000, transcendentals=0),
        name="wgrad",
    )(place, *packs, *halos)


def blocks_kernel(place_ref, keep_ref, got_ref, *block_refs):
    block = block_refs[0].shape[1]
    for m, block_ref in enumerate(block_refs):
        at = pl.ds(pl.multiple_of((place_ref[2] ^ m) * block, block), block)
        block_ref[...] = keep_ref[:, at, :] + got_ref[:, at, :]


def blocks(place, keep, got, parts):
    count, half, width = keep.shape
    shape = jax.ShapeDtypeStruct((count, half // parts, width), F32)
    return pl.pallas_call(
        blocks_kernel,
        out_shape=(shape,) * parts,
        in_specs=[SMEM, VMEM, VMEM],
        out_specs=(VMEM,) * parts,
        compiler_params=params(),
        name="blocks",
    )(place, keep, got)


def total_kernel(scale, *refs):
    *terms, _, out_ref = refs
    total = terms[0][...]
    for term in terms[1:]:
        total = total + term[...]
    out_ref[...] = (total * scale).astype(BF)


def scaled_total(terms, scale, after):
    return pl.pallas_call(
        functools.partial(total_kernel, scale),
        out_shape=jax.ShapeDtypeStruct(terms[0].shape, BF),
        in_specs=[VMEM] * len(terms) + [ANY],
        out_specs=VMEM,
        compiler_params=params(),
        name="total",
    )(*terms, after)


def final_kernel(live_ref, own_ref, back_up_ref, back_down_ref, up_ref, down_ref, after_ref, out_ref, token_ref):
    rows, width = own_ref.shape
    halo = up_ref.shape[1]
    total = own_ref[...]
    iota = lax.broadcasted_iota(jnp.int32, (rows, halo), 0)
    for index_ref, back_ref in ((up_ref, back_up_ref), (down_ref, back_down_ref)):
        chosen = (iota == index_ref[...]).astype(F32).astype(BF)
        for part in split(back_ref[...], 3):
            total = total + dot(chosen, part)
    keep = lax.broadcasted_iota(jnp.int32, (rows, width), 0) < live_ref[0]
    out_ref[...] = jnp.where(keep, total, 0.0).astype(BF)
    token_ref[...] = jnp.zeros_like(token_ref)


def final(live, own_grad, back_up, back_down, send_up, send_down, after):
    return pl.pallas_call(
        final_kernel,
        out_shape=(jax.ShapeDtypeStruct(own_grad.shape, BF), TOKEN),
        in_specs=[SMEM] + [VMEM] * 5 + [ANY],
        out_specs=(VMEM, VMEM),
        compiler_params=params(),
        name="final",
    )(live, own_grad, back_up, back_down, send_up, send_down, after)


def assemble_kernel(groups, place_ref, *refs):
    sources, out_ref, sems = refs[: 2 * groups], refs[-2], refs[-1]
    offsets = out_ref.shape[0]
    parts, count, block, _ = sources[0].shape
    short = offsets - (groups - 1) * count

    def copies(index, part):
        m, o = index // 2, index % 2
        group = place_ref[0] ^ m
        row = ((place_ref[1] ^ o) * parts + (place_ref[2] ^ part)) * block
        row = pl.ds(pl.multiple_of(row, block), block)
        source = sources[index].at[part]
        sem = sems.at[index, part]
        yield group == group, pltpu.make_async_copy(
            source.at[0:short], out_ref.at[pl.ds(group * count, short), row], sem.at[0]
        )
        if short < count:
            yield group < groups - 1, pltpu.make_async_copy(
                source.at[short:count], out_ref.at[pl.ds(group * count + short, count - short), row], sem.at[1]
            )

    for act in ("start", "wait"):
        for index in range(2 * groups):
            for part in range(parts):
                for n, (wanted, copy) in enumerate(copies(index, part)):
                    if n == 0:
                        getattr(copy, act)()
                    else:
                        pl.when(wanted)(getattr(copy, act))


def assemble(place, pieces, offsets, width, after):
    parts = pieces[0].shape[0]
    return pl.pallas_call(
        functools.partial(assemble_kernel, len(pieces) // 2),
        out_shape=jax.ShapeDtypeStruct((offsets, width, width), BF),
        in_specs=[SMEM] + [ANY] * (len(pieces) + len(after)),
        out_specs=ANY,
        scratch_shapes=[pltpu.SemaphoreType.DMA((len(pieces), parts, 2))],
        compiler_params=params(),
        name="assemble",
    )(place, *pieces, *after)


def assemble_plain(place, pieces, offsets, width, after):
    parts, count, block, _ = pieces[0].shape
    groups = len(pieces) // 2
    whole = jnp.zeros((groups * count, width, width), BF)
    for index, piece in enumerate(pieces):
        for part in range(parts):
            row = ((place[1] ^ (index % 2)) * parts + (place[2] ^ part)) * block
            whole = lax.dynamic_update_slice(whole, piece[part], ((place[0] ^ (index // 2)) * count, row, 0))
    return whole[:offsets]


def swap(value, axis, mask):
    return lax.ppermute(value, axis, [(i, i ^ mask) for i in range(lax.axis_size(axis))])


def passed_along(value, axis, steps):
    count = lax.axis_size(axis)
    return lax.ppermute(value, axis, [(i, i + steps) for i in range(max(0, -steps), min(count, count - steps))])


def shards(features, weights, cotangent, kernel_map, live, send_up, send_down):
    rows, width = features.shape
    offsets = weights.shape[0]
    groups = lax.axis_size("dp") // 2
    parts = lax.axis_size("space")
    count = -(-offsets // groups)
    map_rows = -(-(groups * count) // 16) * 16
    dp, space = lax.axis_index("dp"), lax.axis_index("space")
    place = jnp.stack([dp // 2, dp % 2, space]).astype(jnp.int32)

    pack, up_rows, down_rows = prep(live, features, cotangent, kernel_map, send_up, send_down, map_rows)
    lower = passed_along(up_rows, "space", 1)
    upper = passed_along(down_rows, "space", -1)
    packs = [pack] + [swap(pack, "dp", 2 * m) for m in range(1, groups)]
    halo_rows = jnp.concatenate([lower, upper])
    halos = [halo_rows] + [swap(halo_rows, "dp", 2 * m) for m in range(1, groups)]

    keep, send = wgrad(place, packs, halos, count, rows)
    mine = blocks(place, keep, swap(send, "dp", 1), parts)
    got = [swap(mine[m], "space", m) for m in range(1, parts)]
    own_grad, low_grad, high_grad, token = backward(pack, weights, rows, send_up.shape[1], mine[0])
    back_up = passed_along(low_grad, "space", -1)
    back_down = passed_along(high_grad, "space", 1)
    scale = 1.0 / math.sqrt(rows * lax.axis_size("dp") * parts)
    rounded = scaled_total([mine[0], *got], scale, token)
    line = jnp.stack([rounded] + [swap(rounded, "space", m) for m in range(1, parts)])
    out_features, out_token = forward(live, pack, halo_rows, weights, rows, line)
    grad_features, grad_token = final(live, own_grad, back_up, back_down, send_up, send_down, line)
    pieces = []
    for m in range(groups):
        piece = swap(line, "dp", 2 * m) if m else line
        pieces += [piece, swap(piece, "dp", 1)]
    put = assemble if rounded.shape[1] % 16 == 0 else assemble_plain
    grad_weights = put(place, pieces, offsets, width, (out_token, grad_token))
    return (out_features, grad_features, grad_weights)


def solution(mesh):
    placed = (
        P(("dp", "space"), None),
        P(),
        P(("dp", "space"), None),
        P(None, ("dp", "space")),
        P(("dp", "space")),
        P(("dp", "space"), None),
        P(("dp", "space"), None),
    )
    return jax.shard_map(
        shards,
        mesh=mesh,
        in_specs=placed,
        out_specs=(P(("dp", "space"), None), P(("dp", "space"), None), P()),
        check_vma=False,
    )
```

time: 130 us -> 106 us (0.82)
  waiting for transfers between devices: 57.4 us -> 38.7 us
  starting transfers between devices: 40 us -> 35.8 us
    ppermute x23 -> x20, waiting for transfers between devices: 48.6 us -> 32.3 us  [swap(): lax.ppermute(value, axis, [(i, i ^ mask) for i in range(lax.axis_size(axi...]
    ppermute x23 -> x20, starting transfers between devices: 29.8 us -> 23.8 us  [swap(): lax.ppermute(value, axis, [(i, i ^ mask) for i in range(lax.axis_size(axi...]
    ppermute x4, waiting for transfers between devices: 8.81 us -> 6.37 us  [passed_along(): lax.ppermute(value, axis, [(i, i + steps) for i in range(max(0, -steps),...]
    ppermute x4, starting transfers between devices: 10.3 us -> 12 us  [passed_along(): lax.ppermute(value, axis, [(i, i + steps) for i in range(max(0, -steps),...]
    pallas_call x2 -> x4, Pallas kernels: 16.9 us -> 15.6 us  [the longest x1 7.99 us: backward(): pl.pallas_call(backward_kernel, grid=(offsets // per_step,), out_shape=(j...]
    unnamed x18 -> x17, local copies, waits for them, and re-layouts: 3.89 us -> 3.88 us
  transfers between devices with their start and end apart: 27 -> 24, of which waited for: 15 -> 11; matrix products, arithmetic and copies ran while one was open for 0% -> 0% of each run, Pallas kernels for 13% -> 15%
where the time goes in v2:
time: 106 us
  waiting for transfers between devices  38.7 us (37%)
  starting transfers between devices  35.8 us (34%)
  Pallas kernels  25.6 us (24%)
  local copies, waits for them, and re-layouts  3.89 us (4%)
  between operations  1.43 us (1%)
    ppermute x20, waiting for transfers between devices, swap(): lax.ppermute(value, axis, [(i, i ^ mask) for i in range(lax.axis_size(axi...  32.3 us
    ppermute x20, starting transfers between devices, swap(): lax.ppermute(value, axis, [(i, i ^ mask) for i in range(lax.axis_size(axi...  23.8 us
    ppermute x4, starting transfers between devices, passed_along(): lax.ppermute(value, axis, [(i, i + steps) for i in range(max(0, -steps),...  12 us
    pallas_call x1, Pallas kernels, backward(): pl.pallas_call(backward_kernel, grid=(offsets // per_step,), out_shape=(j...  7.99 us
    pallas_call x1, Pallas kernels, forward(): pl.pallas_call(forward_kernel, grid=(offsets // per_step,), out_shape=(ja...  6.52 us
    ppermute x4, waiting for transfers between devices, passed_along(): lax.ppermute(value, axis, [(i, i + steps) for i in range(max(0, -steps),...  6.37 us
    pallas_call x1, Pallas kernels, wgrad(): pl.pallas_call(functools.partial(wgrad_kernel, sources), out_shape=(shape...  5.85 us
    unnamed x17, local copies, waits for them, and re-layouts  3.88 us
  transfers between devices with their start and end apart: 24, of which 11 were waited for; matrix products, arithmetic and copies ran while one was open for 0% of the time, Pallas kernels for 15%

profile of v2, /device:TPU:0, one launch (start us, length us, event | category | flops | bytes accessed | tf_op | source)
XLA Modules:
  0.0 105.6 jit_solution(39499966449952266)
XLA Ops:
  1.3 0.9 copy-done
  2.2 0.9 copy-done.1
  3.1 0.8 copy-done.2
  3.8 0.7 copy-done.3
  4.5 0.7 copy-done.5
  5.2 0.7 prep.1
  5.8 4.9 %collective-permute-start = (bf16[64,256]{1,0:T(8,128)(2,1)S(1)}, bf16[64,256]{1,0:T(8,128)(2,1)S(1)}, u32[]{:S(2)}, u32[]{:S(2)}) collective-permute-start(bf16[64,256]{1,0:T(8,128)(2,1)S(1)} %get-tuple-element.21), channel_id=1, source_target_pairs={{0,1},{1,2},{2,3},{4,5},{5,6},{6,7},{8,9},{9,10},{10,11},{12,13},{... | collective-permute-start | bytes 98312 | tf_op jit(solution)/shard_map/ppermute | solution.py:389
  10.8 2.5 %collective-permute-start.4 = (bf16[544,256]{1,0:T(8,128)(2,1)S(1)}, bf16[544,256]{1,0:T(8,128)(2,1)S(1)}, u32[]{:S(2)}, u32[]{:S(2)}) collective-permute-start(bf16[544,256]{1,0:T(8,128)(2,1)S(1)} %get-tuple-element.20.refs_0_.pack_ref), channel_id=1, source_target_pairs={{0,24},{4,28},{8,16},{12,20},{16,8},{20,12},{24,0},{28,4},{1,25},{... | collective-permute-start | bytes 835592 | tf_op jit(solution)/shard_map/ppermute | solution.py:384
  13.3 0.5 collective-permute-start.3
  13.8 0.5 collective-permute-start.2
  14.3 1.3 %collective-permute-start.1 = (bf16[64,256]{1,0:T(8,128)(2,1)S(1)}, bf16[64,256]{1,0:T(8,128)(2,1)S(1)}, u32[]{:S(2)}, u32[]{:S(2)}) collective-permute-start(bf16[64,256]{1,0:T(8,128)(2,1)S(1)} %get-tuple-element.22), channel_id=1, source_target_pairs={{1,0},{2,1},{3,2},{5,4},{6,5},{7,6},{9,8},{10,9},{11,10},{13,12},{... | collective-permute-start | bytes 98312 | tf_op jit(solution)/shard_map/ppermute | solution.py:389
  15.6 0.0 collective-permute-done
  15.6 4.5 %collective-permute-done.1 = bf16[64,256]{1,0:T(8,128)(2,1)S(1)} collective-permute-done((bf16[64,256]{1,0:T(8,128)(2,1)S(1)}, bf16[64,256]{1,0:T(8,128)(2,1)S(1)}, u32[]{:S(2)}, u32[]{:S(2)}) %collective-permute-start.1) | collective-permute-done | bytes 32800 | tf_op jit(solution)/shard_map/ppermute | solution.py:389
  20.1 2.4 %collective-permute-start.7 = (bf16[128,256]{1,0:T(8,128)(2,1)S(1)}, bf16[128,256]{1,0:T(8,128)(2,1)S(1)}, u32[]{:S(2)}, u32[]{:S(2)}) collective-permute-start(bf16[128,256]{1,0:T(8,128)(2,1)S(1)} %constant_dynamic-update-slice_fusion.refs_4_.halo_ref), channel_id=1, source_target_pairs={{0,24},{4,28},{8,16},{12,20},{16,8},{20,12},{24,0},{28,4},{1,25},{... | collective-permute-start | bytes 196616 | tf_op jit(solution)/shard_map/ppermute | solution.py:384
  22.6 0.5 collective-permute-start.6
  23.1 4.3 %collective-permute-done.7.refs_7_ = bf16[128,256]{1,0:T(8,128)(2,1)S(1)} collective-permute-done((bf16[128,256]{1,0:T(8,128)(2,1)S(1)}, bf16[128,256]{1,0:T(8,128)(2,1)S(1)}, u32[]{:S(2)}, u32[]{:S(2)}) %collective-permute-start.7) | collective-permute-done | bytes 65568 | tf_op jit(solution)/shard_map/ppermute | solution.py:384
  27.4 1.5 %collective-permute-start.5 = (bf16[128,256]{1,0:T(8,128)(2,1)S(1)}, bf16[128,256]{1,0:T(8,128)(2,1)S(1)}, u32[]{:S(2)}, u32[]{:S(2)}) collective-permute-start(bf16[128,256]{1,0:T(8,128)(2,1)S(1)} %constant_dynamic-update-slice_fusion.refs_4_.halo_ref), channel_id=1, source_target_pairs={{0,8},{4,12},{8,0},{12,4},{16,24},{20,28},{24,16},{28,20},{1,9},{5... | collective-permute-start | bytes 196616 | tf_op jit(solution)/shard_map/ppermute | solution.py:384
  28.9 0.1 pad_add_fusion.place_ref
  28.9 2.7 %collective-permute-done.5.refs_5_ = bf16[128,256]{1,0:T(8,128)(2,1)S(1)} collective-permute-done((bf16[128,256]{1,0:T(8,128)(2,1)S(1)}, bf16[128,256]{1,0:T(8,128)(2,1)S(1)}, u32[]{:S(2)}, u32[]{:S(2)}) %collective-permute-start.5) | collective-permute-done | bytes 65568 | tf_op jit(solution)/shard_map/ppermute | solution.py:384
  31.6 5.8 %wgrad.1 = (f32[7,128,256]{2,1,0:T(8,128)S(1)}, f32[7,128,256]{2,1,0:T(8,128)S(1)}) custom-call(s32[3]{0:T(128)S(1)} %pad_add_fusion.place_ref, bf16[544,256]{1,0:T(8,128)(2,1)S(1)} %get-tuple-element.20.refs_0_.pack_ref, bf16[544,256]{1,0:T(8,128)(2,1)S(1)} %collective-permute-done.2.refs_1_, bf16[544,256]{1,0:T(8,128)(2,1)S(1)} %collective-permute-done.3.refs_2_, ...), custom_call_target="tpu_custom_call" | custom-call | flops 4000000000 | bytes 4500000 | tf_op jit(solution)/shard_map/wgrad/pallas_call | solution.py:247
  37.5 0.1 collective-permute-start.8
  37.6 2.5 %collective-permute-done.8.got_ref = f32[7,128,256]{2,1,0:T(8,128)S(1)} collective-permute-done((f32[7,128,256]{2,1,0:T(8,128)S(1)}, f32[7,128,256]{2,1,0:T(8,128)S(1)}, u32[]{:S(2)}, u32[]{:S(2)}) %collective-permute-start.8) | collective-permute-done | bytes 917536 | tf_op jit(solution)/shard_map/ppermute | solution.py:384
  40.0 0.6 blocks.1
  40.7 1.6 %collective-permute-start.9 = (f32[7,32,256]{2,1,0:T(8,128)S(1)}, f32[7,32,256]{2,1,0:T(8,128)S(1)}, u32[]{:S(2)}, u32[]{:S(2)}) collective-permute-start(f32[7,32,256]{2,1,0:T(8,128)S(1)} %get-tuple-element.26), channel_id=1, source_target_pairs={{0,1},{1,0},{2,3},{3,2},{4,5},{5,4},{6,7},{7,6},{8,9},{9,8},{10,11... | collective-permute-start | bytes 688136 | tf_op jit(solution)/shard_map/ppermute | solution.py:384
  42.3 1.1 %collective-permute-start.10 = (f32[7,32,256]{2,1,0:T(8,128)S(1)}, f32[7,32,256]{2,1,0:T(8,128)S(1)}, u32[]{:S(2)}, u32[]{:S(2)}) collective-permute-start(f32[7,32,256]{2,1,0:T(8,128)S(1)} %get-tuple-element.27), channel_id=1, source_target_pairs={{0,2},{1,3},{2,0},{3,1},{4,6},{5,7},{6,4},{7,5},{8,10},{9,11},{10,... | collective-permute-start | bytes 688136 | tf_op jit(solution)/shard_map/ppermute | solution.py:384
  43.4 1.7 %collective-permute-start.11 = (f32[7,32,256]{2,1,0:T(8,128)S(1)}, f32[7,32,256]{2,1,0:T(8,128)S(1)}, u32[]{:S(2)}, u32[]{:S(2)}) collective-permute-start(f32[7,32,256]{2,1,0:T(8,128)S(1)} %get-tuple-element.28), channel_id=1, source_target_pairs={{0,3},{1,2},{2,1},{3,0},{4,7},{5,6},{6,5},{7,4},{8,11},{9,10},{10,... | collective-permute-start | bytes 688136 | tf_op jit(solution)/shard_map/ppermute | solution.py:384
  45.1 8.0 %backward.1 = (f32[256,256]{1,0:T(8,128)S(1)}, f32[64,256]{1,0:T(8,128)S(1)}, f32[64,256]{1,0:T(8,128)S(1)}, f32[8,128]{1,0:T(8,128)S(1)}) custom-call(bf16[544,256]{1,0:T(8,128)(2,1)S(1)} %get-tuple-element.20.refs_0_.pack_ref, bf16[27,256,256]{2,1,0:T(8,128)(2,1)S(1)} %copy-done.7, f32[7,32,256]{2,1,0:T(8,128)S(1)} %get-tuple-element.25.after_ref.refs_0_), custom_call_target="tpu_custom_call" | custom-call | flops 8000000000 | bytes 4500000 | tf_op jit(solution)/shard_map/backward/pallas_call | solution.py:134
  53.2 8.4 %collective-permute-done.10.refs_2_ = f32[7,32,256]{2,1,0:T(8,128)S(1)} collective-permute-done((f32[7,32,256]{2,1,0:T(8,128)S(1)}, f32[7,32,256]{2,1,0:T(8,128)S(1)}, u32[]{:S(2)}, u32[]{:S(2)}) %collective-permute-start.10) | collective-permute-done | bytes 229408 | tf_op jit(solution)/shard_map/ppermute | solution.py:384
  61.5 0.1 total.1
  61.6 2.5 %collective-permute-start.14 = (bf16[7,32,256]{2,1,0:T(8,128)(2,1)S(1)}, bf16[7,32,256]{2,1,0:T(8,128)(2,1)S(1)}, u32[]{:S(2)}, u32[]{:S(2)}) collective-permute-start(bf16[7,32,256]{2,1,0:T(8,128)(2,1)S(1)} %total.1), channel_id=1, source_target_pairs={{0,3},{1,2},{2,1},{3,0},{4,7},{5,6},{6,5},{7,4},{8,11},{9,10},{10,... | collective-permute-start | bytes 344072 | tf_op jit(solution)/shard_map/ppermute | solution.py:384
  64.1 4.6 %collective-permute-start.13 = (bf16[7,32,256]{2,1,0:T(8,128)(2,1)S(1)}, bf16[7,32,256]{2,1,0:T(8,128)(2,1)S(1)}, u32[]{:S(2)}, u32[]{:S(2)}) collective-permute-start(bf16[7,32,256]{2,1,0:T(8,128)(2,1)S(1)} %total.1), channel_id=1, source_target_pairs={{0,2},{1,3},{2,0},{3,1},{4,6},{5,7},{6,4},{7,5},{8,10},{9,11},{10,... | collective-permute-start | bytes 344072 | tf_op jit(solution)/shard_map/ppermute | solution.py:384
  68.8 0.1 collective-permute-start.12
  68.9 6.9 %collective-permute-done.13 = bf16[7,32,256]{2,1,0:T(8,128)(2,1)S(1)} collective-permute-done((bf16[7,32,256]{2,1,0:T(8,128)(2,1)S(1)}, bf16[7,32,256]{2,1,0:T(8,128)(2,1)S(1)}, u32[]{:S(2)}, u32[]{:S(2)}) %collective-permute-start.13) | collective-permute-done | bytes 114720 | tf_op jit(solution)/shard_map/ppermute | solution.py:384
  75.7 0.1 pad_maximum_fusion.after_ref.refs_0_
  75.8 2.5 %collective-permute-start.22 = (bf16[4,7,32,256]{3,2,1,0:T(8,128)(2,1)S(1)}, bf16[4,7,32,256]{3,2,1,0:T(8,128)(2,1)S(1)}, u32[]{:S(2)}, u32[]{:S(2)}) collective-permute-start(bf16[4,7,32,256]{3,2,1,0:T(8,128)(2,1)S(1)} %pad_maximum_fusion.after_ref.refs_0_), channel_id=1, source_target_pairs={{0,24},{4,28},{8,16},{12,20},{16,8},{20,12},{24,0},{28,4},{1,25},{... | collective-permute-start | bytes 1376264 | tf_op jit(solution)/shard_map/ppermute | solution.py:384
  78.3 0.5 collective-permute-start.20
  78.8 0.5 collective-permute-start.18
  79.3 1.3 %collective-permute-start.15 = (f32[64,256]{1,0:T(8,128)S(1)}, f32[64,256]{1,0:T(8,128)S(1)}, u32[]{:S(2)}, u32[]{:S(2)}) collective-permute-start(f32[64,256]{1,0:T(8,128)S(1)} %get-tuple-element.32), channel_id=1, source_target_pairs={{1,0},{2,1},{3,2},{5,4},{6,5},{7,6},{9,8},{10,9},{11,10},{13,12},{... | collective-permute-start | bytes 196616 | tf_op jit(solution)/shard_map/ppermute | solution.py:389
  80.6 4.5 %collective-permute-start.16 = (f32[64,256]{1,0:T(8,128)S(1)}, f32[64,256]{1,0:T(8,128)S(1)}, u32[]{:S(2)}, u32[]{:S(2)}) collective-permute-start(f32[64,256]{1,0:T(8,128)S(1)} %get-tuple-element.33), channel_id=1, source_target_pairs={{0,1},{1,2},{2,3},{4,5},{5,6},{6,7},{8,9},{9,10},{10,11},{12,13},{... | collective-permute-start | bytes 196616 | tf_op jit(solution)/shard_map/ppermute | solution.py:389
  85.2 0.3 collective-permute-done.15.back_up_ref
  85.5 1.6 %collective-permute-done.16.back_down_ref = f32[64,256]{1,0:T(8,128)S(1)} collective-permute-done((f32[64,256]{1,0:T(8,128)S(1)}, f32[64,256]{1,0:T(8,128)S(1)}, u32[]{:S(2)}, u32[]{:S(2)}) %collective-permute-start.16) | collective-permute-done | bytes 65568 | tf_op jit(solution)/shard_map/ppermute | solution.py:389
  87.1 1.0 final.1
  88.1 2.1 %collective-permute-done.22.refs_6_ = bf16[4,7,32,256]{3,2,1,0:T(8,128)(2,1)S(1)} collective-permute-done((bf16[4,7,32,256]{3,2,1,0:T(8,128)(2,1)S(1)}, bf16[4,7,32,256]{3,2,1,0:T(8,128)(2,1)S(1)}, u32[]{:S(2)}, u32[]{:S(2)}) %collective-permute-start.22) | collective-permute-done | bytes 458784 | tf_op jit(solution)/shard_map/ppermute | solution.py:384
  90.2 5.4 %collective-permute-done.20.refs_4_ = bf16[4,7,32,256]{3,2,1,0:T(8,128)(2,1)S(1)} collective-permute-done((bf16[4,7,32,256]{3,2,1,0:T(8,128)(2,1)S(1)}, bf16[4,7,32,256]{3,2,1,0:T(8,128)(2,1)S(1)}, u32[]{:S(2)}, u32[]{:S(2)}) %collective-permute-start.20) | collective-permute-done | bytes 458784 | tf_op jit(solution)/shard_map/ppermute | solution.py:384
  95.6 0.1 collective-permute-done.18.refs_2_
  95.7 0.4 collective-permute-start.19
  96.1 6.5 %forward.1 = (bf16[256,256]{1,0:T(8,128)(2,1)}, f32[8,128]{1,0:T(8,128)S(1)}) custom-call(s32[1]{0:T(128)S(6)} %copy.11.live_ref, bf16[544,256]{1,0:T(8,128)(2,1)S(1)} %get-tuple-element.20.refs_0_.pack_ref, bf16[128,256]{1,0:T(8,128)(2,1)S(1)} %constant_dynamic-update-slice_fusion.refs_4_.halo_ref, bf16[27,256,256]{2,1,0:T(8,128)(2,1)S(1)} %copy-done.7, ...), custom_call_target="tpu_custom_call" | custom-call | flops 5000000000 | bytes 4500000 | tf_op jit(solution)/shard_map/forward/pallas_call | solution.py:191
  102.7 2.9 %assemble.1 = bf16[27,256,256]{2,1,0:T(8,128)(2,1)} custom-call(s32[3]{0:T(128)S(1)} %pad_add_fusion.place_ref, bf16[4,7,32,256]{3,2,1,0:T(8,128)(2,1)S(1)} %pad_maximum_fusion.after_ref.refs_0_, bf16[4,7,32,256]{3,2,1,0:T(8,128)(2,1)S(1)} %collective-permute-done.17.refs_1_, bf16[4,7,32,256]{3,2,1,0:T(8,128)(2,1)S(1)} %collective-permute-done.18.refs_2_, ...), custom_call_target="tpu_custom_call" | custom-call | tf_op jit(solution)/shard_map/assemble/pallas_call | solution.py:361
  (28 shorter events, 0.1 us)
Async XLA Ops:
  1.3 0.9 copy-start
  2.2 0.9 copy-start.1
  3.1 0.8 copy-start.2
  3.8 0.7 copy-start.3
  4.5 0.7 copy-start.5
  5.8 9.8 %collective-permute-start = (bf16[64,256]{1,0:T(8,128)(2,1)S(1)}, bf16[64,256]{1,0:T(8,128)(2,1)S(1)}, u32[]{:S(2)}, u32[]{:S(2)}) collective-permute-start(bf16[64,256]{1,0:T(8,128)(2,1)S(1)} %get-tuple-element.21), channel_id=1, source_target_pairs={{0,1},{1,2},{2,3},{4,5},{5,6},{6,7},{8,9},{9,10},{10,11},{12,13},{... | collective-permute-start | bytes 98312 | tf_op jit(solution)/shard_map/ppermute | solution.py:389
  10.8 20.9 %collective-permute-start.4 = (bf16[544,256]{1,0:T(8,128)(2,1)S(1)}, bf16[544,256]{1,0:T(8,128)(2,1)S(1)}, u32[]{:S(2)}, u32[]{:S(2)}) collective-permute-start(bf16[544,256]{1,0:T(8,128)(2,1)S(1)} %get-tuple-element.20.refs_0_.pack_ref), channel_id=1, source_target_pairs={{0,24},{4,28},{8,16},{12,20},{16,8},{20,12},{24,0},{28,4},{1,25},{... | collective-permute-start | bytes 835592 | tf_op jit(solution)/shard_map/ppermute | solution.py:384
  13.3 18.4 %collective-permute-start.3 = (bf16[544,256]{1,0:T(8,128)(2,1)S(1)}, bf16[544,256]{1,0:T(8,128)(2,1)S(1)}, u32[]{:S(2)}, u32[]{:S(2)}) collective-permute-start(bf16[544,256]{1,0:T(8,128)(2,1)S(1)} %get-tuple-element.20.refs_0_.pack_ref), channel_id=1, source_target_pairs={{0,16},{4,20},{8,24},{12,28},{16,0},{20,4},{24,8},{28,12},{1,17},{... | collective-permute-start | bytes 835592 | tf_op jit(solution)/shard_map/ppermute | solution.py:384
  13.8 17.9 %collective-permute-start.2 = (bf16[544,256]{1,0:T(8,128)(2,1)S(1)}, bf16[544,256]{1,0:T(8,128)(2,1)S(1)}, u32[]{:S(2)}, u32[]{:S(2)}) collective-permute-start(bf16[544,256]{1,0:T(8,128)(2,1)S(1)} %get-tuple-element.20.refs_0_.pack_ref), channel_id=1, source_target_pairs={{0,8},{4,12},{8,0},{12,4},{16,24},{20,28},{24,16},{28,20},{1,9},{5... | collective-permute-start | bytes 835592 | tf_op jit(solution)/shard_map/ppermute | solution.py:384
  14.3 5.8 %collective-permute-start.1 = (bf16[64,256]{1,0:T(8,128)(2,1)S(1)}, bf16[64,256]{1,0:T(8,128)(2,1)S(1)}, u32[]{:S(2)}, u32[]{:S(2)}) collective-permute-start(bf16[64,256]{1,0:T(8,128)(2,1)S(1)} %get-tuple-element.22), channel_id=1, source_target_pairs={{1,0},{2,1},{3,2},{5,4},{6,5},{7,6},{9,8},{10,9},{11,10},{13,12},{... | collective-permute-start | bytes 98312 | tf_op jit(solution)/shard_map/ppermute | solution.py:389
  20.1 7.2 %collective-permute-start.7 = (bf16[128,256]{1,0:T(8,128)(2,1)S(1)}, bf16[128,256]{1,0:T(8,128)(2,1)S(1)}, u32[]{:S(2)}, u32[]{:S(2)}) collective-permute-start(bf16[128,256]{1,0:T(8,128)(2,1)S(1)} %constant_dynamic-update-slice_fusion.refs_4_.halo_ref), channel_id=1, source_target_pairs={{0,24},{4,28},{8,16},{12,20},{16,8},{20,12},{24,0},{28,4},{1,25},{... | collective-permute-start | bytes 196616 | tf_op jit(solution)/shard_map/ppermute | solution.py:384
  22.6 6.4 %collective-permute-start.6 = (bf16[128,256]{1,0:T(8,128)(2,1)S(1)}, bf16[128,256]{1,0:T(8,128)(2,1)S(1)}, u32[]{:S(2)}, u32[]{:S(2)}) collective-permute-start(bf16[128,256]{1,0:T(8,128)(2,1)S(1)} %constant_dynamic-update-slice_fusion.refs_4_.halo_ref), channel_id=1, source_target_pairs={{0,16},{4,20},{8,24},{12,28},{16,0},{20,4},{24,8},{28,12},{1,17},{... | collective-permute-start | bytes 196616 | tf_op jit(solution)/shard_map/ppermute | solution.py:384
  27.4 4.3 %collective-permute-start.5 = (bf16[128,256]{1,0:T(8,128)(2,1)S(1)}, bf16[128,256]{1,0:T(8,128)(2,1)S(1)}, u32[]{:S(2)}, u32[]{:S(2)}) collective-permute-start(bf16[128,256]{1,0:T(8,128)(2,1)S(1)} %constant_dynamic-update-slice_fusion.refs_4_.halo_ref), channel_id=1, source_target_pairs={{0,8},{4,12},{8,0},{12,4},{16,24},{20,28},{24,16},{28,20},{1,9},{5... | collective-permute-start | bytes 196616 | tf_op jit(solution)/shard_map/ppermute | solution.py:384
  28.9 16.2 %copy-start.7 = (bf16[27,256,256]{2,1,0:T(8,128)(2,1)S(1)}, bf16[27,256,256]{2,1,0:T(8,128)(2,1)}, u32[]{:S(2)}) copy-start(bf16[27,256,256]{2,1,0:T(8,128)(2,1)} %w_ref.3) | copy-start | bytes 10616836
  37.5 2.5 %collective-permute-start.8 = (f32[7,128,256]{2,1,0:T(8,128)S(1)}, f32[7,128,256]{2,1,0:T(8,128)S(1)}, u32[]{:S(2)}, u32[]{:S(2)}) collective-permute-start(f32[7,128,256]{2,1,0:T(8,128)S(1)} %get-tuple-element.24), channel_id=1, source_target_pairs={{0,4},{4,0},{8,12},{12,8},{16,20},{20,16},{24,28},{28,24},{1,5},{5... | collective-permute-start | bytes 2752520 | tf_op jit(solution)/shard_map/ppermute | solution.py:384
  40.7 12.5 %collective-permute-start.9 = (f32[7,32,256]{2,1,0:T(8,128)S(1)}, f32[7,32,256]{2,1,0:T(8,128)S(1)}, u32[]{:S(2)}, u32[]{:S(2)}) collective-permute-start(f32[7,32,256]{2,1,0:T(8,128)S(1)} %get-tuple-element.26), channel_id=1, source_target_pairs={{0,1},{1,0},{2,3},{3,2},{4,5},{5,4},{6,7},{7,6},{8,9},{9,8},{10,11... | collective-permute-start | bytes 688136 | tf_op jit(solution)/shard_map/ppermute | solution.py:384
  42.3 19.2 %collective-permute-start.10 = (f32[7,32,256]{2,1,0:T(8,128)S(1)}, f32[7,32,256]{2,1,0:T(8,128)S(1)}, u32[]{:S(2)}, u32[]{:S(2)}) collective-permute-start(f32[7,32,256]{2,1,0:T(8,128)S(1)} %get-tuple-element.27), channel_id=1, source_target_pairs={{0,2},{1,3},{2,0},{3,1},{4,6},{5,7},{6,4},{7,5},{8,10},{9,11},{10,... | collective-permute-start | bytes 688136 | tf_op jit(solution)/shard_map/ppermute | solution.py:384
  43.4 18.1 %collective-permute-start.11 = (f32[7,32,256]{2,1,0:T(8,128)S(1)}, f32[7,32,256]{2,1,0:T(8,128)S(1)}, u32[]{:S(2)}, u32[]{:S(2)}) collective-permute-start(f32[7,32,256]{2,1,0:T(8,128)S(1)} %get-tuple-element.28), channel_id=1, source_target_pairs={{0,3},{1,2},{2,1},{3,0},{4,7},{5,6},{6,5},{7,4},{8,11},{9,10},{10,... | collective-permute-start | bytes 688136 | tf_op jit(solution)/shard_map/ppermute | solution.py:384
  45.1 41.9 %copy-start.4 = (s32[1,64]{1,0:T(1,128)S(1)}, s32[1,64]{1,0:T(1,128)}, u32[]{:S(2)}) copy-start(s32[1,64]{1,0:T(1,128)} %up_ref.1) | copy-start | bytes 772
  45.1 41.9 %copy-start.6 = (s32[1,64]{1,0:T(1,128)S(1)}, s32[1,64]{1,0:T(1,128)}, u32[]{:S(2)}) copy-start(s32[1,64]{1,0:T(1,128)} %down_ref.1) | copy-start | bytes 772
  61.6 7.3 %collective-permute-start.14 = (bf16[7,32,256]{2,1,0:T(8,128)(2,1)S(1)}, bf16[7,32,256]{2,1,0:T(8,128)(2,1)S(1)}, u32[]{:S(2)}, u32[]{:S(2)}) collective-permute-start(bf16[7,32,256]{2,1,0:T(8,128)(2,1)S(1)} %total.1), channel_id=1, source_target_pairs={{0,3},{1,2},{2,1},{3,0},{4,7},{5,6},{6,5},{7,4},{8,11},{9,10},{10,... | collective-permute-start | bytes 344072 | tf_op jit(solution)/shard_map/ppermute | solution.py:384
  64.1 11.6 %collective-permute-start.13 = (bf16[7,32,256]{2,1,0:T(8,128)(2,1)S(1)}, bf16[7,32,256]{2,1,0:T(8,128)(2,1)S(1)}, u32[]{:S(2)}, u32[]{:S(2)}) collective-permute-start(bf16[7,32,256]{2,1,0:T(8,128)(2,1)S(1)} %total.1), channel_id=1, source_target_pairs={{0,2},{1,3},{2,0},{3,1},{4,6},{5,7},{6,4},{7,5},{8,10},{9,11},{10,... | collective-permute-start | bytes 344072 | tf_op jit(solution)/shard_map/ppermute | solution.py:384
  68.8 7.0 %collective-permute-start.12 = (bf16[7,32,256]{2,1,0:T(8,128)(2,1)S(1)}, bf16[7,32,256]{2,1,0:T(8,128)(2,1)S(1)}, u32[]{:S(2)}, u32[]{:S(2)}) collective-permute-start(bf16[7,32,256]{2,1,0:T(8,128)(2,1)S(1)} %total.1), channel_id=1, source_target_pairs={{0,1},{1,0},{2,3},{3,2},{4,5},{5,4},{6,7},{7,6},{8,9},{9,8},{10,11... | collective-permute-start | bytes 344072 | tf_op jit(solution)/shard_map/ppermute | solution.py:384
  75.8 14.4 %collective-permute-start.22 = (bf16[4,7,32,256]{3,2,1,0:T(8,128)(2,1)S(1)}, bf16[4,7,32,256]{3,2,1,0:T(8,128)(2,1)S(1)}, u32[]{:S(2)}, u32[]{:S(2)}) collective-permute-start(bf16[4,7,32,256]{3,2,1,0:T(8,128)(2,1)S(1)} %pad_maximum_fusion.after_ref.refs_0_), channel_id=1, source_target_pairs={{0,24},{4,28},{8,16},{12,20},{16,8},{20,12},{24,0},{28,4},{1,25},{... | collective-permute-start | bytes 1376264 | tf_op jit(solution)/shard_map/ppermute | solution.py:384
  78.3 17.3 %collective-permute-start.20 = (bf16[4,7,32,256]{3,2,1,0:T(8,128)(2,1)S(1)}, bf16[4,7,32,256]{3,2,1,0:T(8,128)(2,1)S(1)}, u32[]{:S(2)}, u32[]{:S(2)}) collective-permute-start(bf16[4,7,32,256]{3,2,1,0:T(8,128)(2,1)S(1)} %pad_maximum_fusion.after_ref.refs_0_), channel_id=1, source_target_pairs={{0,16},{4,20},{8,24},{12,28},{16,0},{20,4},{24,8},{28,12},{1,17},{... | collective-permute-start | bytes 1376264 | tf_op jit(solution)/shard_map/ppermute | solution.py:384
  78.8 16.9 %collective-permute-start.18 = (bf16[4,7,32,256]{3,2,1,0:T(8,128)(2,1)S(1)}, bf16[4,7,32,256]{3,2,1,0:T(8,128)(2,1)S(1)}, u32[]{:S(2)}, u32[]{:S(2)}) collective-permute-start(bf16[4,7,32,256]{3,2,1,0:T(8,128)(2,1)S(1)} %pad_maximum_fusion.after_ref.refs_0_), channel_id=1, source_target_pairs={{0,8},{4,12},{8,0},{12,4},{16,24},{20,28},{24,16},{28,20},{1,9},{5... | collective-permute-start | bytes 1376264 | tf_op jit(solution)/shard_map/ppermute | solution.py:384
  79.3 6.1 %collective-permute-start.15 = (f32[64,256]{1,0:T(8,128)S(1)}, f32[64,256]{1,0:T(8,128)S(1)}, u32[]{:S(2)}, u32[]{:S(2)}) collective-permute-start(f32[64,256]{1,0:T(8,128)S(1)} %get-tuple-element.32), channel_id=1, source_target_pairs={{1,0},{2,1},{3,2},{5,4},{6,5},{7,6},{9,8},{10,9},{11,10},{13,12},{... | collective-permute-start | bytes 196616 | tf_op jit(solution)/shard_map/ppermute | solution.py:389
  80.6 6.4 %collective-permute-start.16 = (f32[64,256]{1,0:T(8,128)S(1)}, f32[64,256]{1,0:T(8,128)S(1)}, u32[]{:S(2)}, u32[]{:S(2)}) collective-permute-start(f32[64,256]{1,0:T(8,128)S(1)} %get-tuple-element.33), channel_id=1, source_target_pairs={{0,1},{1,2},{2,3},{4,5},{5,6},{6,7},{8,9},{9,10},{10,11},{12,13},{... | collective-permute-start | bytes 196616 | tf_op jit(solution)/shard_map/ppermute | solution.py:389
  85.5 17.1 %collective-permute-start.17 = (bf16[4,7,32,256]{3,2,1,0:T(8,128)(2,1)S(1)}, bf16[4,7,32,256]{3,2,1,0:T(8,128)(2,1)S(1)}, u32[]{:S(2)}, u32[]{:S(2)}) collective-permute-start(bf16[4,7,32,256]{3,2,1,0:T(8,128)(2,1)S(1)} %pad_maximum_fusion.after_ref.refs_0_), channel_id=1, source_target_pairs={{0,4},{4,0},{8,12},{12,8},{16,20},{20,16},{24,28},{28,24},{1,5},{5... | collective-permute-start | bytes 1376264 | tf_op jit(solution)/shard_map/ppermute | solution.py:384
  90.2 12.4 %collective-permute-start.23 = (bf16[4,7,32,256]{3,2,1,0:T(8,128)(2,1)S(1)}, bf16[4,7,32,256]{3,2,1,0:T(8,128)(2,1)S(1)}, u32[]{:S(2)}, u32[]{:S(2)}) collective-permute-start(bf16[4,7,32,256]{3,2,1,0:T(8,128)(2,1)S(1)} %collective-permute-done.22.refs_6_), channel_id=1, source_target_pairs={{0,4},{4,0},{8,12},{12,8},{16,20},{20,16},{24,28},{28,24},{1,5},{5... | collective-permute-start | bytes 1376264 | tf_op jit(solution)/shard_map/ppermute | solution.py:384
  95.6 7.0 %collective-permute-start.21 = (bf16[4,7,32,256]{3,2,1,0:T(8,128)(2,1)S(1)}, bf16[4,7,32,256]{3,2,1,0:T(8,128)(2,1)S(1)}, u32[]{:S(2)}, u32[]{:S(2)}) collective-permute-start(bf16[4,7,32,256]{3,2,1,0:T(8,128)(2,1)S(1)} %collective-permute-done.20.refs_4_), channel_id=1, source_target_pairs={{0,4},{4,0},{8,12},{12,8},{16,20},{20,16},{24,28},{28,24},{1,5},{5... | collective-permute-start | bytes 1376264 | tf_op jit(solution)/shard_map/ppermute | solution.py:384
  95.7 7.0 %collective-permute-start.19 = (bf16[4,7,32,256]{3,2,1,0:T(8,128)(2,1)S(1)}, bf16[4,7,32,256]{3,2,1,0:T(8,128)(2,1)S(1)}, u32[]{:S(2)}, u32[]{:S(2)}) collective-permute-start(bf16[4,7,32,256]{3,2,1,0:T(8,128)(2,1)S(1)} %collective-permute-done.18.refs_2_), channel_id=1, source_target_pairs={{0,4},{4,0},{8,12},{12,8},{16,20},{20,16},{24,28},{28,24},{1,5},{5... | collective-permute-start | bytes 1376264 | tf_op jit(solution)/shard_map/ppermute | solution.py:384

commit v3 on v2

v3 whole, which is shorter than its diff:
```python
import functools
import math

import jax
import jax.numpy as jnp
from jax import lax
from jax.experimental import pallas as pl
from jax.experimental.pallas import tpu as pltpu
from jax.sharding import PartitionSpec as P

BF = jnp.bfloat16
F32 = jnp.float32
VMEM_LIMIT = 32 * 1024 * 1024
PREP_LIMIT = 60 * 1024 * 1024
VMEM = pl.BlockSpec(memory_space=pltpu.VMEM)
SMEM = pl.BlockSpec(memory_space=pltpu.SMEM)
ANY = pl.BlockSpec(memory_space=pl.ANY)
HBM = pl.BlockSpec(memory_space=pltpu.HBM)
TOKEN = jax.ShapeDtypeStruct((8, 128), F32)


def params(limit=VMEM_LIMIT):
    return pltpu.CompilerParams(vmem_limit_bytes=limit)


def cost():
    return pl.CostEstimate(flops=100_000_000, bytes_accessed=100_000, transcendentals=0)


def dot(a, b):
    return jnp.dot(a, b, preferred_element_type=F32)


def split(value, terms):
    parts = []
    for _ in range(terms):
        part = value.astype(BF)
        parts.append(part)
        value = value - part.astype(F32)
    return parts


def prep_kernel(live_ref, x_hbm, dy_hbm, map_hbm, up_hbm, down_hbm, pack_ref, *scratch):
    x_ref, dy_ref, map_ref, up_ref, down_ref, map_scr, sems = scratch
    sources = (x_hbm, dy_hbm, map_hbm, up_hbm, down_hbm)
    targets = (x_ref, dy_ref, map_ref, up_ref, down_ref)
    copies = [pltpu.make_async_copy(a, b, sems.at[i]) for i, (a, b) in enumerate(zip(sources, targets))]
    for copy in copies:
        copy.start()
    rows, width = x_ref.shape
    offsets = map_ref.shape[0]
    halo = up_ref.shape[1]
    keep = lax.broadcasted_iota(jnp.int32, (rows, width), 0) < live_ref[0]
    map_scr[...] = jnp.full(map_scr.shape, rows + 2 * halo, jnp.int32)
    for copy in copies:
        copy.wait()
    pack_ref[0:rows] = jnp.where(keep, x_ref[...].astype(F32), 0.0).astype(BF)
    pack_ref[rows : 2 * rows] = jnp.where(keep, dy_ref[...].astype(F32), 0.0).astype(BF)
    map_scr[0:offsets] = map_ref[...]
    map_scr[map_scr.shape[0] - 1 :, 0:halo] = up_ref[...]
    map_scr[map_scr.shape[0] - 1 :, halo : 2 * halo] = down_ref[...]
    slots = map_scr[...]
    pack_ref[2 * rows :] = jnp.where(slots > 256, 256 - slots, slots).astype(F32).astype(BF)


def prep(live, features, cotangent, kernel_map, send_up, send_down, map_rows):
    rows, width = features.shape
    return pl.pallas_call(
        prep_kernel,
        out_shape=jax.ShapeDtypeStruct((2 * rows + map_rows, width), BF),
        in_specs=[SMEM] + [HBM] * 5,
        out_specs=VMEM,
        scratch_shapes=[
            pltpu.VMEM((rows, width), BF),
            pltpu.VMEM((rows, width), BF),
            pltpu.VMEM(kernel_map.shape, jnp.int32),
            pltpu.VMEM(send_up.shape, jnp.int32),
            pltpu.VMEM(send_down.shape, jnp.int32),
            pltpu.VMEM((map_rows, rows), jnp.int32),
            pltpu.SemaphoreType.DMA((5,)),
        ],
        compiler_params=params(PREP_LIMIT),
        name="prep",
    )(live, features, cotangent, kernel_map, send_up, send_down)


def pick_kernel(rows, *refs):
    *packs, up_ref, down_ref = refs
    halo = up_ref.shape[0] // len(packs)
    iota = lax.broadcasted_iota(jnp.int32, (rows, 2 * halo), 0)
    for s, pack in enumerate(packs):
        sent = pack[2 * rows :].astype(F32).astype(jnp.int32)[-1:, 0 : 2 * halo]
        chosen = (iota == sent).astype(F32).astype(BF)
        picked = lax.dot_general(chosen, pack[0:rows], (((0,), (0,)), ((), ())), preferred_element_type=F32)
        up_ref[s * halo : (s + 1) * halo] = picked[0:halo].astype(BF)
        down_ref[s * halo : (s + 1) * halo] = picked[halo:].astype(BF)


def pick(packs, rows, halo, after):
    shape = jax.ShapeDtypeStruct((len(packs) * halo, packs[0].shape[1]), BF)
    return pl.pallas_call(
        functools.partial(pick_kernel_after, rows),
        out_shape=(shape, shape),
        in_specs=[VMEM] * len(packs) + [ANY],
        out_specs=(VMEM, VMEM),
        compiler_params=params(),
        cost_estimate=cost(),
        name="pick",
    )(*packs, after)


def pick_kernel_after(rows, *refs):
    pick_kernel(rows, *refs[:-3], *refs[-2:])


def decoded(code):
    code = code.astype(F32).astype(jnp.int32)
    return jnp.where(code < 0, 256 - code, code)


def backward_kernel(start, end, pack_ref, w_ref, before_ref, *refs):
    outs, (maps, grad_acc, chosen, terms) = refs[:-4], refs[-4:]
    step = pl.program_id(0)
    offsets, width, _ = w_ref.shape
    slots = grad_acc.shape[0]
    rows = chosen.shape[1] // offsets

    @pl.when(step == 0)
    def _():
        maps[...] = decoded(pack_ref[2 * rows :])
        grad_acc[...] = before_ref[...] if start else jnp.zeros_like(grad_acc)

    dy = pack_ref[rows : 2 * rows]
    slot_down = lax.broadcasted_iota(jnp.int32, (slots, rows), 0)
    for i in range(offsets):
        row = maps[pl.ds((start + step) * offsets + i, 1), :]
        chosen[:, i * rows : (i + 1) * rows] = (slot_down == row).astype(F32).astype(BF)
        back = lax.dot_general(dy, w_ref[i], (((1,), (1,)), ((), ())), preferred_element_type=F32)
        for t, part in enumerate(split(back, 2)):
            terms[t, i * rows : (i + 1) * rows] = part
    grad_acc[...] += dot(chosen[...], terms[0]) + dot(chosen[...], terms[1])

    @pl.when(step == end - start - 1)
    def _():
        at = 0
        for out in outs:
            out[...] = grad_acc[at : at + out.shape[0]]
            at += out.shape[0]


def whole(shape):
    return pl.BlockSpec(shape, lambda k: (0,) * len(shape))


def backward(pack, weights, rows, halo, start, end, per_step, before):
    offsets, width, _ = weights.shape
    slots = rows + 2 * halo
    sizes = (rows, halo, halo) if end * per_step == offsets else (slots,)
    return pl.pallas_call(
        functools.partial(backward_kernel, start, end),
        grid=(end - start,),
        out_shape=tuple(jax.ShapeDtypeStruct((n, width), F32) for n in sizes),
        in_specs=[
            whole(pack.shape),
            pl.BlockSpec((per_step, width, width), lambda k: (start + k, 0, 0)),
            whole(before.shape) if start else ANY,
        ],
        out_specs=tuple(whole((n, width)) for n in sizes),
        scratch_shapes=[
            pltpu.VMEM((pack.shape[0] - 2 * rows, rows), jnp.int32),
            pltpu.VMEM((slots, width), F32),
            pltpu.VMEM((slots, per_step * rows), BF),
            pltpu.VMEM((2, per_step * rows, width), BF),
        ],
        compiler_params=params(),
        cost_estimate=cost(),
        name="backward",
    )(pack, weights, before)


def forward_kernel(live_ref, pack_ref, lower_ref, upper_ref, w_ref, after_ref, out_ref, token_ref, table, maps, out_acc, picked):
    step = pl.program_id(0)
    offsets = w_ref.shape[0]
    rows, width = out_ref.shape
    slots = table.shape[0]

    @pl.when(step == 0)
    def _():
        maps[...] = decoded(pack_ref[2 * rows :])
        table[0:rows] = pack_ref[0:rows]
        halo = (slots - rows) // 2
        table[rows : rows + halo] = lower_ref[0:halo]
        table[rows + halo :] = upper_ref[0:halo]
        out_acc[...] = jnp.zeros_like(out_acc)

    along = lax.broadcasted_iota(jnp.int32, (rows, 128), 1)
    for i in range(offsets):
        row = maps[pl.ds(step * offsets + i, 1), :]
        column = jnp.transpose(jnp.broadcast_to(row, (128, rows)))
        chosen = jnp.concatenate(
            [(along + 128 * b == column).astype(F32).astype(BF) for b in range(slots // 128)], axis=1
        )
        picked[:, i * width : (i + 1) * width] = dot(chosen, table[...]).astype(BF)
    out_acc[...] += dot(picked[...], w_ref[...].reshape(offsets * width, width))

    @pl.when(step == pl.num_programs(0) - 1)
    def _():
        keep = lax.broadcasted_iota(jnp.int32, (rows, width), 0) < live_ref[0]
        out_ref[...] = jnp.where(keep, out_acc[...], 0.0).astype(BF)
        token_ref[...] = jnp.zeros_like(token_ref)


def forward(live, pack, lower, upper, weights, rows, halo, after):
    offsets, width, _ = weights.shape
    slots = rows + 2 * halo
    per_step = 3 if offsets % 3 == 0 else 1
    return pl.pallas_call(
        forward_kernel,
        grid=(offsets // per_step,),
        out_shape=(jax.ShapeDtypeStruct((rows, width), BF), TOKEN),
        in_specs=[
            SMEM,
            whole(pack.shape),
            whole(lower.shape),
            whole(upper.shape),
            pl.BlockSpec((per_step, width, width), lambda k: (k, 0, 0)),
            ANY,
        ],
        out_specs=(whole((rows, width)), whole(TOKEN.shape)),
        scratch_shapes=[
            pltpu.VMEM((slots, width), BF),
            pltpu.VMEM((pack.shape[0] - 2 * rows, rows), jnp.int32),
            pltpu.VMEM((rows, width), F32),
            pltpu.VMEM((rows, per_step * width), BF),
        ],
        compiler_params=params(),
        cost_estimate=cost(),
        name="forward",
    )(live, pack, lower, upper, weights, after)


def chosen_slots(maps, s, at, low, high, rows):
    iota = lax.broadcasted_iota(jnp.int32, (high - low, rows), 0) + low
    return (iota == maps[s, pl.ds(at, 1), :]).astype(F32).astype(BF)


def wgrad_own_kernel(sources, place_ref, *refs):
    packs = refs[:sources]
    picked_ref, dys, maps, tables = refs[sources + 1 :]
    count, width, _ = picked_ref.shape
    rows = dys.shape[0] // sources
    for s in range(sources):
        tables[:, s * rows : (s + 1) * rows] = jnp.transpose(packs[s][0:rows])
        dys[s * rows : (s + 1) * rows] = packs[s][rows : 2 * rows]
        maps[s] = decoded(packs[s][2 * rows :])

    def offset(j, carry):
        for s in range(sources):
            chosen = chosen_slots(maps, s, place_ref[0] * count + j, 0, rows, rows)
            picked_ref[j, :, s * rows : (s + 1) * rows] = dot(tables[:, s * rows : (s + 1) * rows], chosen).astype(BF)
        return carry

    lax.fori_loop(0, count, offset, 0)


def wgrad_own(place, packs, count, rows, after):
    sources, width = len(packs), packs[0].shape[1]
    return pl.pallas_call(
        functools.partial(wgrad_own_kernel, sources),
        out_shape=(
            jax.ShapeDtypeStruct((count, width, sources * rows), BF),
            jax.ShapeDtypeStruct((sources * rows, width), BF),
            jax.ShapeDtypeStruct((sources, packs[0].shape[0] - 2 * rows, rows), jnp.int32),
        ),
        in_specs=[SMEM] + [VMEM] * sources + [ANY],
        out_specs=(VMEM, VMEM, VMEM),
        scratch_shapes=[pltpu.VMEM((width, sources * rows), BF)],
        compiler_params=params(),
        cost_estimate=cost(),
        name="wgrad_own",
    )(place, *packs, after)


def wgrad_kernel(place_ref, picked_ref, dys, maps, lower_ref, upper_ref, keep_ref, send_ref, tables, picked):
    count, half, width = keep_ref.shape
    sources, _, rows = maps.shape
    halo = lower_ref.shape[0] // sources
    core = place_ref[1]
    for s in range(sources):
        both = jnp.concatenate([ref[s * halo : (s + 1) * halo].astype(F32) for ref in (lower_ref, upper_ref)], axis=0)
        tables[:, s * 2 * halo : (s + 1) * 2 * halo] = jnp.transpose(both).astype(BF)

    def offset(j, carry):
        for s in range(sources):
            chosen = chosen_slots(maps, s, place_ref[0] * count + j, rows, rows + 2 * halo, rows)
            far = dot(tables[:, s * 2 * halo : (s + 1) * 2 * halo], chosen)
            near = picked_ref[j, :, s * rows : (s + 1) * rows].astype(F32)
            picked[:, s * rows : (s + 1) * rows] = (far + near).astype(BF)
        send_ref[j] = dot(picked[pl.ds(pl.multiple_of((1 - core) * half, half), half), :], dys[...])
        keep_ref[j] = dot(picked[pl.ds(pl.multiple_of(core * half, half), half), :], dys[...])
        return carry

    lax.fori_loop(0, count, offset, 0)


def wgrad(place, picked, dys, maps, lower, upper):
    count, width, columns = picked.shape
    sources = maps.shape[0]
    shape = jax.ShapeDtypeStruct((count, width // 2, width), F32)
    return pl.pallas_call(
        wgrad_kernel,
        out_shape=(shape, shape),
        in_specs=[SMEM] + [VMEM] * 5,
        out_specs=(VMEM, VMEM),
        scratch_shapes=[
            pltpu.VMEM((width, 2 * lower.shape[0]), BF),
            pltpu.VMEM((width, columns), BF),
        ],
        compiler_params=params(),
        cost_estimate=cost(),
        name="wgrad",
    )(place, picked, dys, maps, lower, upper)


def power(exponent):
    value = jnp.ones(exponent.shape, F32)
    size = jnp.abs(exponent)
    for bit in range(7):
        factor = jnp.where(exponent < 0, 0.5 ** (1 << bit), 2.0 ** (1 << bit))
        value = value * jnp.where((size >> bit) & 1 == 1, factor, 1.0)
    return value


def blocks_kernel(place_ref, keep_ref, got_ref, mine_ref, *refs):
    coded_refs, exponents = refs[:-1], refs[-1]
    count, block, width = mine_ref.shape
    for m in range(len(coded_refs) + 1):
        at = pl.ds(pl.multiple_of((place_ref[2] ^ m) * block, block), block)
        if m == 0:
            mine_ref[...] = keep_ref[:, at, :] + got_ref[:, at, :]
            continue
        exponents[...] = jnp.zeros_like(exponents)
        for j in range(count):
            value = keep_ref[j, at, :] + got_ref[j, at, :]
            largest = jnp.max(jnp.abs(value), axis=0, keepdims=True)
            exponent = jnp.ceil(jnp.log(jnp.maximum(largest, 2.0**-100)) * (1.0 / math.log(2.0)))
            exponent = jnp.clip(exponent, -100.0, 100.0).astype(jnp.int32) - 15
            exponents[j : j + 1, :] = exponent
            scaled = jnp.round(jnp.clip(value * power(-exponent), -32767.0, 32767.0))
            coded_refs[m - 1][j * block : (j + 1) * block] = scaled.astype(jnp.int32).astype(jnp.int16)
        coded_refs[m - 1][count * block :] = exponents[...].astype(jnp.int16)


def blocks(place, keep, got, parts):
    count, half, width = keep.shape
    block = half // parts
    extra = -(-count // 16) * 16
    return pl.pallas_call(
        blocks_kernel,
        out_shape=(
            jax.ShapeDtypeStruct((count, block, width), F32),
            *(jax.ShapeDtypeStruct((count * block + extra, width), jnp.int16),) * (parts - 1),
        ),
        in_specs=[SMEM, VMEM, VMEM],
        out_specs=(VMEM,) * parts,
        scratch_shapes=[pltpu.VMEM((extra, width), jnp.int32)],
        compiler_params=params(),
        cost_estimate=cost(),
        name="blocks",
    )(place, keep, got)


def total_kernel(scale, mine_ref, *refs):
    *coded_refs, _, _, out_ref = refs
    count, block, width = mine_ref.shape
    powers = [power(ref[count * block :].astype(jnp.int32)) for ref in coded_refs]
    for j in range(count):
        total = mine_ref[j]
        for ref, factor in zip(coded_refs, powers):
            value = ref[j * block : (j + 1) * block].astype(jnp.int32).astype(F32)
            total = total + value * factor[j : j + 1, :]
        out_ref[j] = (total * scale).astype(BF)


def scaled_total(mine, coded, scale, after):
    return pl.pallas_call(
        functools.partial(total_kernel, scale),
        out_shape=jax.ShapeDtypeStruct(mine.shape, BF),
        in_specs=[VMEM] * (len(coded) + 1) + [ANY] * 2,
        out_specs=VMEM,
        compiler_params=params(),
        cost_estimate=cost(),
        name="total",
    )(mine, *coded, *after)


def final_kernel(live_ref, own_ref, back_up_ref, back_down_ref, up_ref, down_ref, after_ref, out_ref, token_ref):
    rows, width = own_ref.shape
    halo = up_ref.shape[1]
    total = own_ref[...]
    iota = lax.broadcasted_iota(jnp.int32, (rows, halo), 0)
    for index_ref, back_ref in ((up_ref, back_up_ref), (down_ref, back_down_ref)):
        chosen = (iota == index_ref[...]).astype(F32).astype(BF)
        for part in split(back_ref[...], 3):
            total = total + dot(chosen, part)
    keep = lax.broadcasted_iota(jnp.int32, (rows, width), 0) < live_ref[0]
    out_ref[...] = jnp.where(keep, total, 0.0).astype(BF)
    token_ref[...] = jnp.zeros_like(token_ref)


def final(live, own_grad, back_up, back_down, send_up, send_down, after):
    return pl.pallas_call(
        final_kernel,
        out_shape=(jax.ShapeDtypeStruct(own_grad.shape, BF), TOKEN),
        in_specs=[SMEM] + [VMEM] * 5 + [ANY],
        out_specs=(VMEM, VMEM),
        compiler_params=params(),
        name="final",
    )(live, own_grad, back_up, back_down, send_up, send_down, after)


def line_kernel(count, *refs):
    for m in range(count):
        refs[-1][m] = refs[m][...]


def line(blocks, after):
    if len(blocks) == 1:
        return blocks[0][None]
    return pl.pallas_call(
        functools.partial(line_kernel, len(blocks)),
        out_shape=jax.ShapeDtypeStruct((len(blocks), *blocks[0].shape), BF),
        in_specs=[VMEM] * len(blocks) + [ANY] * len(after),
        out_specs=VMEM,
        compiler_params=params(),
        cost_estimate=cost(),
        name="line",
    )(*blocks, *after)


def assemble_kernel(marks, parts, groups, place_ref, *refs):
    out_ref, sems = refs[-2:]
    offsets = out_ref.shape[0]
    _, count, block, _ = refs[0].shape
    short = offsets - (groups - 1) * count

    def each(act):
        for index, (m, o, masks) in enumerate(marks):
            group = place_ref[0] ^ m
            for part, mask in enumerate(masks):
                row = pl.multiple_of(((place_ref[1] ^ o) * parts + (place_ref[2] ^ mask)) * block, block)
                source = refs[index].at[part]

                def copy(lo, hi, sem):
                    target = out_ref.at[pl.ds(group * count + lo, hi - lo), pl.ds(row, block)]
                    return pltpu.make_async_copy(source.at[lo:hi], target, sems.at[index, part, sem])

                getattr(copy(0, short, 0), act)()
                if short < count:
                    pl.when(group < groups - 1)(getattr(copy(short, count, 1), act))

    each("start")
    each("wait")


def assemble(place, pieces, marks, parts, groups, offsets, width):
    return pl.pallas_call(
        functools.partial(assemble_kernel, marks, parts, groups),
        out_shape=jax.ShapeDtypeStruct((offsets, width, width), BF),
        in_specs=[SMEM] + [ANY] * len(pieces),
        out_specs=ANY,
        scratch_shapes=[pltpu.SemaphoreType.DMA((len(pieces), parts, 2))],
        compiler_params=params(),
        name="assemble",
    )(place, *pieces)


def assemble_plain(place, pieces, marks, parts, groups, offsets, width):
    _, count, block, _ = pieces[0].shape
    total = jnp.zeros((groups * count, width, width), BF)
    for piece, (m, o, masks) in zip(pieces, marks):
        for part, mask in enumerate(masks):
            row = ((place[1] ^ o) * parts + (place[2] ^ mask)) * block
            total = lax.dynamic_update_slice(total, piece[part], ((place[0] ^ m) * count, row, 0))
    return total[:offsets]


def swap(value, axis, mask):
    return lax.ppermute(value, axis, [(i, i ^ mask) for i in range(lax.axis_size(axis))])


def passed_along(value, axis, steps):
    count = lax.axis_size(axis)
    return lax.ppermute(value, axis, [(i, i + steps) for i in range(max(0, -steps), min(count, count - steps))])


def SPLITS(parts):
    return [(0,), tuple(range(1, parts))]


def shards(features, weights, cotangent, kernel_map, live, send_up, send_down):
    rows, width = features.shape
    offsets, halo = weights.shape[0], send_up.shape[1]
    groups = lax.axis_size("dp") // 2
    parts = lax.axis_size("space")
    count = -(-offsets // groups)
    map_rows = -(-(groups * count + 1) // 16) * 16
    dp, space = lax.axis_index("dp"), lax.axis_index("space")
    place = jnp.stack([dp // 2, dp % 2, space]).astype(jnp.int32)

    pack = prep(live, features, cotangent, kernel_map, send_up, send_down, map_rows)
    packs = [pack] + [swap(pack, "dp", 2 * m) for m in range(1, groups)]
    per_step = 3 if offsets % 3 == 0 else 1
    own_grad, low_grad, high_grad = backward(pack, weights, rows, halo, 0, offsets // per_step, per_step, pack)
    back_up = passed_along(low_grad, "space", -1)
    back_down = passed_along(high_grad, "space", 1)

    up_rows, down_rows = pick(packs, rows, halo, low_grad)
    lower = passed_along(up_rows, "space", 1)
    upper = passed_along(down_rows, "space", -1)
    picked, dys, maps = wgrad_own(place, packs, count, rows, up_rows)
    keep, send = wgrad(place, picked, dys, maps, lower, upper)
    mine, *coded = blocks(place, keep, swap(send, "dp", 1), parts)
    out_features, token = forward(live, pack, lower, upper, weights, rows, halo, mine)
    grad_features, grad_token = final(live, own_grad, back_up, back_down, send_up, send_down, token)
    scale = 1.0 / math.sqrt(rows * lax.axis_size("dp") * parts)
    rounded = scaled_total(mine, [swap(block, "space", m + 1) for m, block in enumerate(coded)], scale, (token, grad_token))

    in_line = [rounded] + [swap(rounded, "space", m) for m in range(1, parts)]
    pieces, marks = [], []
    for masks in SPLITS(parts):
        lines = line([in_line[m] for m in masks], pieces[2::2][-groups:])
        for m in range(groups):
            piece = swap(lines, "dp", 2 * m) if m else lines
            pieces += [piece, swap(piece, "dp", 1)]
            marks += [(m, 0, masks), (m, 1, masks)]
    dense = rounded.shape[1] % 16 == 0 and groups * count - offsets < count
    put = assemble if dense else assemble_plain
    grad_weights = put(place, pieces, marks, parts, groups, offsets, width)
    return (out_features, grad_features, grad_weights)


def solution(mesh):
    placed = (
        P(("dp", "space"), None),
        P(),
        P(("dp", "space"), None),
        P(None, ("dp", "space")),
        P(("dp", "space")),
        P(("dp", "space"), None),
        P(("dp", "space"), None),
    )
    return jax.shard_map(
        shards,
        mesh=mesh,
        in_specs=placed,
        out_specs=(P(("dp", "space"), None), P(("dp", "space"), None), P()),
        check_vma=False,
    )
```

time: 106 us -> 95.4 us (0.900)
  waiting for transfers between devices: 38.7 us -> 26.9 us
  Pallas kernels: 25.6 us -> 30.3 us
  starting transfers between devices: 35.8 us -> 33.5 us
    ppermute x4, waiting for transfers between devices: 6.37 us -> 0.01 us  [passed_along(): lax.ppermute(value, axis, [(i, i + steps) for i in range(max(0, -steps),...]
    ppermute x20 -> x24, waiting for transfers between devices: 32.3 us -> 26.9 us  [swap(): lax.ppermute(value, axis, [(i, i ^ mask) for i in range(lax.axis_size(axi...]
    pallas_call x5 -> x8, Pallas kernels: 18 us -> 22.5 us  [the longest x1 7.93 us: backward(): pl.pallas_call(functools.partial(backward_kernel, start, end), grid=(end...]
    ppermute x4, starting transfers between devices: 12 us -> 9.71 us  [passed_along(): lax.ppermute(value, axis, [(i, i + steps) for i in range(max(0, -steps),...]
    unnamed x17 -> x12, local copies, waits for them, and re-layouts: 3.88 us -> 2.98 us
    ppermute x20 -> x24, starting transfers between devices: 23.8 us -> 23.8 us  [swap(): lax.ppermute(value, axis, [(i, i ^ mask) for i in range(lax.axis_size(axi...]
  transfers between devices with their start and end apart: 24 -> 28, of which waited for: 11 -> 11; matrix products, arithmetic and copies ran while one was open for 0% -> 0% of each run, Pallas kernels for 15% -> 20%
where the time goes in v3:
time: 95.4 us; the launch traced here: 95.1 us
  starting transfers between devices  33.5 us (35%)
  Pallas kernels  30.3 us (32%)
  waiting for transfers between devices  26.9 us (28%)
  local copies, waits for them, and re-layouts  2.98 us (3%)
  between operations  1.49 us (2%)
    ppermute x24, waiting for transfers between devices, swap(): lax.ppermute(value, axis, [(i, i ^ mask) for i in range(lax.axis_size(axi...  26.9 us
    ppermute x24, starting transfers between devices, swap(): lax.ppermute(value, axis, [(i, i ^ mask) for i in range(lax.axis_size(axi...  23.8 us
    ppermute x4, starting transfers between devices, passed_along(): lax.ppermute(value, axis, [(i, i + steps) for i in range(max(0, -steps),...  9.71 us
    pallas_call x1, Pallas kernels, backward(): pl.pallas_call(functools.partial(backward_kernel, start, end), grid=(end...  7.93 us
    pallas_call x1, Pallas kernels, forward(): pl.pallas_call(forward_kernel, grid=(offsets // per_step,), out_shape=(ja...  6.55 us
    pallas_call x1, Pallas kernels, wgrad(): pl.pallas_call(wgrad_kernel, out_shape=(shape, shape), in_specs=[SMEM] +...  4.74 us
    pallas_call x1, Pallas kernels, assemble(): pl.pallas_call(functools.partial(assemble_kernel, marks, parts, groups),...  3.47 us
    pallas_call x1, Pallas kernels, wgrad_own(): pl.pallas_call(functools.partial(wgrad_own_kernel, sources), out_shape=(j...  3.23 us
  transfers between devices with their start and end apart: 28, of which 11 were waited for; matrix products, arithmetic and copies ran while one was open for 0% of the time, Pallas kernels for 20%

profile of v3, /device:TPU:0, one launch (start us, length us, event | category | flops | bytes accessed | tf_op | source)
XLA Modules:
  0.0 95.1 jit_solution(7996301713969882971)
XLA Ops:
  1.3 1.8 %prep.1.pack_ref.before_ref.refs_0_ = bf16[544,256]{1,0:T(8,128)(2,1)} custom-call(s32[1]{0:T(128)S(6)} %copy.10.live_ref, bf16[256,256]{1,0:T(8,128)(2,1)} %x_hbm.1, bf16[256,256]{1,0:T(8,128)(2,1)} %dy_hbm.1, s32[27,256]{1,0:T(8,128)} %map_hbm.1, s32[1,64]{1,0:T(1,128)} %up_ref.1, s32[1,64]{1,0:T(1,128)} %down_ref.1), custom_call_target="tpu_custom_call" | custom-call | tf_op jit(solution)/shard_map/prep/pallas_call | solution.py:68
  3.1 4.0 %collective-permute-start.2 = (bf16[544,256]{1,0:T(8,128)(2,1)}, bf16[544,256]{1,0:T(8,128)(2,1)S(1)}, u32[]{:S(2)}, u32[]{:S(2)}) collective-permute-start(bf16[544,256]{1,0:T(8,128)(2,1)} %prep.1.pack_ref.before_ref.refs_0_), channel_id=1, source_target_pairs={{0,24},{4,28},{8,16},{12,20},{16,8},{20,12},{24,0},{28,4},{1,25},{... | collective-permute-start | bytes 835592 | tf_op jit(solution)/shard_map/ppermute | solution.py:489
  7.1 0.5 collective-permute-start.1
  7.6 0.1 collective-permute-start
  7.7 2.0 %copy-done = bf16[27,256,256]{2,1,0:T(8,128)(2,1)S(1)} copy-done((bf16[27,256,256]{2,1,0:T(8,128)(2,1)S(1)}, bf16[27,256,256]{2,1,0:T(8,128)(2,1)}, u32[]{:S(2)}) %copy-start) | copy-done | bytes 3538968
  9.7 1.0 %copy-done.2 = bf16[544,256]{1,0:T(8,128)(2,1)S(1)} copy-done((bf16[544,256]{1,0:T(8,128)(2,1)S(1)}, bf16[544,256]{1,0:T(8,128)(2,1)}, u32[]{:S(2)}) %copy-start.2) | copy-done | bytes 278552
  10.7 7.9 %backward.1 = (f32[256,256]{1,0:T(8,128)S(1)}, f32[64,256]{1,0:T(8,128)S(1)}, f32[64,256]{1,0:T(8,128)S(1)}) custom-call(bf16[544,256]{1,0:T(8,128)(2,1)S(1)} %copy-done.2, bf16[27,256,256]{2,1,0:T(8,128)(2,1)S(1)} %copy-done, bf16[544,256]{1,0:T(8,128)(2,1)S(1)} %copy-done.2), custom_call_target="tpu_custom_call" | custom-call | flops 100000000 | bytes 100000 | tf_op jit(solution)/shard_map/backward/pallas_call | solution.py:159
  18.6 1.3 %collective-permute-done.1.refs_2_ = bf16[544,256]{1,0:T(8,128)(2,1)S(1)} collective-permute-done((bf16[544,256]{1,0:T(8,128)(2,1)}, bf16[544,256]{1,0:T(8,128)(2,1)S(1)}, u32[]{:S(2)}, u32[]{:S(2)}) %collective-permute-start.1) | collective-permute-done | bytes 278560 | tf_op jit(solution)/shard_map/ppermute | solution.py:489
  19.9 0.3 collective-permute-done.refs_1_
  20.2 0.3 pick.1
  20.5 1.3 %collective-permute-start.4 = (bf16[256,256]{1,0:T(8,128)(2,1)S(1)}, bf16[256,256]{1,0:T(8,128)(2,1)S(1)}, u32[]{:S(2)}, u32[]{:S(2)}) collective-permute-start(bf16[256,256]{1,0:T(8,128)(2,1)S(1)} %get-tuple-element.23), channel_id=1, source_target_pairs={{1,0},{2,1},{3,2},{5,4},{6,5},{7,6},{9,8},{10,9},{11,10},{13,12},{... | collective-permute-start | bytes 393224 | tf_op jit(solution)/shard_map/ppermute | solution.py:494
  21.8 4.6 %collective-permute-start.3 = (bf16[256,256]{1,0:T(8,128)(2,1)S(1)}, bf16[256,256]{1,0:T(8,128)(2,1)S(1)}, u32[]{:S(2)}, u32[]{:S(2)}) collective-permute-start(bf16[256,256]{1,0:T(8,128)(2,1)S(1)} %get-tuple-element.22.refs_4_), channel_id=1, source_target_pairs={{0,1},{1,2},{2,3},{4,5},{5,6},{6,7},{8,9},{9,10},{10,11},{12,13},{... | collective-permute-start | bytes 393224 | tf_op jit(solution)/shard_map/ppermute | solution.py:494
  26.4 0.1 pad_add_fusion.place_ref
  26.4 3.2 %wgrad_own.1 = (bf16[7,256,1024]{2,1,0:T(8,128)(2,1)S(1)}, bf16[1024,256]{1,0:T(8,128)(2,1)S(1)}, s32[4,32,256]{2,1,0:T(8,128)S(1)}) custom-call(s32[3]{0:T(128)S(1)} %pad_add_fusion.place_ref, bf16[544,256]{1,0:T(8,128)(2,1)S(1)} %copy-done.3, bf16[544,256]{1,0:T(8,128)(2,1)S(1)} %collective-permute-done.refs_1_, ...), custom_call_target="tpu_custom_call" | custom-call | flops 100000000 | bytes 100000 | tf_op jit(solution)/shard_map/wgrad_own/pallas_call | solution.py:268
  29.7 4.7 %wgrad.1 = (f32[7,128,256]{2,1,0:T(8,128)S(1)}, f32[7,128,256]{2,1,0:T(8,128)S(1)}) custom-call(s32[3]{0:T(128)S(1)} %pad_add_fusion.place_ref, bf16[7,256,1024]{2,1,0:T(8,128)(2,1)S(1)} %get-tuple-element.24.picked_ref, bf16[1024,256]{1,0:T(8,128)(2,1)S(1)} %get-tuple-element.25.dys, s32[4,32,256]{2,1,0:T(8,128)S(1)} %get-tuple-element.26.maps, ...), custom_call_target="tpu_custom_call" | custom-call | flops 100000000 | bytes 100000 | tf_op jit(solution)/shard_map/wgrad/pallas_call | solution.py:310
  34.5 0.1 collective-permute-start.5
  34.6 2.5 %collective-permute-done.5.got_ref = f32[7,128,256]{2,1,0:T(8,128)S(1)} collective-permute-done((f32[7,128,256]{2,1,0:T(8,128)S(1)}, f32[7,128,256]{2,1,0:T(8,128)S(1)}, u32[]{:S(2)}, u32[]{:S(2)}) %collective-permute-start.5) | collective-permute-done | bytes 917536 | tf_op jit(solution)/shard_map/ppermute | solution.py:489
  37.0 1.0 %blocks.1 = (f32[7,32,256]{2,1,0:T(8,128)S(1)}, s16[240,256]{1,0:T(8,128)(2,1)S(1)}, s16[240,256]{1,0:T(8,128)(2,1)S(1)}, s16[240,256]{1,0:T(8,128)(2,1)S(1)}) custom-call(s32[3]{0:T(128)S(1)} %pad_add_fusion.place_ref, f32[7,128,256]{2,1,0:T(8,128)S(1)} %get-tuple-element.27.keep_ref, f32[7,128,256]{2,1,0:T(8,128)S(1)} %collective-permute-done.5.got_ref), custom_call_target="tpu_custom_call" | custom-call | flops 100000000 | bytes 100000 | tf_op jit(solution)/shard_map/blocks/pallas_call | solution.py:358
  38.1 1.6 %collective-permute-start.8 = (s16[240,256]{1,0:T(8,128)(2,1)S(1)}, s16[240,256]{1,0:T(8,128)(2,1)S(1)}, u32[]{:S(2)}, u32[]{:S(2)}) collective-permute-start(s16[240,256]{1,0:T(8,128)(2,1)S(1)} %get-tuple-element.35), channel_id=1, source_target_pairs={{0,1},{1,0},{2,3},{3,2},{4,5},{5,4},{6,7},{7,6},{8,9},{9,8},{10,11... | collective-permute-start | bytes 368648 | tf_op jit(solution)/shard_map/ppermute | solution.py:489
  39.7 2.7 %collective-permute-start.9 = (s16[240,256]{1,0:T(8,128)(2,1)S(1)}, s16[240,256]{1,0:T(8,128)(2,1)S(1)}, u32[]{:S(2)}, u32[]{:S(2)}) collective-permute-start(s16[240,256]{1,0:T(8,128)(2,1)S(1)} %get-tuple-element.36), channel_id=1, source_target_pairs={{0,2},{1,3},{2,0},{3,1},{4,6},{5,7},{6,4},{7,5},{8,10},{9,11},{10,... | collective-permute-start | bytes 368648 | tf_op jit(solution)/shard_map/ppermute | solution.py:489
  42.4 0.1 collective-permute-start.10
  42.5 2.6 %collective-permute-start.7 = (f32[64,256]{1,0:T(8,128)S(1)}, f32[64,256]{1,0:T(8,128)S(1)}, u32[]{:S(2)}, u32[]{:S(2)}) collective-permute-start(f32[64,256]{1,0:T(8,128)S(1)} %get-tuple-element.32), channel_id=1, source_target_pairs={{0,1},{1,2},{2,3},{4,5},{5,6},{6,7},{8,9},{9,10},{10,11},{12,13},{... | collective-permute-start | bytes 196616 | tf_op jit(solution)/shard_map/ppermute | solution.py:494
  45.1 1.3 %collective-permute-start.6 = (f32[64,256]{1,0:T(8,128)S(1)}, f32[64,256]{1,0:T(8,128)S(1)}, u32[]{:S(2)}, u32[]{:S(2)}) collective-permute-start(f32[64,256]{1,0:T(8,128)S(1)} %get-tuple-element.21.refs_4_), channel_id=1, source_target_pairs={{1,0},{2,1},{3,2},{5,4},{6,5},{7,6},{9,8},{10,9},{11,10},{13,12},{... | collective-permute-start | bytes 196616 | tf_op jit(solution)/shard_map/ppermute | solution.py:494
  46.4 6.5 %forward.1 = (bf16[256,256]{1,0:T(8,128)(2,1)}, f32[8,128]{1,0:T(8,128)S(1)}) custom-call(s32[1]{0:T(128)S(6)} %copy.10.live_ref, bf16[544,256]{1,0:T(8,128)(2,1)S(1)} %copy-done.3, bf16[256,256]{1,0:T(8,128)(2,1)S(1)} %collective-permute-done.3.lower_ref, bf16[256,256]{1,0:T(8,128)(2,1)S(1)} %collective-permute-done.4.upper_ref, ...), custom_call_target="tpu_custom_call" | custom-call | flops 100000000 | bytes 100000 | tf_op jit(solution)/shard_map/forward/pallas_call | solution.py:217
  53.0 1.0 %final.1 = (bf16[256,256]{1,0:T(8,128)(2,1)}, f32[8,128]{1,0:T(8,128)S(1)}) custom-call(s32[1]{0:T(128)S(6)} %copy.10.live_ref, f32[256,256]{1,0:T(8,128)S(1)} %get-tuple-element.31.own_ref, f32[64,256]{1,0:T(8,128)S(1)} %collective-permute-done.6.back_up_ref, f32[64,256]{1,0:T(8,128)S(1)} %collective-permute-done.7.back_down_ref, s32[1,64]{1,0:T(1,128)S(1)} %copy-done.4, ...), custom_call_target="tpu_custom_call" | custom-call | tf_op jit(solution)/shard_map/final/pallas_call | solution.py:412
  54.0 0.2 total.1
  54.2 1.7 %collective-permute-start.16 = (bf16[1,7,32,256]{3,2,1,0:T(8,128)(2,1)S(1)}, bf16[1,7,32,256]{3,2,1,0:T(8,128)(2,1)S(1)}, u32[]{:S(2)}, u32[]{:S(2)}) collective-permute-start(bf16[1,7,32,256]{3,2,1,0:T(8,128)(2,1)S(1)} %bitcast.4), channel_id=1, source_target_pairs={{0,24},{4,28},{8,16},{12,20},{16,8},{20,12},{24,0},{28,4},{1,25},{... | collective-permute-start | bytes 344072 | tf_op jit(solution)/shard_map/ppermute | solution.py:489
  55.9 1.4 %collective-permute-start.14 = (bf16[1,7,32,256]{3,2,1,0:T(8,128)(2,1)S(1)}, bf16[1,7,32,256]{3,2,1,0:T(8,128)(2,1)S(1)}, u32[]{:S(2)}, u32[]{:S(2)}) collective-permute-start(bf16[1,7,32,256]{3,2,1,0:T(8,128)(2,1)S(1)} %bitcast.5), channel_id=1, source_target_pairs={{0,16},{4,20},{8,24},{12,28},{16,0},{20,4},{24,8},{28,12},{1,17},{... | collective-permute-start | bytes 344072 | tf_op jit(solution)/shard_map/ppermute | solution.py:489
  57.2 0.5 collective-permute-start.12
  57.7 5.6 %collective-permute-start.20 = (bf16[7,32,256]{2,1,0:T(8,128)(2,1)S(1)}, bf16[7,32,256]{2,1,0:T(8,128)(2,1)S(1)}, u32[]{:S(2)}, u32[]{:S(2)}) collective-permute-start(bf16[7,32,256]{2,1,0:T(8,128)(2,1)S(1)} %total.1), channel_id=1, source_target_pairs={{0,3},{1,2},{2,1},{3,0},{4,7},{5,6},{6,5},{7,4},{8,11},{9,10},{10,... | collective-permute-start | bytes 344072 | tf_op jit(solution)/shard_map/ppermute | solution.py:489
  63.4 0.6 collective-permute-start.18
  63.9 2.7 %collective-permute-done.20.refs_2_ = bf16[7,32,256]{2,1,0:T(8,128)(2,1)S(1)} collective-permute-done((bf16[7,32,256]{2,1,0:T(8,128)(2,1)S(1)}, bf16[7,32,256]{2,1,0:T(8,128)(2,1)S(1)}, u32[]{:S(2)}, u32[]{:S(2)}) %collective-permute-start.20) | collective-permute-done | bytes 114720 | tf_op jit(solution)/shard_map/ppermute | solution.py:489
  66.6 4.1 %collective-permute-done.19.refs_1_ = bf16[7,32,256]{2,1,0:T(8,128)(2,1)S(1)} collective-permute-done((bf16[7,32,256]{2,1,0:T(8,128)(2,1)S(1)}, bf16[7,32,256]{2,1,0:T(8,128)(2,1)S(1)}, u32[]{:S(2)}, u32[]{:S(2)}) %collective-permute-start.19) | collective-permute-done | bytes 114720 | tf_op jit(solution)/shard_map/ppermute | solution.py:489
  70.8 1.6 %collective-permute-start.26 = (bf16[3,7,32,256]{3,2,1,0:T(8,128)(2,1)S(1)}, bf16[3,7,32,256]{3,2,1,0:T(8,128)(2,1)S(1)}, u32[]{:S(2)}, u32[]{:S(2)}) collective-permute-start(bf16[3,7,32,256]{3,2,1,0:T(8,128)(2,1)S(1)} %line.1.refs_8_), channel_id=1, source_target_pairs={{0,24},{4,28},{8,16},{12,20},{16,8},{20,12},{24,0},{28,4},{1,25},{... | collective-permute-start | bytes 1032200 | tf_op jit(solution)/shard_map/ppermute | solution.py:489
  72.4 1.4 %collective-permute-start.24 = (bf16[3,7,32,256]{3,2,1,0:T(8,128)(2,1)S(1)}, bf16[3,7,32,256]{3,2,1,0:T(8,128)(2,1)S(1)}, u32[]{:S(2)}, u32[]{:S(2)}) collective-permute-start(bf16[3,7,32,256]{3,2,1,0:T(8,128)(2,1)S(1)} %line.1.refs_8_), channel_id=1, source_target_pairs={{0,16},{4,20},{8,24},{12,28},{16,0},{20,4},{24,8},{28,12},{1,17},{... | collective-permute-start | bytes 1032200 | tf_op jit(solution)/shard_map/ppermute | solution.py:489
  73.8 0.5 collective-permute-start.22
  74.4 0.5 collective-permute-start.21
  74.9 0.8 collective-permute-done.11.refs_1_
  75.7 0.2 collective-permute-start.17
  75.8 7.0 %collective-permute-done.26.refs_14_ = bf16[3,7,32,256]{3,2,1,0:T(8,128)(2,1)S(1)} collective-permute-done((bf16[3,7,32,256]{3,2,1,0:T(8,128)(2,1)S(1)}, bf16[3,7,32,256]{3,2,1,0:T(8,128)(2,1)S(1)}, u32[]{:S(2)}, u32[]{:S(2)}) %collective-permute-start.26) | collective-permute-done | bytes 344096 | tf_op jit(solution)/shard_map/ppermute | solution.py:489
  82.8 5.2 %collective-permute-done.24.refs_12_ = bf16[3,7,32,256]{3,2,1,0:T(8,128)(2,1)S(1)} collective-permute-done((bf16[3,7,32,256]{3,2,1,0:T(8,128)(2,1)S(1)}, bf16[3,7,32,256]{3,2,1,0:T(8,128)(2,1)S(1)}, u32[]{:S(2)}, u32[]{:S(2)}) %collective-permute-start.24) | collective-permute-done | bytes 344096 | tf_op jit(solution)/shard_map/ppermute | solution.py:489
  88.0 0.1 collective-permute-done.22.refs_10_
  88.1 0.4 collective-permute-start.23
  88.5 0.1 collective-permute-start.15
  88.6 1.7 %collective-permute-done.15.refs_5_ = bf16[1,7,32,256]{3,2,1,0:T(8,128)(2,1)S(1)} collective-permute-done((bf16[1,7,32,256]{3,2,1,0:T(8,128)(2,1)S(1)}, bf16[1,7,32,256]{3,2,1,0:T(8,128)(2,1)S(1)}, u32[]{:S(2)}, u32[]{:S(2)}) %collective-permute-start.15) | collective-permute-done | bytes 114720 | tf_op jit(solution)/shard_map/ppermute | solution.py:489
  90.3 0.1 collective-permute-start.13
  90.5 1.2 %collective-permute-done.13.refs_3_ = bf16[1,7,32,256]{3,2,1,0:T(8,128)(2,1)S(1)} collective-permute-done((bf16[1,7,32,256]{3,2,1,0:T(8,128)(2,1)S(1)}, bf16[1,7,32,256]{3,2,1,0:T(8,128)(2,1)S(1)}, u32[]{:S(2)}, u32[]{:S(2)}) %collective-permute-start.13) | collective-permute-done | bytes 114720 | tf_op jit(solution)/shard_map/ppermute | solution.py:489
  91.7 3.5 %assemble.1 = bf16[27,256,256]{2,1,0:T(8,128)(2,1)} custom-call(s32[3]{0:T(128)S(1)} %pad_add_fusion.place_ref, bf16[1,7,32,256]{3,2,1,0:T(8,128)(2,1)S(1)} %bitcast.8, bf16[1,7,32,256]{3,2,1,0:T(8,128)(2,1)S(1)} %collective-permute-done.11.refs_1_, bf16[1,7,32,256]{3,2,1,0:T(8,128)(2,1)S(1)} %collective-permute-done.12.refs_3_.refs_2_, ...), custom_call_target="tpu_custom_call" | custom-call | tf_op jit(solution)/shard_map/assemble/pallas_call | solution.py:467
  (32 shorter events, 0.1 us)
Async XLA Ops:
  3.1 15.5 %collective-permute-start.2 = (bf16[544,256]{1,0:T(8,128)(2,1)}, bf16[544,256]{1,0:T(8,128)(2,1)S(1)}, u32[]{:S(2)}, u32[]{:S(2)}) collective-permute-start(bf16[544,256]{1,0:T(8,128)(2,1)} %prep.1.pack_ref.before_ref.refs_0_), channel_id=1, source_target_pairs={{0,24},{4,28},{8,16},{12,20},{16,8},{20,12},{24,0},{28,4},{1,25},{... | collective-permute-start | bytes 835592 | tf_op jit(solution)/shard_map/ppermute | solution.py:489
  7.1 12.8 %collective-permute-start.1 = (bf16[544,256]{1,0:T(8,128)(2,1)}, bf16[544,256]{1,0:T(8,128)(2,1)S(1)}, u32[]{:S(2)}, u32[]{:S(2)}) collective-permute-start(bf16[544,256]{1,0:T(8,128)(2,1)} %prep.1.pack_ref.before_ref.refs_0_), channel_id=1, source_target_pairs={{0,16},{4,20},{8,24},{12,28},{16,0},{20,4},{24,8},{28,12},{1,17},{... | collective-permute-start | bytes 835592 | tf_op jit(solution)/shard_map/ppermute | solution.py:489
  7.6 12.6 %collective-permute-start = (bf16[544,256]{1,0:T(8,128)(2,1)}, bf16[544,256]{1,0:T(8,128)(2,1)S(1)}, u32[]{:S(2)}, u32[]{:S(2)}) collective-permute-start(bf16[544,256]{1,0:T(8,128)(2,1)} %prep.1.pack_ref.before_ref.refs_0_), channel_id=1, source_target_pairs={{0,8},{4,12},{8,0},{12,4},{16,24},{20,28},{24,16},{28,20},{1,9},{5... | collective-permute-start | bytes 835592 | tf_op jit(solution)/shard_map/ppermute | solution.py:489
  7.7 2.0 %copy-start = (bf16[27,256,256]{2,1,0:T(8,128)(2,1)S(1)}, bf16[27,256,256]{2,1,0:T(8,128)(2,1)}, u32[]{:S(2)}) copy-start(bf16[27,256,256]{2,1,0:T(8,128)(2,1)} %w_ref.3) | copy-start | bytes 10616836
  9.7 1.0 %copy-start.2 = (bf16[544,256]{1,0:T(8,128)(2,1)S(1)}, bf16[544,256]{1,0:T(8,128)(2,1)}, u32[]{:S(2)}) copy-start(bf16[544,256]{1,0:T(8,128)(2,1)} %prep.1.pack_ref.before_ref.refs_0_) | copy-start | bytes 835588
  10.7 15.8 %copy-start.3 = (bf16[544,256]{1,0:T(8,128)(2,1)S(1)}, bf16[544,256]{1,0:T(8,128)(2,1)}, u32[]{:S(2)}) copy-start(bf16[544,256]{1,0:T(8,128)(2,1)} %prep.1.pack_ref.before_ref.refs_0_) | copy-start | bytes 835588
  20.5 9.2 %collective-permute-start.4 = (bf16[256,256]{1,0:T(8,128)(2,1)S(1)}, bf16[256,256]{1,0:T(8,128)(2,1)S(1)}, u32[]{:S(2)}, u32[]{:S(2)}) collective-permute-start(bf16[256,256]{1,0:T(8,128)(2,1)S(1)} %get-tuple-element.23), channel_id=1, source_target_pairs={{1,0},{2,1},{3,2},{5,4},{6,5},{7,6},{9,8},{10,9},{11,10},{13,12},{... | collective-permute-start | bytes 393224 | tf_op jit(solution)/shard_map/ppermute | solution.py:494
  21.8 7.9 %collective-permute-start.3 = (bf16[256,256]{1,0:T(8,128)(2,1)S(1)}, bf16[256,256]{1,0:T(8,128)(2,1)S(1)}, u32[]{:S(2)}, u32[]{:S(2)}) collective-permute-start(bf16[256,256]{1,0:T(8,128)(2,1)S(1)} %get-tuple-element.22.refs_4_), channel_id=1, source_target_pairs={{0,1},{1,2},{2,3},{4,5},{5,6},{6,7},{8,9},{9,10},{10,11},{12,13},{... | collective-permute-start | bytes 393224 | tf_op jit(solution)/shard_map/ppermute | solution.py:494
  26.4 20.0 %copy-start.1 = (bf16[27,256,256]{2,1,0:T(8,128)(2,1)S(1)}, bf16[27,256,256]{2,1,0:T(8,128)(2,1)}, u32[]{:S(2)}) copy-start(bf16[27,256,256]{2,1,0:T(8,128)(2,1)} %w_ref.3) | copy-start | bytes 10616836
  34.5 18.5 %copy-start.4 = (s32[1,64]{1,0:T(1,128)S(1)}, s32[1,64]{1,0:T(1,128)}, u32[]{:S(2)}) copy-start(s32[1,64]{1,0:T(1,128)} %up_ref.1) | copy-start | bytes 772
  34.5 18.5 %copy-start.5 = (s32[1,64]{1,0:T(1,128)S(1)}, s32[1,64]{1,0:T(1,128)}, u32[]{:S(2)}) copy-start(s32[1,64]{1,0:T(1,128)} %down_ref.1) | copy-start | bytes 772
  34.5 2.5 %collective-permute-start.5 = (f32[7,128,256]{2,1,0:T(8,128)S(1)}, f32[7,128,256]{2,1,0:T(8,128)S(1)}, u32[]{:S(2)}, u32[]{:S(2)}) collective-permute-start(f32[7,128,256]{2,1,0:T(8,128)S(1)} %get-tuple-element.28), channel_id=1, source_target_pairs={{0,4},{4,0},{8,12},{12,8},{16,20},{20,16},{24,28},{28,24},{1,5},{5... | collective-permute-start | bytes 2752520 | tf_op jit(solution)/shard_map/ppermute | solution.py:489
  38.1 15.9 %collective-permute-start.8 = (s16[240,256]{1,0:T(8,128)(2,1)S(1)}, s16[240,256]{1,0:T(8,128)(2,1)S(1)}, u32[]{:S(2)}, u32[]{:S(2)}) collective-permute-start(s16[240,256]{1,0:T(8,128)(2,1)S(1)} %get-tuple-element.35), channel_id=1, source_target_pairs={{0,1},{1,0},{2,3},{3,2},{4,5},{5,4},{6,7},{7,6},{8,9},{9,8},{10,11... | collective-permute-start | bytes 368648 | tf_op jit(solution)/shard_map/ppermute | solution.py:489
  39.7 14.3 %collective-permute-start.9 = (s16[240,256]{1,0:T(8,128)(2,1)S(1)}, s16[240,256]{1,0:T(8,128)(2,1)S(1)}, u32[]{:S(2)}, u32[]{:S(2)}) collective-permute-start(s16[240,256]{1,0:T(8,128)(2,1)S(1)} %get-tuple-element.36), channel_id=1, source_target_pairs={{0,2},{1,3},{2,0},{3,1},{4,6},{5,7},{6,4},{7,5},{8,10},{9,11},{10,... | collective-permute-start | bytes 368648 | tf_op jit(solution)/shard_map/ppermute | solution.py:489
  42.4 11.6 %collective-permute-start.10 = (s16[240,256]{1,0:T(8,128)(2,1)S(1)}, s16[240,256]{1,0:T(8,128)(2,1)S(1)}, u32[]{:S(2)}, u32[]{:S(2)}) collective-permute-start(s16[240,256]{1,0:T(8,128)(2,1)S(1)} %get-tuple-element.37), channel_id=1, source_target_pairs={{0,3},{1,2},{2,1},{3,0},{4,7},{5,6},{6,5},{7,4},{8,11},{9,10},{10,... | collective-permute-start | bytes 368648 | tf_op jit(solution)/shard_map/ppermute | solution.py:489
  42.5 10.4 %collective-permute-start.7 = (f32[64,256]{1,0:T(8,128)S(1)}, f32[64,256]{1,0:T(8,128)S(1)}, u32[]{:S(2)}, u32[]{:S(2)}) collective-permute-start(f32[64,256]{1,0:T(8,128)S(1)} %get-tuple-element.32), channel_id=1, source_target_pairs={{0,1},{1,2},{2,3},{4,5},{5,6},{6,7},{8,9},{9,10},{10,11},{12,13},{... | collective-permute-start | bytes 196616 | tf_op jit(solution)/shard_map/ppermute | solution.py:494
  45.1 7.9 %collective-permute-start.6 = (f32[64,256]{1,0:T(8,128)S(1)}, f32[64,256]{1,0:T(8,128)S(1)}, u32[]{:S(2)}, u32[]{:S(2)}) collective-permute-start(f32[64,256]{1,0:T(8,128)S(1)} %get-tuple-element.21.refs_4_), channel_id=1, source_target_pairs={{1,0},{2,1},{3,2},{5,4},{6,5},{7,6},{9,8},{10,9},{11,10},{13,12},{... | collective-permute-start | bytes 196616 | tf_op jit(solution)/shard_map/ppermute | solution.py:494
  54.2 9.2 %collective-permute-start.16 = (bf16[1,7,32,256]{3,2,1,0:T(8,128)(2,1)S(1)}, bf16[1,7,32,256]{3,2,1,0:T(8,128)(2,1)S(1)}, u32[]{:S(2)}, u32[]{:S(2)}) collective-permute-start(bf16[1,7,32,256]{3,2,1,0:T(8,128)(2,1)S(1)} %bitcast.4), channel_id=1, source_target_pairs={{0,24},{4,28},{8,16},{12,20},{16,8},{20,12},{24,0},{28,4},{1,25},{... | collective-permute-start | bytes 344072 | tf_op jit(solution)/shard_map/ppermute | solution.py:489
  55.9 8.1 %collective-permute-start.14 = (bf16[1,7,32,256]{3,2,1,0:T(8,128)(2,1)S(1)}, bf16[1,7,32,256]{3,2,1,0:T(8,128)(2,1)S(1)}, u32[]{:S(2)}, u32[]{:S(2)}) collective-permute-start(bf16[1,7,32,256]{3,2,1,0:T(8,128)(2,1)S(1)} %bitcast.5), channel_id=1, source_target_pairs={{0,16},{4,20},{8,24},{12,28},{16,0},{20,4},{24,8},{28,12},{1,17},{... | collective-permute-start | bytes 344072 | tf_op jit(solution)/shard_map/ppermute | solution.py:489
  57.2 6.7 %collective-permute-start.12 = (bf16[1,7,32,256]{3,2,1,0:T(8,128)(2,1)S(1)}, bf16[1,7,32,256]{3,2,1,0:T(8,128)(2,1)S(1)}, u32[]{:S(2)}, u32[]{:S(2)}) collective-permute-start(bf16[1,7,32,256]{3,2,1,0:T(8,128)(2,1)S(1)} %bitcast.6), channel_id=1, source_target_pairs={{0,8},{4,12},{8,0},{12,4},{16,24},{20,28},{24,16},{28,20},{1,9},{5... | collective-permute-start | bytes 344072 | tf_op jit(solution)/shard_map/ppermute | solution.py:489
  57.7 8.9 %collective-permute-start.20 = (bf16[7,32,256]{2,1,0:T(8,128)(2,1)S(1)}, bf16[7,32,256]{2,1,0:T(8,128)(2,1)S(1)}, u32[]{:S(2)}, u32[]{:S(2)}) collective-permute-start(bf16[7,32,256]{2,1,0:T(8,128)(2,1)S(1)} %total.1), channel_id=1, source_target_pairs={{0,3},{1,2},{2,1},{3,0},{4,7},{5,6},{6,5},{7,4},{8,11},{9,10},{10,... | collective-permute-start | bytes 344072 | tf_op jit(solution)/shard_map/ppermute | solution.py:489
  63.4 7.4 %collective-permute-start.19 = (bf16[7,32,256]{2,1,0:T(8,128)(2,1)S(1)}, bf16[7,32,256]{2,1,0:T(8,128)(2,1)S(1)}, u32[]{:S(2)}, u32[]{:S(2)}) collective-permute-start(bf16[7,32,256]{2,1,0:T(8,128)(2,1)S(1)} %total.1), channel_id=1, source_target_pairs={{0,2},{1,3},{2,0},{3,1},{4,6},{5,7},{6,4},{7,5},{8,10},{9,11},{10,... | collective-permute-start | bytes 344072 | tf_op jit(solution)/shard_map/ppermute | solution.py:489
  63.4 7.4 %collective-permute-start.18 = (bf16[7,32,256]{2,1,0:T(8,128)(2,1)S(1)}, bf16[7,32,256]{2,1,0:T(8,128)(2,1)S(1)}, u32[]{:S(2)}, u32[]{:S(2)}) collective-permute-start(bf16[7,32,256]{2,1,0:T(8,128)(2,1)S(1)} %total.1), channel_id=1, source_target_pairs={{0,1},{1,0},{2,3},{3,2},{4,5},{5,4},{6,7},{7,6},{8,9},{9,8},{10,11... | collective-permute-start | bytes 344072 | tf_op jit(solution)/shard_map/ppermute | solution.py:489
  70.8 12.0 %collective-permute-start.26 = (bf16[3,7,32,256]{3,2,1,0:T(8,128)(2,1)S(1)}, bf16[3,7,32,256]{3,2,1,0:T(8,128)(2,1)S(1)}, u32[]{:S(2)}, u32[]{:S(2)}) collective-permute-start(bf16[3,7,32,256]{3,2,1,0:T(8,128)(2,1)S(1)} %line.1.refs_8_), channel_id=1, source_target_pairs={{0,24},{4,28},{8,16},{12,20},{16,8},{20,12},{24,0},{28,4},{1,25},{... | collective-permute-start | bytes 1032200 | tf_op jit(solution)/shard_map/ppermute | solution.py:489
  72.4 15.6 %collective-permute-start.24 = (bf16[3,7,32,256]{3,2,1,0:T(8,128)(2,1)S(1)}, bf16[3,7,32,256]{3,2,1,0:T(8,128)(2,1)S(1)}, u32[]{:S(2)}, u32[]{:S(2)}) collective-permute-start(bf16[3,7,32,256]{3,2,1,0:T(8,128)(2,1)S(1)} %line.1.refs_8_), channel_id=1, source_target_pairs={{0,16},{4,20},{8,24},{12,28},{16,0},{20,4},{24,8},{28,12},{1,17},{... | collective-permute-start | bytes 1032200 | tf_op jit(solution)/shard_map/ppermute | solution.py:489
  73.8 14.3 %collective-permute-start.22 = (bf16[3,7,32,256]{3,2,1,0:T(8,128)(2,1)S(1)}, bf16[3,7,32,256]{3,2,1,0:T(8,128)(2,1)S(1)}, u32[]{:S(2)}, u32[]{:S(2)}) collective-permute-start(bf16[3,7,32,256]{3,2,1,0:T(8,128)(2,1)S(1)} %line.1.refs_8_), channel_id=1, source_target_pairs={{0,8},{4,12},{8,0},{12,4},{16,24},{20,28},{24,16},{28,20},{1,9},{5... | collective-permute-start | bytes 1032200 | tf_op jit(solution)/shard_map/ppermute | solution.py:489
  74.3 1.3 %collective-permute-start.11 = (bf16[1,7,32,256]{3,2,1,0:T(8,128)(2,1)S(1)}, bf16[1,7,32,256]{3,2,1,0:T(8,128)(2,1)S(1)}, u32[]{:S(2)}, u32[]{:S(2)}) collective-permute-start(bf16[1,7,32,256]{3,2,1,0:T(8,128)(2,1)S(1)} %bitcast.7), channel_id=1, source_target_pairs={{0,4},{4,0},{8,12},{12,8},{16,20},{20,16},{24,28},{28,24},{1,5},{5... | collective-permute-start | bytes 344072 | tf_op jit(solution)/shard_map/ppermute | solution.py:489
  74.4 17.3 %collective-permute-start.21 = (bf16[3,7,32,256]{3,2,1,0:T(8,128)(2,1)S(1)}, bf16[3,7,32,256]{3,2,1,0:T(8,128)(2,1)S(1)}, u32[]{:S(2)}, u32[]{:S(2)}) collective-permute-start(bf16[3,7,32,256]{3,2,1,0:T(8,128)(2,1)S(1)} %line.1.refs_8_), channel_id=1, source_target_pairs={{0,4},{4,0},{8,12},{12,8},{16,20},{20,16},{24,28},{28,24},{1,5},{5... | collective-permute-start | bytes 1032200 | tf_op jit(solution)/shard_map/ppermute | solution.py:489
  75.7 12.9 %collective-permute-start.17 = (bf16[1,7,32,256]{3,2,1,0:T(8,128)(2,1)S(1)}, bf16[1,7,32,256]{3,2,1,0:T(8,128)(2,1)S(1)}, u32[]{:S(2)}, u32[]{:S(2)}) collective-permute-start(bf16[1,7,32,256]{3,2,1,0:T(8,128)(2,1)S(1)} %collective-permute-done.16.refs_5_.refs_6_), channel_id=1, source_target_pairs={{0,4},{4,0},{8,12},{12,8},{16,20},{20,16},{24,28},{28,24},{1,5},{5... | collective-permute-start | bytes 344072 | tf_op jit(solution)/shard_map/ppermute | solution.py:489
  82.8 8.9 %collective-permute-start.27 = (bf16[3,7,32,256]{3,2,1,0:T(8,128)(2,1)S(1)}, bf16[3,7,32,256]{3,2,1,0:T(8,128)(2,1)S(1)}, u32[]{:S(2)}, u32[]{:S(2)}) collective-permute-start(bf16[3,7,32,256]{3,2,1,0:T(8,128)(2,1)S(1)} %collective-permute-done.26.refs_14_), channel_id=1, source_target_pairs={{0,4},{4,0},{8,12},{12,8},{16,20},{20,16},{24,28},{28,24},{1,5},{5... | collective-permute-start | bytes 1032200 | tf_op jit(solution)/shard_map/ppermute | solution.py:489
  88.0 3.6 %collective-permute-start.25 = (bf16[3,7,32,256]{3,2,1,0:T(8,128)(2,1)S(1)}, bf16[3,7,32,256]{3,2,1,0:T(8,128)(2,1)S(1)}, u32[]{:S(2)}, u32[]{:S(2)}) collective-permute-start(bf16[3,7,32,256]{3,2,1,0:T(8,128)(2,1)S(1)} %collective-permute-done.24.refs_12_), channel_id=1, source_target_pairs={{0,4},{4,0},{8,12},{12,8},{16,20},{20,16},{24,28},{28,24},{1,5},{5... | collective-permute-start | bytes 1032200 | tf_op jit(solution)/shard_map/ppermute | solution.py:489
  88.1 3.6 %collective-permute-start.23 = (bf16[3,7,32,256]{3,2,1,0:T(8,128)(2,1)S(1)}, bf16[3,7,32,256]{3,2,1,0:T(8,128)(2,1)S(1)}, u32[]{:S(2)}, u32[]{:S(2)}) collective-permute-start(bf16[3,7,32,256]{3,2,1,0:T(8,128)(2,1)S(1)} %collective-permute-done.22.refs_10_), channel_id=1, source_target_pairs={{0,4},{4,0},{8,12},{12,8},{16,20},{20,16},{24,28},{28,24},{1,5},{5... | collective-permute-start | bytes 1032200 | tf_op jit(solution)/shard_map/ppermute | solution.py:489
  88.5 1.8 %collective-permute-start.15 = (bf16[1,7,32,256]{3,2,1,0:T(8,128)(2,1)S(1)}, bf16[1,7,32,256]{3,2,1,0:T(8,128)(2,1)S(1)}, u32[]{:S(2)}, u32[]{:S(2)}) collective-permute-start(bf16[1,7,32,256]{3,2,1,0:T(8,128)(2,1)S(1)} %collective-permute-done.14.refs_4_), channel_id=1, source_target_pairs={{0,4},{4,0},{8,12},{12,8},{16,20},{20,16},{24,28},{28,24},{1,5},{5... | collective-permute-start | bytes 344072 | tf_op jit(solution)/shard_map/ppermute | solution.py:489
  90.3 1.3 %collective-permute-start.13 = (bf16[1,7,32,256]{3,2,1,0:T(8,128)(2,1)S(1)}, bf16[1,7,32,256]{3,2,1,0:T(8,128)(2,1)S(1)}, u32[]{:S(2)}, u32[]{:S(2)}) collective-permute-start(bf16[1,7,32,256]{3,2,1,0:T(8,128)(2,1)S(1)} %collective-permute-done.12.refs_3_.refs_2_), channel_id=1, source_target_pairs={{0,4},{4,0},{8,12},{12,8},{16,20},{20,16},{24,28},{28,24},{1,5},{5... | collective-permute-start | bytes 344072 | tf_op jit(solution)/shard_map/ppermute | solution.py:489

commit v4 on v3

--- a/solution.py
+++ b/solution.py
@@ -40,7 +40,7 @@
     return parts
 
 
-def prep_kernel(live_ref, x_hbm, dy_hbm, map_hbm, up_hbm, down_hbm, pack_ref, *scratch):
+def prep_kernel(live_ref, x_hbm, dy_hbm, map_hbm, up_hbm, down_hbm, pack_ref, up_rows_ref, down_rows_ref, *scratch):
     x_ref, dy_ref, map_ref, up_ref, down_ref, map_scr, sems = scratch
     sources = (x_hbm, dy_hbm, map_hbm, up_hbm, down_hbm)
     targets = (x_ref, dy_ref, map_ref, up_ref, down_ref)
@@ -54,11 +54,14 @@
     map_scr[...] = jnp.full(map_scr.shape, rows + 2 * halo, jnp.int32)
     for copy in copies:
         copy.wait()
-    pack_ref[0:rows] = jnp.where(keep, x_ref[...].astype(F32), 0.0).astype(BF)
+    x_live = jnp.where(keep, x_ref[...].astype(F32), 0.0).astype(BF)
+    pack_ref[0:rows] = x_live
+    iota = lax.broadcasted_iota(jnp.int32, (rows, halo), 0)
+    for index_ref, picked_ref in ((up_ref, up_rows_ref), (down_ref, down_rows_ref)):
+        chosen = (iota == index_ref[...]).astype(F32).astype(BF)
+        picked_ref[...] = lax.dot_general(chosen, x_live, (((0,), (0,)), ((), ())), preferred_element_type=F32).astype(BF)
     pack_ref[rows : 2 * rows] = jnp.where(keep, dy_ref[...].astype(F32), 0.0).astype(BF)
     map_scr[0:offsets] = map_ref[...]
-    map_scr[map_scr.shape[0] - 1 :, 0:halo] = up_ref[...]
-    map_scr[map_scr.shape[0] - 1 :, halo : 2 * halo] = down_ref[...]
     slots = map_scr[...]
     pack_ref[2 * rows :] = jnp.where(slots > 256, 256 - slots, slots).astype(F32).astype(BF)
 
@@ -67,9 +70,13 @@
     rows, width = features.shape
     return pl.pallas_call(
         prep_kernel,
-        out_shape=jax.ShapeDtypeStruct((2 * rows + map_rows, width), BF),
+        out_shape=(
+            jax.ShapeDtypeStruct((2 * rows + map_rows, width), BF),
+            jax.ShapeDtypeStruct((send_up.shape[1], width), BF),
+            jax.ShapeDtypeStruct((send_up.shape[1], width), BF),
+        ),
         in_specs=[SMEM] + [HBM] * 5,
-        out_specs=VMEM,
+        out_specs=(VMEM,) * 3,
         scratch_shapes=[
             pltpu.VMEM((rows, width), BF),
             pltpu.VMEM((rows, width), BF),
@@ -84,42 +91,13 @@
     )(live, features, cotangent, kernel_map, send_up, send_down)
 
 
-def pick_kernel(rows, *refs):
-    *packs, up_ref, down_ref = refs
-    halo = up_ref.shape[0] // len(packs)
-    iota = lax.broadcasted_iota(jnp.int32, (rows, 2 * halo), 0)
-    for s, pack in enumerate(packs):
-        sent = pack[2 * rows :].astype(F32).astype(jnp.int32)[-1:, 0 : 2 * halo]
-        chosen = (iota == sent).astype(F32).astype(BF)
-        picked = lax.dot_general(chosen, pack[0:rows], (((0,), (0,)), ((), ())), preferred_element_type=F32)
-        up_ref[s * halo : (s + 1) * halo] = picked[0:halo].astype(BF)
-        down_ref[s * halo : (s + 1) * halo] = picked[halo:].astype(BF)
-
-
-def pick(packs, rows, halo, after):
-    shape = jax.ShapeDtypeStruct((len(packs) * halo, packs[0].shape[1]), BF)
-    return pl.pallas_call(
-        functools.partial(pick_kernel_after, rows),
-        out_shape=(shape, shape),
-        in_specs=[VMEM] * len(packs) + [ANY],
-        out_specs=(VMEM, VMEM),
-        compiler_params=params(),
-        cost_estimate=cost(),
-        name="pick",
-    )(*packs, after)
-
-
-def pick_kernel_after(rows, *refs):
-    pick_kernel(rows, *refs[:-3], *refs[-2:])
-
-
 def decoded(code):
     code = code.astype(F32).astype(jnp.int32)
     return jnp.where(code < 0, 256 - code, code)
 
 
-def backward_kernel(start, end, pack_ref, w_ref, before_ref, *refs):
-    outs, (maps, grad_acc, chosen, terms) = refs[:-4], refs[-4:]
+def backward_kernel(pack_ref, w_ref, after_ref, own_ref, low_ref, high_ref, token_ref, *refs):
+    maps, grad_acc, chosen, terms = refs
     step = pl.program_id(0)
     offsets, width, _ = w_ref.shape
     slots = grad_acc.shape[0]
@@ -128,22 +106,23 @@
     @pl.when(step == 0)
     def _():
         maps[...] = decoded(pack_ref[2 * rows :])
-        grad_acc[...] = before_ref[...] if start else jnp.zeros_like(grad_acc)
+        grad_acc[...] = jnp.zeros_like(grad_acc)
 
     dy = pack_ref[rows : 2 * rows]
     slot_down = lax.broadcasted_iota(jnp.int32, (slots, rows), 0)
     for i in range(offsets):
-        row = maps[pl.ds((start + step) * offsets + i, 1), :]
+        row = maps[pl.ds(step * offsets + i, 1), :]
         chosen[:, i * rows : (i + 1) * rows] = (slot_down == row).astype(F32).astype(BF)
         back = lax.dot_general(dy, w_ref[i], (((1,), (1,)), ((), ())), preferred_element_type=F32)
         for t, part in enumerate(split(back, 2)):
             terms[t, i * rows : (i + 1) * rows] = part
     grad_acc[...] += dot(chosen[...], terms[0]) + dot(chosen[...], terms[1])
 
-    @pl.when(step == end - start - 1)
+    @pl.when(step == pl.num_programs(0) - 1)
     def _():
+        token_ref[...] = jnp.zeros_like(token_ref)
         at = 0
-        for out in outs:
+        for out in (own_ref, low_ref, high_ref):
             out[...] = grad_acc[at : at + out.shape[0]]
             at += out.shape[0]
 
@@ -152,20 +131,17 @@
     return pl.BlockSpec(shape, lambda k: (0,) * len(shape))
 
 
-def backward(pack, weights, rows, halo, start, end, per_step, before):
+def backward(pack, weights, rows, halo, after):
     offsets, width, _ = weights.shape
     slots = rows + 2 * halo
-    sizes = (rows, halo, halo) if end * per_step == offsets else (slots,)
-    return pl.pallas_call(
-        functools.partial(backward_kernel, start, end),
-        grid=(end - start,),
-        out_shape=tuple(jax.ShapeDtypeStruct((n, width), F32) for n in sizes),
-        in_specs=[
-            whole(pack.shape),
-            pl.BlockSpec((per_step, width, width), lambda k: (start + k, 0, 0)),
-            whole(before.shape) if start else ANY,
-        ],
-        out_specs=tuple(whole((n, width)) for n in sizes),
+    per_step = 3 if offsets % 3 == 0 else 1
+    shapes = [jax.ShapeDtypeStruct((n, width), F32) for n in (rows, halo, halo)] + [TOKEN]
+    return pl.pallas_call(
+        backward_kernel,
+        grid=(offsets // per_step,),
+        out_shape=tuple(shapes),
+        in_specs=[whole(pack.shape), pl.BlockSpec((per_step, width, width), lambda k: (k, 0, 0)), ANY],
+        out_specs=tuple(whole(shape.shape) for shape in shapes),
         scratch_shapes=[
             pltpu.VMEM((pack.shape[0] - 2 * rows, rows), jnp.int32),
             pltpu.VMEM((slots, width), F32),
@@ -175,10 +151,10 @@
         compiler_params=params(),
         cost_estimate=cost(),
         name="backward",
-    )(pack, weights, before)
-
-
-def forward_kernel(live_ref, pack_ref, lower_ref, upper_ref, w_ref, after_ref, out_ref, token_ref, table, maps, out_acc, picked):
+    )(pack, weights, after)
+
+
+def forward_kernel(live_ref, pack_ref, halo_ref, w_ref, after_ref, out_ref, token_ref, table, maps, out_acc, picked):
     step = pl.program_id(0)
     offsets = w_ref.shape[0]
     rows, width = out_ref.shape
@@ -188,9 +164,7 @@
     def _():
         maps[...] = decoded(pack_ref[2 * rows :])
         table[0:rows] = pack_ref[0:rows]
-        halo = (slots - rows) // 2
-        table[rows : rows + halo] = lower_ref[0:halo]
-        table[rows + halo :] = upper_ref[0:halo]
+        table[rows:] = halo_ref[...]
         out_acc[...] = jnp.zeros_like(out_acc)
 
     along = lax.broadcasted_iota(jnp.int32, (rows, 128), 1)
@@ -210,9 +184,9 @@
         token_ref[...] = jnp.zeros_like(token_ref)
 
 
-def forward(live, pack, lower, upper, weights, rows, halo, after):
+def forward(live, pack, halo_rows, weights, rows, after):
     offsets, width, _ = weights.shape
-    slots = rows + 2 * halo
+    slots = rows + halo_rows.shape[0]
     per_step = 3 if offsets % 3 == 0 else 1
     return pl.pallas_call(
         forward_kernel,
@@ -221,8 +195,7 @@
         in_specs=[
             SMEM,
             whole(pack.shape),
-            whole(lower.shape),
-            whole(upper.shape),
+            whole(halo_rows.shape),
             pl.BlockSpec((per_step, width, width), lambda k: (k, 0, 0)),
             ANY,
         ],
@@ -236,7 +209,7 @@
         compiler_params=params(),
         cost_estimate=cost(),
         name="forward",
-    )(live, pack, lower, upper, weights, after)
+    )(live, pack, halo_rows, weights, after)
 
 
 def chosen_slots(maps, s, at, low, high, rows):
@@ -246,7 +219,7 @@
 
 def wgrad_own_kernel(sources, place_ref, *refs):
     packs = refs[:sources]
-    picked_ref, dys, maps, tables = refs[sources + 1 :]
+    picked_ref, dys, maps, tables = refs[sources:]
     count, width, _ = picked_ref.shape
     rows = dys.shape[0] // sources
     for s in range(sources):
@@ -263,7 +236,7 @@
     lax.fori_loop(0, count, offset, 0)
 
 
-def wgrad_own(place, packs, count, rows, after):
+def wgrad_own(place, packs, count, rows):
     sources, width = len(packs), packs[0].shape[1]
     return pl.pallas_call(
         functools.partial(wgrad_own_kernel, sources),
@@ -272,54 +245,49 @@
             jax.ShapeDtypeStruct((sources * rows, width), BF),
             jax.ShapeDtypeStruct((sources, packs[0].shape[0] - 2 * rows, rows), jnp.int32),
         ),
-        in_specs=[SMEM] + [VMEM] * sources + [ANY],
+        in_specs=[SMEM] + [VMEM] * sources,
         out_specs=(VMEM, VMEM, VMEM),
         scratch_shapes=[pltpu.VMEM((width, sources * rows), BF)],
         compiler_params=params(),
         cost_estimate=cost(),
         name="wgrad_own",
-    )(place, *packs, after)
-
-
-def wgrad_kernel(place_ref, picked_ref, dys, maps, lower_ref, upper_ref, keep_ref, send_ref, tables, picked):
+    )(place, *packs)
+
+
+def wgrad_kernel(sources, first, place_ref, picked_ref, dys, maps, *refs):
+    halos, (after_ref, keep_ref, send_ref, tables, picked) = refs[:sources], refs[sources:]
     count, half, width = keep_ref.shape
-    sources, _, rows = maps.shape
-    halo = lower_ref.shape[0] // sources
+    rows = maps.shape[2]
+    far = halos[0].shape[0]
     core = place_ref[1]
     for s in range(sources):
-        both = jnp.concatenate([ref[s * halo : (s + 1) * halo].astype(F32) for ref in (lower_ref, upper_ref)], axis=0)
-        tables[:, s * 2 * halo : (s + 1) * 2 * halo] = jnp.transpose(both).astype(BF)
-
-    def offset(j, carry):
+        tables[:, s * far : (s + 1) * far] = jnp.transpose(halos[s][...])
+    for j in range(count):
         for s in range(sources):
-            chosen = chosen_slots(maps, s, place_ref[0] * count + j, rows, rows + 2 * halo, rows)
-            far = dot(tables[:, s * 2 * halo : (s + 1) * 2 * halo], chosen)
-            near = picked_ref[j, :, s * rows : (s + 1) * rows].astype(F32)
-            picked[:, s * rows : (s + 1) * rows] = (far + near).astype(BF)
-        send_ref[j] = dot(picked[pl.ds(pl.multiple_of((1 - core) * half, half), half), :], dys[...])
-        keep_ref[j] = dot(picked[pl.ds(pl.multiple_of(core * half, half), half), :], dys[...])
-        return carry
-
-    lax.fori_loop(0, count, offset, 0)
-
-
-def wgrad(place, picked, dys, maps, lower, upper):
-    count, width, columns = picked.shape
+            chosen = chosen_slots(maps, s, place_ref[0] * picked_ref.shape[0] + first + j, rows, rows + far, rows)
+            near = picked_ref[first + j, :, s * rows : (s + 1) * rows].astype(F32)
+            picked[j, :, s * rows : (s + 1) * rows] = (dot(tables[:, s * far : (s + 1) * far], chosen) + near).astype(BF)
+        send_ref[j] = dot(picked[j, pl.ds(pl.multiple_of((1 - core) * half, half), half), :], dys[...])
+        keep_ref[j] = dot(picked[j, pl.ds(pl.multiple_of(core * half, half), half), :], dys[...])
+
+
+def wgrad(place, picked, dys, maps, halos, first, count, after):
+    _, width, columns = picked.shape
     sources = maps.shape[0]
     shape = jax.ShapeDtypeStruct((count, width // 2, width), F32)
     return pl.pallas_call(
-        wgrad_kernel,
+        functools.partial(wgrad_kernel, sources, first),
         out_shape=(shape, shape),
-        in_specs=[SMEM] + [VMEM] * 5,
+        in_specs=[SMEM] + [VMEM] * (3 + sources) + [ANY],
         out_specs=(VMEM, VMEM),
         scratch_shapes=[
-            pltpu.VMEM((width, 2 * lower.shape[0]), BF),
-            pltpu.VMEM((width, columns), BF),
+            pltpu.VMEM((width, sources * halos[0].shape[0]), BF),
+            pltpu.VMEM((count, width, columns), BF),
         ],
         compiler_params=params(),
         cost_estimate=cost(),
         name="wgrad",
-    )(place, picked, dys, maps, lower, upper)
+    )(place, picked, dys, maps, *halos, after)
 
 
 def power(exponent):
@@ -463,19 +431,19 @@
     each("wait")
 
 
-def assemble(place, pieces, marks, parts, groups, offsets, width):
+def assemble(place, pieces, marks, parts, groups, offsets, width, after):
     return pl.pallas_call(
         functools.partial(assemble_kernel, marks, parts, groups),
         out_shape=jax.ShapeDtypeStruct((offsets, width, width), BF),
-        in_specs=[SMEM] + [ANY] * len(pieces),
+        in_specs=[SMEM] + [ANY] * (len(pieces) + 1),
         out_specs=ANY,
         scratch_shapes=[pltpu.SemaphoreType.DMA((len(pieces), parts, 2))],
         compiler_params=params(),
         name="assemble",
-    )(place, *pieces)
-
-
-def assemble_plain(place, pieces, marks, parts, groups, offsets, width):
+    )(place, *pieces, after)
+
+
+def assemble_plain(place, pieces, marks, parts, groups, offsets, width, after):
     _, count, block, _ = pieces[0].shape
     total = jnp.zeros((groups * count, width, width), BF)
     for piece, (m, o, masks) in zip(pieces, marks):
@@ -504,39 +472,38 @@
     groups = lax.axis_size("dp") // 2
     parts = lax.axis_size("space")
     count = -(-offsets // groups)
-    map_rows = -(-(groups * count + 1) // 16) * 16
+    map_rows = -(-(groups * count) // 16) * 16
     dp, space = lax.axis_index("dp"), lax.axis_index("space")
     place = jnp.stack([dp // 2, dp % 2, space]).astype(jnp.int32)
 
-    pack = prep(live, features, cotangent, kernel_map, send_up, send_down, map_rows)
+    pack, up_rows, down_rows = prep(live, features, cotangent, kernel_map, send_up, send_down, map_rows)
     packs = [pack] + [swap(pack, "dp", 2 * m) for m in range(1, groups)]
-    per_step = 3 if offsets % 3 == 0 else 1
-    own_grad, low_grad, high_grad = backward(pack, weights, rows, halo, 0, offsets // per_step, per_step, pack)
+    lower = passed_along(up_rows, "space", 1)
+    upper = passed_along(down_rows, "space", -1)
+    halo_rows = jnp.concatenate([lower, upper])
+    halos = [halo_rows] + [swap(halo_rows, "dp", 2 * m) for m in range(1, groups)]
+    picked, dys, maps = wgrad_own(place, packs, count, rows)
+    keep, send = wgrad(place, picked, dys, maps, halos, 0, count, dys)
+    mine, *coded = blocks(place, keep, swap(send, "dp", 1), parts)
+    own_grad, low_grad, high_grad, token = backward(pack, weights, rows, halo, mine)
     back_up = passed_along(low_grad, "space", -1)
     back_down = passed_along(high_grad, "space", 1)
-
-    up_rows, down_rows = pick(packs, rows, halo, low_grad)
-    lower = passed_along(up_rows, "space", 1)
-    upper = passed_along(down_rows, "space", -1)
-    picked, dys, maps = wgrad_own(place, packs, count, rows, up_rows)
-    keep, send = wgrad(place, picked, dys, maps, lower, upper)
-    mine, *coded = blocks(place, keep, swap(send, "dp", 1), parts)
-    out_features, token = forward(live, pack, lower, upper, weights, rows, halo, mine)
-    grad_features, grad_token = final(live, own_grad, back_up, back_down, send_up, send_down, token)
     scale = 1.0 / math.sqrt(rows * lax.axis_size("dp") * parts)
-    rounded = scaled_total(mine, [swap(block, "space", m + 1) for m, block in enumerate(coded)], scale, (token, grad_token))
+    rounded = scaled_total(mine, [swap(block, "space", m + 1) for m, block in enumerate(coded)], scale, (token, token))
+    out_features, token = forward(live, pack, halo_rows, weights, rows, rounded)
 
     in_line = [rounded] + [swap(rounded, "space", m) for m in range(1, parts)]
     pieces, marks = [], []
     for masks in SPLITS(parts):
-        lines = line([in_line[m] for m in masks], pieces[2::2][-groups:])
+        lines = line([in_line[m] for m in masks], pieces[2::2][-groups:] + [token])
         for m in range(groups):
             piece = swap(lines, "dp", 2 * m) if m else lines
             pieces += [piece, swap(piece, "dp", 1)]
             marks += [(m, 0, masks), (m, 1, masks)]
+    grad_features, token = final(live, own_grad, back_up, back_down, send_up, send_down, lines)
     dense = rounded.shape[1] % 16 == 0 and groups * count - offsets < count
     put = assemble if dense else assemble_plain
-    grad_weights = put(place, pieces, marks, parts, groups, offsets, width)
+    grad_weights = put(place, pieces, marks, parts, groups, offsets, width, token)
     return (out_features, grad_features, grad_weights)
 
 

time: 95.4 us -> 86.1 us (0.903); the launches traced: 95.1 us -> 84.6 us
  waiting for transfers between devices: 26.9 us -> 17.9 us
  local copies, waits for them, and re-layouts: 2.98 us -> 0.99 us
  starting transfers between devices: 33.5 us -> 35.1 us
  Pallas kernels: 30.3 us -> 29 us
    ppermute x24 -> x27, waiting for transfers between devices: 26.9 us -> 6.54 us  [swap(): lax.ppermute(value, axis, [(i, i ^ mask) for i in range(lax.axis_size(axi...]
    ppermute x4, waiting for transfers between devices: 0.01 us -> 11.3 us  [passed_along(): lax.ppermute(value, axis, [(i, i + steps) for i in range(max(0, -steps),...]
    ppermute x24 -> x27, starting transfers between devices: 23.8 us -> 26.8 us  [swap(): lax.ppermute(value, axis, [(i, i ^ mask) for i in range(lax.axis_size(axi...]
    unnamed x12 -> x11, local copies, waits for them, and re-layouts: 2.98 us -> 0.98 us
    ppermute x4, starting transfers between devices: 9.71 us -> 8.37 us  [passed_along(): lax.ppermute(value, axis, [(i, i + steps) for i in range(max(0, -steps),...]
    pallas_call x4 -> x3, Pallas kernels: 14.8 us -> 13.5 us  [the longest x1 7.99 us: backward(): pl.pallas_call(backward_kernel, grid=(offsets // per_step,), out_shape=tu...]
  transfers between devices with their start and end apart: 28 -> 31, of which waited for: 11 -> 10; matrix products, arithmetic and copies ran while one was open for 0% -> 0% of each run, Pallas kernels for 20% -> 22%
where the time goes in v4:
time: 86.1 us; the launch traced here: 84.6 us
  starting transfers between devices  35.1 us (41%)
  Pallas kernels  29 us (34%)
  waiting for transfers between devices  17.9 us (21%)
  between operations  1.53 us (2%)
  local copies, waits for them, and re-layouts  0.99 us (1%)
    ppermute x27, starting transfers between devices, swap(): lax.ppermute(value, axis, [(i, i ^ mask) for i in range(lax.axis_size(axi...  26.8 us
    ppermute x4, waiting for transfers between devices, passed_along(): lax.ppermute(value, axis, [(i, i + steps) for i in range(max(0, -steps),...  11.3 us
    ppermute x4, starting transfers between devices, passed_along(): lax.ppermute(value, axis, [(i, i + steps) for i in range(max(0, -steps),...  8.37 us
    pallas_call x1, Pallas kernels, backward(): pl.pallas_call(backward_kernel, grid=(offsets // per_step,), out_shape=tu...  7.99 us
    ppermute x27, waiting for transfers between devices, swap(): lax.ppermute(value, axis, [(i, i ^ mask) for i in range(lax.axis_size(axi...  6.54 us
    pallas_call x1, Pallas kernels, forward(): pl.pallas_call(forward_kernel, grid=(offsets // per_step,), out_shape=(ja...  6.53 us
    pallas_call x1, Pallas kernels, wgrad(): pl.pallas_call(functools.partial(wgrad_kernel, sources, first), out_shape...  3.7 us
    pallas_call x1, Pallas kernels, assemble(): pl.pallas_call(functools.partial(assemble_kernel, marks, parts, groups),...  3.47 us
  transfers between devices with their start and end apart: 31, of which 10 were waited for; matrix products, arithmetic and copies ran while one was open for 0% of the time, Pallas kernels for 22%

profile of v4, /device:TPU:0, one launch (start us, length us, event | category | flops | bytes accessed | tf_op | source)
XLA Modules:
  0.0 84.6 jit_solution(9152337094946562611)
XLA Ops:
  1.3 1.9 %prep.1 = (bf16[544,256]{1,0:T(8,128)(2,1)}, bf16[64,256]{1,0:T(8,128)(2,1)}, bf16[64,256]{1,0:T(8,128)(2,1)}) custom-call(s32[1]{0:T(128)S(6)} %copy.11.live_ref, bf16[256,256]{1,0:T(8,128)(2,1)} %x_hbm.1, bf16[256,256]{1,0:T(8,128)(2,1)} %dy_hbm.1, s32[27,256]{1,0:T(8,128)} %map_hbm.1, s32[1,64]{1,0:T(1,128)} %up_ref.1, s32[1,64]{1,0:T(1,128)} %down_ref.1), custom_call_target="tpu_custom_call" | custom-call | tf_op jit(solution)/shard_map/prep/pallas_call | solution.py:71
  3.1 4.0 %collective-permute-start.4 = (bf16[544,256]{1,0:T(8,128)(2,1)}, bf16[544,256]{1,0:T(8,128)(2,1)S(1)}, u32[]{:S(2)}, u32[]{:S(2)}) collective-permute-start(bf16[544,256]{1,0:T(8,128)(2,1)} %get-tuple-element.23.refs_0_.pack_ref), channel_id=1, source_target_pairs={{0,24},{4,28},{8,16},{12,20},{16,8},{20,12},{24,0},{28,4},{1,25},{... | collective-permute-start | bytes 835592 | tf_op jit(solution)/shard_map/ppermute | solution.py:457
  7.1 3.5 %collective-permute-start = (bf16[64,256]{1,0:T(8,128)(2,1)}, bf16[64,256]{1,0:T(8,128)(2,1)S(1)}, u32[]{:S(2)}, u32[]{:S(2)}) collective-permute-start(bf16[64,256]{1,0:T(8,128)(2,1)} %get-tuple-element.24), channel_id=1, source_target_pairs={{0,1},{1,2},{2,3},{4,5},{5,6},{6,7},{8,9},{9,10},{10,11},{12,13},{... | collective-permute-start | bytes 98312 | tf_op jit(solution)/shard_map/ppermute | solution.py:462
  10.6 0.6 collective-permute-start.3
  11.1 0.5 collective-permute-start.2
  11.7 1.3 %collective-permute-start.1 = (bf16[64,256]{1,0:T(8,128)(2,1)}, bf16[64,256]{1,0:T(8,128)(2,1)S(1)}, u32[]{:S(2)}, u32[]{:S(2)}) collective-permute-start(bf16[64,256]{1,0:T(8,128)(2,1)} %get-tuple-element.25), channel_id=1, source_target_pairs={{1,0},{2,1},{3,2},{5,4},{6,5},{7,6},{9,8},{10,9},{11,10},{13,12},{... | collective-permute-start | bytes 98312 | tf_op jit(solution)/shard_map/ppermute | solution.py:462
  13.0 4.7 %collective-permute-done.1 = bf16[64,256]{1,0:T(8,128)(2,1)S(1)} collective-permute-done((bf16[64,256]{1,0:T(8,128)(2,1)}, bf16[64,256]{1,0:T(8,128)(2,1)S(1)}, u32[]{:S(2)}, u32[]{:S(2)}) %collective-permute-start.1) | collective-permute-done | bytes 32800 | tf_op jit(solution)/shard_map/ppermute | solution.py:462
  17.7 2.4 %collective-permute-start.7 = (bf16[128,256]{1,0:T(8,128)(2,1)S(1)}, bf16[128,256]{1,0:T(8,128)(2,1)S(1)}, u32[]{:S(2)}, u32[]{:S(2)}) collective-permute-start(bf16[128,256]{1,0:T(8,128)(2,1)S(1)} %constant_dynamic-update-slice_fusion.refs_0_.halo_ref), channel_id=1, source_target_pairs={{0,24},{4,28},{8,16},{12,20},{16,8},{20,12},{24,0},{28,4},{1,25},{... | collective-permute-start | bytes 196616 | tf_op jit(solution)/shard_map/ppermute | solution.py:457
  20.1 0.5 collective-permute-start.6
  20.7 0.5 collective-permute-start.5
  21.2 0.1 pad_add_fusion.place_ref
  21.3 1.0 %copy-done.1 = bf16[544,256]{1,0:T(8,128)(2,1)S(1)} copy-done((bf16[544,256]{1,0:T(8,128)(2,1)S(1)}, bf16[544,256]{1,0:T(8,128)(2,1)}, u32[]{:S(2)}) %copy-start.1) | copy-done | bytes 278552
  22.2 3.2 %wgrad_own.1 = (bf16[7,256,1024]{2,1,0:T(8,128)(2,1)S(1)}, bf16[1024,256]{1,0:T(8,128)(2,1)S(1)}, s32[4,32,256]{2,1,0:T(8,128)S(1)}) custom-call(s32[3]{0:T(128)S(1)} %pad_add_fusion.place_ref, bf16[544,256]{1,0:T(8,128)(2,1)S(1)} %copy-done.1, bf16[544,256]{1,0:T(8,128)(2,1)S(1)} %collective-permute-done.2.refs_1_, ...), custom_call_target="tpu_custom_call" | custom-call | flops 100000000 | bytes 100000 | tf_op jit(solution)/shard_map/wgrad_own/pallas_call | solution.py:241
  25.5 3.7 %wgrad.1 = (f32[7,128,256]{2,1,0:T(8,128)S(1)}, f32[7,128,256]{2,1,0:T(8,128)S(1)}) custom-call(s32[3]{0:T(128)S(1)} %pad_add_fusion.place_ref, bf16[7,256,1024]{2,1,0:T(8,128)(2,1)S(1)} %get-tuple-element.26.picked_ref, bf16[1024,256]{1,0:T(8,128)(2,1)S(1)} %get-tuple-element.27.dys.refs_4_, s32[4,32,256]{2,1,0:T(8,128)S(1)} %get-tuple-element.28.maps, ...), custom_call_target="tpu_custom_call" | custom-call | flops 100000000 | bytes 100000 | tf_op jit(solution)/shard_map/wgrad/pallas_call | solution.py:278
  29.2 0.1 collective-permute-start.8
  29.3 2.5 %collective-permute-done.8.got_ref = f32[7,128,256]{2,1,0:T(8,128)S(1)} collective-permute-done((f32[7,128,256]{2,1,0:T(8,128)S(1)}, f32[7,128,256]{2,1,0:T(8,128)S(1)}, u32[]{:S(2)}, u32[]{:S(2)}) %collective-permute-start.8) | collective-permute-done | bytes 917536 | tf_op jit(solution)/shard_map/ppermute | solution.py:457
  31.8 1.1 %blocks.1 = (f32[7,32,256]{2,1,0:T(8,128)S(1)}, s16[240,256]{1,0:T(8,128)(2,1)S(1)}, s16[240,256]{1,0:T(8,128)(2,1)S(1)}, s16[240,256]{1,0:T(8,128)(2,1)S(1)}) custom-call(s32[3]{0:T(128)S(1)} %pad_add_fusion.place_ref, f32[7,128,256]{2,1,0:T(8,128)S(1)} %get-tuple-element.29.keep_ref, f32[7,128,256]{2,1,0:T(8,128)S(1)} %collective-permute-done.8.got_ref), custom_call_target="tpu_custom_call" | custom-call | flops 100000000 | bytes 100000 | tf_op jit(solution)/shard_map/blocks/pallas_call | solution.py:326
  32.8 1.6 %collective-permute-start.9 = (s16[240,256]{1,0:T(8,128)(2,1)S(1)}, s16[240,256]{1,0:T(8,128)(2,1)S(1)}, u32[]{:S(2)}, u32[]{:S(2)}) collective-permute-start(s16[240,256]{1,0:T(8,128)(2,1)S(1)} %get-tuple-element.32), channel_id=1, source_target_pairs={{0,1},{1,0},{2,3},{3,2},{4,5},{5,4},{6,7},{7,6},{8,9},{9,8},{10,11... | collective-permute-start | bytes 368648 | tf_op jit(solution)/shard_map/ppermute | solution.py:457
  34.5 2.7 %collective-permute-start.10 = (s16[240,256]{1,0:T(8,128)(2,1)S(1)}, s16[240,256]{1,0:T(8,128)(2,1)S(1)}, u32[]{:S(2)}, u32[]{:S(2)}) collective-permute-start(s16[240,256]{1,0:T(8,128)(2,1)S(1)} %get-tuple-element.33), channel_id=1, source_target_pairs={{0,2},{1,3},{2,0},{3,1},{4,6},{5,7},{6,4},{7,5},{8,10},{9,11},{10,... | collective-permute-start | bytes 368648 | tf_op jit(solution)/shard_map/ppermute | solution.py:457
  37.2 0.1 collective-permute-start.11
  37.3 8.0 %backward.1 = (f32[256,256]{1,0:T(8,128)S(1)}, f32[64,256]{1,0:T(8,128)S(1)}, f32[64,256]{1,0:T(8,128)S(1)}, f32[8,128]{1,0:T(8,128)S(1)}) custom-call(bf16[544,256]{1,0:T(8,128)(2,1)S(1)} %copy-done.2, bf16[27,256,256]{2,1,0:T(8,128)(2,1)S(1)} %copy-done, f32[7,32,256]{2,1,0:T(8,128)S(1)} %get-tuple-element.31.after_ref.mine_ref), custom_call_target="tpu_custom_call" | custom-call | flops 100000000 | bytes 100000 | tf_op jit(solution)/shard_map/backward/pallas_call | solution.py:139
  45.3 1.5 %collective-permute-done.10.refs_1_ = s16[240,256]{1,0:T(8,128)(2,1)S(1)} collective-permute-done((s16[240,256]{1,0:T(8,128)(2,1)S(1)}, s16[240,256]{1,0:T(8,128)(2,1)S(1)}, u32[]{:S(2)}, u32[]{:S(2)}) %collective-permute-start.10) | collective-permute-done | bytes 122912 | tf_op jit(solution)/shard_map/ppermute | solution.py:457
  46.9 0.1 total.1.after_ref
  47.0 2.5 %collective-permute-start.19 = (bf16[1,7,32,256]{3,2,1,0:T(8,128)(2,1)S(1)}, bf16[1,7,32,256]{3,2,1,0:T(8,128)(2,1)S(1)}, u32[]{:S(2)}, u32[]{:S(2)}) collective-permute-start(bf16[1,7,32,256]{3,2,1,0:T(8,128)(2,1)S(1)} %bitcast.4), channel_id=1, source_target_pairs={{0,24},{4,28},{8,16},{12,20},{16,8},{20,12},{24,0},{28,4},{1,25},{... | collective-permute-start | bytes 344072 | tf_op jit(solution)/shard_map/ppermute | solution.py:457
  49.5 0.5 collective-permute-start.18
  50.0 0.5 collective-permute-start.17
  50.6 2.5 %collective-permute-start.16 = (bf16[7,32,256]{2,1,0:T(8,128)(2,1)S(1)}, bf16[7,32,256]{2,1,0:T(8,128)(2,1)S(1)}, u32[]{:S(2)}, u32[]{:S(2)}) collective-permute-start(bf16[7,32,256]{2,1,0:T(8,128)(2,1)S(1)} %total.1.after_ref), channel_id=1, source_target_pairs={{0,3},{1,2},{2,1},{3,0},{4,7},{5,6},{6,5},{7,4},{8,11},{9,10},{10,... | collective-permute-start | bytes 344072 | tf_op jit(solution)/shard_map/ppermute | solution.py:457
  53.0 1.2 %collective-permute-start.15 = (bf16[7,32,256]{2,1,0:T(8,128)(2,1)S(1)}, bf16[7,32,256]{2,1,0:T(8,128)(2,1)S(1)}, u32[]{:S(2)}, u32[]{:S(2)}) collective-permute-start(bf16[7,32,256]{2,1,0:T(8,128)(2,1)S(1)} %total.1.after_ref), channel_id=1, source_target_pairs={{0,2},{1,3},{2,0},{3,1},{4,6},{5,7},{6,4},{7,5},{8,10},{9,11},{10,... | collective-permute-start | bytes 344072 | tf_op jit(solution)/shard_map/ppermute | solution.py:457
  54.2 1.6 %collective-permute-start.14 = (bf16[7,32,256]{2,1,0:T(8,128)(2,1)S(1)}, bf16[7,32,256]{2,1,0:T(8,128)(2,1)S(1)}, u32[]{:S(2)}, u32[]{:S(2)}) collective-permute-start(bf16[7,32,256]{2,1,0:T(8,128)(2,1)S(1)} %total.1.after_ref), channel_id=1, source_target_pairs={{0,1},{1,0},{2,3},{3,2},{4,5},{5,4},{6,7},{7,6},{8,9},{9,8},{10,11... | collective-permute-start | bytes 344072 | tf_op jit(solution)/shard_map/ppermute | solution.py:457
  55.8 6.5 %forward.1 = (bf16[256,256]{1,0:T(8,128)(2,1)}, f32[8,128]{1,0:T(8,128)S(1)}) custom-call(s32[1]{0:T(128)S(6)} %copy.11.live_ref, bf16[544,256]{1,0:T(8,128)(2,1)S(1)} %copy-done.2, bf16[128,256]{1,0:T(8,128)(2,1)S(1)} %constant_dynamic-update-slice_fusion.refs_0_.halo_ref, bf16[27,256,256]{2,1,0:T(8,128)(2,1)S(1)} %copy-done, ...), custom_call_target="tpu_custom_call" | custom-call | flops 100000000 | bytes 100000 | tf_op jit(solution)/shard_map/forward/pallas_call | solution.py:191
  62.4 2.3 %collective-permute-start.29 = (bf16[3,7,32,256]{3,2,1,0:T(8,128)(2,1)S(1)}, bf16[3,7,32,256]{3,2,1,0:T(8,128)(2,1)S(1)}, u32[]{:S(2)}, u32[]{:S(2)}) collective-permute-start(bf16[3,7,32,256]{3,2,1,0:T(8,128)(2,1)S(1)} %line.1.after_ref.refs_8_), channel_id=1, source_target_pairs={{0,24},{4,28},{8,16},{12,20},{16,8},{20,12},{24,0},{28,4},{1,25},{... | collective-permute-start | bytes 1032200 | tf_op jit(solution)/shard_map/ppermute | solution.py:457
  64.7 0.7 collective-permute-start.27
  65.3 0.6 collective-permute-start.25
  65.9 1.3 %collective-permute-start.12 = (f32[64,256]{1,0:T(8,128)S(1)}, f32[64,256]{1,0:T(8,128)S(1)}, u32[]{:S(2)}, u32[]{:S(2)}) collective-permute-start(f32[64,256]{1,0:T(8,128)S(1)} %get-tuple-element.38), channel_id=1, source_target_pairs={{1,0},{2,1},{3,2},{5,4},{6,5},{7,6},{9,8},{10,9},{11,10},{13,12},{... | collective-permute-start | bytes 196616 | tf_op jit(solution)/shard_map/ppermute | solution.py:462
  67.3 4.8 %collective-permute-done.12.back_up_ref = f32[64,256]{1,0:T(8,128)S(1)} collective-permute-done((f32[64,256]{1,0:T(8,128)S(1)}, f32[64,256]{1,0:T(8,128)S(1)}, u32[]{:S(2)}, u32[]{:S(2)}) %collective-permute-start.12) | collective-permute-done | bytes 65568 | tf_op jit(solution)/shard_map/ppermute | solution.py:462
  72.1 2.3 %collective-permute-start.13 = (f32[64,256]{1,0:T(8,128)S(1)}, f32[64,256]{1,0:T(8,128)S(1)}, u32[]{:S(2)}, u32[]{:S(2)}) collective-permute-start(f32[64,256]{1,0:T(8,128)S(1)} %get-tuple-element.39), channel_id=1, source_target_pairs={{0,1},{1,2},{2,3},{4,5},{5,6},{6,7},{8,9},{9,10},{10,11},{12,13},{... | collective-permute-start | bytes 196616 | tf_op jit(solution)/shard_map/ppermute | solution.py:462
  74.4 1.9 %collective-permute-done.13.back_down_ref = f32[64,256]{1,0:T(8,128)S(1)} collective-permute-done((f32[64,256]{1,0:T(8,128)S(1)}, f32[64,256]{1,0:T(8,128)S(1)}, u32[]{:S(2)}, u32[]{:S(2)}) %collective-permute-start.13) | collective-permute-done | bytes 65568 | tf_op jit(solution)/shard_map/ppermute | solution.py:462
  76.3 0.5 collective-permute-start.23
  76.9 0.6 collective-permute-done.27.refs_12_
  77.5 0.1 collective-permute-done.25.refs_10_
  77.6 0.4 collective-permute-start.26
  78.0 0.1 collective-permute-done.23.refs_7_
  78.1 0.1 collective-permute-start.22
  78.3 1.5 %collective-permute-done.22.refs_5_ = bf16[1,7,32,256]{3,2,1,0:T(8,128)(2,1)S(1)} collective-permute-done((bf16[1,7,32,256]{3,2,1,0:T(8,128)(2,1)S(1)}, bf16[1,7,32,256]{3,2,1,0:T(8,128)(2,1)S(1)}, u32[]{:S(2)}, u32[]{:S(2)}) %collective-permute-start.22) | collective-permute-done | bytes 114720 | tf_op jit(solution)/shard_map/ppermute | solution.py:457
  79.8 0.1 collective-permute-start.21
  79.9 1.0 %final.1 = (bf16[256,256]{1,0:T(8,128)(2,1)}, f32[8,128]{1,0:T(8,128)S(1)}) custom-call(s32[1]{0:T(128)S(6)} %copy.11.live_ref, f32[256,256]{1,0:T(8,128)S(1)} %get-tuple-element.37.own_ref, f32[64,256]{1,0:T(8,128)S(1)} %collective-permute-done.12.back_up_ref, f32[64,256]{1,0:T(8,128)S(1)} %collective-permute-done.13.back_down_ref, s32[1,64]{1,0:T(1,128)S(1)} %copy-done.3, ...), custom_call_target="tpu_custom_call" | custom-call | tf_op jit(solution)/shard_map/final/pallas_call | solution.py:380
  81.0 0.2 collective-permute-done.21.refs_3_
  81.1 3.5 %assemble.1 = bf16[27,256,256]{2,1,0:T(8,128)(2,1)} custom-call(s32[3]{0:T(128)S(1)} %pad_add_fusion.place_ref, bf16[1,7,32,256]{3,2,1,0:T(8,128)(2,1)S(1)} %bitcast.8, bf16[1,7,32,256]{3,2,1,0:T(8,128)(2,1)S(1)} %collective-permute-done.20.refs_1_, bf16[1,7,32,256]{3,2,1,0:T(8,128)(2,1)S(1)} %collective-permute-done.17.refs_3_.refs_2_, ...), custom_call_target="tpu_custom_call" | custom-call | tf_op jit(solution)/shard_map/assemble/pallas_call | solution.py:435
  (37 shorter events, 0.3 us)
Async XLA Ops:
  3.1 17.5 %collective-permute-start.4 = (bf16[544,256]{1,0:T(8,128)(2,1)}, bf16[544,256]{1,0:T(8,128)(2,1)S(1)}, u32[]{:S(2)}, u32[]{:S(2)}) collective-permute-start(bf16[544,256]{1,0:T(8,128)(2,1)} %get-tuple-element.23.refs_0_.pack_ref), channel_id=1, source_target_pairs={{0,24},{4,28},{8,16},{12,20},{16,8},{20,12},{24,0},{28,4},{1,25},{... | collective-permute-start | bytes 835592 | tf_op jit(solution)/shard_map/ppermute | solution.py:457
  7.1 5.9 %collective-permute-start = (bf16[64,256]{1,0:T(8,128)(2,1)}, bf16[64,256]{1,0:T(8,128)(2,1)S(1)}, u32[]{:S(2)}, u32[]{:S(2)}) collective-permute-start(bf16[64,256]{1,0:T(8,128)(2,1)} %get-tuple-element.24), channel_id=1, source_target_pairs={{0,1},{1,2},{2,3},{4,5},{5,6},{6,7},{8,9},{9,10},{10,11},{12,13},{... | collective-permute-start | bytes 98312 | tf_op jit(solution)/shard_map/ppermute | solution.py:462
  10.6 10.7 %collective-permute-start.3 = (bf16[544,256]{1,0:T(8,128)(2,1)}, bf16[544,256]{1,0:T(8,128)(2,1)S(1)}, u32[]{:S(2)}, u32[]{:S(2)}) collective-permute-start(bf16[544,256]{1,0:T(8,128)(2,1)} %get-tuple-element.23.refs_0_.pack_ref), channel_id=1, source_target_pairs={{0,16},{4,20},{8,24},{12,28},{16,0},{20,4},{24,8},{28,12},{1,17},{... | collective-permute-start | bytes 835592 | tf_op jit(solution)/shard_map/ppermute | solution.py:457
  11.1 10.1 %collective-permute-start.2 = (bf16[544,256]{1,0:T(8,128)(2,1)}, bf16[544,256]{1,0:T(8,128)(2,1)S(1)}, u32[]{:S(2)}, u32[]{:S(2)}) collective-permute-start(bf16[544,256]{1,0:T(8,128)(2,1)} %get-tuple-element.23.refs_0_.pack_ref), channel_id=1, source_target_pairs={{0,8},{4,12},{8,0},{12,4},{16,24},{20,28},{24,16},{28,20},{1,9},{5... | collective-permute-start | bytes 835592 | tf_op jit(solution)/shard_map/ppermute | solution.py:457
  11.7 6.0 %collective-permute-start.1 = (bf16[64,256]{1,0:T(8,128)(2,1)}, bf16[64,256]{1,0:T(8,128)(2,1)S(1)}, u32[]{:S(2)}, u32[]{:S(2)}) collective-permute-start(bf16[64,256]{1,0:T(8,128)(2,1)} %get-tuple-element.25), channel_id=1, source_target_pairs={{1,0},{2,1},{3,2},{5,4},{6,5},{7,6},{9,8},{10,9},{11,10},{13,12},{... | collective-permute-start | bytes 98312 | tf_op jit(solution)/shard_map/ppermute | solution.py:462
  17.7 7.8 %collective-permute-start.7 = (bf16[128,256]{1,0:T(8,128)(2,1)S(1)}, bf16[128,256]{1,0:T(8,128)(2,1)S(1)}, u32[]{:S(2)}, u32[]{:S(2)}) collective-permute-start(bf16[128,256]{1,0:T(8,128)(2,1)S(1)} %constant_dynamic-update-slice_fusion.refs_0_.halo_ref), channel_id=1, source_target_pairs={{0,24},{4,28},{8,16},{12,20},{16,8},{20,12},{24,0},{28,4},{1,25},{... | collective-permute-start | bytes 196616 | tf_op jit(solution)/shard_map/ppermute | solution.py:457
  20.1 5.4 %collective-permute-start.6 = (bf16[128,256]{1,0:T(8,128)(2,1)S(1)}, bf16[128,256]{1,0:T(8,128)(2,1)S(1)}, u32[]{:S(2)}, u32[]{:S(2)}) collective-permute-start(bf16[128,256]{1,0:T(8,128)(2,1)S(1)} %constant_dynamic-update-slice_fusion.refs_0_.halo_ref), channel_id=1, source_target_pairs={{0,16},{4,20},{8,24},{12,28},{16,0},{20,4},{24,8},{28,12},{1,17},{... | collective-permute-start | bytes 196616 | tf_op jit(solution)/shard_map/ppermute | solution.py:457
  20.7 4.9 %collective-permute-start.5 = (bf16[128,256]{1,0:T(8,128)(2,1)S(1)}, bf16[128,256]{1,0:T(8,128)(2,1)S(1)}, u32[]{:S(2)}, u32[]{:S(2)}) collective-permute-start(bf16[128,256]{1,0:T(8,128)(2,1)S(1)} %constant_dynamic-update-slice_fusion.refs_0_.halo_ref), channel_id=1, source_target_pairs={{0,8},{4,12},{8,0},{12,4},{16,24},{20,28},{24,16},{28,20},{1,9},{5... | collective-permute-start | bytes 196616 | tf_op jit(solution)/shard_map/ppermute | solution.py:457
  21.3 1.0 %copy-start.1 = (bf16[544,256]{1,0:T(8,128)(2,1)S(1)}, bf16[544,256]{1,0:T(8,128)(2,1)}, u32[]{:S(2)}) copy-start(bf16[544,256]{1,0:T(8,128)(2,1)} %get-tuple-element.23.refs_0_.pack_ref) | copy-start | bytes 835588
  25.5 11.8 %copy-start = (bf16[27,256,256]{2,1,0:T(8,128)(2,1)S(1)}, bf16[27,256,256]{2,1,0:T(8,128)(2,1)}, u32[]{:S(2)}) copy-start(bf16[27,256,256]{2,1,0:T(8,128)(2,1)} %w_ref.3) | copy-start | bytes 10616836
  25.5 11.8 %copy-start.2 = (bf16[544,256]{1,0:T(8,128)(2,1)S(1)}, bf16[544,256]{1,0:T(8,128)(2,1)}, u32[]{:S(2)}) copy-start(bf16[544,256]{1,0:T(8,128)(2,1)} %get-tuple-element.23.refs_0_.pack_ref) | copy-start | bytes 835588
  29.2 2.5 %collective-permute-start.8 = (f32[7,128,256]{2,1,0:T(8,128)S(1)}, f32[7,128,256]{2,1,0:T(8,128)S(1)}, u32[]{:S(2)}, u32[]{:S(2)}) collective-permute-start(f32[7,128,256]{2,1,0:T(8,128)S(1)} %get-tuple-element.30), channel_id=1, source_target_pairs={{0,4},{4,0},{8,12},{12,8},{16,20},{20,16},{24,28},{28,24},{1,5},{5... | collective-permute-start | bytes 2752520 | tf_op jit(solution)/shard_map/ppermute | solution.py:457
  32.8 12.5 %collective-permute-start.9 = (s16[240,256]{1,0:T(8,128)(2,1)S(1)}, s16[240,256]{1,0:T(8,128)(2,1)S(1)}, u32[]{:S(2)}, u32[]{:S(2)}) collective-permute-start(s16[240,256]{1,0:T(8,128)(2,1)S(1)} %get-tuple-element.32), channel_id=1, source_target_pairs={{0,1},{1,0},{2,3},{3,2},{4,5},{5,4},{6,7},{7,6},{8,9},{9,8},{10,11... | collective-permute-start | bytes 368648 | tf_op jit(solution)/shard_map/ppermute | solution.py:457
  34.5 12.4 %collective-permute-start.10 = (s16[240,256]{1,0:T(8,128)(2,1)S(1)}, s16[240,256]{1,0:T(8,128)(2,1)S(1)}, u32[]{:S(2)}, u32[]{:S(2)}) collective-permute-start(s16[240,256]{1,0:T(8,128)(2,1)S(1)} %get-tuple-element.33), channel_id=1, source_target_pairs={{0,2},{1,3},{2,0},{3,1},{4,6},{5,7},{6,4},{7,5},{8,10},{9,11},{10,... | collective-permute-start | bytes 368648 | tf_op jit(solution)/shard_map/ppermute | solution.py:457
  37.2 9.7 %collective-permute-start.11 = (s16[240,256]{1,0:T(8,128)(2,1)S(1)}, s16[240,256]{1,0:T(8,128)(2,1)S(1)}, u32[]{:S(2)}, u32[]{:S(2)}) collective-permute-start(s16[240,256]{1,0:T(8,128)(2,1)S(1)} %get-tuple-element.34), channel_id=1, source_target_pairs={{0,3},{1,2},{2,1},{3,0},{4,7},{5,6},{6,5},{7,4},{8,11},{9,10},{10,... | collective-permute-start | bytes 368648 | tf_op jit(solution)/shard_map/ppermute | solution.py:457
  45.3 34.7 %copy-start.3 = (s32[1,64]{1,0:T(1,128)S(1)}, s32[1,64]{1,0:T(1,128)}, u32[]{:S(2)}) copy-start(s32[1,64]{1,0:T(1,128)} %up_ref.1) | copy-start | bytes 772
  45.3 34.6 %copy-start.4 = (s32[1,64]{1,0:T(1,128)S(1)}, s32[1,64]{1,0:T(1,128)}, u32[]{:S(2)}) copy-start(s32[1,64]{1,0:T(1,128)} %down_ref.1) | copy-start | bytes 772
  47.0 7.2 %collective-permute-start.19 = (bf16[1,7,32,256]{3,2,1,0:T(8,128)(2,1)S(1)}, bf16[1,7,32,256]{3,2,1,0:T(8,128)(2,1)S(1)}, u32[]{:S(2)}, u32[]{:S(2)}) collective-permute-start(bf16[1,7,32,256]{3,2,1,0:T(8,128)(2,1)S(1)} %bitcast.4), channel_id=1, source_target_pairs={{0,24},{4,28},{8,16},{12,20},{16,8},{20,12},{24,0},{28,4},{1,25},{... | collective-permute-start | bytes 344072 | tf_op jit(solution)/shard_map/ppermute | solution.py:457
  49.5 12.8 %collective-permute-start.18 = (bf16[1,7,32,256]{3,2,1,0:T(8,128)(2,1)S(1)}, bf16[1,7,32,256]{3,2,1,0:T(8,128)(2,1)S(1)}, u32[]{:S(2)}, u32[]{:S(2)}) collective-permute-start(bf16[1,7,32,256]{3,2,1,0:T(8,128)(2,1)S(1)} %bitcast.5), channel_id=1, source_target_pairs={{0,16},{4,20},{8,24},{12,28},{16,0},{20,4},{24,8},{28,12},{1,17},{... | collective-permute-start | bytes 344072 | tf_op jit(solution)/shard_map/ppermute | solution.py:457
  50.0 12.3 %collective-permute-start.17 = (bf16[1,7,32,256]{3,2,1,0:T(8,128)(2,1)S(1)}, bf16[1,7,32,256]{3,2,1,0:T(8,128)(2,1)S(1)}, u32[]{:S(2)}, u32[]{:S(2)}) collective-permute-start(bf16[1,7,32,256]{3,2,1,0:T(8,128)(2,1)S(1)} %bitcast.6), channel_id=1, source_target_pairs={{0,8},{4,12},{8,0},{12,4},{16,24},{20,28},{24,16},{28,20},{1,9},{5... | collective-permute-start | bytes 344072 | tf_op jit(solution)/shard_map/ppermute | solution.py:457
  50.6 11.8 %collective-permute-start.16 = (bf16[7,32,256]{2,1,0:T(8,128)(2,1)S(1)}, bf16[7,32,256]{2,1,0:T(8,128)(2,1)S(1)}, u32[]{:S(2)}, u32[]{:S(2)}) collective-permute-start(bf16[7,32,256]{2,1,0:T(8,128)(2,1)S(1)} %total.1.after_ref), channel_id=1, source_target_pairs={{0,3},{1,2},{2,1},{3,0},{4,7},{5,6},{6,5},{7,4},{8,11},{9,10},{10,... | collective-permute-start | bytes 344072 | tf_op jit(solution)/shard_map/ppermute | solution.py:457
  53.0 9.3 %collective-permute-start.15 = (bf16[7,32,256]{2,1,0:T(8,128)(2,1)S(1)}, bf16[7,32,256]{2,1,0:T(8,128)(2,1)S(1)}, u32[]{:S(2)}, u32[]{:S(2)}) collective-permute-start(bf16[7,32,256]{2,1,0:T(8,128)(2,1)S(1)} %total.1.after_ref), channel_id=1, source_target_pairs={{0,2},{1,3},{2,0},{3,1},{4,6},{5,7},{6,4},{7,5},{8,10},{9,11},{10,... | collective-permute-start | bytes 344072 | tf_op jit(solution)/shard_map/ppermute | solution.py:457
  54.2 8.1 %collective-permute-start.14 = (bf16[7,32,256]{2,1,0:T(8,128)(2,1)S(1)}, bf16[7,32,256]{2,1,0:T(8,128)(2,1)S(1)}, u32[]{:S(2)}, u32[]{:S(2)}) collective-permute-start(bf16[7,32,256]{2,1,0:T(8,128)(2,1)S(1)} %total.1.after_ref), channel_id=1, source_target_pairs={{0,1},{1,0},{2,3},{3,2},{4,5},{5,4},{6,7},{7,6},{8,9},{9,8},{10,11... | collective-permute-start | bytes 344072 | tf_op jit(solution)/shard_map/ppermute | solution.py:457
  62.4 14.4 %collective-permute-start.29 = (bf16[3,7,32,256]{3,2,1,0:T(8,128)(2,1)S(1)}, bf16[3,7,32,256]{3,2,1,0:T(8,128)(2,1)S(1)}, u32[]{:S(2)}, u32[]{:S(2)}) collective-permute-start(bf16[3,7,32,256]{3,2,1,0:T(8,128)(2,1)S(1)} %line.1.after_ref.refs_8_), channel_id=1, source_target_pairs={{0,24},{4,28},{8,16},{12,20},{16,8},{20,12},{24,0},{28,4},{1,25},{... | collective-permute-start | bytes 1032200 | tf_op jit(solution)/shard_map/ppermute | solution.py:457
  64.7 12.8 %collective-permute-start.27 = (bf16[3,7,32,256]{3,2,1,0:T(8,128)(2,1)S(1)}, bf16[3,7,32,256]{3,2,1,0:T(8,128)(2,1)S(1)}, u32[]{:S(2)}, u32[]{:S(2)}) collective-permute-start(bf16[3,7,32,256]{3,2,1,0:T(8,128)(2,1)S(1)} %line.1.after_ref.refs_8_), channel_id=1, source_target_pairs={{0,16},{4,20},{8,24},{12,28},{16,0},{20,4},{24,8},{28,12},{1,17},{... | collective-permute-start | bytes 1032200 | tf_op jit(solution)/shard_map/ppermute | solution.py:457
  65.3 12.2 %collective-permute-start.25 = (bf16[3,7,32,256]{3,2,1,0:T(8,128)(2,1)S(1)}, bf16[3,7,32,256]{3,2,1,0:T(8,128)(2,1)S(1)}, u32[]{:S(2)}, u32[]{:S(2)}) collective-permute-start(bf16[3,7,32,256]{3,2,1,0:T(8,128)(2,1)S(1)} %line.1.after_ref.refs_8_), channel_id=1, source_target_pairs={{0,8},{4,12},{8,0},{12,4},{16,24},{20,28},{24,16},{28,20},{1,9},{5... | collective-permute-start | bytes 1032200 | tf_op jit(solution)/shard_map/ppermute | solution.py:457
  65.9 6.1 %collective-permute-start.12 = (f32[64,256]{1,0:T(8,128)S(1)}, f32[64,256]{1,0:T(8,128)S(1)}, u32[]{:S(2)}, u32[]{:S(2)}) collective-permute-start(f32[64,256]{1,0:T(8,128)S(1)} %get-tuple-element.38), channel_id=1, source_target_pairs={{1,0},{2,1},{3,2},{5,4},{6,5},{7,6},{9,8},{10,9},{11,10},{13,12},{... | collective-permute-start | bytes 196616 | tf_op jit(solution)/shard_map/ppermute | solution.py:462
  67.2 9.1 %collective-permute-start.20 = (bf16[1,7,32,256]{3,2,1,0:T(8,128)(2,1)S(1)}, bf16[1,7,32,256]{3,2,1,0:T(8,128)(2,1)S(1)}, u32[]{:S(2)}, u32[]{:S(2)}) collective-permute-start(bf16[1,7,32,256]{3,2,1,0:T(8,128)(2,1)S(1)} %bitcast.7), channel_id=1, source_target_pairs={{0,4},{4,0},{8,12},{12,8},{16,20},{20,16},{24,28},{28,24},{1,5},{5... | collective-permute-start | bytes 344072 | tf_op jit(solution)/shard_map/ppermute | solution.py:457
  72.1 4.2 %collective-permute-start.13 = (f32[64,256]{1,0:T(8,128)S(1)}, f32[64,256]{1,0:T(8,128)S(1)}, u32[]{:S(2)}, u32[]{:S(2)}) collective-permute-start(f32[64,256]{1,0:T(8,128)S(1)} %get-tuple-element.39), channel_id=1, source_target_pairs={{0,1},{1,2},{2,3},{4,5},{5,6},{6,7},{8,9},{9,10},{10,11},{12,13},{... | collective-permute-start | bytes 196616 | tf_op jit(solution)/shard_map/ppermute | solution.py:462
  76.3 4.8 %collective-permute-start.24 = (bf16[3,7,32,256]{3,2,1,0:T(8,128)(2,1)S(1)}, bf16[3,7,32,256]{3,2,1,0:T(8,128)(2,1)S(1)}, u32[]{:S(2)}, u32[]{:S(2)}) collective-permute-start(bf16[3,7,32,256]{3,2,1,0:T(8,128)(2,1)S(1)} %line.1.after_ref.refs_8_), channel_id=1, source_target_pairs={{0,4},{4,0},{8,12},{12,8},{16,20},{20,16},{24,28},{28,24},{1,5},{5... | collective-permute-start | bytes 1032200 | tf_op jit(solution)/shard_map/ppermute | solution.py:457
  76.3 1.8 %collective-permute-start.23 = (bf16[1,7,32,256]{3,2,1,0:T(8,128)(2,1)S(1)}, bf16[1,7,32,256]{3,2,1,0:T(8,128)(2,1)S(1)}, u32[]{:S(2)}, u32[]{:S(2)}) collective-permute-start(bf16[1,7,32,256]{3,2,1,0:T(8,128)(2,1)S(1)} %collective-permute-done.19.refs_5_.refs_6_), channel_id=1, source_target_pairs={{0,4},{4,0},{8,12},{12,8},{16,20},{20,16},{24,28},{28,24},{1,5},{5... | collective-permute-start | bytes 344072 | tf_op jit(solution)/shard_map/ppermute | solution.py:457
  76.8 4.3 %collective-permute-start.30 = (bf16[3,7,32,256]{3,2,1,0:T(8,128)(2,1)S(1)}, bf16[3,7,32,256]{3,2,1,0:T(8,128)(2,1)S(1)}, u32[]{:S(2)}, u32[]{:S(2)}) collective-permute-start(bf16[3,7,32,256]{3,2,1,0:T(8,128)(2,1)S(1)} %collective-permute-done.29.refs_14_), channel_id=1, source_target_pairs={{0,4},{4,0},{8,12},{12,8},{16,20},{20,16},{24,28},{28,24},{1,5},{5... | collective-permute-start | bytes 1032200 | tf_op jit(solution)/shard_map/ppermute | solution.py:457
  77.5 3.6 %collective-permute-start.28 = (bf16[3,7,32,256]{3,2,1,0:T(8,128)(2,1)S(1)}, bf16[3,7,32,256]{3,2,1,0:T(8,128)(2,1)S(1)}, u32[]{:S(2)}, u32[]{:S(2)}) collective-permute-start(bf16[3,7,32,256]{3,2,1,0:T(8,128)(2,1)S(1)} %collective-permute-done.27.refs_12_), channel_id=1, source_target_pairs={{0,4},{4,0},{8,12},{12,8},{16,20},{20,16},{24,28},{28,24},{1,5},{5... | collective-permute-start | bytes 1032200 | tf_op jit(solution)/shard_map/ppermute | solution.py:457
  77.6 3.6 %collective-permute-start.26 = (bf16[3,7,32,256]{3,2,1,0:T(8,128)(2,1)S(1)}, bf16[3,7,32,256]{3,2,1,0:T(8,128)(2,1)S(1)}, u32[]{:S(2)}, u32[]{:S(2)}) collective-permute-start(bf16[3,7,32,256]{3,2,1,0:T(8,128)(2,1)S(1)} %collective-permute-done.25.refs_10_), channel_id=1, source_target_pairs={{0,4},{4,0},{8,12},{12,8},{16,20},{20,16},{24,28},{28,24},{1,5},{5... | collective-permute-start | bytes 1032200 | tf_op jit(solution)/shard_map/ppermute | solution.py:457
  78.1 1.7 %collective-permute-start.22 = (bf16[1,7,32,256]{3,2,1,0:T(8,128)(2,1)S(1)}, bf16[1,7,32,256]{3,2,1,0:T(8,128)(2,1)S(1)}, u32[]{:S(2)}, u32[]{:S(2)}) collective-permute-start(bf16[1,7,32,256]{3,2,1,0:T(8,128)(2,1)S(1)} %collective-permute-done.18.refs_4_), channel_id=1, source_target_pairs={{0,4},{4,0},{8,12},{12,8},{16,20},{20,16},{24,28},{28,24},{1,5},{5... | collective-permute-start | bytes 344072 | tf_op jit(solution)/shard_map/ppermute | solution.py:457
  79.8 1.3 %collective-permute-start.21 = (bf16[1,7,32,256]{3,2,1,0:T(8,128)(2,1)S(1)}, bf16[1,7,32,256]{3,2,1,0:T(8,128)(2,1)S(1)}, u32[]{:S(2)}, u32[]{:S(2)}) collective-permute-start(bf16[1,7,32,256]{3,2,1,0:T(8,128)(2,1)S(1)} %collective-permute-done.17.refs_3_.refs_2_), channel_id=1, source_target_pairs={{0,4},{4,0},{8,12},{12,8},{16,20},{20,16},{24,28},{28,24},{1,5},{5... | collective-permute-start | bytes 344072 | tf_op jit(solution)/shard_map/ppermute | solution.py:457

commit v5 on v4

--- a/solution.py
+++ b/solution.py
@@ -96,57 +96,42 @@
     return jnp.where(code < 0, 256 - code, code)
 
 
-def backward_kernel(pack_ref, w_ref, after_ref, own_ref, low_ref, high_ref, token_ref, *refs):
-    maps, grad_acc, chosen, terms = refs
-    step = pl.program_id(0)
+def backward_kernel(group, pack_ref, w_ref, after_ref, own_ref, low_ref, high_ref, token_ref, maps, chosen, terms):
     offsets, width, _ = w_ref.shape
-    slots = grad_acc.shape[0]
-    rows = chosen.shape[1] // offsets
-
-    @pl.when(step == 0)
-    def _():
-        maps[...] = decoded(pack_ref[2 * rows :])
-        grad_acc[...] = jnp.zeros_like(grad_acc)
-
+    rows = own_ref.shape[0]
+    slots = chosen.shape[1]
+    maps[...] = decoded(pack_ref[2 * rows :])
     dy = pack_ref[rows : 2 * rows]
     slot_down = lax.broadcasted_iota(jnp.int32, (slots, rows), 0)
-    for i in range(offsets):
-        row = maps[pl.ds(step * offsets + i, 1), :]
-        chosen[:, i * rows : (i + 1) * rows] = (slot_down == row).astype(F32).astype(BF)
-        back = lax.dot_general(dy, w_ref[i], (((1,), (1,)), ((), ())), preferred_element_type=F32)
+    for k in range(offsets):
+        at = slice(k % group * rows, (k % group + 1) * rows)
+        chosen[k // group, :, at] = (slot_down == maps[k : k + 1, :]).astype(F32).astype(BF)
+        back = lax.dot_general(dy, w_ref[k], (((1,), (1,)), ((), ())), preferred_element_type=F32)
         for t, part in enumerate(split(back, 2)):
-            terms[t, i * rows : (i + 1) * rows] = part
-    grad_acc[...] += dot(chosen[...], terms[0]) + dot(chosen[...], terms[1])
-
-    @pl.when(step == pl.num_programs(0) - 1)
-    def _():
-        token_ref[...] = jnp.zeros_like(token_ref)
+            terms[k // group, t, at] = part
+    for g in range(offsets // group):
         at = 0
         for out in (own_ref, low_ref, high_ref):
-            out[...] = grad_acc[at : at + out.shape[0]]
+            some = chosen[g, at : at + out.shape[0]]
+            value = dot(some, terms[g, 0]) + dot(some, terms[g, 1])
+            out[...] = value if g == 0 else out[...] + value
             at += out.shape[0]
-
-
-def whole(shape):
-    return pl.BlockSpec(shape, lambda k: (0,) * len(shape))
+    token_ref[...] = jnp.zeros_like(token_ref)
 
 
 def backward(pack, weights, rows, halo, after):
     offsets, width, _ = weights.shape
     slots = rows + 2 * halo
-    per_step = 3 if offsets % 3 == 0 else 1
-    shapes = [jax.ShapeDtypeStruct((n, width), F32) for n in (rows, halo, halo)] + [TOKEN]
-    return pl.pallas_call(
-        backward_kernel,
-        grid=(offsets // per_step,),
-        out_shape=tuple(shapes),
-        in_specs=[whole(pack.shape), pl.BlockSpec((per_step, width, width), lambda k: (k, 0, 0)), ANY],
-        out_specs=tuple(whole(shape.shape) for shape in shapes),
+    group = 3 if offsets % 3 == 0 else 1
+    return pl.pallas_call(
+        functools.partial(backward_kernel, group),
+        out_shape=tuple(jax.ShapeDtypeStruct((n, width), F32) for n in (rows, halo, halo)) + (TOKEN,),
+        in_specs=[VMEM, VMEM, ANY],
+        out_specs=(VMEM,) * 4,
         scratch_shapes=[
             pltpu.VMEM((pack.shape[0] - 2 * rows, rows), jnp.int32),
-            pltpu.VMEM((slots, width), F32),
-            pltpu.VMEM((slots, per_step * rows), BF),
-            pltpu.VMEM((2, per_step * rows, width), BF),
+            pltpu.VMEM((offsets // group, slots, group * rows), BF),
+            pltpu.VMEM((offsets // group, 2, group * rows, width), BF),
         ],
         compiler_params=params(),
         cost_estimate=cost(),
@@ -154,57 +139,43 @@
     )(pack, weights, after)
 
 
-def forward_kernel(live_ref, pack_ref, halo_ref, w_ref, after_ref, out_ref, token_ref, table, maps, out_acc, picked):
-    step = pl.program_id(0)
-    offsets = w_ref.shape[0]
-    rows, width = out_ref.shape
+def forward_kernel(group, live_ref, pack_ref, halo_ref, w_ref, after_ref, out_ref, token_ref, table, maps, out_acc, picked):
+    offsets, width, _ = w_ref.shape
+    rows = out_ref.shape[0]
     slots = table.shape[0]
-
-    @pl.when(step == 0)
-    def _():
-        maps[...] = decoded(pack_ref[2 * rows :])
-        table[0:rows] = pack_ref[0:rows]
-        table[rows:] = halo_ref[...]
-        out_acc[...] = jnp.zeros_like(out_acc)
-
+    table[0:rows] = pack_ref[0:rows]
+    table[rows:] = halo_ref[...]
+    codes = decoded(pack_ref[2 * rows :])
+    maps[...] = jnp.transpose(jnp.concatenate([codes] * (maps.shape[1] // codes.shape[0]), axis=0))
     along = lax.broadcasted_iota(jnp.int32, (rows, 128), 1)
-    for i in range(offsets):
-        row = maps[pl.ds(step * offsets + i, 1), :]
-        column = jnp.transpose(jnp.broadcast_to(row, (128, rows)))
+    for k in range(offsets):
+        column = jnp.broadcast_to(maps[:, k : k + 1], (rows, 128))
         chosen = jnp.concatenate(
             [(along + 128 * b == column).astype(F32).astype(BF) for b in range(slots // 128)], axis=1
         )
-        picked[:, i * width : (i + 1) * width] = dot(chosen, table[...]).astype(BF)
-    out_acc[...] += dot(picked[...], w_ref[...].reshape(offsets * width, width))
-
-    @pl.when(step == pl.num_programs(0) - 1)
-    def _():
-        keep = lax.broadcasted_iota(jnp.int32, (rows, width), 0) < live_ref[0]
-        out_ref[...] = jnp.where(keep, out_acc[...], 0.0).astype(BF)
-        token_ref[...] = jnp.zeros_like(token_ref)
+        picked[k // group, :, k % group * width : (k % group + 1) * width] = dot(chosen, table[...]).astype(BF)
+    for g in range(offsets // group):
+        value = dot(picked[g], w_ref[g * group : (g + 1) * group].reshape(group * width, width))
+        out_acc[...] = value if g == 0 else out_acc[...] + value
+    keep = lax.broadcasted_iota(jnp.int32, (rows, width), 0) < live_ref[0]
+    out_ref[...] = jnp.where(keep, out_acc[...], 0.0).astype(BF)
+    token_ref[...] = jnp.zeros_like(token_ref)
 
 
 def forward(live, pack, halo_rows, weights, rows, after):
     offsets, width, _ = weights.shape
     slots = rows + halo_rows.shape[0]
-    per_step = 3 if offsets % 3 == 0 else 1
-    return pl.pallas_call(
-        forward_kernel,
-        grid=(offsets // per_step,),
+    group = 3 if offsets % 3 == 0 else 1
+    return pl.pallas_call(
+        functools.partial(forward_kernel, group),
         out_shape=(jax.ShapeDtypeStruct((rows, width), BF), TOKEN),
-        in_specs=[
-            SMEM,
-            whole(pack.shape),
-            whole(halo_rows.shape),
-            pl.BlockSpec((per_step, width, width), lambda k: (k, 0, 0)),
-            ANY,
-        ],
-        out_specs=(whole((rows, width)), whole(TOKEN.shape)),
+        in_specs=[SMEM, VMEM, VMEM, VMEM, ANY],
+        out_specs=(VMEM, VMEM),
         scratch_shapes=[
             pltpu.VMEM((slots, width), BF),
-            pltpu.VMEM((pack.shape[0] - 2 * rows, rows), jnp.int32),
+            pltpu.VMEM((rows, 128), jnp.int32),
             pltpu.VMEM((rows, width), F32),
-            pltpu.VMEM((rows, per_step * width), BF),
+            pltpu.VMEM((offsets // group, rows, group * width), BF),
         ],
         compiler_params=params(),
         cost_estimate=cost(),
@@ -227,13 +198,10 @@
         dys[s * rows : (s + 1) * rows] = packs[s][rows : 2 * rows]
         maps[s] = decoded(packs[s][2 * rows :])
 
-    def offset(j, carry):
+    for j in range(count):
         for s in range(sources):
             chosen = chosen_slots(maps, s, place_ref[0] * count + j, 0, rows, rows)
             picked_ref[j, :, s * rows : (s + 1) * rows] = dot(tables[:, s * rows : (s + 1) * rows], chosen).astype(BF)
-        return carry
-
-    lax.fori_loop(0, count, offset, 0)
 
 
 def wgrad_own(place, packs, count, rows):
@@ -267,6 +235,7 @@
             chosen = chosen_slots(maps, s, place_ref[0] * picked_ref.shape[0] + first + j, rows, rows + far, rows)
             near = picked_ref[first + j, :, s * rows : (s + 1) * rows].astype(F32)
             picked[j, :, s * rows : (s + 1) * rows] = (dot(tables[:, s * far : (s + 1) * far], chosen) + near).astype(BF)
+    for j in range(count):
         send_ref[j] = dot(picked[j, pl.ds(pl.multiple_of((1 - core) * half, half), half), :], dys[...])
         keep_ref[j] = dot(picked[j, pl.ds(pl.multiple_of(core * half, half), half), :], dys[...])
 

time: 86.1 us -> 83.5 us (0.970); the launches traced: 84.6 us -> 83.1 us
  Pallas kernels: 29 us -> 21.9 us
  waiting for transfers between devices: 17.9 us -> 24 us
    ppermute x27, waiting for transfers between devices: 6.54 us -> 12.6 us  [swap(): lax.ppermute(value, axis, [(i, i ^ mask) for i in range(lax.axis_size(axi...]
    pallas_call x2, Pallas kernels: 14.5 us -> 9.61 us  [the longest x1 5.46 us: backward(): pl.pallas_call(functools.partial(backward_kernel, group), out_shape=tuple...]
    pallas_call x1, Pallas kernels: 3.22 us -> 1.8 us  [wgrad_own(): pl.pallas_call(functools.partial(wgrad_own_kernel, sources), out_shape=(j...]
  transfers between devices with their start and end apart: 31 -> 31, of which waited for: 10 -> 12; matrix products, arithmetic and copies ran while one was open for 0% -> 0% of each run, Pallas kernels for 22% -> 15%
where the time goes in v5:
time: 83.5 us; the launch traced here: 83.1 us
  starting transfers between devices  34.5 us (41%)
  waiting for transfers between devices  24 us (29%)
  Pallas kernels  21.9 us (26%)
  between operations  1.66 us (2%)
  local copies, waits for them, and re-layouts  0.99 us (1%)
    ppermute x27, starting transfers between devices, swap(): lax.ppermute(value, axis, [(i, i ^ mask) for i in range(lax.axis_size(axi...  26.8 us
    ppermute x27, waiting for transfers between devices, swap(): lax.ppermute(value, axis, [(i, i ^ mask) for i in range(lax.axis_size(axi...  12.6 us
    ppermute x4, waiting for transfers between devices, passed_along(): lax.ppermute(value, axis, [(i, i + steps) for i in range(max(0, -steps),...  11.3 us
    ppermute x4, starting transfers between devices, passed_along(): lax.ppermute(value, axis, [(i, i + steps) for i in range(max(0, -steps),...  7.68 us
    pallas_call x1, Pallas kernels, backward(): pl.pallas_call(functools.partial(backward_kernel, group), out_shape=tuple...  5.46 us
    pallas_call x1, Pallas kernels, forward(): pl.pallas_call(functools.partial(forward_kernel, group), out_shape=(jax.S...  4.14 us
    pallas_call x1, Pallas kernels, assemble(): pl.pallas_call(functools.partial(assemble_kernel, marks, parts, groups),...  3.47 us
    pallas_call x1, Pallas kernels, wgrad(): pl.pallas_call(functools.partial(wgrad_kernel, sources, first), out_shape...  2.89 us
  transfers between devices with their start and end apart: 31, of which 12 were waited for; matrix products, arithmetic and copies ran while one was open for 0% of the time, Pallas kernels for 15%

profile of v5, /device:TPU:0, one launch (start us, length us, event | category | flops | bytes accessed | tf_op | source)
XLA Modules:
  0.0 83.1 jit_solution(10468569261294464970)
XLA Ops:
  1.3 1.9 %prep.1 = (bf16[544,256]{1,0:T(8,128)(2,1)}, bf16[64,256]{1,0:T(8,128)(2,1)}, bf16[64,256]{1,0:T(8,128)(2,1)}) custom-call(s32[1]{0:T(128)S(6)} %copy.11.live_ref, bf16[256,256]{1,0:T(8,128)(2,1)} %x_hbm.1, bf16[256,256]{1,0:T(8,128)(2,1)} %dy_hbm.1, s32[27,256]{1,0:T(8,128)} %map_hbm.1, s32[1,64]{1,0:T(1,128)} %up_ref.1, s32[1,64]{1,0:T(1,128)} %down_ref.1), custom_call_target="tpu_custom_call" | custom-call | tf_op jit(solution)/shard_map/prep/pallas_call | solution.py:71
  3.1 4.0 %collective-permute-start.4 = (bf16[544,256]{1,0:T(8,128)(2,1)}, bf16[544,256]{1,0:T(8,128)(2,1)S(1)}, u32[]{:S(2)}, u32[]{:S(2)}) collective-permute-start(bf16[544,256]{1,0:T(8,128)(2,1)} %get-tuple-element.23.refs_0_.pack_ref), channel_id=1, source_target_pairs={{0,24},{4,28},{8,16},{12,20},{16,8},{20,12},{24,0},{28,4},{1,25},{... | collective-permute-start | bytes 835592 | tf_op jit(solution)/shard_map/ppermute | solution.py:426
  7.1 3.5 %collective-permute-start = (bf16[64,256]{1,0:T(8,128)(2,1)}, bf16[64,256]{1,0:T(8,128)(2,1)S(1)}, u32[]{:S(2)}, u32[]{:S(2)}) collective-permute-start(bf16[64,256]{1,0:T(8,128)(2,1)} %get-tuple-element.24), channel_id=1, source_target_pairs={{0,1},{1,2},{2,3},{4,5},{5,6},{6,7},{8,9},{9,10},{10,11},{12,13},{... | collective-permute-start | bytes 98312 | tf_op jit(solution)/shard_map/ppermute | solution.py:431
  10.6 0.6 collective-permute-start.3
  11.1 0.5 collective-permute-start.2
  11.7 1.3 %collective-permute-start.1 = (bf16[64,256]{1,0:T(8,128)(2,1)}, bf16[64,256]{1,0:T(8,128)(2,1)S(1)}, u32[]{:S(2)}, u32[]{:S(2)}) collective-permute-start(bf16[64,256]{1,0:T(8,128)(2,1)} %get-tuple-element.25), channel_id=1, source_target_pairs={{1,0},{2,1},{3,2},{5,4},{6,5},{7,6},{9,8},{10,9},{11,10},{13,12},{... | collective-permute-start | bytes 98312 | tf_op jit(solution)/shard_map/ppermute | solution.py:431
  13.0 4.7 %collective-permute-done.1 = bf16[64,256]{1,0:T(8,128)(2,1)S(1)} collective-permute-done((bf16[64,256]{1,0:T(8,128)(2,1)}, bf16[64,256]{1,0:T(8,128)(2,1)S(1)}, u32[]{:S(2)}, u32[]{:S(2)}) %collective-permute-start.1) | collective-permute-done | bytes 32800 | tf_op jit(solution)/shard_map/ppermute | solution.py:431
  17.7 2.4 %collective-permute-start.7 = (bf16[128,256]{1,0:T(8,128)(2,1)S(1)}, bf16[128,256]{1,0:T(8,128)(2,1)S(1)}, u32[]{:S(2)}, u32[]{:S(2)}) collective-permute-start(bf16[128,256]{1,0:T(8,128)(2,1)S(1)} %constant_dynamic-update-slice_fusion.refs_0_.halo_ref), channel_id=1, source_target_pairs={{0,24},{4,28},{8,16},{12,20},{16,8},{20,12},{24,0},{28,4},{1,25},{... | collective-permute-start | bytes 196616 | tf_op jit(solution)/shard_map/ppermute | solution.py:426
  20.1 0.5 collective-permute-start.6
  20.6 0.5 collective-permute-start.5
  21.3 1.0 %copy-done.1 = bf16[544,256]{1,0:T(8,128)(2,1)S(1)} copy-done((bf16[544,256]{1,0:T(8,128)(2,1)S(1)}, bf16[544,256]{1,0:T(8,128)(2,1)}, u32[]{:S(2)}) %copy-start.1) | copy-done | bytes 278552
  22.2 1.8 %wgrad_own.1 = (bf16[7,256,1024]{2,1,0:T(8,128)(2,1)S(1)}, bf16[1024,256]{1,0:T(8,128)(2,1)S(1)}, s32[4,32,256]{2,1,0:T(8,128)S(1)}) custom-call(s32[3]{0:T(128)S(1)} %pad_add_fusion.place_ref, bf16[544,256]{1,0:T(8,128)(2,1)S(1)} %copy-done.1, bf16[544,256]{1,0:T(8,128)(2,1)S(1)} %collective-permute-done.2.refs_1_, ...), custom_call_target="tpu_custom_call" | custom-call | flops 100000000 | bytes 100000 | tf_op jit(solution)/shard_map/wgrad_own/pallas_call | solution.py:209
  24.1 0.3 collective-permute-done.6.refs_2_
  24.4 0.5 collective-permute-done.5.refs_1_
  24.9 2.9 %wgrad.1 = (f32[7,128,256]{2,1,0:T(8,128)S(1)}, f32[7,128,256]{2,1,0:T(8,128)S(1)}) custom-call(s32[3]{0:T(128)S(1)} %pad_add_fusion.place_ref, bf16[7,256,1024]{2,1,0:T(8,128)(2,1)S(1)} %get-tuple-element.26.picked_ref, bf16[1024,256]{1,0:T(8,128)(2,1)S(1)} %get-tuple-element.27.dys.refs_4_, s32[4,32,256]{2,1,0:T(8,128)S(1)} %get-tuple-element.28.maps, ...), custom_call_target="tpu_custom_call" | custom-call | flops 100000000 | bytes 100000 | tf_op jit(solution)/shard_map/wgrad/pallas_call | solution.py:247
  27.9 2.5 %collective-permute-done.8.got_ref = f32[7,128,256]{2,1,0:T(8,128)S(1)} collective-permute-done((f32[7,128,256]{2,1,0:T(8,128)S(1)}, f32[7,128,256]{2,1,0:T(8,128)S(1)}, u32[]{:S(2)}, u32[]{:S(2)}) %collective-permute-start.8) | collective-permute-done | bytes 917536 | tf_op jit(solution)/shard_map/ppermute | solution.py:426
  30.3 1.1 %blocks.1 = (f32[7,32,256]{2,1,0:T(8,128)S(1)}, s16[240,256]{1,0:T(8,128)(2,1)S(1)}, s16[240,256]{1,0:T(8,128)(2,1)S(1)}, s16[240,256]{1,0:T(8,128)(2,1)S(1)}) custom-call(s32[3]{0:T(128)S(1)} %pad_add_fusion.place_ref, f32[7,128,256]{2,1,0:T(8,128)S(1)} %get-tuple-element.29.keep_ref, f32[7,128,256]{2,1,0:T(8,128)S(1)} %collective-permute-done.8.got_ref), custom_call_target="tpu_custom_call" | custom-call | flops 100000000 | bytes 100000 | tf_op jit(solution)/shard_map/blocks/pallas_call | solution.py:295
  31.4 1.6 %collective-permute-start.9 = (s16[240,256]{1,0:T(8,128)(2,1)S(1)}, s16[240,256]{1,0:T(8,128)(2,1)S(1)}, u32[]{:S(2)}, u32[]{:S(2)}) collective-permute-start(s16[240,256]{1,0:T(8,128)(2,1)S(1)} %get-tuple-element.32), channel_id=1, source_target_pairs={{0,1},{1,0},{2,3},{3,2},{4,5},{5,4},{6,7},{7,6},{8,9},{9,8},{10,11... | collective-permute-start | bytes 368648 | tf_op jit(solution)/shard_map/ppermute | solution.py:426
  33.1 1.9 %collective-permute-start.10 = (s16[240,256]{1,0:T(8,128)(2,1)S(1)}, s16[240,256]{1,0:T(8,128)(2,1)S(1)}, u32[]{:S(2)}, u32[]{:S(2)}) collective-permute-start(s16[240,256]{1,0:T(8,128)(2,1)S(1)} %get-tuple-element.33), channel_id=1, source_target_pairs={{0,2},{1,3},{2,0},{3,1},{4,6},{5,7},{6,4},{7,5},{8,10},{9,11},{10,... | collective-permute-start | bytes 368648 | tf_op jit(solution)/shard_map/ppermute | solution.py:426
  34.9 0.9 %collective-permute-start.11 = (s16[240,256]{1,0:T(8,128)(2,1)S(1)}, s16[240,256]{1,0:T(8,128)(2,1)S(1)}, u32[]{:S(2)}, u32[]{:S(2)}) collective-permute-start(s16[240,256]{1,0:T(8,128)(2,1)S(1)} %get-tuple-element.34), channel_id=1, source_target_pairs={{0,3},{1,2},{2,1},{3,0},{4,7},{5,6},{6,5},{7,4},{8,11},{9,10},{10,... | collective-permute-start | bytes 368648 | tf_op jit(solution)/shard_map/ppermute | solution.py:426
  35.9 5.5 %backward.1 = (f32[256,256]{1,0:T(8,128)S(1)}, f32[64,256]{1,0:T(8,128)S(1)}, f32[64,256]{1,0:T(8,128)S(1)}, f32[8,128]{1,0:T(8,128)S(1)}) custom-call(bf16[544,256]{1,0:T(8,128)(2,1)S(1)} %copy-done.2, bf16[27,256,256]{2,1,0:T(8,128)(2,1)S(1)} %copy-done, f32[7,32,256]{2,1,0:T(8,128)S(1)} %get-tuple-element.31.after_ref.mine_ref), custom_call_target="tpu_custom_call" | custom-call | flops 100000000 | bytes 100000 | tf_op jit(solution)/shard_map/backward/pallas_call | solution.py:126
  41.4 4.1 %collective-permute-done.10.refs_1_ = s16[240,256]{1,0:T(8,128)(2,1)S(1)} collective-permute-done((s16[240,256]{1,0:T(8,128)(2,1)S(1)}, s16[240,256]{1,0:T(8,128)(2,1)S(1)}, u32[]{:S(2)}, u32[]{:S(2)}) %collective-permute-start.10) | collective-permute-done | bytes 122912 | tf_op jit(solution)/shard_map/ppermute | solution.py:426
  45.4 0.1 total.1.after_ref
  45.6 1.7 %collective-permute-start.19 = (bf16[1,7,32,256]{3,2,1,0:T(8,128)(2,1)S(1)}, bf16[1,7,32,256]{3,2,1,0:T(8,128)(2,1)S(1)}, u32[]{:S(2)}, u32[]{:S(2)}) collective-permute-start(bf16[1,7,32,256]{3,2,1,0:T(8,128)(2,1)S(1)} %bitcast.4), channel_id=1, source_target_pairs={{0,24},{4,28},{8,16},{12,20},{16,8},{20,12},{24,0},{28,4},{1,25},{... | collective-permute-start | bytes 344072 | tf_op jit(solution)/shard_map/ppermute | solution.py:426
  47.3 0.5 collective-permute-start.18
  47.8 1.3 %collective-permute-start.17 = (bf16[1,7,32,256]{3,2,1,0:T(8,128)(2,1)S(1)}, bf16[1,7,32,256]{3,2,1,0:T(8,128)(2,1)S(1)}, u32[]{:S(2)}, u32[]{:S(2)}) collective-permute-start(bf16[1,7,32,256]{3,2,1,0:T(8,128)(2,1)S(1)} %bitcast.6), channel_id=1, source_target_pairs={{0,8},{4,12},{8,0},{12,4},{16,24},{20,28},{24,16},{28,20},{1,9},{5... | collective-permute-start | bytes 344072 | tf_op jit(solution)/shard_map/ppermute | solution.py:426
  49.1 2.2 %collective-permute-start.16 = (bf16[7,32,256]{2,1,0:T(8,128)(2,1)S(1)}, bf16[7,32,256]{2,1,0:T(8,128)(2,1)S(1)}, u32[]{:S(2)}, u32[]{:S(2)}) collective-permute-start(bf16[7,32,256]{2,1,0:T(8,128)(2,1)S(1)} %total.1.after_ref), channel_id=1, source_target_pairs={{0,3},{1,2},{2,1},{3,0},{4,7},{5,6},{6,5},{7,4},{8,11},{9,10},{10,... | collective-permute-start | bytes 344072 | tf_op jit(solution)/shard_map/ppermute | solution.py:426
  51.3 1.4 %collective-permute-start.15 = (bf16[7,32,256]{2,1,0:T(8,128)(2,1)S(1)}, bf16[7,32,256]{2,1,0:T(8,128)(2,1)S(1)}, u32[]{:S(2)}, u32[]{:S(2)}) collective-permute-start(bf16[7,32,256]{2,1,0:T(8,128)(2,1)S(1)} %total.1.after_ref), channel_id=1, source_target_pairs={{0,2},{1,3},{2,0},{3,1},{4,6},{5,7},{6,4},{7,5},{8,10},{9,11},{10,... | collective-permute-start | bytes 344072 | tf_op jit(solution)/shard_map/ppermute | solution.py:426
  52.7 1.8 %collective-permute-start.14 = (bf16[7,32,256]{2,1,0:T(8,128)(2,1)S(1)}, bf16[7,32,256]{2,1,0:T(8,128)(2,1)S(1)}, u32[]{:S(2)}, u32[]{:S(2)}) collective-permute-start(bf16[7,32,256]{2,1,0:T(8,128)(2,1)S(1)} %total.1.after_ref), channel_id=1, source_target_pairs={{0,1},{1,0},{2,3},{3,2},{4,5},{5,4},{6,7},{7,6},{8,9},{9,8},{10,11... | collective-permute-start | bytes 344072 | tf_op jit(solution)/shard_map/ppermute | solution.py:426
  54.5 4.1 %forward.1 = (bf16[256,256]{1,0:T(8,128)(2,1)}, f32[8,128]{1,0:T(8,128)S(1)}) custom-call(s32[1]{0:T(128)S(6)} %copy.11.live_ref, bf16[544,256]{1,0:T(8,128)(2,1)S(1)} %copy-done.2, bf16[128,256]{1,0:T(8,128)(2,1)S(1)} %constant_dynamic-update-slice_fusion.refs_0_.halo_ref, bf16[27,256,256]{2,1,0:T(8,128)(2,1)S(1)} %copy-done, ...), custom_call_target="tpu_custom_call" | custom-call | flops 100000000 | bytes 100000 | tf_op jit(solution)/shard_map/forward/pallas_call | solution.py:169
  58.7 1.9 %collective-permute-done.15.refs_1_ = bf16[7,32,256]{2,1,0:T(8,128)(2,1)S(1)} collective-permute-done((bf16[7,32,256]{2,1,0:T(8,128)(2,1)S(1)}, bf16[7,32,256]{2,1,0:T(8,128)(2,1)S(1)}, u32[]{:S(2)}, u32[]{:S(2)}) %collective-permute-start.15) | collective-permute-done | bytes 114720 | tf_op jit(solution)/shard_map/ppermute | solution.py:426
  60.6 1.7 %collective-permute-start.29 = (bf16[3,7,32,256]{3,2,1,0:T(8,128)(2,1)S(1)}, bf16[3,7,32,256]{3,2,1,0:T(8,128)(2,1)S(1)}, u32[]{:S(2)}, u32[]{:S(2)}) collective-permute-start(bf16[3,7,32,256]{3,2,1,0:T(8,128)(2,1)S(1)} %line.1.after_ref.refs_8_), channel_id=1, source_target_pairs={{0,24},{4,28},{8,16},{12,20},{16,8},{20,12},{24,0},{28,4},{1,25},{... | collective-permute-start | bytes 1032200 | tf_op jit(solution)/shard_map/ppermute | solution.py:426
  62.3 0.5 collective-permute-start.27
  62.8 1.3 %collective-permute-start.25 = (bf16[3,7,32,256]{3,2,1,0:T(8,128)(2,1)S(1)}, bf16[3,7,32,256]{3,2,1,0:T(8,128)(2,1)S(1)}, u32[]{:S(2)}, u32[]{:S(2)}) collective-permute-start(bf16[3,7,32,256]{3,2,1,0:T(8,128)(2,1)S(1)} %line.1.after_ref.refs_8_), channel_id=1, source_target_pairs={{0,8},{4,12},{8,0},{12,4},{16,24},{20,28},{24,16},{28,20},{1,9},{5... | collective-permute-start | bytes 1032200 | tf_op jit(solution)/shard_map/ppermute | solution.py:426
  64.2 1.3 %collective-permute-start.12 = (f32[64,256]{1,0:T(8,128)S(1)}, f32[64,256]{1,0:T(8,128)S(1)}, u32[]{:S(2)}, u32[]{:S(2)}) collective-permute-start(f32[64,256]{1,0:T(8,128)S(1)} %get-tuple-element.38), channel_id=1, source_target_pairs={{1,0},{2,1},{3,2},{5,4},{6,5},{7,6},{9,8},{10,9},{11,10},{13,12},{... | collective-permute-start | bytes 196616 | tf_op jit(solution)/shard_map/ppermute | solution.py:431
  65.5 4.8 %collective-permute-done.12.back_up_ref = f32[64,256]{1,0:T(8,128)S(1)} collective-permute-done((f32[64,256]{1,0:T(8,128)S(1)}, f32[64,256]{1,0:T(8,128)S(1)}, u32[]{:S(2)}, u32[]{:S(2)}) %collective-permute-start.12) | collective-permute-done | bytes 65568 | tf_op jit(solution)/shard_map/ppermute | solution.py:431
  70.3 1.6 %collective-permute-start.13 = (f32[64,256]{1,0:T(8,128)S(1)}, f32[64,256]{1,0:T(8,128)S(1)}, u32[]{:S(2)}, u32[]{:S(2)}) collective-permute-start(f32[64,256]{1,0:T(8,128)S(1)} %get-tuple-element.39), channel_id=1, source_target_pairs={{0,1},{1,2},{2,3},{4,5},{5,6},{6,7},{8,9},{9,10},{10,11},{12,13},{... | collective-permute-start | bytes 196616 | tf_op jit(solution)/shard_map/ppermute | solution.py:431
  72.0 1.9 %collective-permute-done.13.back_down_ref = f32[64,256]{1,0:T(8,128)S(1)} collective-permute-done((f32[64,256]{1,0:T(8,128)S(1)}, f32[64,256]{1,0:T(8,128)S(1)}, u32[]{:S(2)}, u32[]{:S(2)}) %collective-permute-start.13) | collective-permute-done | bytes 65568 | tf_op jit(solution)/shard_map/ppermute | solution.py:431
  73.9 0.5 collective-permute-start.23
  74.4 1.3 %collective-permute-done.27.refs_12_ = bf16[3,7,32,256]{3,2,1,0:T(8,128)(2,1)S(1)} collective-permute-done((bf16[3,7,32,256]{3,2,1,0:T(8,128)(2,1)S(1)}, bf16[3,7,32,256]{3,2,1,0:T(8,128)(2,1)S(1)}, u32[]{:S(2)}, u32[]{:S(2)}) %collective-permute-start.27) | collective-permute-done | bytes 344096 | tf_op jit(solution)/shard_map/ppermute | solution.py:426
  75.8 0.1 collective-permute-done.25.refs_10_
  75.9 0.4 collective-permute-start.26
  76.3 0.1 collective-permute-start.22
  76.4 1.7 %collective-permute-done.22.refs_5_ = bf16[1,7,32,256]{3,2,1,0:T(8,128)(2,1)S(1)} collective-permute-done((bf16[1,7,32,256]{3,2,1,0:T(8,128)(2,1)S(1)}, bf16[1,7,32,256]{3,2,1,0:T(8,128)(2,1)S(1)}, u32[]{:S(2)}, u32[]{:S(2)}) %collective-permute-start.22) | collective-permute-done | bytes 114720 | tf_op jit(solution)/shard_map/ppermute | solution.py:426
  78.1 0.1 collective-permute-start.21
  78.2 1.0 %final.1 = (bf16[256,256]{1,0:T(8,128)(2,1)}, f32[8,128]{1,0:T(8,128)S(1)}) custom-call(s32[1]{0:T(128)S(6)} %copy.11.live_ref, f32[256,256]{1,0:T(8,128)S(1)} %get-tuple-element.37.own_ref, f32[64,256]{1,0:T(8,128)S(1)} %collective-permute-done.12.back_up_ref, f32[64,256]{1,0:T(8,128)S(1)} %collective-permute-done.13.back_down_ref, s32[1,64]{1,0:T(1,128)S(1)} %copy-done.3, ...), custom_call_target="tpu_custom_call" | custom-call | tf_op jit(solution)/shard_map/final/pallas_call | solution.py:349
  79.2 0.2 collective-permute-done.21.refs_3_
  79.4 3.5 %assemble.1 = bf16[27,256,256]{2,1,0:T(8,128)(2,1)} custom-call(s32[3]{0:T(128)S(1)} %pad_add_fusion.place_ref, bf16[1,7,32,256]{3,2,1,0:T(8,128)(2,1)S(1)} %bitcast.8, bf16[1,7,32,256]{3,2,1,0:T(8,128)(2,1)S(1)} %collective-permute-done.20.refs_1_, bf16[1,7,32,256]{3,2,1,0:T(8,128)(2,1)S(1)} %collective-permute-done.17.refs_3_.refs_2_, ...), custom_call_target="tpu_custom_call" | custom-call | tf_op jit(solution)/shard_map/assemble/pallas_call | solution.py:404
  (37 shorter events, 0.4 us)
Async XLA Ops:
  3.1 17.5 %collective-permute-start.4 = (bf16[544,256]{1,0:T(8,128)(2,1)}, bf16[544,256]{1,0:T(8,128)(2,1)S(1)}, u32[]{:S(2)}, u32[]{:S(2)}) collective-permute-start(bf16[544,256]{1,0:T(8,128)(2,1)} %get-tuple-element.23.refs_0_.pack_ref), channel_id=1, source_target_pairs={{0,24},{4,28},{8,16},{12,20},{16,8},{20,12},{24,0},{28,4},{1,25},{... | collective-permute-start | bytes 835592 | tf_op jit(solution)/shard_map/ppermute | solution.py:426
  7.1 5.9 %collective-permute-start = (bf16[64,256]{1,0:T(8,128)(2,1)}, bf16[64,256]{1,0:T(8,128)(2,1)S(1)}, u32[]{:S(2)}, u32[]{:S(2)}) collective-permute-start(bf16[64,256]{1,0:T(8,128)(2,1)} %get-tuple-element.24), channel_id=1, source_target_pairs={{0,1},{1,2},{2,3},{4,5},{5,6},{6,7},{8,9},{9,10},{10,11},{12,13},{... | collective-permute-start | bytes 98312 | tf_op jit(solution)/shard_map/ppermute | solution.py:431
  10.6 10.7 %collective-permute-start.3 = (bf16[544,256]{1,0:T(8,128)(2,1)}, bf16[544,256]{1,0:T(8,128)(2,1)S(1)}, u32[]{:S(2)}, u32[]{:S(2)}) collective-permute-start(bf16[544,256]{1,0:T(8,128)(2,1)} %get-tuple-element.23.refs_0_.pack_ref), channel_id=1, source_target_pairs={{0,16},{4,20},{8,24},{12,28},{16,0},{20,4},{24,8},{28,12},{1,17},{... | collective-permute-start | bytes 835592 | tf_op jit(solution)/shard_map/ppermute | solution.py:426
  11.1 10.1 %collective-permute-start.2 = (bf16[544,256]{1,0:T(8,128)(2,1)}, bf16[544,256]{1,0:T(8,128)(2,1)S(1)}, u32[]{:S(2)}, u32[]{:S(2)}) collective-permute-start(bf16[544,256]{1,0:T(8,128)(2,1)} %get-tuple-element.23.refs_0_.pack_ref), channel_id=1, source_target_pairs={{0,8},{4,12},{8,0},{12,4},{16,24},{20,28},{24,16},{28,20},{1,9},{5... | collective-permute-start | bytes 835592 | tf_op jit(solution)/shard_map/ppermute | solution.py:426
  11.7 6.0 %collective-permute-start.1 = (bf16[64,256]{1,0:T(8,128)(2,1)}, bf16[64,256]{1,0:T(8,128)(2,1)S(1)}, u32[]{:S(2)}, u32[]{:S(2)}) collective-permute-start(bf16[64,256]{1,0:T(8,128)(2,1)} %get-tuple-element.25), channel_id=1, source_target_pairs={{1,0},{2,1},{3,2},{5,4},{6,5},{7,6},{9,8},{10,9},{11,10},{13,12},{... | collective-permute-start | bytes 98312 | tf_op jit(solution)/shard_map/ppermute | solution.py:431
  17.7 6.4 %collective-permute-start.7 = (bf16[128,256]{1,0:T(8,128)(2,1)S(1)}, bf16[128,256]{1,0:T(8,128)(2,1)S(1)}, u32[]{:S(2)}, u32[]{:S(2)}) collective-permute-start(bf16[128,256]{1,0:T(8,128)(2,1)S(1)} %constant_dynamic-update-slice_fusion.refs_0_.halo_ref), channel_id=1, source_target_pairs={{0,24},{4,28},{8,16},{12,20},{16,8},{20,12},{24,0},{28,4},{1,25},{... | collective-permute-start | bytes 196616 | tf_op jit(solution)/shard_map/ppermute | solution.py:426
  20.1 4.3 %collective-permute-start.6 = (bf16[128,256]{1,0:T(8,128)(2,1)S(1)}, bf16[128,256]{1,0:T(8,128)(2,1)S(1)}, u32[]{:S(2)}, u32[]{:S(2)}) collective-permute-start(bf16[128,256]{1,0:T(8,128)(2,1)S(1)} %constant_dynamic-update-slice_fusion.refs_0_.halo_ref), channel_id=1, source_target_pairs={{0,16},{4,20},{8,24},{12,28},{16,0},{20,4},{24,8},{28,12},{1,17},{... | collective-permute-start | bytes 196616 | tf_op jit(solution)/shard_map/ppermute | solution.py:426
  20.6 4.3 %collective-permute-start.5 = (bf16[128,256]{1,0:T(8,128)(2,1)S(1)}, bf16[128,256]{1,0:T(8,128)(2,1)S(1)}, u32[]{:S(2)}, u32[]{:S(2)}) collective-permute-start(bf16[128,256]{1,0:T(8,128)(2,1)S(1)} %constant_dynamic-update-slice_fusion.refs_0_.halo_ref), channel_id=1, source_target_pairs={{0,8},{4,12},{8,0},{12,4},{16,24},{20,28},{24,16},{28,20},{1,9},{5... | collective-permute-start | bytes 196616 | tf_op jit(solution)/shard_map/ppermute | solution.py:426
  21.3 1.0 %copy-start.1 = (bf16[544,256]{1,0:T(8,128)(2,1)S(1)}, bf16[544,256]{1,0:T(8,128)(2,1)}, u32[]{:S(2)}) copy-start(bf16[544,256]{1,0:T(8,128)(2,1)} %get-tuple-element.23.refs_0_.pack_ref) | copy-start | bytes 835588
  24.0 11.8 %copy-start = (bf16[27,256,256]{2,1,0:T(8,128)(2,1)S(1)}, bf16[27,256,256]{2,1,0:T(8,128)(2,1)}, u32[]{:S(2)}) copy-start(bf16[27,256,256]{2,1,0:T(8,128)(2,1)} %w_ref.3) | copy-start | bytes 10616836
  24.1 11.8 %copy-start.2 = (bf16[544,256]{1,0:T(8,128)(2,1)S(1)}, bf16[544,256]{1,0:T(8,128)(2,1)}, u32[]{:S(2)}) copy-start(bf16[544,256]{1,0:T(8,128)(2,1)} %get-tuple-element.23.refs_0_.pack_ref) | copy-start | bytes 835588
  27.8 2.5 %collective-permute-start.8 = (f32[7,128,256]{2,1,0:T(8,128)S(1)}, f32[7,128,256]{2,1,0:T(8,128)S(1)}, u32[]{:S(2)}, u32[]{:S(2)}) collective-permute-start(f32[7,128,256]{2,1,0:T(8,128)S(1)} %get-tuple-element.30), channel_id=1, source_target_pairs={{0,4},{4,0},{8,12},{12,8},{16,20},{20,16},{24,28},{28,24},{1,5},{5... | collective-permute-start | bytes 2752520 | tf_op jit(solution)/shard_map/ppermute | solution.py:426
  31.4 10.0 %collective-permute-start.9 = (s16[240,256]{1,0:T(8,128)(2,1)S(1)}, s16[240,256]{1,0:T(8,128)(2,1)S(1)}, u32[]{:S(2)}, u32[]{:S(2)}) collective-permute-start(s16[240,256]{1,0:T(8,128)(2,1)S(1)} %get-tuple-element.32), channel_id=1, source_target_pairs={{0,1},{1,0},{2,3},{3,2},{4,5},{5,4},{6,7},{7,6},{8,9},{9,8},{10,11... | collective-permute-start | bytes 368648 | tf_op jit(solution)/shard_map/ppermute | solution.py:426
  33.1 12.4 %collective-permute-start.10 = (s16[240,256]{1,0:T(8,128)(2,1)S(1)}, s16[240,256]{1,0:T(8,128)(2,1)S(1)}, u32[]{:S(2)}, u32[]{:S(2)}) collective-permute-start(s16[240,256]{1,0:T(8,128)(2,1)S(1)} %get-tuple-element.33), channel_id=1, source_target_pairs={{0,2},{1,3},{2,0},{3,1},{4,6},{5,7},{6,4},{7,5},{8,10},{9,11},{10,... | collective-permute-start | bytes 368648 | tf_op jit(solution)/shard_map/ppermute | solution.py:426
  34.9 10.5 %collective-permute-start.11 = (s16[240,256]{1,0:T(8,128)(2,1)S(1)}, s16[240,256]{1,0:T(8,128)(2,1)S(1)}, u32[]{:S(2)}, u32[]{:S(2)}) collective-permute-start(s16[240,256]{1,0:T(8,128)(2,1)S(1)} %get-tuple-element.34), channel_id=1, source_target_pairs={{0,3},{1,2},{2,1},{3,0},{4,7},{5,6},{6,5},{7,4},{8,11},{9,10},{10,... | collective-permute-start | bytes 368648 | tf_op jit(solution)/shard_map/ppermute | solution.py:426
  41.3 36.9 %copy-start.3 = (s32[1,64]{1,0:T(1,128)S(1)}, s32[1,64]{1,0:T(1,128)}, u32[]{:S(2)}) copy-start(s32[1,64]{1,0:T(1,128)} %up_ref.1) | copy-start | bytes 772
  41.4 36.9 %copy-start.4 = (s32[1,64]{1,0:T(1,128)S(1)}, s32[1,64]{1,0:T(1,128)}, u32[]{:S(2)}) copy-start(s32[1,64]{1,0:T(1,128)} %down_ref.1) | copy-start | bytes 772
  45.6 7.1 %collective-permute-start.19 = (bf16[1,7,32,256]{3,2,1,0:T(8,128)(2,1)S(1)}, bf16[1,7,32,256]{3,2,1,0:T(8,128)(2,1)S(1)}, u32[]{:S(2)}, u32[]{:S(2)}) collective-permute-start(bf16[1,7,32,256]{3,2,1,0:T(8,128)(2,1)S(1)} %bitcast.4), channel_id=1, source_target_pairs={{0,24},{4,28},{8,16},{12,20},{16,8},{20,12},{24,0},{28,4},{1,25},{... | collective-permute-start | bytes 344072 | tf_op jit(solution)/shard_map/ppermute | solution.py:426
  47.3 11.4 %collective-permute-start.18 = (bf16[1,7,32,256]{3,2,1,0:T(8,128)(2,1)S(1)}, bf16[1,7,32,256]{3,2,1,0:T(8,128)(2,1)S(1)}, u32[]{:S(2)}, u32[]{:S(2)}) collective-permute-start(bf16[1,7,32,256]{3,2,1,0:T(8,128)(2,1)S(1)} %bitcast.5), channel_id=1, source_target_pairs={{0,16},{4,20},{8,24},{12,28},{16,0},{20,4},{24,8},{28,12},{1,17},{... | collective-permute-start | bytes 344072 | tf_op jit(solution)/shard_map/ppermute | solution.py:426
  47.8 10.9 %collective-permute-start.17 = (bf16[1,7,32,256]{3,2,1,0:T(8,128)(2,1)S(1)}, bf16[1,7,32,256]{3,2,1,0:T(8,128)(2,1)S(1)}, u32[]{:S(2)}, u32[]{:S(2)}) collective-permute-start(bf16[1,7,32,256]{3,2,1,0:T(8,128)(2,1)S(1)} %bitcast.6), channel_id=1, source_target_pairs={{0,8},{4,12},{8,0},{12,4},{16,24},{20,28},{24,16},{28,20},{1,9},{5... | collective-permute-start | bytes 344072 | tf_op jit(solution)/shard_map/ppermute | solution.py:426
  49.1 9.5 %collective-permute-start.16 = (bf16[7,32,256]{2,1,0:T(8,128)(2,1)S(1)}, bf16[7,32,256]{2,1,0:T(8,128)(2,1)S(1)}, u32[]{:S(2)}, u32[]{:S(2)}) collective-permute-start(bf16[7,32,256]{2,1,0:T(8,128)(2,1)S(1)} %total.1.after_ref), channel_id=1, source_target_pairs={{0,3},{1,2},{2,1},{3,0},{4,7},{5,6},{6,5},{7,4},{8,11},{9,10},{10,... | collective-permute-start | bytes 344072 | tf_op jit(solution)/shard_map/ppermute | solution.py:426
  51.3 9.3 %collective-permute-start.15 = (bf16[7,32,256]{2,1,0:T(8,128)(2,1)S(1)}, bf16[7,32,256]{2,1,0:T(8,128)(2,1)S(1)}, u32[]{:S(2)}, u32[]{:S(2)}) collective-permute-start(bf16[7,32,256]{2,1,0:T(8,128)(2,1)S(1)} %total.1.after_ref), channel_id=1, source_target_pairs={{0,2},{1,3},{2,0},{3,1},{4,6},{5,7},{6,4},{7,5},{8,10},{9,11},{10,... | collective-permute-start | bytes 344072 | tf_op jit(solution)/shard_map/ppermute | solution.py:426
  52.7 7.9 %collective-permute-start.14 = (bf16[7,32,256]{2,1,0:T(8,128)(2,1)S(1)}, bf16[7,32,256]{2,1,0:T(8,128)(2,1)S(1)}, u32[]{:S(2)}, u32[]{:S(2)}) collective-permute-start(bf16[7,32,256]{2,1,0:T(8,128)(2,1)S(1)} %total.1.after_ref), channel_id=1, source_target_pairs={{0,1},{1,0},{2,3},{3,2},{4,5},{5,4},{6,7},{7,6},{8,9},{9,8},{10,11... | collective-permute-start | bytes 344072 | tf_op jit(solution)/shard_map/ppermute | solution.py:426
  60.6 13.8 %collective-permute-start.29 = (bf16[3,7,32,256]{3,2,1,0:T(8,128)(2,1)S(1)}, bf16[3,7,32,256]{3,2,1,0:T(8,128)(2,1)S(1)}, u32[]{:S(2)}, u32[]{:S(2)}) collective-permute-start(bf16[3,7,32,256]{3,2,1,0:T(8,128)(2,1)S(1)} %line.1.after_ref.refs_8_), channel_id=1, source_target_pairs={{0,24},{4,28},{8,16},{12,20},{16,8},{20,12},{24,0},{28,4},{1,25},{... | collective-permute-start | bytes 1032200 | tf_op jit(solution)/shard_map/ppermute | solution.py:426
  62.3 13.5 %collective-permute-start.27 = (bf16[3,7,32,256]{3,2,1,0:T(8,128)(2,1)S(1)}, bf16[3,7,32,256]{3,2,1,0:T(8,128)(2,1)S(1)}, u32[]{:S(2)}, u32[]{:S(2)}) collective-permute-start(bf16[3,7,32,256]{3,2,1,0:T(8,128)(2,1)S(1)} %line.1.after_ref.refs_8_), channel_id=1, source_target_pairs={{0,16},{4,20},{8,24},{12,28},{16,0},{20,4},{24,8},{28,12},{1,17},{... | collective-permute-start | bytes 1032200 | tf_op jit(solution)/shard_map/ppermute | solution.py:426
  62.8 13.0 %collective-permute-start.25 = (bf16[3,7,32,256]{3,2,1,0:T(8,128)(2,1)S(1)}, bf16[3,7,32,256]{3,2,1,0:T(8,128)(2,1)S(1)}, u32[]{:S(2)}, u32[]{:S(2)}) collective-permute-start(bf16[3,7,32,256]{3,2,1,0:T(8,128)(2,1)S(1)} %line.1.after_ref.refs_8_), channel_id=1, source_target_pairs={{0,8},{4,12},{8,0},{12,4},{16,24},{20,28},{24,16},{28,20},{1,9},{5... | collective-permute-start | bytes 1032200 | tf_op jit(solution)/shard_map/ppermute | solution.py:426
  64.2 6.1 %collective-permute-start.12 = (f32[64,256]{1,0:T(8,128)S(1)}, f32[64,256]{1,0:T(8,128)S(1)}, u32[]{:S(2)}, u32[]{:S(2)}) collective-permute-start(f32[64,256]{1,0:T(8,128)S(1)} %get-tuple-element.38), channel_id=1, source_target_pairs={{1,0},{2,1},{3,2},{5,4},{6,5},{7,6},{9,8},{10,9},{11,10},{13,12},{... | collective-permute-start | bytes 196616 | tf_op jit(solution)/shard_map/ppermute | solution.py:431
  65.5 8.4 %collective-permute-start.20 = (bf16[1,7,32,256]{3,2,1,0:T(8,128)(2,1)S(1)}, bf16[1,7,32,256]{3,2,1,0:T(8,128)(2,1)S(1)}, u32[]{:S(2)}, u32[]{:S(2)}) collective-permute-start(bf16[1,7,32,256]{3,2,1,0:T(8,128)(2,1)S(1)} %bitcast.7), channel_id=1, source_target_pairs={{0,4},{4,0},{8,12},{12,8},{16,20},{20,16},{24,28},{28,24},{1,5},{5... | collective-permute-start | bytes 344072 | tf_op jit(solution)/shard_map/ppermute | solution.py:426
  70.3 3.5 %collective-permute-start.13 = (f32[64,256]{1,0:T(8,128)S(1)}, f32[64,256]{1,0:T(8,128)S(1)}, u32[]{:S(2)}, u32[]{:S(2)}) collective-permute-start(f32[64,256]{1,0:T(8,128)S(1)} %get-tuple-element.39), channel_id=1, source_target_pairs={{0,1},{1,2},{2,3},{4,5},{5,6},{6,7},{8,9},{9,10},{10,11},{12,13},{... | collective-permute-start | bytes 196616 | tf_op jit(solution)/shard_map/ppermute | solution.py:431
  73.9 5.6 %collective-permute-start.24 = (bf16[3,7,32,256]{3,2,1,0:T(8,128)(2,1)S(1)}, bf16[3,7,32,256]{3,2,1,0:T(8,128)(2,1)S(1)}, u32[]{:S(2)}, u32[]{:S(2)}) collective-permute-start(bf16[3,7,32,256]{3,2,1,0:T(8,128)(2,1)S(1)} %line.1.after_ref.refs_8_), channel_id=1, source_target_pairs={{0,4},{4,0},{8,12},{12,8},{16,20},{20,16},{24,28},{28,24},{1,5},{5... | collective-permute-start | bytes 1032200 | tf_op jit(solution)/shard_map/ppermute | solution.py:426
  73.9 2.4 %collective-permute-start.23 = (bf16[1,7,32,256]{3,2,1,0:T(8,128)(2,1)S(1)}, bf16[1,7,32,256]{3,2,1,0:T(8,128)(2,1)S(1)}, u32[]{:S(2)}, u32[]{:S(2)}) collective-permute-start(bf16[1,7,32,256]{3,2,1,0:T(8,128)(2,1)S(1)} %collective-permute-done.19.refs_5_.refs_6_), channel_id=1, source_target_pairs={{0,4},{4,0},{8,12},{12,8},{16,20},{20,16},{24,28},{28,24},{1,5},{5... | collective-permute-start | bytes 344072 | tf_op jit(solution)/shard_map/ppermute | solution.py:426
  74.4 5.0 %collective-permute-start.30 = (bf16[3,7,32,256]{3,2,1,0:T(8,128)(2,1)S(1)}, bf16[3,7,32,256]{3,2,1,0:T(8,128)(2,1)S(1)}, u32[]{:S(2)}, u32[]{:S(2)}) collective-permute-start(bf16[3,7,32,256]{3,2,1,0:T(8,128)(2,1)S(1)} %collective-permute-done.29.refs_14_), channel_id=1, source_target_pairs={{0,4},{4,0},{8,12},{12,8},{16,20},{20,16},{24,28},{28,24},{1,5},{5... | collective-permute-start | bytes 1032200 | tf_op jit(solution)/shard_map/ppermute | solution.py:426
  75.8 3.6 %collective-permute-start.28 = (bf16[3,7,32,256]{3,2,1,0:T(8,128)(2,1)S(1)}, bf16[3,7,32,256]{3,2,1,0:T(8,128)(2,1)S(1)}, u32[]{:S(2)}, u32[]{:S(2)}) collective-permute-start(bf16[3,7,32,256]{3,2,1,0:T(8,128)(2,1)S(1)} %collective-permute-done.27.refs_12_), channel_id=1, source_target_pairs={{0,4},{4,0},{8,12},{12,8},{16,20},{20,16},{24,28},{28,24},{1,5},{5... | collective-permute-start | bytes 1032200 | tf_op jit(solution)/shard_map/ppermute | solution.py:426
  75.9 3.6 %collective-permute-start.26 = (bf16[3,7,32,256]{3,2,1,0:T(8,128)(2,1)S(1)}, bf16[3,7,32,256]{3,2,1,0:T(8,128)(2,1)S(1)}, u32[]{:S(2)}, u32[]{:S(2)}) collective-permute-start(bf16[3,7,32,256]{3,2,1,0:T(8,128)(2,1)S(1)} %collective-permute-done.25.refs_10_), channel_id=1, source_target_pairs={{0,4},{4,0},{8,12},{12,8},{16,20},{20,16},{24,28},{28,24},{1,5},{5... | collective-permute-start | bytes 1032200 | tf_op jit(solution)/shard_map/ppermute | solution.py:426
  76.3 1.8 %collective-permute-start.22 = (bf16[1,7,32,256]{3,2,1,0:T(8,128)(2,1)S(1)}, bf16[1,7,32,256]{3,2,1,0:T(8,128)(2,1)S(1)}, u32[]{:S(2)}, u32[]{:S(2)}) collective-permute-start(bf16[1,7,32,256]{3,2,1,0:T(8,128)(2,1)S(1)} %collective-permute-done.18.refs_4_), channel_id=1, source_target_pairs={{0,4},{4,0},{8,12},{12,8},{16,20},{20,16},{24,28},{28,24},{1,5},{5... | collective-permute-start | bytes 344072 | tf_op jit(solution)/shard_map/ppermute | solution.py:426
  78.1 1.3 %collective-permute-start.21 = (bf16[1,7,32,256]{3,2,1,0:T(8,128)(2,1)S(1)}, bf16[1,7,32,256]{3,2,1,0:T(8,128)(2,1)S(1)}, u32[]{:S(2)}, u32[]{:S(2)}) collective-permute-start(bf16[1,7,32,256]{3,2,1,0:T(8,128)(2,1)S(1)} %collective-permute-done.17.refs_3_.refs_2_), channel_id=1, source_target_pairs={{0,4},{4,0},{8,12},{12,8},{16,20},{20,16},{24,28},{28,24},{1,5},{5... | collective-permute-start | bytes 344072 | tf_op jit(solution)/shard_map/ppermute | solution.py:426

commit v6 on v5

--- a/solution.py
+++ b/solution.py
@@ -40,7 +40,17 @@
     return parts
 
 
-def prep_kernel(live_ref, x_hbm, dy_hbm, map_hbm, up_hbm, down_hbm, pack_ref, up_rows_ref, down_rows_ref, *scratch):
+def place():
+    dp = lax.axis_index("dp")
+    return dp // 2, lax.rem(dp, 2), lax.axis_index("space")
+
+
+def turns(up, down):
+    even = lax.rem(place()[2], 2) == 0
+    return jnp.where(even, up, down), jnp.where(even, down, up)
+
+
+def prep_kernel(live_ref, x_hbm, dy_hbm, map_hbm, up_hbm, down_hbm, pack_ref, first_ref, second_ref, *scratch):
     x_ref, dy_ref, map_ref, up_ref, down_ref, map_scr, sems = scratch
     sources = (x_hbm, dy_hbm, map_hbm, up_hbm, down_hbm)
     targets = (x_ref, dy_ref, map_ref, up_ref, down_ref)
@@ -57,8 +67,8 @@
     x_live = jnp.where(keep, x_ref[...].astype(F32), 0.0).astype(BF)
     pack_ref[0:rows] = x_live
     iota = lax.broadcasted_iota(jnp.int32, (rows, halo), 0)
-    for index_ref, picked_ref in ((up_ref, up_rows_ref), (down_ref, down_rows_ref)):
-        chosen = (iota == index_ref[...]).astype(F32).astype(BF)
+    for index, picked_ref in zip(turns(up_ref[...], down_ref[...]), (first_ref, second_ref)):
+        chosen = (iota == index).astype(F32).astype(BF)
         picked_ref[...] = lax.dot_general(chosen, x_live, (((0,), (0,)), ((), ())), preferred_element_type=F32).astype(BF)
     pack_ref[rows : 2 * rows] = jnp.where(keep, dy_ref[...].astype(F32), 0.0).astype(BF)
     map_scr[0:offsets] = map_ref[...]
@@ -96,7 +106,8 @@
     return jnp.where(code < 0, 256 - code, code)
 
 
-def backward_kernel(group, pack_ref, w_ref, after_ref, own_ref, low_ref, high_ref, token_ref, maps, chosen, terms):
+def backward_kernel(group, pack_ref, w_ref, after_ref, own_ref, first_ref, second_ref, token_ref, *scratch):
+    maps, chosen, terms, low_ref, high_ref = scratch
     offsets, width, _ = w_ref.shape
     rows = own_ref.shape[0]
     slots = chosen.shape[1]
@@ -116,6 +127,7 @@
             value = dot(some, terms[g, 0]) + dot(some, terms[g, 1])
             out[...] = value if g == 0 else out[...] + value
             at += out.shape[0]
+    first_ref[...], second_ref[...] = turns(high_ref[...], low_ref[...])
     token_ref[...] = jnp.zeros_like(token_ref)
 
 
@@ -132,6 +144,8 @@
             pltpu.VMEM((pack.shape[0] - 2 * rows, rows), jnp.int32),
             pltpu.VMEM((offsets // group, slots, group * rows), BF),
             pltpu.VMEM((offsets // group, 2, group * rows, width), BF),
+            pltpu.VMEM((halo, width), F32),
+            pltpu.VMEM((halo, width), F32),
         ],
         compiler_params=params(),
         cost_estimate=cost(),
@@ -188,7 +202,7 @@
     return (iota == maps[s, pl.ds(at, 1), :]).astype(F32).astype(BF)
 
 
-def wgrad_own_kernel(sources, place_ref, *refs):
+def wgrad_own_kernel(sources, *refs):
     packs = refs[:sources]
     picked_ref, dys, maps, tables = refs[sources:]
     count, width, _ = picked_ref.shape
@@ -200,11 +214,11 @@
 
     for j in range(count):
         for s in range(sources):
-            chosen = chosen_slots(maps, s, place_ref[0] * count + j, 0, rows, rows)
+            chosen = chosen_slots(maps, s, place()[0] * count + j, 0, rows, rows)
             picked_ref[j, :, s * rows : (s + 1) * rows] = dot(tables[:, s * rows : (s + 1) * rows], chosen).astype(BF)
 
 
-def wgrad_own(place, packs, count, rows):
+def wgrad_own(packs, count, rows):
     sources, width = len(packs), packs[0].shape[1]
     return pl.pallas_call(
         functools.partial(wgrad_own_kernel, sources),
@@ -213,26 +227,26 @@
             jax.ShapeDtypeStruct((sources * rows, width), BF),
             jax.ShapeDtypeStruct((sources, packs[0].shape[0] - 2 * rows, rows), jnp.int32),
         ),
-        in_specs=[SMEM] + [VMEM] * sources,
+        in_specs=[VMEM] * sources,
         out_specs=(VMEM, VMEM, VMEM),
         scratch_shapes=[pltpu.VMEM((width, sources * rows), BF)],
         compiler_params=params(),
         cost_estimate=cost(),
         name="wgrad_own",
-    )(place, *packs)
-
-
-def wgrad_kernel(sources, first, place_ref, picked_ref, dys, maps, *refs):
+    )(*packs)
+
+
+def wgrad_kernel(sources, first, picked_ref, dys, maps, *refs):
     halos, (after_ref, keep_ref, send_ref, tables, picked) = refs[:sources], refs[sources:]
     count, half, width = keep_ref.shape
     rows = maps.shape[2]
     far = halos[0].shape[0]
-    core = place_ref[1]
+    core = place()[1]
     for s in range(sources):
         tables[:, s * far : (s + 1) * far] = jnp.transpose(halos[s][...])
     for j in range(count):
         for s in range(sources):
-            chosen = chosen_slots(maps, s, place_ref[0] * picked_ref.shape[0] + first + j, rows, rows + far, rows)
+            chosen = chosen_slots(maps, s, place()[0] * picked_ref.shape[0] + first + j, rows, rows + far, rows)
             near = picked_ref[first + j, :, s * rows : (s + 1) * rows].astype(F32)
             picked[j, :, s * rows : (s + 1) * rows] = (dot(tables[:, s * far : (s + 1) * far], chosen) + near).astype(BF)
     for j in range(count):
@@ -240,14 +254,14 @@
         keep_ref[j] = dot(picked[j, pl.ds(pl.multiple_of(core * half, half), half), :], dys[...])
 
 
-def wgrad(place, picked, dys, maps, halos, first, count, after):
+def wgrad(picked, dys, maps, halos, first, count, after):
     _, width, columns = picked.shape
     sources = maps.shape[0]
     shape = jax.ShapeDtypeStruct((count, width // 2, width), F32)
     return pl.pallas_call(
         functools.partial(wgrad_kernel, sources, first),
         out_shape=(shape, shape),
-        in_specs=[SMEM] + [VMEM] * (3 + sources) + [ANY],
+        in_specs=[VMEM] * (3 + sources) + [ANY],
         out_specs=(VMEM, VMEM),
         scratch_shapes=[
             pltpu.VMEM((width, sources * halos[0].shape[0]), BF),
@@ -256,7 +270,7 @@
         compiler_params=params(),
         cost_estimate=cost(),
         name="wgrad",
-    )(place, picked, dys, maps, *halos, after)
+    )(picked, dys, maps, *halos, after)
 
 
 def power(exponent):
@@ -268,11 +282,34 @@
     return value
 
 
-def blocks_kernel(place_ref, keep_ref, got_ref, mine_ref, *refs):
+def joined_kernel(first_ref, second_ref, pack_ref, out_ref, copy_ref):
+    halo = first_ref.shape[0]
+    second, first = turns(0, halo)
+    out_ref[pl.ds(pl.multiple_of(first, halo), halo)] = first_ref[...]
+    out_ref[pl.ds(pl.multiple_of(second, halo), halo)] = second_ref[...]
+    copy_ref[...] = pack_ref[...]
+
+
+def joined(first, second, pack):
+    return pl.pallas_call(
+        joined_kernel,
+        out_shape=(
+            jax.ShapeDtypeStruct((2 * first.shape[0], first.shape[1]), BF),
+            jax.ShapeDtypeStruct(pack.shape, BF),
+        ),
+        in_specs=[VMEM] * 3,
+        out_specs=(VMEM, VMEM),
+        compiler_params=params(),
+        cost_estimate=cost(),
+        name="joined",
+    )(first, second, pack)
+
+
+def blocks_kernel(keep_ref, got_ref, mine_ref, *refs):
     coded_refs, exponents = refs[:-1], refs[-1]
     count, block, width = mine_ref.shape
     for m in range(len(coded_refs) + 1):
-        at = pl.ds(pl.multiple_of((place_ref[2] ^ m) * block, block), block)
+        at = pl.ds(pl.multiple_of((place()[2] ^ m) * block, block), block)
         if m == 0:
             mine_ref[...] = keep_ref[:, at, :] + got_ref[:, at, :]
             continue
@@ -288,7 +325,7 @@
         coded_refs[m - 1][count * block :] = exponents[...].astype(jnp.int16)
 
 
-def blocks(place, keep, got, parts):
+def blocks(keep, got, parts):
     count, half, width = keep.shape
     block = half // parts
     extra = -(-count // 16) * 16
@@ -298,13 +335,13 @@
             jax.ShapeDtypeStruct((count, block, width), F32),
             *(jax.ShapeDtypeStruct((count * block + extra, width), jnp.int16),) * (parts - 1),
         ),
-        in_specs=[SMEM, VMEM, VMEM],
+        in_specs=[VMEM, VMEM],
         out_specs=(VMEM,) * parts,
         scratch_shapes=[pltpu.VMEM((extra, width), jnp.int32)],
         compiler_params=params(),
         cost_estimate=cost(),
         name="blocks",
-    )(place, keep, got)
+    )(keep, got)
 
 
 def total_kernel(scale, mine_ref, *refs):
@@ -331,21 +368,21 @@
     )(mine, *coded, *after)
 
 
-def final_kernel(live_ref, own_ref, back_up_ref, back_down_ref, up_ref, down_ref, after_ref, out_ref, token_ref):
+def final_kernel(live_ref, own_ref, first_ref, second_ref, up_ref, down_ref, after_ref, out_ref, token_ref):
     rows, width = own_ref.shape
     halo = up_ref.shape[1]
     total = own_ref[...]
     iota = lax.broadcasted_iota(jnp.int32, (rows, halo), 0)
-    for index_ref, back_ref in ((up_ref, back_up_ref), (down_ref, back_down_ref)):
-        chosen = (iota == index_ref[...]).astype(F32).astype(BF)
-        for part in split(back_ref[...], 3):
-            total = total + dot(chosen, part)
+    chosen = [(iota == index).astype(F32) for index in turns(up_ref[...], down_ref[...])]
+    chosen = jnp.concatenate(chosen, axis=1).astype(BF)
+    for part in split(jnp.concatenate([first_ref[...], second_ref[...]], axis=0), 3):
+        total = total + dot(chosen, part)
     keep = lax.broadcasted_iota(jnp.int32, (rows, width), 0) < live_ref[0]
     out_ref[...] = jnp.where(keep, total, 0.0).astype(BF)
     token_ref[...] = jnp.zeros_like(token_ref)
 
 
-def final(live, own_grad, back_up, back_down, send_up, send_down, after):
+def final(live, own_grad, first_back, second_back, send_up, send_down, after):
     return pl.pallas_call(
         final_kernel,
         out_shape=(jax.ShapeDtypeStruct(own_grad.shape, BF), TOKEN),
@@ -353,39 +390,58 @@
         out_specs=(VMEM, VMEM),
         compiler_params=params(),
         name="final",
-    )(live, own_grad, back_up, back_down, send_up, send_down, after)
-
-
-def line_kernel(count, *refs):
-    for m in range(count):
-        refs[-1][m] = refs[m][...]
-
-
-def line(blocks, after):
-    if len(blocks) == 1:
-        return blocks[0][None]
-    return pl.pallas_call(
-        functools.partial(line_kernel, len(blocks)),
-        out_shape=jax.ShapeDtypeStruct((len(blocks), *blocks[0].shape), BF),
-        in_specs=[VMEM] * len(blocks) + [ANY] * len(after),
+    )(live, own_grad, first_back, second_back, send_up, send_down, after)
+
+
+def stack_kernel(count, *refs):
+    at = 0
+    for ref in refs[:count]:
+        for m in range(ref.shape[0] if len(ref.shape) == 4 else 1):
+            refs[-1][at] = ref[m] if len(ref.shape) == 4 else ref[...]
+            at += 1
+
+
+def stack(arrays, after):
+    blocks = sum(array.shape[0] if array.ndim == 4 else 1 for array in arrays)
+    return pl.pallas_call(
+        functools.partial(stack_kernel, len(arrays)),
+        out_shape=jax.ShapeDtypeStruct((blocks, *arrays[0].shape[-3:]), BF),
+        in_specs=[VMEM] * len(arrays) + [ANY] * len(after),
         out_specs=VMEM,
         compiler_params=params(),
         cost_estimate=cost(),
-        name="line",
-    )(*blocks, *after)
-
-
-def assemble_kernel(marks, parts, groups, place_ref, *refs):
+        name="stack",
+    )(*arrays, *after)
+
+
+def gate_kernel(*refs):
+    pass
+
+
+def gate(value, after):
+    return pl.pallas_call(
+        gate_kernel,
+        out_shape=jax.ShapeDtypeStruct(value.shape, value.dtype),
+        in_specs=[ANY] * (1 + len(after)),
+        out_specs=ANY,
+        input_output_aliases={0: 0},
+        compiler_params=params(),
+        cost_estimate=cost(),
+        name="gate",
+    )(value, *after)
+
+
+def assemble_kernel(marks, parts, groups, *refs):
     out_ref, sems = refs[-2:]
     offsets = out_ref.shape[0]
     _, count, block, _ = refs[0].shape
     short = offsets - (groups - 1) * count
 
     def each(act):
-        for index, (m, o, masks) in enumerate(marks):
-            group = place_ref[0] ^ m
-            for part, mask in enumerate(masks):
-                row = pl.multiple_of(((place_ref[1] ^ o) * parts + (place_ref[2] ^ mask)) * block, block)
+        for index, (o, sources) in enumerate(marks):
+            for part, (m, mask) in enumerate(sources):
+                group = place()[0] ^ m
+                row = pl.multiple_of(((place()[1] ^ o) * parts + (place()[2] ^ mask)) * block, block)
                 source = refs[index].at[part]
 
                 def copy(lo, hi, sem):
@@ -400,25 +456,28 @@
     each("wait")
 
 
-def assemble(place, pieces, marks, parts, groups, offsets, width, after):
+def assemble(pieces, marks, parts, groups, offsets, width, after, base=()):
+    most = max(piece.shape[0] for piece in pieces)
     return pl.pallas_call(
         functools.partial(assemble_kernel, marks, parts, groups),
         out_shape=jax.ShapeDtypeStruct((offsets, width, width), BF),
-        in_specs=[SMEM] + [ANY] * (len(pieces) + 1),
+        in_specs=[ANY] * (len(pieces) + len(after) + len(base)),
         out_specs=ANY,
-        scratch_shapes=[pltpu.SemaphoreType.DMA((len(pieces), parts, 2))],
-        compiler_params=params(),
+        scratch_shapes=[pltpu.SemaphoreType.DMA((len(pieces), most, 2))],
+        input_output_aliases={len(pieces) + len(after): 0} if base else {},
+        compiler_params=params(),
+        cost_estimate=cost(),
         name="assemble",
-    )(place, *pieces, after)
-
-
-def assemble_plain(place, pieces, marks, parts, groups, offsets, width, after):
+    )(*pieces, *after, *base)
+
+
+def assemble_plain(pieces, marks, parts, groups, offsets, width):
     _, count, block, _ = pieces[0].shape
     total = jnp.zeros((groups * count, width, width), BF)
-    for piece, (m, o, masks) in zip(pieces, marks):
-        for part, mask in enumerate(masks):
-            row = ((place[1] ^ o) * parts + (place[2] ^ mask)) * block
-            total = lax.dynamic_update_slice(total, piece[part], ((place[0] ^ m) * count, row, 0))
+    for piece, (o, sources) in zip(pieces, marks):
+        for part, (m, mask) in enumerate(sources):
+            row = ((place()[1] ^ o) * parts + (place()[2] ^ mask)) * block
+            total = lax.dynamic_update_slice(total, piece[part], ((place()[0] ^ m) * count, row, 0))
     return total[:offsets]
 
 
@@ -426,13 +485,10 @@
     return lax.ppermute(value, axis, [(i, i ^ mask) for i in range(lax.axis_size(axis))])
 
 
-def passed_along(value, axis, steps):
-    count = lax.axis_size(axis)
-    return lax.ppermute(value, axis, [(i, i + steps) for i in range(max(0, -steps), min(count, count - steps))])
-
-
-def SPLITS(parts):
-    return [(0,), tuple(range(1, parts))]
+def met(value, turn):
+    count = lax.axis_size("space")
+    starts = range(turn, count - 1, 2)
+    return lax.ppermute(value, "space", [(i, i + 1) for i in starts] + [(i + 1, i) for i in starts])
 
 
 def shards(features, weights, cotangent, kernel_map, live, send_up, send_down):
@@ -442,37 +498,43 @@
     parts = lax.axis_size("space")
     count = -(-offsets // groups)
     map_rows = -(-(groups * count) // 16) * 16
-    dp, space = lax.axis_index("dp"), lax.axis_index("space")
-    place = jnp.stack([dp // 2, dp % 2, space]).astype(jnp.int32)
-
-    pack, up_rows, down_rows = prep(live, features, cotangent, kernel_map, send_up, send_down, map_rows)
+
+    pack, first_rows, second_rows = prep(live, features, cotangent, kernel_map, send_up, send_down, map_rows)
     packs = [pack] + [swap(pack, "dp", 2 * m) for m in range(1, groups)]
-    lower = passed_along(up_rows, "space", 1)
-    upper = passed_along(down_rows, "space", -1)
-    halo_rows = jnp.concatenate([lower, upper])
+    halo_rows, pack = joined(met(first_rows, 0), met(second_rows, 1), pack)
+    packs[0] = pack
     halos = [halo_rows] + [swap(halo_rows, "dp", 2 * m) for m in range(1, groups)]
-    picked, dys, maps = wgrad_own(place, packs, count, rows)
-    keep, send = wgrad(place, picked, dys, maps, halos, 0, count, dys)
-    mine, *coded = blocks(place, keep, swap(send, "dp", 1), parts)
-    own_grad, low_grad, high_grad, token = backward(pack, weights, rows, halo, mine)
-    back_up = passed_along(low_grad, "space", -1)
-    back_down = passed_along(high_grad, "space", 1)
+    picked, dys, maps = wgrad_own(packs, count, rows)
+    keep, send = wgrad(picked, dys, maps, halos, 0, count, dys)
+    mine, *coded = blocks(keep, swap(send, "dp", 1), parts)
+    own_grad, first_grad, second_grad, token = backward(pack, weights, rows, halo, mine)
+    first_back, second_back = met(first_grad, 0), met(second_grad, 1)
     scale = 1.0 / math.sqrt(rows * lax.axis_size("dp") * parts)
     rounded = scaled_total(mine, [swap(block, "space", m + 1) for m, block in enumerate(coded)], scale, (token, token))
     out_features, token = forward(live, pack, halo_rows, weights, rows, rounded)
 
-    in_line = [rounded] + [swap(rounded, "space", m) for m in range(1, parts)]
-    pieces, marks = [], []
-    for masks in SPLITS(parts):
-        lines = line([in_line[m] for m in masks], pieces[2::2][-groups:] + [token])
-        for m in range(groups):
-            piece = swap(lines, "dp", 2 * m) if m else lines
-            pieces += [piece, swap(piece, "dp", 1)]
-            marks += [(m, 0, masks), (m, 1, masks)]
-    grad_features, token = final(live, own_grad, back_up, back_down, send_up, send_down, lines)
+    along = [swap(rounded, "space", m) for m in range(1, parts)]
+    across = {m: swap(rounded, "dp", 2 * m) for m in reversed(range(1, groups))}
+    lines = gate(stack(along, [token]), list(across.values()))
+    far = {m: swap(lines, "dp", 2 * m) for m in reversed(range(1, groups))}
+    line_masks = range(1, parts)
+    near = stack([rounded, lines], [])
+    sides = stack([across[m] for m in range(1, groups)], [])
+    near_marks = [(0, mask) for mask in range(parts)]
+    side_marks = [(m, 0) for m in range(1, groups)]
+    pieces = [near, swap(near, "dp", 1), sides, swap(sides, "dp", 1)]
+    marks = [(0, near_marks), (1, near_marks), (0, side_marks), (1, side_marks)]
+    grad_features, token = final(live, own_grad, first_back, second_back, send_up, send_down, lines)
     dense = rounded.shape[1] % 16 == 0 and groups * count - offsets < count
-    put = assemble if dense else assemble_plain
-    grad_weights = put(place, pieces, marks, parts, groups, offsets, width, token)
+    sizes = (parts, groups, offsets, width)
+    first = ()
+    for m in range(1, groups):
+        pieces += [far[m], swap(far[m], "dp", 1)]
+        marks += [(o, [(m, mask) for mask in line_masks]) for o in range(2)]
+    if dense:
+        grad_weights = assemble(pieces, marks, *sizes, (token,), first)
+    else:
+        grad_weights = assemble_plain(pieces, marks, *sizes)
     return (out_features, grad_features, grad_weights)
 
 

time: 83.5 us -> 78.6 us (0.941)
  Pallas kernels: 21.9 us -> 18.9 us
  waiting for transfers between devices: 24 us -> 21.8 us
    ppermute x4, waiting for transfers between devices: 11.3 us -> 3.62 us  [met(): lax.ppermute(value, 'space', [(i, i + 1) for i in starts] + [(i + 1, i) f...]
    ppermute x27 -> x24, waiting for transfers between devices: 12.6 us -> 18.2 us  [swap(): lax.ppermute(value, axis, [(i, i ^ mask) for i in range(lax.axis_size(axi...]
    pallas_call x1, Pallas kernels: 3.47 us -> 2.48 us  [assemble(): pl.pallas_call(functools.partial(assemble_kernel, marks, parts, groups),...]
    ppermute x27 -> x24, starting transfers between devices: 26.8 us -> 26.2 us  [swap(): lax.ppermute(value, axis, [(i, i ^ mask) for i in range(lax.axis_size(axi...]
  transfers between devices with their start and end apart: 31 -> 28, of which waited for: 12 -> 15; matrix products, arithmetic and copies ran while one was open for 0% -> 0% of each run, Pallas kernels for 15% -> 15%
where the time goes in v6:
time: 78.6 us; the launch traced here: 77.9 us
  starting transfers between devices  34.7 us (44%)
  waiting for transfers between devices  21.8 us (28%)
  Pallas kernels  18.9 us (24%)
  between operations  1.48 us (2%)
  local copies, waits for them, and re-layouts  0.98 us (1%)
    ppermute x24, starting transfers between devices, swap(): lax.ppermute(value, axis, [(i, i ^ mask) for i in range(lax.axis_size(axi...  26.2 us
    ppermute x24, waiting for transfers between devices, swap(): lax.ppermute(value, axis, [(i, i ^ mask) for i in range(lax.axis_size(axi...  18.2 us
    ppermute x4, starting transfers between devices, met(): lax.ppermute(value, 'space', [(i, i + 1) for i in starts] + [(i + 1, i) f...  8.47 us
    pallas_call x1, Pallas kernels, backward(): pl.pallas_call(functools.partial(backward_kernel, group), out_shape=tuple...  5.46 us
    pallas_call x1, Pallas kernels, forward(): pl.pallas_call(functools.partial(forward_kernel, group), out_shape=(jax.S...  3.91 us
    ppermute x4, waiting for transfers between devices, met(): lax.ppermute(value, 'space', [(i, i + 1) for i in starts] + [(i + 1, i) f...  3.62 us
    pallas_call x1, Pallas kernels, assemble(): pl.pallas_call(functools.partial(assemble_kernel, marks, parts, groups),...  2.48 us
    pallas_call x1, Pallas kernels, wgrad(): pl.pallas_call(functools.partial(wgrad_kernel, sources, first), out_shape...  2.21 us
  transfers between devices with their start and end apart: 28, of which 15 were waited for; matrix products, arithmetic and copies ran while one was open for 0% of the time, Pallas kernels for 15%

profile of v6, /device:TPU:0, one launch (start us, length us, event | category | flops | bytes accessed | tf_op | source)
XLA Modules:
  0.0 77.9 jit_solution(12865269905095767942)
XLA Ops:
  1.3 1.9 %prep.1 = (bf16[544,256]{1,0:T(8,128)(2,1)}, bf16[64,256]{1,0:T(8,128)(2,1)}, bf16[64,256]{1,0:T(8,128)(2,1)}) custom-call(s32[1]{0:T(128)S(6)} %copy.12.live_ref, bf16[256,256]{1,0:T(8,128)(2,1)} %x_hbm.1, bf16[256,256]{1,0:T(8,128)(2,1)} %dy_hbm.1, s32[27,256]{1,0:T(8,128)} %map_hbm.1, s32[1,64]{1,0:T(1,128)} %up_ref.1, s32[1,64]{1,0:T(1,128)} %down_ref.1), custom_call_target="tpu_custom_call" | custom-call | tf_op jit(solution)/shard_map/prep/pallas_call | solution.py:81
  3.2 4.0 %collective-permute-start.4 = (bf16[544,256]{1,0:T(8,128)(2,1)}, bf16[544,256]{1,0:T(8,128)(2,1)S(1)}, u32[]{:S(2)}, u32[]{:S(2)}) collective-permute-start(bf16[544,256]{1,0:T(8,128)(2,1)} %get-tuple-element.27.pack_ref), channel_id=1, source_target_pairs={{0,24},{4,28},{8,16},{12,20},{16,8},{20,12},{24,0},{28,4},{1,25},{... | collective-permute-start | bytes 835592 | tf_op jit(solution)/shard_map/ppermute | solution.py:485
  7.1 0.5 collective-permute-start.3
  7.6 0.1 collective-permute-start.2
  7.8 2.0 %collective-permute-start = (bf16[64,256]{1,0:T(8,128)(2,1)}, bf16[64,256]{1,0:T(8,128)(2,1)S(1)}, u32[]{:S(2)}, u32[]{:S(2)}) collective-permute-start(bf16[64,256]{1,0:T(8,128)(2,1)} %get-tuple-element.25), channel_id=1, source_target_pairs={{0,1},{2,3},{1,0},{3,2},{4,5},{6,7},{5,4},{7,6},{8,9},{10,11},{9,8... | collective-permute-start | bytes 98312 | tf_op jit(solution)/shard_map/ppermute | solution.py:491
  9.7 0.7 collective-permute-start.1
  10.4 1.5 %collective-permute-done.first_ref = bf16[64,256]{1,0:T(8,128)(2,1)S(1)} collective-permute-done((bf16[64,256]{1,0:T(8,128)(2,1)}, bf16[64,256]{1,0:T(8,128)(2,1)S(1)}, u32[]{:S(2)}, u32[]{:S(2)}) %collective-permute-start) | collective-permute-done | bytes 32800 | tf_op jit(solution)/shard_map/ppermute | solution.py:491
  11.9 1.0 %copy-done.3 = bf16[544,256]{1,0:T(8,128)(2,1)S(1)} copy-done((bf16[544,256]{1,0:T(8,128)(2,1)S(1)}, bf16[544,256]{1,0:T(8,128)(2,1)}, u32[]{:S(2)}) %copy-start.3) | copy-done | bytes 278552
  12.9 2.9 %collective-permute-start.7 = (bf16[128,256]{1,0:T(8,128)(2,1)S(1)}, bf16[128,256]{1,0:T(8,128)(2,1)S(1)}, u32[]{:S(2)}, u32[]{:S(2)}) collective-permute-start(bf16[128,256]{1,0:T(8,128)(2,1)S(1)} %get-tuple-element.29.refs_0_.halo_ref), channel_id=1, source_target_pairs={{0,24},{4,28},{8,16},{12,20},{16,8},{20,12},{24,0},{28,4},{1,25},{... | collective-permute-start | bytes 196616 | tf_op jit(solution)/shard_map/ppermute | solution.py:485
  15.8 0.5 collective-permute-start.6
  16.3 0.6 collective-permute-start.5
  16.9 3.9 %collective-permute-done.3.refs_2_ = bf16[544,256]{1,0:T(8,128)(2,1)S(1)} collective-permute-done((bf16[544,256]{1,0:T(8,128)(2,1)}, bf16[544,256]{1,0:T(8,128)(2,1)S(1)}, u32[]{:S(2)}, u32[]{:S(2)}) %collective-permute-start.3) | collective-permute-done | bytes 278560 | tf_op jit(solution)/shard_map/ppermute | solution.py:485
  20.7 0.6 collective-permute-done.2.refs_1_
  21.4 1.3 %wgrad_own.1 = (bf16[7,256,1024]{2,1,0:T(8,128)(2,1)S(1)}, bf16[1024,256]{1,0:T(8,128)(2,1)S(1)}, s32[4,32,256]{2,1,0:T(8,128)S(1)}) custom-call(bf16[544,256]{1,0:T(8,128)(2,1)S(1)} %get-tuple-element.28.refs_0_.pack_ref, bf16[544,256]{1,0:T(8,128)(2,1)S(1)} %collective-permute-done.2.refs_1_, bf16[544,256]{1,0:T(8,128)(2,1)S(1)} %collective-permute-done.3.refs_2_, ...), custom_call_target="tpu_custom_call" | custom-call | flops 100000000 | bytes 100000 | tf_op jit(solution)/shard_map/wgrad_own/pallas_call | solution.py:223
  22.8 0.3 collective-permute-done.5.refs_1_
  23.0 2.2 %wgrad.1 = (f32[7,128,256]{2,1,0:T(8,128)S(1)}, f32[7,128,256]{2,1,0:T(8,128)S(1)}) custom-call(bf16[7,256,1024]{2,1,0:T(8,128)(2,1)S(1)} %get-tuple-element.30.picked_ref, bf16[1024,256]{1,0:T(8,128)(2,1)S(1)} %get-tuple-element.31.dys.refs_4_, s32[4,32,256]{2,1,0:T(8,128)S(1)} %get-tuple-element.32.maps, ...), custom_call_target="tpu_custom_call" | custom-call | flops 100000000 | bytes 100000 | tf_op jit(solution)/shard_map/wgrad/pallas_call | solution.py:261
  25.3 2.5 %collective-permute-done.8.got_ref = f32[7,128,256]{2,1,0:T(8,128)S(1)} collective-permute-done((f32[7,128,256]{2,1,0:T(8,128)S(1)}, f32[7,128,256]{2,1,0:T(8,128)S(1)}, u32[]{:S(2)}, u32[]{:S(2)}) %collective-permute-start.8) | collective-permute-done | bytes 917536 | tf_op jit(solution)/shard_map/ppermute | solution.py:485
  27.8 0.5 blocks.1
  28.3 2.2 %collective-permute-start.9 = (s16[240,256]{1,0:T(8,128)(2,1)S(1)}, s16[240,256]{1,0:T(8,128)(2,1)S(1)}, u32[]{:S(2)}, u32[]{:S(2)}) collective-permute-start(s16[240,256]{1,0:T(8,128)(2,1)S(1)} %get-tuple-element.36), channel_id=1, source_target_pairs={{0,1},{1,0},{2,3},{3,2},{4,5},{5,4},{6,7},{7,6},{8,9},{9,8},{10,11... | collective-permute-start | bytes 368648 | tf_op jit(solution)/shard_map/ppermute | solution.py:485
  30.5 2.1 %collective-permute-start.10 = (s16[240,256]{1,0:T(8,128)(2,1)S(1)}, s16[240,256]{1,0:T(8,128)(2,1)S(1)}, u32[]{:S(2)}, u32[]{:S(2)}) collective-permute-start(s16[240,256]{1,0:T(8,128)(2,1)S(1)} %get-tuple-element.37), channel_id=1, source_target_pairs={{0,2},{1,3},{2,0},{3,1},{4,6},{5,7},{6,4},{7,5},{8,10},{9,11},{10,... | collective-permute-start | bytes 368648 | tf_op jit(solution)/shard_map/ppermute | solution.py:485
  32.5 0.8 %collective-permute-start.11 = (s16[240,256]{1,0:T(8,128)(2,1)S(1)}, s16[240,256]{1,0:T(8,128)(2,1)S(1)}, u32[]{:S(2)}, u32[]{:S(2)}) collective-permute-start(s16[240,256]{1,0:T(8,128)(2,1)S(1)} %get-tuple-element.38), channel_id=1, source_target_pairs={{0,3},{1,2},{2,1},{3,0},{4,7},{5,6},{6,5},{7,4},{8,11},{9,10},{10,... | collective-permute-start | bytes 368648 | tf_op jit(solution)/shard_map/ppermute | solution.py:485
  33.4 5.5 %backward.1 = (f32[256,256]{1,0:T(8,128)S(1)}, f32[64,256]{1,0:T(8,128)S(1)}, f32[64,256]{1,0:T(8,128)S(1)}, f32[8,128]{1,0:T(8,128)S(1)}) custom-call(bf16[544,256]{1,0:T(8,128)(2,1)S(1)} %get-tuple-element.28.refs_0_.pack_ref, bf16[27,256,256]{2,1,0:T(8,128)(2,1)S(1)} %copy-done, f32[7,32,256]{2,1,0:T(8,128)S(1)} %get-tuple-element.35.after_ref.mine_ref), custom_call_target="tpu_custom_call" | custom-call | flops 100000000 | bytes 100000 | tf_op jit(solution)/shard_map/backward/pallas_call | solution.py:138
  38.9 3.9 %collective-permute-done.10.refs_1_ = s16[240,256]{1,0:T(8,128)(2,1)S(1)} collective-permute-done((s16[240,256]{1,0:T(8,128)(2,1)S(1)}, s16[240,256]{1,0:T(8,128)(2,1)S(1)}, u32[]{:S(2)}, u32[]{:S(2)}) %collective-permute-start.10) | collective-permute-done | bytes 122912 | tf_op jit(solution)/shard_map/ppermute | solution.py:485
  42.8 0.1 total.1.after_ref.refs_0_
  43.0 2.5 %collective-permute-start.16 = (bf16[7,32,256]{2,1,0:T(8,128)(2,1)S(1)}, bf16[7,32,256]{2,1,0:T(8,128)(2,1)S(1)}, u32[]{:S(2)}, u32[]{:S(2)}) collective-permute-start(bf16[7,32,256]{2,1,0:T(8,128)(2,1)S(1)} %total.1.after_ref.refs_0_), channel_id=1, source_target_pairs={{0,3},{1,2},{2,1},{3,0},{4,7},{5,6},{6,5},{7,4},{8,11},{9,10},{10,... | collective-permute-start | bytes 344072 | tf_op jit(solution)/shard_map/ppermute | solution.py:485
  45.5 1.2 %collective-permute-start.15 = (bf16[7,32,256]{2,1,0:T(8,128)(2,1)S(1)}, bf16[7,32,256]{2,1,0:T(8,128)(2,1)S(1)}, u32[]{:S(2)}, u32[]{:S(2)}) collective-permute-start(bf16[7,32,256]{2,1,0:T(8,128)(2,1)S(1)} %total.1.after_ref.refs_0_), channel_id=1, source_target_pairs={{0,2},{1,3},{2,0},{3,1},{4,6},{5,7},{6,4},{7,5},{8,10},{9,11},{10,... | collective-permute-start | bytes 344072 | tf_op jit(solution)/shard_map/ppermute | solution.py:485
  46.7 0.7 collective-permute-start.14
  47.4 1.0 %collective-permute-start.19 = (bf16[7,32,256]{2,1,0:T(8,128)(2,1)S(1)}, bf16[7,32,256]{2,1,0:T(8,128)(2,1)S(1)}, u32[]{:S(2)}, u32[]{:S(2)}) collective-permute-start(bf16[7,32,256]{2,1,0:T(8,128)(2,1)S(1)} %total.1.after_ref.refs_0_), channel_id=1, source_target_pairs={{0,8},{4,12},{8,0},{12,4},{16,24},{20,28},{24,16},{28,20},{1,9},{5... | collective-permute-start | bytes 344072 | tf_op jit(solution)/shard_map/ppermute | solution.py:485
  48.4 1.0 %collective-permute-start.18 = (bf16[7,32,256]{2,1,0:T(8,128)(2,1)S(1)}, bf16[7,32,256]{2,1,0:T(8,128)(2,1)S(1)}, u32[]{:S(2)}, u32[]{:S(2)}) collective-permute-start(bf16[7,32,256]{2,1,0:T(8,128)(2,1)S(1)} %total.1.after_ref.refs_0_), channel_id=1, source_target_pairs={{0,16},{4,20},{8,24},{12,28},{16,0},{20,4},{24,8},{28,12},{1,17},{... | collective-permute-start | bytes 344072 | tf_op jit(solution)/shard_map/ppermute | solution.py:485
  49.5 0.5 collective-permute-done.16.refs_2_
  50.0 1.6 %collective-permute-start.17 = (bf16[7,32,256]{2,1,0:T(8,128)(2,1)S(1)}, bf16[7,32,256]{2,1,0:T(8,128)(2,1)S(1)}, u32[]{:S(2)}, u32[]{:S(2)}) collective-permute-start(bf16[7,32,256]{2,1,0:T(8,128)(2,1)S(1)} %total.1.after_ref.refs_0_), channel_id=1, source_target_pairs={{0,24},{4,28},{8,16},{12,20},{16,8},{20,12},{24,0},{28,4},{1,25},{... | collective-permute-start | bytes 344072 | tf_op jit(solution)/shard_map/ppermute | solution.py:485
  51.6 3.9 %forward.1 = (bf16[256,256]{1,0:T(8,128)(2,1)}, f32[8,128]{1,0:T(8,128)S(1)}) custom-call(s32[1]{0:T(128)S(6)} %copy.12.live_ref, bf16[544,256]{1,0:T(8,128)(2,1)S(1)} %get-tuple-element.28.refs_0_.pack_ref, bf16[128,256]{1,0:T(8,128)(2,1)S(1)} %get-tuple-element.29.refs_0_.halo_ref, bf16[27,256,256]{2,1,0:T(8,128)(2,1)S(1)} %copy-done, ...), custom_call_target="tpu_custom_call" | custom-call | flops 100000000 | bytes 100000 | tf_op jit(solution)/shard_map/forward/pallas_call | solution.py:183
  55.5 0.3 collective-permute-done.15.refs_1_
  55.9 1.6 %collective-permute-start.26 = (bf16[3,7,32,256]{3,2,1,0:T(8,128)(2,1)S(1)}, bf16[3,7,32,256]{3,2,1,0:T(8,128)(2,1)S(1)}, u32[]{:S(2)}, u32[]{:S(2)}) collective-permute-start(bf16[3,7,32,256]{3,2,1,0:T(8,128)(2,1)S(1)} %gate.1.after_ref.refs_1_), channel_id=1, source_target_pairs={{0,24},{4,28},{8,16},{12,20},{16,8},{20,12},{24,0},{28,4},{1,25},{... | collective-permute-start | bytes 1032200 | tf_op jit(solution)/shard_map/ppermute | solution.py:485
  57.4 1.7 %collective-permute-start.24 = (bf16[3,7,32,256]{3,2,1,0:T(8,128)(2,1)S(1)}, bf16[3,7,32,256]{3,2,1,0:T(8,128)(2,1)S(1)}, u32[]{:S(2)}, u32[]{:S(2)}) collective-permute-start(bf16[3,7,32,256]{3,2,1,0:T(8,128)(2,1)S(1)} %gate.1.after_ref.refs_1_), channel_id=1, source_target_pairs={{0,16},{4,20},{8,24},{12,28},{16,0},{20,4},{24,8},{28,12},{1,17},{... | collective-permute-start | bytes 1032200 | tf_op jit(solution)/shard_map/ppermute | solution.py:485
  59.1 0.3 collective-permute-start.22
  59.4 5.2 %collective-permute-start.12 = (f32[64,256]{1,0:T(8,128)S(1)}, f32[64,256]{1,0:T(8,128)S(1)}, u32[]{:S(2)}, u32[]{:S(2)}) collective-permute-start(f32[64,256]{1,0:T(8,128)S(1)} %get-tuple-element.42), channel_id=1, source_target_pairs={{0,1},{2,3},{1,0},{3,2},{4,5},{6,7},{5,4},{7,6},{8,9},{10,11},{9,8... | collective-permute-start | bytes 196616 | tf_op jit(solution)/shard_map/ppermute | solution.py:491
  64.7 2.1 %collective-permute-done.12.first_ref = f32[64,256]{1,0:T(8,128)S(1)} collective-permute-done((f32[64,256]{1,0:T(8,128)S(1)}, f32[64,256]{1,0:T(8,128)S(1)}, u32[]{:S(2)}, u32[]{:S(2)}) %collective-permute-start.12) | collective-permute-done | bytes 65568 | tf_op jit(solution)/shard_map/ppermute | solution.py:491
  66.9 0.7 collective-permute-start.13
  67.6 0.2 collective-permute-done.26.refs_8_
  67.9 0.3 collective-permute-start.27
  68.1 5.1 %collective-permute-done.24.refs_6_ = bf16[3,7,32,256]{3,2,1,0:T(8,128)(2,1)S(1)} collective-permute-done((bf16[3,7,32,256]{3,2,1,0:T(8,128)(2,1)S(1)}, bf16[3,7,32,256]{3,2,1,0:T(8,128)(2,1)S(1)}, u32[]{:S(2)}, u32[]{:S(2)}) %collective-permute-start.24) | collective-permute-done | bytes 344096 | tf_op jit(solution)/shard_map/ppermute | solution.py:485
  73.3 0.1 collective-permute-done.22.refs_4_
  73.4 0.4 collective-permute-start.23
  73.8 1.0 %final.1 = (bf16[256,256]{1,0:T(8,128)(2,1)}, f32[8,128]{1,0:T(8,128)S(1)}) custom-call(s32[1]{0:T(128)S(6)} %copy.12.live_ref, f32[256,256]{1,0:T(8,128)S(1)} %get-tuple-element.41.own_ref, f32[64,256]{1,0:T(8,128)S(1)} %collective-permute-done.12.first_ref, f32[64,256]{1,0:T(8,128)S(1)} %collective-permute-done.13.second_ref, s32[1,64]{1,0:T(1,128)S(1)} %copy-done.1, ...), custom_call_target="tpu_custom_call" | custom-call | tf_op jit(solution)/shard_map/final/pallas_call | solution.py:386
  74.8 0.1 collective-permute-done.25.refs_7_
  74.9 0.5 collective-permute-done.23.refs_5_
  75.4 2.5 %assemble.1 = bf16[27,256,256]{2,1,0:T(8,128)(2,1)} custom-call(bf16[4,7,32,256]{3,2,1,0:T(8,128)(2,1)S(1)} %stack.4.refs_0_, bf16[4,7,32,256]{3,2,1,0:T(8,128)(2,1)S(1)} %collective-permute-done.20.refs_1_, bf16[3,7,32,256]{3,2,1,0:T(8,128)(2,1)S(1)} %stack.5.refs_2_, bf16[3,7,32,256]{3,2,1,0:T(8,128)(2,1)S(1)} %collective-permute-done.21.refs_3_, ...), custom_call_target="tpu_custom_call" | custom-call | flops 100000000 | bytes 100000 | tf_op jit(solution)/shard_map/assemble/pallas_call | solution.py:461
  (30 shorter events, 0.5 us)
Async XLA Ops:
  3.2 13.1 %collective-permute-start.4 = (bf16[544,256]{1,0:T(8,128)(2,1)}, bf16[544,256]{1,0:T(8,128)(2,1)S(1)}, u32[]{:S(2)}, u32[]{:S(2)}) collective-permute-start(bf16[544,256]{1,0:T(8,128)(2,1)} %get-tuple-element.27.pack_ref), channel_id=1, source_target_pairs={{0,24},{4,28},{8,16},{12,20},{16,8},{20,12},{24,0},{28,4},{1,25},{... | collective-permute-start | bytes 835592 | tf_op jit(solution)/shard_map/ppermute | solution.py:485
  7.1 13.6 %collective-permute-start.3 = (bf16[544,256]{1,0:T(8,128)(2,1)}, bf16[544,256]{1,0:T(8,128)(2,1)S(1)}, u32[]{:S(2)}, u32[]{:S(2)}) collective-permute-start(bf16[544,256]{1,0:T(8,128)(2,1)} %get-tuple-element.27.pack_ref), channel_id=1, source_target_pairs={{0,16},{4,20},{8,24},{12,28},{16,0},{20,4},{24,8},{28,12},{1,17},{... | collective-permute-start | bytes 835592 | tf_op jit(solution)/shard_map/ppermute | solution.py:485
  7.6 13.8 %collective-permute-start.2 = (bf16[544,256]{1,0:T(8,128)(2,1)}, bf16[544,256]{1,0:T(8,128)(2,1)S(1)}, u32[]{:S(2)}, u32[]{:S(2)}) collective-permute-start(bf16[544,256]{1,0:T(8,128)(2,1)} %get-tuple-element.27.pack_ref), channel_id=1, source_target_pairs={{0,8},{4,12},{8,0},{12,4},{16,24},{20,28},{24,16},{28,20},{1,9},{5... | collective-permute-start | bytes 835592 | tf_op jit(solution)/shard_map/ppermute | solution.py:485
  7.8 4.1 %collective-permute-start = (bf16[64,256]{1,0:T(8,128)(2,1)}, bf16[64,256]{1,0:T(8,128)(2,1)S(1)}, u32[]{:S(2)}, u32[]{:S(2)}) collective-permute-start(bf16[64,256]{1,0:T(8,128)(2,1)} %get-tuple-element.25), channel_id=1, source_target_pairs={{0,1},{2,3},{1,0},{3,2},{4,5},{6,7},{5,4},{7,6},{8,9},{10,11},{9,8... | collective-permute-start | bytes 98312 | tf_op jit(solution)/shard_map/ppermute | solution.py:491
  9.7 2.2 %collective-permute-start.1 = (bf16[64,256]{1,0:T(8,128)(2,1)}, bf16[64,256]{1,0:T(8,128)(2,1)S(1)}, u32[]{:S(2)}, u32[]{:S(2)}) collective-permute-start(bf16[64,256]{1,0:T(8,128)(2,1)} %get-tuple-element.26), channel_id=1, source_target_pairs={{1,2},{2,1},{5,6},{6,5},{9,10},{10,9},{13,14},{14,13},{17,18},{18,... | collective-permute-start | bytes 98312 | tf_op jit(solution)/shard_map/ppermute | solution.py:491
  11.9 1.0 %copy-start.3 = (bf16[544,256]{1,0:T(8,128)(2,1)S(1)}, bf16[544,256]{1,0:T(8,128)(2,1)}, u32[]{:S(2)}) copy-start(bf16[544,256]{1,0:T(8,128)(2,1)} %get-tuple-element.27.pack_ref) | copy-start | bytes 835588
  12.9 9.8 %collective-permute-start.7 = (bf16[128,256]{1,0:T(8,128)(2,1)S(1)}, bf16[128,256]{1,0:T(8,128)(2,1)S(1)}, u32[]{:S(2)}, u32[]{:S(2)}) collective-permute-start(bf16[128,256]{1,0:T(8,128)(2,1)S(1)} %get-tuple-element.29.refs_0_.halo_ref), channel_id=1, source_target_pairs={{0,24},{4,28},{8,16},{12,20},{16,8},{20,12},{24,0},{28,4},{1,25},{... | collective-permute-start | bytes 196616 | tf_op jit(solution)/shard_map/ppermute | solution.py:485
  15.8 7.0 %collective-permute-start.6 = (bf16[128,256]{1,0:T(8,128)(2,1)S(1)}, bf16[128,256]{1,0:T(8,128)(2,1)S(1)}, u32[]{:S(2)}, u32[]{:S(2)}) collective-permute-start(bf16[128,256]{1,0:T(8,128)(2,1)S(1)} %get-tuple-element.29.refs_0_.halo_ref), channel_id=1, source_target_pairs={{0,16},{4,20},{8,24},{12,28},{16,0},{20,4},{24,8},{28,12},{1,17},{... | collective-permute-start | bytes 196616 | tf_op jit(solution)/shard_map/ppermute | solution.py:485
  16.3 6.8 %collective-permute-start.5 = (bf16[128,256]{1,0:T(8,128)(2,1)S(1)}, bf16[128,256]{1,0:T(8,128)(2,1)S(1)}, u32[]{:S(2)}, u32[]{:S(2)}) collective-permute-start(bf16[128,256]{1,0:T(8,128)(2,1)S(1)} %get-tuple-element.29.refs_0_.halo_ref), channel_id=1, source_target_pairs={{0,8},{4,12},{8,0},{12,4},{16,24},{20,28},{24,16},{28,20},{1,9},{5... | collective-permute-start | bytes 196616 | tf_op jit(solution)/shard_map/ppermute | solution.py:485
  22.7 10.7 %copy-start = (bf16[27,256,256]{2,1,0:T(8,128)(2,1)S(1)}, bf16[27,256,256]{2,1,0:T(8,128)(2,1)}, u32[]{:S(2)}) copy-start(bf16[27,256,256]{2,1,0:T(8,128)(2,1)} %w_ref.3) | copy-start | bytes 10616836
  25.3 2.5 %collective-permute-start.8 = (f32[7,128,256]{2,1,0:T(8,128)S(1)}, f32[7,128,256]{2,1,0:T(8,128)S(1)}, u32[]{:S(2)}, u32[]{:S(2)}) collective-permute-start(f32[7,128,256]{2,1,0:T(8,128)S(1)} %get-tuple-element.34), channel_id=1, source_target_pairs={{0,4},{4,0},{8,12},{12,8},{16,20},{20,16},{24,28},{28,24},{1,5},{5... | collective-permute-start | bytes 2752520 | tf_op jit(solution)/shard_map/ppermute | solution.py:485
  28.3 10.6 %collective-permute-start.9 = (s16[240,256]{1,0:T(8,128)(2,1)S(1)}, s16[240,256]{1,0:T(8,128)(2,1)S(1)}, u32[]{:S(2)}, u32[]{:S(2)}) collective-permute-start(s16[240,256]{1,0:T(8,128)(2,1)S(1)} %get-tuple-element.36), channel_id=1, source_target_pairs={{0,1},{1,0},{2,3},{3,2},{4,5},{5,4},{6,7},{7,6},{8,9},{9,8},{10,11... | collective-permute-start | bytes 368648 | tf_op jit(solution)/shard_map/ppermute | solution.py:485
  30.5 12.3 %collective-permute-start.10 = (s16[240,256]{1,0:T(8,128)(2,1)S(1)}, s16[240,256]{1,0:T(8,128)(2,1)S(1)}, u32[]{:S(2)}, u32[]{:S(2)}) collective-permute-start(s16[240,256]{1,0:T(8,128)(2,1)S(1)} %get-tuple-element.37), channel_id=1, source_target_pairs={{0,2},{1,3},{2,0},{3,1},{4,6},{5,7},{6,4},{7,5},{8,10},{9,11},{10,... | collective-permute-start | bytes 368648 | tf_op jit(solution)/shard_map/ppermute | solution.py:485
  32.5 10.2 %collective-permute-start.11 = (s16[240,256]{1,0:T(8,128)(2,1)S(1)}, s16[240,256]{1,0:T(8,128)(2,1)S(1)}, u32[]{:S(2)}, u32[]{:S(2)}) collective-permute-start(s16[240,256]{1,0:T(8,128)(2,1)S(1)} %get-tuple-element.38), channel_id=1, source_target_pairs={{0,3},{1,2},{2,1},{3,0},{4,7},{5,6},{6,5},{7,4},{8,11},{9,10},{10,... | collective-permute-start | bytes 368648 | tf_op jit(solution)/shard_map/ppermute | solution.py:485
  42.9 30.8 %copy-start.1 = (s32[1,64]{1,0:T(1,128)S(1)}, s32[1,64]{1,0:T(1,128)}, u32[]{:S(2)}) copy-start(s32[1,64]{1,0:T(1,128)} %up_ref.1) | copy-start | bytes 772
  42.9 30.8 %copy-start.2 = (s32[1,64]{1,0:T(1,128)S(1)}, s32[1,64]{1,0:T(1,128)}, u32[]{:S(2)}) copy-start(s32[1,64]{1,0:T(1,128)} %down_ref.1) | copy-start | bytes 772
  43.0 7.1 %collective-permute-start.16 = (bf16[7,32,256]{2,1,0:T(8,128)(2,1)S(1)}, bf16[7,32,256]{2,1,0:T(8,128)(2,1)S(1)}, u32[]{:S(2)}, u32[]{:S(2)}) collective-permute-start(bf16[7,32,256]{2,1,0:T(8,128)(2,1)S(1)} %total.1.after_ref.refs_0_), channel_id=1, source_target_pairs={{0,3},{1,2},{2,1},{3,0},{4,7},{5,6},{6,5},{7,4},{8,11},{9,10},{10,... | collective-permute-start | bytes 344072 | tf_op jit(solution)/shard_map/ppermute | solution.py:485
  45.5 10.3 %collective-permute-start.15 = (bf16[7,32,256]{2,1,0:T(8,128)(2,1)S(1)}, bf16[7,32,256]{2,1,0:T(8,128)(2,1)S(1)}, u32[]{:S(2)}, u32[]{:S(2)}) collective-permute-start(bf16[7,32,256]{2,1,0:T(8,128)(2,1)S(1)} %total.1.after_ref.refs_0_), channel_id=1, source_target_pairs={{0,2},{1,3},{2,0},{3,1},{4,6},{5,7},{6,4},{7,5},{8,10},{9,11},{10,... | collective-permute-start | bytes 344072 | tf_op jit(solution)/shard_map/ppermute | solution.py:485
  46.7 9.1 %collective-permute-start.14 = (bf16[7,32,256]{2,1,0:T(8,128)(2,1)S(1)}, bf16[7,32,256]{2,1,0:T(8,128)(2,1)S(1)}, u32[]{:S(2)}, u32[]{:S(2)}) collective-permute-start(bf16[7,32,256]{2,1,0:T(8,128)(2,1)S(1)} %total.1.after_ref.refs_0_), channel_id=1, source_target_pairs={{0,1},{1,0},{2,3},{3,2},{4,5},{5,4},{6,7},{7,6},{8,9},{9,8},{10,11... | collective-permute-start | bytes 344072 | tf_op jit(solution)/shard_map/ppermute | solution.py:485
  47.4 8.4 %collective-permute-start.19 = (bf16[7,32,256]{2,1,0:T(8,128)(2,1)S(1)}, bf16[7,32,256]{2,1,0:T(8,128)(2,1)S(1)}, u32[]{:S(2)}, u32[]{:S(2)}) collective-permute-start(bf16[7,32,256]{2,1,0:T(8,128)(2,1)S(1)} %total.1.after_ref.refs_0_), channel_id=1, source_target_pairs={{0,8},{4,12},{8,0},{12,4},{16,24},{20,28},{24,16},{28,20},{1,9},{5... | collective-permute-start | bytes 344072 | tf_op jit(solution)/shard_map/ppermute | solution.py:485
  48.4 7.4 %collective-permute-start.18 = (bf16[7,32,256]{2,1,0:T(8,128)(2,1)S(1)}, bf16[7,32,256]{2,1,0:T(8,128)(2,1)S(1)}, u32[]{:S(2)}, u32[]{:S(2)}) collective-permute-start(bf16[7,32,256]{2,1,0:T(8,128)(2,1)S(1)} %total.1.after_ref.refs_0_), channel_id=1, source_target_pairs={{0,16},{4,20},{8,24},{12,28},{16,0},{20,4},{24,8},{28,12},{1,17},{... | collective-permute-start | bytes 344072 | tf_op jit(solution)/shard_map/ppermute | solution.py:485
  50.0 5.8 %collective-permute-start.17 = (bf16[7,32,256]{2,1,0:T(8,128)(2,1)S(1)}, bf16[7,32,256]{2,1,0:T(8,128)(2,1)S(1)}, u32[]{:S(2)}, u32[]{:S(2)}) collective-permute-start(bf16[7,32,256]{2,1,0:T(8,128)(2,1)S(1)} %total.1.after_ref.refs_0_), channel_id=1, source_target_pairs={{0,24},{4,28},{8,16},{12,20},{16,8},{20,12},{24,0},{28,4},{1,25},{... | collective-permute-start | bytes 344072 | tf_op jit(solution)/shard_map/ppermute | solution.py:485
  55.9 12.0 %collective-permute-start.26 = (bf16[3,7,32,256]{3,2,1,0:T(8,128)(2,1)S(1)}, bf16[3,7,32,256]{3,2,1,0:T(8,128)(2,1)S(1)}, u32[]{:S(2)}, u32[]{:S(2)}) collective-permute-start(bf16[3,7,32,256]{3,2,1,0:T(8,128)(2,1)S(1)} %gate.1.after_ref.refs_1_), channel_id=1, source_target_pairs={{0,24},{4,28},{8,16},{12,20},{16,8},{20,12},{24,0},{28,4},{1,25},{... | collective-permute-start | bytes 1032200 | tf_op jit(solution)/shard_map/ppermute | solution.py:485
  57.4 15.8 %collective-permute-start.24 = (bf16[3,7,32,256]{3,2,1,0:T(8,128)(2,1)S(1)}, bf16[3,7,32,256]{3,2,1,0:T(8,128)(2,1)S(1)}, u32[]{:S(2)}, u32[]{:S(2)}) collective-permute-start(bf16[3,7,32,256]{3,2,1,0:T(8,128)(2,1)S(1)} %gate.1.after_ref.refs_1_), channel_id=1, source_target_pairs={{0,16},{4,20},{8,24},{12,28},{16,0},{20,4},{24,8},{28,12},{1,17},{... | collective-permute-start | bytes 1032200 | tf_op jit(solution)/shard_map/ppermute | solution.py:485
  59.1 14.3 %collective-permute-start.22 = (bf16[3,7,32,256]{3,2,1,0:T(8,128)(2,1)S(1)}, bf16[3,7,32,256]{3,2,1,0:T(8,128)(2,1)S(1)}, u32[]{:S(2)}, u32[]{:S(2)}) collective-permute-start(bf16[3,7,32,256]{3,2,1,0:T(8,128)(2,1)S(1)} %gate.1.after_ref.refs_1_), channel_id=1, source_target_pairs={{0,8},{4,12},{8,0},{12,4},{16,24},{20,28},{24,16},{28,20},{1,9},{5... | collective-permute-start | bytes 1032200 | tf_op jit(solution)/shard_map/ppermute | solution.py:485
  59.4 7.4 %collective-permute-start.12 = (f32[64,256]{1,0:T(8,128)S(1)}, f32[64,256]{1,0:T(8,128)S(1)}, u32[]{:S(2)}, u32[]{:S(2)}) collective-permute-start(f32[64,256]{1,0:T(8,128)S(1)} %get-tuple-element.42), channel_id=1, source_target_pairs={{0,1},{2,3},{1,0},{3,2},{4,5},{6,7},{5,4},{7,6},{8,9},{10,11},{9,8... | collective-permute-start | bytes 196616 | tf_op jit(solution)/shard_map/ppermute | solution.py:491
  64.7 10.1 %collective-permute-start.20 = (bf16[4,7,32,256]{3,2,1,0:T(8,128)(2,1)S(1)}, bf16[4,7,32,256]{3,2,1,0:T(8,128)(2,1)S(1)}, u32[]{:S(2)}, u32[]{:S(2)}) collective-permute-start(bf16[4,7,32,256]{3,2,1,0:T(8,128)(2,1)S(1)} %stack.4.refs_0_), channel_id=1, source_target_pairs={{0,4},{4,0},{8,12},{12,8},{16,20},{20,16},{24,28},{28,24},{1,5},{5... | collective-permute-start | bytes 1376264 | tf_op jit(solution)/shard_map/ppermute | solution.py:485
  66.9 0.7 collective-permute-start.13
  67.6 7.2 %collective-permute-start.21 = (bf16[3,7,32,256]{3,2,1,0:T(8,128)(2,1)S(1)}, bf16[3,7,32,256]{3,2,1,0:T(8,128)(2,1)S(1)}, u32[]{:S(2)}, u32[]{:S(2)}) collective-permute-start(bf16[3,7,32,256]{3,2,1,0:T(8,128)(2,1)S(1)} %stack.5.refs_2_), channel_id=1, source_target_pairs={{0,4},{4,0},{8,12},{12,8},{16,20},{20,16},{24,28},{28,24},{1,5},{5... | collective-permute-start | bytes 1032200 | tf_op jit(solution)/shard_map/ppermute | solution.py:485
  67.9 6.9 %collective-permute-start.27 = (bf16[3,7,32,256]{3,2,1,0:T(8,128)(2,1)S(1)}, bf16[3,7,32,256]{3,2,1,0:T(8,128)(2,1)S(1)}, u32[]{:S(2)}, u32[]{:S(2)}) collective-permute-start(bf16[3,7,32,256]{3,2,1,0:T(8,128)(2,1)S(1)} %collective-permute-done.26.refs_8_), channel_id=1, source_target_pairs={{0,4},{4,0},{8,12},{12,8},{16,20},{20,16},{24,28},{28,24},{1,5},{5... | collective-permute-start | bytes 1032200 | tf_op jit(solution)/shard_map/ppermute | solution.py:485
  73.3 1.7 %collective-permute-start.25 = (bf16[3,7,32,256]{3,2,1,0:T(8,128)(2,1)S(1)}, bf16[3,7,32,256]{3,2,1,0:T(8,128)(2,1)S(1)}, u32[]{:S(2)}, u32[]{:S(2)}) collective-permute-start(bf16[3,7,32,256]{3,2,1,0:T(8,128)(2,1)S(1)} %collective-permute-done.24.refs_6_), channel_id=1, source_target_pairs={{0,4},{4,0},{8,12},{12,8},{16,20},{20,16},{24,28},{28,24},{1,5},{5... | collective-permute-start | bytes 1032200 | tf_op jit(solution)/shard_map/ppermute | solution.py:485
  73.4 2.0 %collective-permute-start.23 = (bf16[3,7,32,256]{3,2,1,0:T(8,128)(2,1)S(1)}, bf16[3,7,32,256]{3,2,1,0:T(8,128)(2,1)S(1)}, u32[]{:S(2)}, u32[]{:S(2)}) collective-permute-start(bf16[3,7,32,256]{3,2,1,0:T(8,128)(2,1)S(1)} %collective-permute-done.22.refs_4_), channel_id=1, source_target_pairs={{0,4},{4,0},{8,12},{12,8},{16,20},{20,16},{24,28},{28,24},{1,5},{5... | collective-permute-start | bytes 1032200 | tf_op jit(solution)/shard_map/ppermute | solution.py:485

commit v7 on v6

--- a/solution.py
+++ b/solution.py
@@ -461,8 +461,8 @@
     return pl.pallas_call(
         functools.partial(assemble_kernel, marks, parts, groups),
         out_shape=jax.ShapeDtypeStruct((offsets, width, width), BF),
-        in_specs=[ANY] * (len(pieces) + len(after) + len(base)),
-        out_specs=ANY,
+        in_specs=[ANY] * (len(pieces) + len(after)) + [HBM] * len(base),
+        out_specs=HBM,
         scratch_shapes=[pltpu.SemaphoreType.DMA((len(pieces), most, 2))],
         input_output_aliases={len(pieces) + len(after): 0} if base else {},
         compiler_params=params(),
@@ -514,20 +514,24 @@
     out_features, token = forward(live, pack, halo_rows, weights, rows, rounded)
 
     along = [swap(rounded, "space", m) for m in range(1, parts)]
-    across = {m: swap(rounded, "dp", 2 * m) for m in reversed(range(1, groups))}
+    across = {m: swap(rounded, "dp", 2 * m) for m in range(1, groups)}
     lines = gate(stack(along, [token]), list(across.values()))
-    far = {m: swap(lines, "dp", 2 * m) for m in reversed(range(1, groups))}
+    far = {m: swap(lines, "dp", 2 * m) for m in range(1, groups)}
     line_masks = range(1, parts)
-    near = stack([rounded, lines], [])
+    grad_features, token = final(live, own_grad, first_back, second_back, send_up, send_down, lines)
+    near = stack([rounded, lines], [token])
     sides = stack([across[m] for m in range(1, groups)], [])
     near_marks = [(0, mask) for mask in range(parts)]
     side_marks = [(m, 0) for m in range(1, groups)]
     pieces = [near, swap(near, "dp", 1), sides, swap(sides, "dp", 1)]
     marks = [(0, near_marks), (1, near_marks), (0, side_marks), (1, side_marks)]
-    grad_features, token = final(live, own_grad, first_back, second_back, send_up, send_down, lines)
     dense = rounded.shape[1] % 16 == 0 and groups * count - offsets < count
     sizes = (parts, groups, offsets, width)
     first = ()
+    if dense:
+        first = (assemble(pieces, marks, *sizes, ()),)
+        pieces, marks = [], []
+        pass
     for m in range(1, groups):
         pieces += [far[m], swap(far[m], "dp", 1)]
         marks += [(o, [(m, mask) for mask in line_masks]) for o in range(2)]

time: 78.6 us -> 77.1 us (0.981)
  waiting for transfers between devices: 21.8 us -> 20 us
    ppermute x24, waiting for transfers between devices: 18.2 us -> 17 us  [swap(): lax.ppermute(value, axis, [(i, i ^ mask) for i in range(lax.axis_size(axi...]
    ppermute x24, starting transfers between devices: 26.2 us -> 27.3 us  [swap(): lax.ppermute(value, axis, [(i, i ^ mask) for i in range(lax.axis_size(axi...]
    pallas_call x1 -> x2, Pallas kernels: 2.48 us -> 2.98 us  [assemble(): pl.pallas_call(functools.partial(assemble_kernel, marks, parts, groups),...]
  transfers between devices with their start and end apart: 28 -> 28, of which waited for: 15 -> 12; matrix products, arithmetic and copies ran while one was open for 0% -> 0% of each run, Pallas kernels for 15% -> 17%
where the time goes in v7:
time: 77.1 us; the launch traced here: 76.9 us
  starting transfers between devices  35 us (45%)
  waiting for transfers between devices  20 us (26%)
  Pallas kernels  19.4 us (25%)
  between operations  1.49 us (2%)
  local copies, waits for them, and re-layouts  0.98 us (1%)
    ppermute x24, starting transfers between devices, swap(): lax.ppermute(value, axis, [(i, i ^ mask) for i in range(lax.axis_size(axi...  27.3 us
    ppermute x24, waiting for transfers between devices, swap(): lax.ppermute(value, axis, [(i, i ^ mask) for i in range(lax.axis_size(axi...  17 us
    ppermute x4, starting transfers between devices, met(): lax.ppermute(value, 'space', [(i, i + 1) for i in starts] + [(i + 1, i) f...  7.75 us
    pallas_call x1, Pallas kernels, backward(): pl.pallas_call(functools.partial(backward_kernel, group), out_shape=tuple...  5.46 us
    pallas_call x1, Pallas kernels, forward(): pl.pallas_call(functools.partial(forward_kernel, group), out_shape=(jax.S...  3.91 us
    ppermute x4, waiting for transfers between devices, met(): lax.ppermute(value, 'space', [(i, i + 1) for i in starts] + [(i + 1, i) f...  3.08 us
    pallas_call x2, Pallas kernels, assemble(): pl.pallas_call(functools.partial(assemble_kernel, marks, parts, groups),...  2.98 us
    pallas_call x1, Pallas kernels, wgrad(): pl.pallas_call(functools.partial(wgrad_kernel, sources, first), out_shape...  2.21 us
  transfers between devices with their start and end apart: 28, of which 12 were waited for; matrix products, arithmetic and copies ran while one was open for 0% of the time, Pallas kernels for 17%

profile of v7, /device:TPU:0, one launch (start us, length us, event | category | flops | bytes accessed | tf_op | source)
XLA Modules:
  0.0 76.9 jit_solution(16372846973315589566)
XLA Ops:
  1.3 1.9 %prep.1 = (bf16[544,256]{1,0:T(8,128)(2,1)}, bf16[64,256]{1,0:T(8,128)(2,1)}, bf16[64,256]{1,0:T(8,128)(2,1)}) custom-call(s32[1]{0:T(128)S(6)} %copy.14.live_ref, bf16[256,256]{1,0:T(8,128)(2,1)} %x_hbm.1, bf16[256,256]{1,0:T(8,128)(2,1)} %dy_hbm.1, s32[27,256]{1,0:T(8,128)} %map_hbm.1, s32[1,64]{1,0:T(1,128)} %up_ref.1, s32[1,64]{1,0:T(1,128)} %down_ref.1), custom_call_target="tpu_custom_call" | custom-call | tf_op jit(solution)/shard_map/prep/pallas_call | solution.py:81
  3.2 4.0 %collective-permute-start.4 = (bf16[544,256]{1,0:T(8,128)(2,1)}, bf16[544,256]{1,0:T(8,128)(2,1)S(1)}, u32[]{:S(2)}, u32[]{:S(2)}) collective-permute-start(bf16[544,256]{1,0:T(8,128)(2,1)} %get-tuple-element.27.pack_ref), channel_id=1, source_target_pairs={{0,24},{4,28},{8,16},{12,20},{16,8},{20,12},{24,0},{28,4},{1,25},{... | collective-permute-start | bytes 835592 | tf_op jit(solution)/shard_map/ppermute | solution.py:485
  7.1 0.5 collective-permute-start.3
  7.6 0.1 collective-permute-start.2
  7.8 2.0 %collective-permute-start = (bf16[64,256]{1,0:T(8,128)(2,1)}, bf16[64,256]{1,0:T(8,128)(2,1)S(1)}, u32[]{:S(2)}, u32[]{:S(2)}) collective-permute-start(bf16[64,256]{1,0:T(8,128)(2,1)} %get-tuple-element.25), channel_id=1, source_target_pairs={{0,1},{2,3},{1,0},{3,2},{4,5},{6,7},{5,4},{7,6},{8,9},{10,11},{9,8... | collective-permute-start | bytes 98312 | tf_op jit(solution)/shard_map/ppermute | solution.py:491
  9.7 0.7 collective-permute-start.1
  10.4 1.5 %collective-permute-done.first_ref = bf16[64,256]{1,0:T(8,128)(2,1)S(1)} collective-permute-done((bf16[64,256]{1,0:T(8,128)(2,1)}, bf16[64,256]{1,0:T(8,128)(2,1)S(1)}, u32[]{:S(2)}, u32[]{:S(2)}) %collective-permute-start) | collective-permute-done | bytes 32800 | tf_op jit(solution)/shard_map/ppermute | solution.py:491
  11.9 1.0 %copy-done.3 = bf16[544,256]{1,0:T(8,128)(2,1)S(1)} copy-done((bf16[544,256]{1,0:T(8,128)(2,1)S(1)}, bf16[544,256]{1,0:T(8,128)(2,1)}, u32[]{:S(2)}) %copy-start.3) | copy-done | bytes 278552
  12.9 2.9 %collective-permute-start.7 = (bf16[128,256]{1,0:T(8,128)(2,1)S(1)}, bf16[128,256]{1,0:T(8,128)(2,1)S(1)}, u32[]{:S(2)}, u32[]{:S(2)}) collective-permute-start(bf16[128,256]{1,0:T(8,128)(2,1)S(1)} %get-tuple-element.29.refs_0_.halo_ref), channel_id=1, source_target_pairs={{0,24},{4,28},{8,16},{12,20},{16,8},{20,12},{24,0},{28,4},{1,25},{... | collective-permute-start | bytes 196616 | tf_op jit(solution)/shard_map/ppermute | solution.py:485
  15.8 0.5 collective-permute-start.6
  16.3 0.6 collective-permute-start.5
  16.9 3.9 %collective-permute-done.3.refs_2_ = bf16[544,256]{1,0:T(8,128)(2,1)S(1)} collective-permute-done((bf16[544,256]{1,0:T(8,128)(2,1)}, bf16[544,256]{1,0:T(8,128)(2,1)S(1)}, u32[]{:S(2)}, u32[]{:S(2)}) %collective-permute-start.3) | collective-permute-done | bytes 278560 | tf_op jit(solution)/shard_map/ppermute | solution.py:485
  20.7 0.6 collective-permute-done.2.refs_1_
  21.4 1.3 %wgrad_own.1 = (bf16[7,256,1024]{2,1,0:T(8,128)(2,1)S(1)}, bf16[1024,256]{1,0:T(8,128)(2,1)S(1)}, s32[4,32,256]{2,1,0:T(8,128)S(1)}) custom-call(bf16[544,256]{1,0:T(8,128)(2,1)S(1)} %get-tuple-element.28.refs_0_.pack_ref, bf16[544,256]{1,0:T(8,128)(2,1)S(1)} %collective-permute-done.2.refs_1_, bf16[544,256]{1,0:T(8,128)(2,1)S(1)} %collective-permute-done.3.refs_2_, ...), custom_call_target="tpu_custom_call" | custom-call | flops 100000000 | bytes 100000 | tf_op jit(solution)/shard_map/wgrad_own/pallas_call | solution.py:223
  22.8 0.3 collective-permute-done.5.refs_1_
  23.0 2.2 %wgrad.1 = (f32[7,128,256]{2,1,0:T(8,128)S(1)}, f32[7,128,256]{2,1,0:T(8,128)S(1)}) custom-call(bf16[7,256,1024]{2,1,0:T(8,128)(2,1)S(1)} %get-tuple-element.30.picked_ref, bf16[1024,256]{1,0:T(8,128)(2,1)S(1)} %get-tuple-element.31.dys.refs_4_, s32[4,32,256]{2,1,0:T(8,128)S(1)} %get-tuple-element.32.maps, ...), custom_call_target="tpu_custom_call" | custom-call | flops 100000000 | bytes 100000 | tf_op jit(solution)/shard_map/wgrad/pallas_call | solution.py:261
  25.3 0.1 collective-permute-start.8
  25.3 2.5 %collective-permute-done.8.got_ref = f32[7,128,256]{2,1,0:T(8,128)S(1)} collective-permute-done((f32[7,128,256]{2,1,0:T(8,128)S(1)}, f32[7,128,256]{2,1,0:T(8,128)S(1)}, u32[]{:S(2)}, u32[]{:S(2)}) %collective-permute-start.8) | collective-permute-done | bytes 917536 | tf_op jit(solution)/shard_map/ppermute | solution.py:485
  27.8 0.5 blocks.1
  28.3 2.2 %collective-permute-start.9 = (s16[240,256]{1,0:T(8,128)(2,1)S(1)}, s16[240,256]{1,0:T(8,128)(2,1)S(1)}, u32[]{:S(2)}, u32[]{:S(2)}) collective-permute-start(s16[240,256]{1,0:T(8,128)(2,1)S(1)} %get-tuple-element.36), channel_id=1, source_target_pairs={{0,1},{1,0},{2,3},{3,2},{4,5},{5,4},{6,7},{7,6},{8,9},{9,8},{10,11... | collective-permute-start | bytes 368648 | tf_op jit(solution)/shard_map/ppermute | solution.py:485
  30.5 2.1 %collective-permute-start.10 = (s16[240,256]{1,0:T(8,128)(2,1)S(1)}, s16[240,256]{1,0:T(8,128)(2,1)S(1)}, u32[]{:S(2)}, u32[]{:S(2)}) collective-permute-start(s16[240,256]{1,0:T(8,128)(2,1)S(1)} %get-tuple-element.37), channel_id=1, source_target_pairs={{0,2},{1,3},{2,0},{3,1},{4,6},{5,7},{6,4},{7,5},{8,10},{9,11},{10,... | collective-permute-start | bytes 368648 | tf_op jit(solution)/shard_map/ppermute | solution.py:485
  32.5 0.8 %collective-permute-start.11 = (s16[240,256]{1,0:T(8,128)(2,1)S(1)}, s16[240,256]{1,0:T(8,128)(2,1)S(1)}, u32[]{:S(2)}, u32[]{:S(2)}) collective-permute-start(s16[240,256]{1,0:T(8,128)(2,1)S(1)} %get-tuple-element.38), channel_id=1, source_target_pairs={{0,3},{1,2},{2,1},{3,0},{4,7},{5,6},{6,5},{7,4},{8,11},{9,10},{10,... | collective-permute-start | bytes 368648 | tf_op jit(solution)/shard_map/ppermute | solution.py:485
  33.4 5.5 %backward.1 = (f32[256,256]{1,0:T(8,128)S(1)}, f32[64,256]{1,0:T(8,128)S(1)}, f32[64,256]{1,0:T(8,128)S(1)}, f32[8,128]{1,0:T(8,128)S(1)}) custom-call(bf16[544,256]{1,0:T(8,128)(2,1)S(1)} %get-tuple-element.28.refs_0_.pack_ref, bf16[27,256,256]{2,1,0:T(8,128)(2,1)S(1)} %copy-done, f32[7,32,256]{2,1,0:T(8,128)S(1)} %get-tuple-element.35.after_ref.mine_ref), custom_call_target="tpu_custom_call" | custom-call | flops 100000000 | bytes 100000 | tf_op jit(solution)/shard_map/backward/pallas_call | solution.py:138
  38.9 3.9 %collective-permute-done.10.refs_1_ = s16[240,256]{1,0:T(8,128)(2,1)S(1)} collective-permute-done((s16[240,256]{1,0:T(8,128)(2,1)S(1)}, s16[240,256]{1,0:T(8,128)(2,1)S(1)}, u32[]{:S(2)}, u32[]{:S(2)}) %collective-permute-start.10) | collective-permute-done | bytes 122912 | tf_op jit(solution)/shard_map/ppermute | solution.py:485
  42.8 0.1 total.1.after_ref.refs_0_
  42.9 2.5 %collective-permute-start.16 = (bf16[7,32,256]{2,1,0:T(8,128)(2,1)S(1)}, bf16[7,32,256]{2,1,0:T(8,128)(2,1)S(1)}, u32[]{:S(2)}, u32[]{:S(2)}) collective-permute-start(bf16[7,32,256]{2,1,0:T(8,128)(2,1)S(1)} %total.1.after_ref.refs_0_), channel_id=1, source_target_pairs={{0,3},{1,2},{2,1},{3,0},{4,7},{5,6},{6,5},{7,4},{8,11},{9,10},{10,... | collective-permute-start | bytes 344072 | tf_op jit(solution)/shard_map/ppermute | solution.py:485
  45.5 1.2 %collective-permute-start.15 = (bf16[7,32,256]{2,1,0:T(8,128)(2,1)S(1)}, bf16[7,32,256]{2,1,0:T(8,128)(2,1)S(1)}, u32[]{:S(2)}, u32[]{:S(2)}) collective-permute-start(bf16[7,32,256]{2,1,0:T(8,128)(2,1)S(1)} %total.1.after_ref.refs_0_), channel_id=1, source_target_pairs={{0,2},{1,3},{2,0},{3,1},{4,6},{5,7},{6,4},{7,5},{8,10},{9,11},{10,... | collective-permute-start | bytes 344072 | tf_op jit(solution)/shard_map/ppermute | solution.py:485
  46.7 0.7 collective-permute-start.14
  47.4 1.5 %collective-permute-start.19 = (bf16[7,32,256]{2,1,0:T(8,128)(2,1)S(1)}, bf16[7,32,256]{2,1,0:T(8,128)(2,1)S(1)}, u32[]{:S(2)}, u32[]{:S(2)}) collective-permute-start(bf16[7,32,256]{2,1,0:T(8,128)(2,1)S(1)} %total.1.after_ref.refs_0_), channel_id=1, source_target_pairs={{0,24},{4,28},{8,16},{12,20},{16,8},{20,12},{24,0},{28,4},{1,25},{... | collective-permute-start | bytes 344072 | tf_op jit(solution)/shard_map/ppermute | solution.py:485
  48.9 1.0 %collective-permute-start.18 = (bf16[7,32,256]{2,1,0:T(8,128)(2,1)S(1)}, bf16[7,32,256]{2,1,0:T(8,128)(2,1)S(1)}, u32[]{:S(2)}, u32[]{:S(2)}) collective-permute-start(bf16[7,32,256]{2,1,0:T(8,128)(2,1)S(1)} %total.1.after_ref.refs_0_), channel_id=1, source_target_pairs={{0,16},{4,20},{8,24},{12,28},{16,0},{20,4},{24,8},{28,12},{1,17},{... | collective-permute-start | bytes 344072 | tf_op jit(solution)/shard_map/ppermute | solution.py:485
  49.9 0.1 collective-permute-done.16.refs_2_
  50.0 1.9 %collective-permute-start.17 = (bf16[7,32,256]{2,1,0:T(8,128)(2,1)S(1)}, bf16[7,32,256]{2,1,0:T(8,128)(2,1)S(1)}, u32[]{:S(2)}, u32[]{:S(2)}) collective-permute-start(bf16[7,32,256]{2,1,0:T(8,128)(2,1)S(1)} %total.1.after_ref.refs_0_), channel_id=1, source_target_pairs={{0,8},{4,12},{8,0},{12,4},{16,24},{20,28},{24,16},{28,20},{1,9},{5... | collective-permute-start | bytes 344072 | tf_op jit(solution)/shard_map/ppermute | solution.py:485
  51.9 3.9 %forward.1 = (bf16[256,256]{1,0:T(8,128)(2,1)}, f32[8,128]{1,0:T(8,128)S(1)}) custom-call(s32[1]{0:T(128)S(6)} %copy.14.live_ref, bf16[544,256]{1,0:T(8,128)(2,1)S(1)} %get-tuple-element.28.refs_0_.pack_ref, bf16[128,256]{1,0:T(8,128)(2,1)S(1)} %get-tuple-element.29.refs_0_.halo_ref, bf16[27,256,256]{2,1,0:T(8,128)(2,1)S(1)} %copy-done, ...), custom_call_target="tpu_custom_call" | custom-call | flops 100000000 | bytes 100000 | tf_op jit(solution)/shard_map/forward/pallas_call | solution.py:183
  55.9 1.5 %collective-permute-start.24 = (bf16[3,7,32,256]{3,2,1,0:T(8,128)(2,1)S(1)}, bf16[3,7,32,256]{3,2,1,0:T(8,128)(2,1)S(1)}, u32[]{:S(2)}, u32[]{:S(2)}) collective-permute-start(bf16[3,7,32,256]{3,2,1,0:T(8,128)(2,1)S(1)} %gate.1.after_ref.refs_1_), channel_id=1, source_target_pairs={{0,24},{4,28},{8,16},{12,20},{16,8},{20,12},{24,0},{28,4},{1,25},{... | collective-permute-start | bytes 1032200 | tf_op jit(solution)/shard_map/ppermute | solution.py:485
  57.4 0.8 collective-permute-start.22
  58.2 1.3 %collective-permute-start.20 = (bf16[3,7,32,256]{3,2,1,0:T(8,128)(2,1)S(1)}, bf16[3,7,32,256]{3,2,1,0:T(8,128)(2,1)S(1)}, u32[]{:S(2)}, u32[]{:S(2)}) collective-permute-start(bf16[3,7,32,256]{3,2,1,0:T(8,128)(2,1)S(1)} %gate.1.after_ref.refs_1_), channel_id=1, source_target_pairs={{0,8},{4,12},{8,0},{12,4},{16,24},{20,28},{24,16},{28,20},{1,9},{5... | collective-permute-start | bytes 1032200 | tf_op jit(solution)/shard_map/ppermute | solution.py:485
  59.5 4.5 %collective-permute-start.12 = (f32[64,256]{1,0:T(8,128)S(1)}, f32[64,256]{1,0:T(8,128)S(1)}, u32[]{:S(2)}, u32[]{:S(2)}) collective-permute-start(f32[64,256]{1,0:T(8,128)S(1)} %get-tuple-element.42), channel_id=1, source_target_pairs={{0,1},{2,3},{1,0},{3,2},{4,5},{6,7},{5,4},{7,6},{8,9},{10,11},{9,8... | collective-permute-start | bytes 196616 | tf_op jit(solution)/shard_map/ppermute | solution.py:491
  63.9 0.7 collective-permute-start.13
  64.6 1.6 %collective-permute-done.12.first_ref = f32[64,256]{1,0:T(8,128)S(1)} collective-permute-done((f32[64,256]{1,0:T(8,128)S(1)}, f32[64,256]{1,0:T(8,128)S(1)}, u32[]{:S(2)}, u32[]{:S(2)}) %collective-permute-start.12) | collective-permute-done | bytes 65568 | tf_op jit(solution)/shard_map/ppermute | solution.py:491
  66.2 1.0 %final.1 = (bf16[256,256]{1,0:T(8,128)(2,1)}, f32[8,128]{1,0:T(8,128)S(1)}) custom-call(s32[1]{0:T(128)S(6)} %copy.14.live_ref, f32[256,256]{1,0:T(8,128)S(1)} %get-tuple-element.41.own_ref, f32[64,256]{1,0:T(8,128)S(1)} %collective-permute-done.12.first_ref, f32[64,256]{1,0:T(8,128)S(1)} %collective-permute-done.13.second_ref, s32[1,64]{1,0:T(1,128)S(1)} %copy-done.1, ...), custom_call_target="tpu_custom_call" | custom-call | tf_op jit(solution)/shard_map/final/pallas_call | solution.py:386
  67.2 0.1 collective-permute-start.26
  67.3 0.6 collective-permute-start.27
  68.0 5.3 %collective-permute-done.22.refs_2_ = bf16[3,7,32,256]{3,2,1,0:T(8,128)(2,1)S(1)} collective-permute-done((bf16[3,7,32,256]{3,2,1,0:T(8,128)(2,1)S(1)}, bf16[3,7,32,256]{3,2,1,0:T(8,128)(2,1)S(1)}, u32[]{:S(2)}, u32[]{:S(2)}) %collective-permute-start.22) | collective-permute-done | bytes 344096 | tf_op jit(solution)/shard_map/ppermute | solution.py:485
  73.2 0.1 collective-permute-done.20.refs_0_
  73.3 0.4 collective-permute-start.21
  73.8 1.4 %assemble.2.refs_7_ = bf16[27,256,256]{2,1,0:T(8,128)(2,1)} custom-call(bf16[4,7,32,256]{3,2,1,0:T(8,128)(2,1)S(1)} %stack.4.refs_0_, bf16[4,7,32,256]{3,2,1,0:T(8,128)(2,1)S(1)} %collective-permute-done.26.refs_1_, bf16[3,7,32,256]{3,2,1,0:T(8,128)(2,1)S(1)} %stack.5.refs_2_, bf16[3,7,32,256]{3,2,1,0:T(8,128)(2,1)S(1)} %collective-permute-done.27.refs_3_), custom_call_target="tpu_custom_call" | custom-call | flops 100000000 | bytes 100000 | tf_op jit(solution)/shard_map/assemble/pallas_call | solution.py:461
  75.2 0.2 collective-permute-done.21.refs_1_
  75.4 1.6 %assemble.3 = bf16[27,256,256]{2,1,0:T(8,128)(2,1)} custom-call(bf16[3,7,32,256]{3,2,1,0:T(8,128)(2,1)S(1)} %collective-permute-done.20.refs_0_, bf16[3,7,32,256]{3,2,1,0:T(8,128)(2,1)S(1)} %collective-permute-done.21.refs_1_, bf16[3,7,32,256]{3,2,1,0:T(8,128)(2,1)S(1)} %collective-permute-done.22.refs_2_, ...), custom_call_target="tpu_custom_call", output_to_operand_aliasing={{}: (7, {})} | custom-call | flops 100000000 | bytes 100000 | tf_op jit(solution)/shard_map/assemble/pallas_call | solution.py:461
  (31 shorter events, 0.3 us)
Async XLA Ops:
  3.2 13.1 %collective-permute-start.4 = (bf16[544,256]{1,0:T(8,128)(2,1)}, bf16[544,256]{1,0:T(8,128)(2,1)S(1)}, u32[]{:S(2)}, u32[]{:S(2)}) collective-permute-start(bf16[544,256]{1,0:T(8,128)(2,1)} %get-tuple-element.27.pack_ref), channel_id=1, source_target_pairs={{0,24},{4,28},{8,16},{12,20},{16,8},{20,12},{24,0},{28,4},{1,25},{... | collective-permute-start | bytes 835592 | tf_op jit(solution)/shard_map/ppermute | solution.py:485
  7.1 13.6 %collective-permute-start.3 = (bf16[544,256]{1,0:T(8,128)(2,1)}, bf16[544,256]{1,0:T(8,128)(2,1)S(1)}, u32[]{:S(2)}, u32[]{:S(2)}) collective-permute-start(bf16[544,256]{1,0:T(8,128)(2,1)} %get-tuple-element.27.pack_ref), channel_id=1, source_target_pairs={{0,16},{4,20},{8,24},{12,28},{16,0},{20,4},{24,8},{28,12},{1,17},{... | collective-permute-start | bytes 835592 | tf_op jit(solution)/shard_map/ppermute | solution.py:485
  7.6 13.8 %collective-permute-start.2 = (bf16[544,256]{1,0:T(8,128)(2,1)}, bf16[544,256]{1,0:T(8,128)(2,1)S(1)}, u32[]{:S(2)}, u32[]{:S(2)}) collective-permute-start(bf16[544,256]{1,0:T(8,128)(2,1)} %get-tuple-element.27.pack_ref), channel_id=1, source_target_pairs={{0,8},{4,12},{8,0},{12,4},{16,24},{20,28},{24,16},{28,20},{1,9},{5... | collective-permute-start | bytes 835592 | tf_op jit(solution)/shard_map/ppermute | solution.py:485
  7.8 4.1 %collective-permute-start = (bf16[64,256]{1,0:T(8,128)(2,1)}, bf16[64,256]{1,0:T(8,128)(2,1)S(1)}, u32[]{:S(2)}, u32[]{:S(2)}) collective-permute-start(bf16[64,256]{1,0:T(8,128)(2,1)} %get-tuple-element.25), channel_id=1, source_target_pairs={{0,1},{2,3},{1,0},{3,2},{4,5},{6,7},{5,4},{7,6},{8,9},{10,11},{9,8... | collective-permute-start | bytes 98312 | tf_op jit(solution)/shard_map/ppermute | solution.py:491
  9.7 2.2 %collective-permute-start.1 = (bf16[64,256]{1,0:T(8,128)(2,1)}, bf16[64,256]{1,0:T(8,128)(2,1)S(1)}, u32[]{:S(2)}, u32[]{:S(2)}) collective-permute-start(bf16[64,256]{1,0:T(8,128)(2,1)} %get-tuple-element.26), channel_id=1, source_target_pairs={{1,2},{2,1},{5,6},{6,5},{9,10},{10,9},{13,14},{14,13},{17,18},{18,... | collective-permute-start | bytes 98312 | tf_op jit(solution)/shard_map/ppermute | solution.py:491
  11.9 1.0 %copy-start.3 = (bf16[544,256]{1,0:T(8,128)(2,1)S(1)}, bf16[544,256]{1,0:T(8,128)(2,1)}, u32[]{:S(2)}) copy-start(bf16[544,256]{1,0:T(8,128)(2,1)} %get-tuple-element.27.pack_ref) | copy-start | bytes 835588
  12.9 9.8 %collective-permute-start.7 = (bf16[128,256]{1,0:T(8,128)(2,1)S(1)}, bf16[128,256]{1,0:T(8,128)(2,1)S(1)}, u32[]{:S(2)}, u32[]{:S(2)}) collective-permute-start(bf16[128,256]{1,0:T(8,128)(2,1)S(1)} %get-tuple-element.29.refs_0_.halo_ref), channel_id=1, source_target_pairs={{0,24},{4,28},{8,16},{12,20},{16,8},{20,12},{24,0},{28,4},{1,25},{... | collective-permute-start | bytes 196616 | tf_op jit(solution)/shard_map/ppermute | solution.py:485
  15.8 7.0 %collective-permute-start.6 = (bf16[128,256]{1,0:T(8,128)(2,1)S(1)}, bf16[128,256]{1,0:T(8,128)(2,1)S(1)}, u32[]{:S(2)}, u32[]{:S(2)}) collective-permute-start(bf16[128,256]{1,0:T(8,128)(2,1)S(1)} %get-tuple-element.29.refs_0_.halo_ref), channel_id=1, source_target_pairs={{0,16},{4,20},{8,24},{12,28},{16,0},{20,4},{24,8},{28,12},{1,17},{... | collective-permute-start | bytes 196616 | tf_op jit(solution)/shard_map/ppermute | solution.py:485
  16.3 6.8 %collective-permute-start.5 = (bf16[128,256]{1,0:T(8,128)(2,1)S(1)}, bf16[128,256]{1,0:T(8,128)(2,1)S(1)}, u32[]{:S(2)}, u32[]{:S(2)}) collective-permute-start(bf16[128,256]{1,0:T(8,128)(2,1)S(1)} %get-tuple-element.29.refs_0_.halo_ref), channel_id=1, source_target_pairs={{0,8},{4,12},{8,0},{12,4},{16,24},{20,28},{24,16},{28,20},{1,9},{5... | collective-permute-start | bytes 196616 | tf_op jit(solution)/shard_map/ppermute | solution.py:485
  22.7 10.7 %copy-start = (bf16[27,256,256]{2,1,0:T(8,128)(2,1)S(1)}, bf16[27,256,256]{2,1,0:T(8,128)(2,1)}, u32[]{:S(2)}) copy-start(bf16[27,256,256]{2,1,0:T(8,128)(2,1)} %w_ref.3) | copy-start | bytes 10616836
  25.3 2.5 %collective-permute-start.8 = (f32[7,128,256]{2,1,0:T(8,128)S(1)}, f32[7,128,256]{2,1,0:T(8,128)S(1)}, u32[]{:S(2)}, u32[]{:S(2)}) collective-permute-start(f32[7,128,256]{2,1,0:T(8,128)S(1)} %get-tuple-element.34), channel_id=1, source_target_pairs={{0,4},{4,0},{8,12},{12,8},{16,20},{20,16},{24,28},{28,24},{1,5},{5... | collective-permute-start | bytes 2752520 | tf_op jit(solution)/shard_map/ppermute | solution.py:485
  28.3 10.6 %collective-permute-start.9 = (s16[240,256]{1,0:T(8,128)(2,1)S(1)}, s16[240,256]{1,0:T(8,128)(2,1)S(1)}, u32[]{:S(2)}, u32[]{:S(2)}) collective-permute-start(s16[240,256]{1,0:T(8,128)(2,1)S(1)} %get-tuple-element.36), channel_id=1, source_target_pairs={{0,1},{1,0},{2,3},{3,2},{4,5},{5,4},{6,7},{7,6},{8,9},{9,8},{10,11... | collective-permute-start | bytes 368648 | tf_op jit(solution)/shard_map/ppermute | solution.py:485
  30.5 12.3 %collective-permute-start.10 = (s16[240,256]{1,0:T(8,128)(2,1)S(1)}, s16[240,256]{1,0:T(8,128)(2,1)S(1)}, u32[]{:S(2)}, u32[]{:S(2)}) collective-permute-start(s16[240,256]{1,0:T(8,128)(2,1)S(1)} %get-tuple-element.37), channel_id=1, source_target_pairs={{0,2},{1,3},{2,0},{3,1},{4,6},{5,7},{6,4},{7,5},{8,10},{9,11},{10,... | collective-permute-start | bytes 368648 | tf_op jit(solution)/shard_map/ppermute | solution.py:485
  32.5 10.2 %collective-permute-start.11 = (s16[240,256]{1,0:T(8,128)(2,1)S(1)}, s16[240,256]{1,0:T(8,128)(2,1)S(1)}, u32[]{:S(2)}, u32[]{:S(2)}) collective-permute-start(s16[240,256]{1,0:T(8,128)(2,1)S(1)} %get-tuple-element.38), channel_id=1, source_target_pairs={{0,3},{1,2},{2,1},{3,0},{4,7},{5,6},{6,5},{7,4},{8,11},{9,10},{10,... | collective-permute-start | bytes 368648 | tf_op jit(solution)/shard_map/ppermute | solution.py:485
  38.9 27.3 %copy-start.1 = (s32[1,64]{1,0:T(1,128)S(1)}, s32[1,64]{1,0:T(1,128)}, u32[]{:S(2)}) copy-start(s32[1,64]{1,0:T(1,128)} %up_ref.1) | copy-start | bytes 772
  38.9 27.3 %copy-start.2 = (s32[1,64]{1,0:T(1,128)S(1)}, s32[1,64]{1,0:T(1,128)}, u32[]{:S(2)}) copy-start(s32[1,64]{1,0:T(1,128)} %down_ref.1) | copy-start | bytes 772
  42.9 7.1 %collective-permute-start.16 = (bf16[7,32,256]{2,1,0:T(8,128)(2,1)S(1)}, bf16[7,32,256]{2,1,0:T(8,128)(2,1)S(1)}, u32[]{:S(2)}, u32[]{:S(2)}) collective-permute-start(bf16[7,32,256]{2,1,0:T(8,128)(2,1)S(1)} %total.1.after_ref.refs_0_), channel_id=1, source_target_pairs={{0,3},{1,2},{2,1},{3,0},{4,7},{5,6},{6,5},{7,4},{8,11},{9,10},{10,... | collective-permute-start | bytes 344072 | tf_op jit(solution)/shard_map/ppermute | solution.py:485
  45.5 10.4 %collective-permute-start.15 = (bf16[7,32,256]{2,1,0:T(8,128)(2,1)S(1)}, bf16[7,32,256]{2,1,0:T(8,128)(2,1)S(1)}, u32[]{:S(2)}, u32[]{:S(2)}) collective-permute-start(bf16[7,32,256]{2,1,0:T(8,128)(2,1)S(1)} %total.1.after_ref.refs_0_), channel_id=1, source_target_pairs={{0,2},{1,3},{2,0},{3,1},{4,6},{5,7},{6,4},{7,5},{8,10},{9,11},{10,... | collective-permute-start | bytes 344072 | tf_op jit(solution)/shard_map/ppermute | solution.py:485
  46.7 9.2 %collective-permute-start.14 = (bf16[7,32,256]{2,1,0:T(8,128)(2,1)S(1)}, bf16[7,32,256]{2,1,0:T(8,128)(2,1)S(1)}, u32[]{:S(2)}, u32[]{:S(2)}) collective-permute-start(bf16[7,32,256]{2,1,0:T(8,128)(2,1)S(1)} %total.1.after_ref.refs_0_), channel_id=1, source_target_pairs={{0,1},{1,0},{2,3},{3,2},{4,5},{5,4},{6,7},{7,6},{8,9},{9,8},{10,11... | collective-permute-start | bytes 344072 | tf_op jit(solution)/shard_map/ppermute | solution.py:485
  47.4 8.5 %collective-permute-start.19 = (bf16[7,32,256]{2,1,0:T(8,128)(2,1)S(1)}, bf16[7,32,256]{2,1,0:T(8,128)(2,1)S(1)}, u32[]{:S(2)}, u32[]{:S(2)}) collective-permute-start(bf16[7,32,256]{2,1,0:T(8,128)(2,1)S(1)} %total.1.after_ref.refs_0_), channel_id=1, source_target_pairs={{0,24},{4,28},{8,16},{12,20},{16,8},{20,12},{24,0},{28,4},{1,25},{... | collective-permute-start | bytes 344072 | tf_op jit(solution)/shard_map/ppermute | solution.py:485
  48.9 7.0 %collective-permute-start.18 = (bf16[7,32,256]{2,1,0:T(8,128)(2,1)S(1)}, bf16[7,32,256]{2,1,0:T(8,128)(2,1)S(1)}, u32[]{:S(2)}, u32[]{:S(2)}) collective-permute-start(bf16[7,32,256]{2,1,0:T(8,128)(2,1)S(1)} %total.1.after_ref.refs_0_), channel_id=1, source_target_pairs={{0,16},{4,20},{8,24},{12,28},{16,0},{20,4},{24,8},{28,12},{1,17},{... | collective-permute-start | bytes 344072 | tf_op jit(solution)/shard_map/ppermute | solution.py:485
  50.0 5.9 %collective-permute-start.17 = (bf16[7,32,256]{2,1,0:T(8,128)(2,1)S(1)}, bf16[7,32,256]{2,1,0:T(8,128)(2,1)S(1)}, u32[]{:S(2)}, u32[]{:S(2)}) collective-permute-start(bf16[7,32,256]{2,1,0:T(8,128)(2,1)S(1)} %total.1.after_ref.refs_0_), channel_id=1, source_target_pairs={{0,8},{4,12},{8,0},{12,4},{16,24},{20,28},{24,16},{28,20},{1,9},{5... | collective-permute-start | bytes 344072 | tf_op jit(solution)/shard_map/ppermute | solution.py:485
  55.9 12.0 %collective-permute-start.24 = (bf16[3,7,32,256]{3,2,1,0:T(8,128)(2,1)S(1)}, bf16[3,7,32,256]{3,2,1,0:T(8,128)(2,1)S(1)}, u32[]{:S(2)}, u32[]{:S(2)}) collective-permute-start(bf16[3,7,32,256]{3,2,1,0:T(8,128)(2,1)S(1)} %gate.1.after_ref.refs_1_), channel_id=1, source_target_pairs={{0,24},{4,28},{8,16},{12,20},{16,8},{20,12},{24,0},{28,4},{1,25},{... | collective-permute-start | bytes 1032200 | tf_op jit(solution)/shard_map/ppermute | solution.py:485
  57.4 15.8 %collective-permute-start.22 = (bf16[3,7,32,256]{3,2,1,0:T(8,128)(2,1)S(1)}, bf16[3,7,32,256]{3,2,1,0:T(8,128)(2,1)S(1)}, u32[]{:S(2)}, u32[]{:S(2)}) collective-permute-start(bf16[3,7,32,256]{3,2,1,0:T(8,128)(2,1)S(1)} %gate.1.after_ref.refs_1_), channel_id=1, source_target_pairs={{0,16},{4,20},{8,24},{12,28},{16,0},{20,4},{24,8},{28,12},{1,17},{... | collective-permute-start | bytes 1032200 | tf_op jit(solution)/shard_map/ppermute | solution.py:485
  58.2 15.2 %collective-permute-start.20 = (bf16[3,7,32,256]{3,2,1,0:T(8,128)(2,1)S(1)}, bf16[3,7,32,256]{3,2,1,0:T(8,128)(2,1)S(1)}, u32[]{:S(2)}, u32[]{:S(2)}) collective-permute-start(bf16[3,7,32,256]{3,2,1,0:T(8,128)(2,1)S(1)} %gate.1.after_ref.refs_1_), channel_id=1, source_target_pairs={{0,8},{4,12},{8,0},{12,4},{16,24},{20,28},{24,16},{28,20},{1,9},{5... | collective-permute-start | bytes 1032200 | tf_op jit(solution)/shard_map/ppermute | solution.py:485
  59.5 6.7 %collective-permute-start.12 = (f32[64,256]{1,0:T(8,128)S(1)}, f32[64,256]{1,0:T(8,128)S(1)}, u32[]{:S(2)}, u32[]{:S(2)}) collective-permute-start(f32[64,256]{1,0:T(8,128)S(1)} %get-tuple-element.42), channel_id=1, source_target_pairs={{0,1},{2,3},{1,0},{3,2},{4,5},{6,7},{5,4},{7,6},{8,9},{10,11},{9,8... | collective-permute-start | bytes 196616 | tf_op jit(solution)/shard_map/ppermute | solution.py:491
  63.9 2.2 %collective-permute-start.13 = (f32[64,256]{1,0:T(8,128)S(1)}, f32[64,256]{1,0:T(8,128)S(1)}, u32[]{:S(2)}, u32[]{:S(2)}) collective-permute-start(f32[64,256]{1,0:T(8,128)S(1)} %get-tuple-element.43), channel_id=1, source_target_pairs={{1,2},{2,1},{5,6},{6,5},{9,10},{10,9},{13,14},{14,13},{17,18},{18,... | collective-permute-start | bytes 196616 | tf_op jit(solution)/shard_map/ppermute | solution.py:491
  67.2 6.6 %collective-permute-start.26 = (bf16[4,7,32,256]{3,2,1,0:T(8,128)(2,1)S(1)}, bf16[4,7,32,256]{3,2,1,0:T(8,128)(2,1)S(1)}, u32[]{:S(2)}, u32[]{:S(2)}) collective-permute-start(bf16[4,7,32,256]{3,2,1,0:T(8,128)(2,1)S(1)} %stack.4.refs_0_), channel_id=1, source_target_pairs={{0,4},{4,0},{8,12},{12,8},{16,20},{20,16},{24,28},{28,24},{1,5},{5... | collective-permute-start | bytes 1376264 | tf_op jit(solution)/shard_map/ppermute | solution.py:485
  67.3 6.4 %collective-permute-start.27 = (bf16[3,7,32,256]{3,2,1,0:T(8,128)(2,1)S(1)}, bf16[3,7,32,256]{3,2,1,0:T(8,128)(2,1)S(1)}, u32[]{:S(2)}, u32[]{:S(2)}) collective-permute-start(bf16[3,7,32,256]{3,2,1,0:T(8,128)(2,1)S(1)} %stack.5.refs_2_), channel_id=1, source_target_pairs={{0,4},{4,0},{8,12},{12,8},{16,20},{20,16},{24,28},{28,24},{1,5},{5... | collective-permute-start | bytes 1032200 | tf_op jit(solution)/shard_map/ppermute | solution.py:485
  67.9 7.3 %collective-permute-start.25 = (bf16[3,7,32,256]{3,2,1,0:T(8,128)(2,1)S(1)}, bf16[3,7,32,256]{3,2,1,0:T(8,128)(2,1)S(1)}, u32[]{:S(2)}, u32[]{:S(2)}) collective-permute-start(bf16[3,7,32,256]{3,2,1,0:T(8,128)(2,1)S(1)} %collective-permute-done.24.refs_4_), channel_id=1, source_target_pairs={{0,4},{4,0},{8,12},{12,8},{16,20},{20,16},{24,28},{28,24},{1,5},{5... | collective-permute-start | bytes 1032200 | tf_op jit(solution)/shard_map/ppermute | solution.py:485
  73.2 1.9 %collective-permute-start.23 = (bf16[3,7,32,256]{3,2,1,0:T(8,128)(2,1)S(1)}, bf16[3,7,32,256]{3,2,1,0:T(8,128)(2,1)S(1)}, u32[]{:S(2)}, u32[]{:S(2)}) collective-permute-start(bf16[3,7,32,256]{3,2,1,0:T(8,128)(2,1)S(1)} %collective-permute-done.22.refs_2_), channel_id=1, source_target_pairs={{0,4},{4,0},{8,12},{12,8},{16,20},{20,16},{24,28},{28,24},{1,5},{5... | collective-permute-start | bytes 1032200 | tf_op jit(solution)/shard_map/ppermute | solution.py:485
  73.3 2.0 %collective-permute-start.21 = (bf16[3,7,32,256]{3,2,1,0:T(8,128)(2,1)S(1)}, bf16[3,7,32,256]{3,2,1,0:T(8,128)(2,1)S(1)}, u32[]{:S(2)}, u32[]{:S(2)}) collective-permute-start(bf16[3,7,32,256]{3,2,1,0:T(8,128)(2,1)S(1)} %collective-permute-done.20.refs_0_), channel_id=1, source_target_pairs={{0,4},{4,0},{8,12},{12,8},{16,20},{20,16},{24,28},{28,24},{1,5},{5... | collective-permute-start | bytes 1032200 | tf_op jit(solution)/shard_map/ppermute | solution.py:485

commit v8 on v7

--- a/solution.py
+++ b/solution.py
@@ -13,7 +13,6 @@
 VMEM_LIMIT = 32 * 1024 * 1024
 PREP_LIMIT = 60 * 1024 * 1024
 VMEM = pl.BlockSpec(memory_space=pltpu.VMEM)
-SMEM = pl.BlockSpec(memory_space=pltpu.SMEM)
 ANY = pl.BlockSpec(memory_space=pl.ANY)
 HBM = pl.BlockSpec(memory_space=pltpu.HBM)
 TOKEN = jax.ShapeDtypeStruct((8, 128), F32)
@@ -50,8 +49,14 @@
     return jnp.where(even, up, down), jnp.where(even, down, up)
 
 
-def prep_kernel(live_ref, x_hbm, dy_hbm, map_hbm, up_hbm, down_hbm, pack_ref, first_ref, second_ref, *scratch):
-    x_ref, dy_ref, map_ref, up_ref, down_ref, map_scr, sems = scratch
+def live_rows(maps, offsets, width, zero_slot):
+    rows = maps.shape[1]
+    centre = jnp.transpose(jnp.broadcast_to(maps[offsets // 2 : offsets // 2 + 1, :], (128, rows)))
+    return jnp.concatenate([centre] * (width // 128), axis=1) != zero_slot
+
+
+def prep_kernel(x_hbm, dy_hbm, map_hbm, up_hbm, down_hbm, pack_ref, first_ref, second_ref, *refs):
+    part_refs, (x_ref, dy_ref, map_ref, up_ref, down_ref, map_scr, turned, sems) = refs[:-8], refs[-8:]
     sources = (x_hbm, dy_hbm, map_hbm, up_hbm, down_hbm)
     targets = (x_ref, dy_ref, map_ref, up_ref, down_ref)
     copies = [pltpu.make_async_copy(a, b, sems.at[i]) for i, (a, b) in enumerate(zip(sources, targets))]
@@ -60,10 +65,11 @@
     rows, width = x_ref.shape
     offsets = map_ref.shape[0]
     halo = up_ref.shape[1]
-    keep = lax.broadcasted_iota(jnp.int32, (rows, width), 0) < live_ref[0]
-    map_scr[...] = jnp.full(map_scr.shape, rows + 2 * halo, jnp.int32)
+    zero_slot = rows + 2 * halo
+    map_scr[...] = jnp.full(map_scr.shape, zero_slot, jnp.int32)
     for copy in copies:
         copy.wait()
+    keep = live_rows(map_ref[...], offsets, width, zero_slot)
     x_live = jnp.where(keep, x_ref[...].astype(F32), 0.0).astype(BF)
     pack_ref[0:rows] = x_live
     iota = lax.broadcasted_iota(jnp.int32, (rows, halo), 0)
@@ -74,9 +80,14 @@
     map_scr[0:offsets] = map_ref[...]
     slots = map_scr[...]
     pack_ref[2 * rows :] = jnp.where(slots > 256, 256 - slots, slots).astype(F32).astype(BF)
-
-
-def prep(live, features, cotangent, kernel_map, send_up, send_down, map_rows):
+    turned[...] = jnp.transpose(x_live)
+    for m, part_ref in enumerate(part_refs):
+        slab = part_ref.shape[0] - (pack_ref.shape[0] - rows)
+        part_ref[0:slab] = turned[pl.ds(pl.multiple_of((place()[0] ^ (m + 1)) * slab, slab), slab), :]
+        part_ref[slab:] = pack_ref[rows:]
+
+
+def prep(features, cotangent, kernel_map, send_up, send_down, map_rows, groups):
     rows, width = features.shape
     return pl.pallas_call(
         prep_kernel,
@@ -84,9 +95,10 @@
             jax.ShapeDtypeStruct((2 * rows + map_rows, width), BF),
             jax.ShapeDtypeStruct((send_up.shape[1], width), BF),
             jax.ShapeDtypeStruct((send_up.shape[1], width), BF),
+            *(jax.ShapeDtypeStruct((width // groups + rows + map_rows, rows), BF),) * (groups - 1),
         ),
-        in_specs=[SMEM] + [HBM] * 5,
-        out_specs=(VMEM,) * 3,
+        in_specs=[HBM] * 5,
+        out_specs=(VMEM,) * (2 + groups),
         scratch_shapes=[
             pltpu.VMEM((rows, width), BF),
             pltpu.VMEM((rows, width), BF),
@@ -94,11 +106,12 @@
             pltpu.VMEM(send_up.shape, jnp.int32),
             pltpu.VMEM(send_down.shape, jnp.int32),
             pltpu.VMEM((map_rows, rows), jnp.int32),
+            pltpu.VMEM((width, rows), BF),
             pltpu.SemaphoreType.DMA((5,)),
         ],
         compiler_params=params(PREP_LIMIT),
         name="prep",
-    )(live, features, cotangent, kernel_map, send_up, send_down)
+    )(features, cotangent, kernel_map, send_up, send_down)
 
 
 def decoded(code):
@@ -153,7 +166,7 @@
     )(pack, weights, after)
 
 
-def forward_kernel(group, live_ref, pack_ref, halo_ref, w_ref, after_ref, out_ref, token_ref, table, maps, out_acc, picked):
+def forward_kernel(group, pack_ref, halo_ref, w_ref, after_ref, out_ref, token_ref, table, maps, out_acc, picked):
     offsets, width, _ = w_ref.shape
     rows = out_ref.shape[0]
     slots = table.shape[0]
@@ -171,19 +184,19 @@
     for g in range(offsets // group):
         value = dot(picked[g], w_ref[g * group : (g + 1) * group].reshape(group * width, width))
         out_acc[...] = value if g == 0 else out_acc[...] + value
-    keep = lax.broadcasted_iota(jnp.int32, (rows, width), 0) < live_ref[0]
+    keep = jnp.broadcast_to(maps[:, offsets // 2 : offsets // 2 + 1], (rows, width)) != slots
     out_ref[...] = jnp.where(keep, out_acc[...], 0.0).astype(BF)
     token_ref[...] = jnp.zeros_like(token_ref)
 
 
-def forward(live, pack, halo_rows, weights, rows, after):
+def forward(pack, halo_rows, weights, rows, after):
     offsets, width, _ = weights.shape
     slots = rows + halo_rows.shape[0]
     group = 3 if offsets % 3 == 0 else 1
     return pl.pallas_call(
         functools.partial(forward_kernel, group),
         out_shape=(jax.ShapeDtypeStruct((rows, width), BF), TOKEN),
-        in_specs=[SMEM, VMEM, VMEM, VMEM, ANY],
+        in_specs=[VMEM, VMEM, VMEM, ANY],
         out_specs=(VMEM, VMEM),
         scratch_shapes=[
             pltpu.VMEM((slots, width), BF),
@@ -194,83 +207,87 @@
         compiler_params=params(),
         cost_estimate=cost(),
         name="forward",
-    )(live, pack, halo_rows, weights, after)
+    )(pack, halo_rows, weights, after)
 
 
 def chosen_slots(maps, s, at, low, high, rows):
-    iota = lax.broadcasted_iota(jnp.int32, (high - low, rows), 0) + low
-    return (iota == maps[s, pl.ds(at, 1), :]).astype(F32).astype(BF)
-
-
-def wgrad_own_kernel(sources, *refs):
-    packs = refs[:sources]
-    picked_ref, dys, maps, tables = refs[sources:]
-    count, width, _ = picked_ref.shape
-    rows = dys.shape[0] // sources
+    slot = (lax.broadcasted_iota(jnp.int32, (high - low, rows), 0) + low).astype(jnp.int16)
+    wanted = jnp.broadcast_to(maps[s, at : at + 1, :].astype(jnp.int16), (high - low, rows))
+    return jnp.where(slot == wanted, jnp.ones((), BF), jnp.zeros((), BF))
+
+
+def wgrad_own_kernel(offsets, *refs):
+    packs, (picked_ref, dys, maps) = refs[:-3], refs[-3:]
+    sources, _, rows = maps.shape
+    slab = picked_ref.shape[1]
     for s in range(sources):
-        tables[:, s * rows : (s + 1) * rows] = jnp.transpose(packs[s][0:rows])
-        dys[s * rows : (s + 1) * rows] = packs[s][rows : 2 * rows]
-        maps[s] = decoded(packs[s][2 * rows :])
-
-    for j in range(count):
+        dys[s * rows : (s + 1) * rows] = packs[s][slab : slab + rows]
+        maps[s] = decoded(packs[s][slab + rows :])
+    for j in range(offsets):
         for s in range(sources):
-            chosen = chosen_slots(maps, s, place()[0] * count + j, 0, rows, rows)
-            picked_ref[j, :, s * rows : (s + 1) * rows] = dot(tables[:, s * rows : (s + 1) * rows], chosen).astype(BF)
-
-
-def wgrad_own(packs, count, rows):
+            chosen = chosen_slots(maps, s, j, 0, rows, rows)
+            picked_ref[j, :, s * rows : (s + 1) * rows] = dot(packs[s][0:slab], chosen).astype(BF)
+
+
+def wgrad_own(packs, offsets, slab, rows):
     sources, width = len(packs), packs[0].shape[1]
     return pl.pallas_call(
-        functools.partial(wgrad_own_kernel, sources),
+        functools.partial(wgrad_own_kernel, offsets),
         out_shape=(
-            jax.ShapeDtypeStruct((count, width, sources * rows), BF),
+            jax.ShapeDtypeStruct((offsets, slab, sources * rows), BF),
             jax.ShapeDtypeStruct((sources * rows, width), BF),
-            jax.ShapeDtypeStruct((sources, packs[0].shape[0] - 2 * rows, rows), jnp.int32),
+            jax.ShapeDtypeStruct((sources, packs[0].shape[0] - slab - rows, rows), jnp.int32),
         ),
         in_specs=[VMEM] * sources,
         out_specs=(VMEM, VMEM, VMEM),
-        scratch_shapes=[pltpu.VMEM((width, sources * rows), BF)],
         compiler_params=params(),
         cost_estimate=cost(),
         name="wgrad_own",
     )(*packs)
 
 
-def wgrad_kernel(sources, first, picked_ref, dys, maps, *refs):
-    halos, (after_ref, keep_ref, send_ref, tables, picked) = refs[:sources], refs[sources:]
+def wgrad_kernel(sizes, *refs):
+    sets = [refs[3 * n : 3 * n + 3] for n in range(len(sizes))]
+    halos, (keep_ref, send_ref, picked) = refs[3 * len(sizes) : -3], refs[-3:]
     count, half, width = keep_ref.shape
-    rows = maps.shape[2]
-    far = halos[0].shape[0]
+    far = halos[0].shape[1]
+    offsets = sets[0][0].shape[0]
+    rows = sets[0][2].shape[2]
     core = place()[1]
-    for s in range(sources):
-        tables[:, s * far : (s + 1) * far] = jnp.transpose(halos[s][...])
-    for j in range(count):
-        for s in range(sources):
-            chosen = chosen_slots(maps, s, place()[0] * picked_ref.shape[0] + first + j, rows, rows + far, rows)
-            near = picked_ref[first + j, :, s * rows : (s + 1) * rows].astype(F32)
-            picked[j, :, s * rows : (s + 1) * rows] = (dot(tables[:, s * far : (s + 1) * far], chosen) + near).astype(BF)
-    for j in range(count):
-        send_ref[j] = dot(picked[j, pl.ds(pl.multiple_of((1 - core) * half, half), half), :], dys[...])
-        keep_ref[j] = dot(picked[j, pl.ds(pl.multiple_of(core * half, half), half), :], dys[...])
-
-
-def wgrad(picked, dys, maps, halos, first, count, after):
-    _, width, columns = picked.shape
-    sources = maps.shape[0]
-    shape = jax.ShapeDtypeStruct((count, width // 2, width), F32)
-    return pl.pallas_call(
-        functools.partial(wgrad_kernel, sources, first),
+    for j in range(offsets):
+        s = 0
+        for (picked_ref, _, maps), size in zip(sets, sizes):
+            for i in range(size):
+                chosen = chosen_slots(maps, i, j, rows, rows + far, rows)
+                near = picked_ref[j, :, i * rows : (i + 1) * rows].astype(F32)
+                value = (dot(halos[s][...], chosen) + near).astype(BF)
+                for h in range(2):
+                    picked[h, j * half : (j + 1) * half, s * rows : (s + 1) * rows] = value[h * half : (h + 1) * half]
+                s += 1
+    picked[:, offsets * half :] = jnp.zeros((2, (count - offsets) * half, picked.shape[2]), BF)
+    for out_ref, h in ((send_ref, 1 - core), (keep_ref, core)):
+        total, s = 0.0, 0
+        for (_, dys, _), size in zip(sets, sizes):
+            total = total + dot(picked[h, :, s * rows : (s + size) * rows], dys[...])
+            s += size
+        out_ref[...] = total.reshape(out_ref.shape)
+
+
+def wgrad(sets, halos, count):
+    sizes = [maps.shape[0] for _, _, maps in sets]
+    _, slab, _ = sets[0][0].shape
+    columns = sum(picked.shape[2] for picked, _, _ in sets)
+    shape = jax.ShapeDtypeStruct((count, slab // 2, sets[0][1].shape[1]), F32)
+    return pl.pallas_call(
+        functools.partial(wgrad_kernel, sizes),
         out_shape=(shape, shape),
-        in_specs=[VMEM] * (3 + sources) + [ANY],
+        in_specs=[VMEM] * (3 * len(sizes) + len(halos)),
         out_specs=(VMEM, VMEM),
-        scratch_shapes=[
-            pltpu.VMEM((width, sources * halos[0].shape[0]), BF),
-            pltpu.VMEM((count, width, columns), BF),
-        ],
+        scratch_shapes=[pltpu.VMEM((2, count * slab // 2, columns), BF)],
         compiler_params=params(),
         cost_estimate=cost(),
         name="wgrad",
-    )(picked, dys, maps, *halos, after)
+    )(*[array for one in sets for array in one], *halos)
 
 
 def power(exponent):
@@ -282,40 +299,73 @@
     return value
 
 
-def joined_kernel(first_ref, second_ref, pack_ref, out_ref, copy_ref):
+def near_kernel(pack_ref, copy_ref, own_ref, turned):
+    slab = own_ref.shape[0] - (pack_ref.shape[0] - turned.shape[1])
+    rows = turned.shape[1]
+    copy_ref[...] = pack_ref[...]
+    turned[...] = jnp.transpose(pack_ref[0:rows])
+    own_ref[0:slab] = turned[pl.ds(pl.multiple_of(place()[0] * slab, slab), slab), :]
+    own_ref[slab:] = pack_ref[rows:]
+
+
+def near_pack(pack, rows, slab):
+    width = pack.shape[1]
+    return pl.pallas_call(
+        near_kernel,
+        out_shape=(
+            jax.ShapeDtypeStruct(pack.shape, BF),
+            jax.ShapeDtypeStruct((slab + pack.shape[0] - rows, width), BF),
+        ),
+        in_specs=[VMEM],
+        out_specs=(VMEM, VMEM),
+        scratch_shapes=[pltpu.VMEM((width, rows), BF)],
+        compiler_params=params(),
+        cost_estimate=cost(),
+        name="near_pack",
+    )(pack)
+
+
+def joined_kernel(first_ref, second_ref, after_ref, out_ref, *refs):
+    turned, halo_refs = refs[-1], refs[:-1]
     halo = first_ref.shape[0]
+    slab = halo_refs[0].shape[0]
     second, first = turns(0, halo)
     out_ref[pl.ds(pl.multiple_of(first, halo), halo)] = first_ref[...]
     out_ref[pl.ds(pl.multiple_of(second, halo), halo)] = second_ref[...]
-    copy_ref[...] = pack_ref[...]
-
-
-def joined(first, second, pack):
+    turned[...] = jnp.transpose(out_ref[...])
+    for m, halo_ref in enumerate(halo_refs):
+        halo_ref[...] = turned[pl.ds(pl.multiple_of((place()[0] ^ m) * slab, slab), slab), :]
+
+
+def joined(first, second, groups, after):
+    halo, width = first.shape
+    slab = width // groups
     return pl.pallas_call(
         joined_kernel,
         out_shape=(
-            jax.ShapeDtypeStruct((2 * first.shape[0], first.shape[1]), BF),
-            jax.ShapeDtypeStruct(pack.shape, BF),
+            jax.ShapeDtypeStruct((2 * halo, width), BF),
+            *(jax.ShapeDtypeStruct((slab, 2 * halo), BF),) * groups,
         ),
-        in_specs=[VMEM] * 3,
-        out_specs=(VMEM, VMEM),
+        in_specs=[VMEM] * 2 + [ANY],
+        out_specs=(VMEM,) * (1 + groups),
+        scratch_shapes=[pltpu.VMEM((width, 2 * halo), BF)],
         compiler_params=params(),
         cost_estimate=cost(),
         name="joined",
-    )(first, second, pack)
+    )(first, second, after)
 
 
 def blocks_kernel(keep_ref, got_ref, mine_ref, *refs):
     coded_refs, exponents = refs[:-1], refs[-1]
     count, block, width = mine_ref.shape
     for m in range(len(coded_refs) + 1):
-        at = pl.ds(pl.multiple_of((place()[2] ^ m) * block, block), block)
+        at = (place()[2] ^ m) * count
         if m == 0:
-            mine_ref[...] = keep_ref[:, at, :] + got_ref[:, at, :]
+            mine_ref[...] = keep_ref[pl.ds(at, count)] + got_ref[pl.ds(at, count)]
             continue
         exponents[...] = jnp.zeros_like(exponents)
         for j in range(count):
-            value = keep_ref[j, at, :] + got_ref[j, at, :]
+            value = keep_ref[at + j] + got_ref[at + j]
             largest = jnp.max(jnp.abs(value), axis=0, keepdims=True)
             exponent = jnp.ceil(jnp.log(jnp.maximum(largest, 2.0**-100)) * (1.0 / math.log(2.0)))
             exponent = jnp.clip(exponent, -100.0, 100.0).astype(jnp.int32) - 15
@@ -326,8 +376,8 @@
 
 
 def blocks(keep, got, parts):
-    count, half, width = keep.shape
-    block = half // parts
+    total, block, width = keep.shape
+    count = total // parts
     extra = -(-count // 16) * 16
     return pl.pallas_call(
         blocks_kernel,
@@ -368,7 +418,7 @@
     )(mine, *coded, *after)
 
 
-def final_kernel(live_ref, own_ref, first_ref, second_ref, up_ref, down_ref, after_ref, out_ref, token_ref):
+def final_kernel(offsets, pack_ref, own_ref, first_ref, second_ref, up_ref, down_ref, after_ref, out_ref, token_ref):
     rows, width = own_ref.shape
     halo = up_ref.shape[1]
     total = own_ref[...]
@@ -377,20 +427,20 @@
     chosen = jnp.concatenate(chosen, axis=1).astype(BF)
     for part in split(jnp.concatenate([first_ref[...], second_ref[...]], axis=0), 3):
         total = total + dot(chosen, part)
-    keep = lax.broadcasted_iota(jnp.int32, (rows, width), 0) < live_ref[0]
+    keep = live_rows(decoded(pack_ref[2 * rows :]), offsets, width, rows + 2 * halo)
     out_ref[...] = jnp.where(keep, total, 0.0).astype(BF)
     token_ref[...] = jnp.zeros_like(token_ref)
 
 
-def final(live, own_grad, first_back, second_back, send_up, send_down, after):
-    return pl.pallas_call(
-        final_kernel,
+def final(offsets, pack, own_grad, first_back, second_back, send_up, send_down, after):
+    return pl.pallas_call(
+        functools.partial(final_kernel, offsets),
         out_shape=(jax.ShapeDtypeStruct(own_grad.shape, BF), TOKEN),
-        in_specs=[SMEM] + [VMEM] * 5 + [ANY],
+        in_specs=[VMEM] * 6 + [ANY],
         out_specs=(VMEM, VMEM),
         compiler_params=params(),
         name="final",
-    )(live, own_grad, first_back, second_back, send_up, send_down, after)
+    )(pack, own_grad, first_back, second_back, send_up, send_down, after)
 
 
 def stack_kernel(count, *refs):
@@ -433,24 +483,24 @@
 
 def assemble_kernel(marks, parts, groups, *refs):
     out_ref, sems = refs[-2:]
-    offsets = out_ref.shape[0]
     _, count, block, _ = refs[0].shape
-    short = offsets - (groups - 1) * count
+    short = out_ref.shape[0] - (parts - 1) * count
 
     def each(act):
         for index, (o, sources) in enumerate(marks):
             for part, (m, mask) in enumerate(sources):
-                group = place()[0] ^ m
-                row = pl.multiple_of(((place()[1] ^ o) * parts + (place()[2] ^ mask)) * block, block)
+                group, core, space = place()
+                at = (space ^ mask) * count
+                row = pl.multiple_of(((group ^ m) * 2 + (core ^ o)) * block, block)
                 source = refs[index].at[part]
 
                 def copy(lo, hi, sem):
-                    target = out_ref.at[pl.ds(group * count + lo, hi - lo), pl.ds(row, block)]
+                    target = out_ref.at[pl.ds(at + lo, hi - lo), pl.ds(row, block)]
                     return pltpu.make_async_copy(source.at[lo:hi], target, sems.at[index, part, sem])
 
                 getattr(copy(0, short, 0), act)()
                 if short < count:
-                    pl.when(group < groups - 1)(getattr(copy(short, count, 1), act))
+                    pl.when((space ^ mask) < parts - 1)(getattr(copy(short, count, 1), act))
 
     each("start")
     each("wait")
@@ -473,11 +523,12 @@
 
 def assemble_plain(pieces, marks, parts, groups, offsets, width):
     _, count, block, _ = pieces[0].shape
-    total = jnp.zeros((groups * count, width, width), BF)
+    total = jnp.zeros((parts * count, width, width), BF)
     for piece, (o, sources) in zip(pieces, marks):
         for part, (m, mask) in enumerate(sources):
-            row = ((place()[1] ^ o) * parts + (place()[2] ^ mask)) * block
-            total = lax.dynamic_update_slice(total, piece[part], ((place()[0] ^ m) * count, row, 0))
+            group, core, space = place()
+            row = ((group ^ m) * 2 + (core ^ o)) * block
+            total = lax.dynamic_update_slice(total, piece[part], ((space ^ mask) * count, row, 0))
     return total[:offsets]
 
 
@@ -496,42 +547,45 @@
     offsets, halo = weights.shape[0], send_up.shape[1]
     groups = lax.axis_size("dp") // 2
     parts = lax.axis_size("space")
-    count = -(-offsets // groups)
-    map_rows = -(-(groups * count) // 16) * 16
-
-    pack, first_rows, second_rows = prep(live, features, cotangent, kernel_map, send_up, send_down, map_rows)
-    packs = [pack] + [swap(pack, "dp", 2 * m) for m in range(1, groups)]
-    halo_rows, pack = joined(met(first_rows, 0), met(second_rows, 1), pack)
-    packs[0] = pack
-    halos = [halo_rows] + [swap(halo_rows, "dp", 2 * m) for m in range(1, groups)]
-    picked, dys, maps = wgrad_own(packs, count, rows)
-    keep, send = wgrad(picked, dys, maps, halos, 0, count, dys)
+    count = -(-offsets // parts)
+    slab = width // groups
+    map_rows = -(-offsets // 16) * 16
+
+    pack, first_rows, second_rows, *packs = prep(
+        features, cotangent, kernel_map, send_up, send_down, map_rows, groups
+    )
+    packs = [swap(part, "dp", 2 * m) for m, part in enumerate(packs, 1)]
+    pack, own_part = near_pack(pack, rows, slab)
+    own_set = wgrad_own([own_part], offsets, slab, rows)
+    halo_rows, own_halo, *halos = joined(met(first_rows, 0), met(second_rows, 1), groups, own_set[1])
+    halos = [swap(part, "dp", 2 * m) for m, part in enumerate(halos, 1)]
+    sets = [own_set, wgrad_own(packs, offsets, slab, rows)]
+    keep, send = wgrad(sets, [own_halo, *halos], parts * count)
     mine, *coded = blocks(keep, swap(send, "dp", 1), parts)
     own_grad, first_grad, second_grad, token = backward(pack, weights, rows, halo, mine)
     first_back, second_back = met(first_grad, 0), met(second_grad, 1)
     scale = 1.0 / math.sqrt(rows * lax.axis_size("dp") * parts)
     rounded = scaled_total(mine, [swap(block, "space", m + 1) for m, block in enumerate(coded)], scale, (token, token))
-    out_features, token = forward(live, pack, halo_rows, weights, rows, rounded)
+    out_features, token = forward(pack, halo_rows, weights, rows, rounded)
 
     along = [swap(rounded, "space", m) for m in range(1, parts)]
     across = {m: swap(rounded, "dp", 2 * m) for m in range(1, groups)}
     lines = gate(stack(along, [token]), list(across.values()))
     far = {m: swap(lines, "dp", 2 * m) for m in range(1, groups)}
     line_masks = range(1, parts)
-    grad_features, token = final(live, own_grad, first_back, second_back, send_up, send_down, lines)
+    grad_features, token = final(offsets, pack, own_grad, first_back, second_back, send_up, send_down, lines)
     near = stack([rounded, lines], [token])
     sides = stack([across[m] for m in range(1, groups)], [])
     near_marks = [(0, mask) for mask in range(parts)]
     side_marks = [(m, 0) for m in range(1, groups)]
     pieces = [near, swap(near, "dp", 1), sides, swap(sides, "dp", 1)]
     marks = [(0, near_marks), (1, near_marks), (0, side_marks), (1, side_marks)]
-    dense = rounded.shape[1] % 16 == 0 and groups * count - offsets < count
+    dense = rounded.shape[1] % 16 == 0 and parts * count - offsets < count
     sizes = (parts, groups, offsets, width)
     first = ()
     if dense:
         first = (assemble(pieces, marks, *sizes, ()),)
         pieces, marks = [], []
-        pass
     for m in range(1, groups):
         pieces += [far[m], swap(far[m], "dp", 1)]
         marks += [(o, [(m, mask) for mask in line_masks]) for o in range(2)]

time: 77.1 us -> 76.4 us (level)
  waiting for transfers between devices: 20 us -> 16.1 us
  Pallas kernels: 19.4 us -> 21.5 us
  starting transfers between devices: 35 us -> 35.9 us
    ppermute x24, waiting for transfers between devices: 17 us -> 14.5 us  [swap(): lax.ppermute(value, axis, [(i, i ^ mask) for i in range(lax.axis_size(axi...]
    pallas_call x4 -> x6, Pallas kernels: 4.49 us -> 6.1 us  [the longest x2 2.74 us: wgrad_own(): pl.pallas_call(functools.partial(wgrad_own_kernel, offsets), out_shape=(j...]
    ppermute x4, waiting for transfers between devices: 3.08 us -> 1.59 us  [met(): lax.ppermute(value, 'space', [(i, i + 1) for i in starts] + [(i + 1, i) f...]
  transfers between devices with their start and end apart: 28 -> 28, of which waited for: 12 -> 9; matrix products, arithmetic and copies ran while one was open for 0% -> 0% of each run, Pallas kernels for 17% -> 20%
where the time goes in v8:
time: 76.4 us; the launch traced here: 75.5 us
  starting transfers between devices  35.9 us (47%)
  Pallas kernels  21.5 us (28%)
  waiting for transfers between devices  16.1 us (21%)
  between operations  1.02 us (1%)
  local copies, waits for them, and re-layouts  0.97 us (1%)
    ppermute x24, starting transfers between devices, swap(): lax.ppermute(value, axis, [(i, i ^ mask) for i in range(lax.axis_size(axi...  27.9 us
    ppermute x24, waiting for transfers between devices, swap(): lax.ppermute(value, axis, [(i, i ^ mask) for i in range(lax.axis_size(axi...  14.5 us
    ppermute x4, starting transfers between devices, met(): lax.ppermute(value, 'space', [(i, i + 1) for i in starts] + [(i + 1, i) f...  8.04 us
    pallas_call x1, Pallas kernels, backward(): pl.pallas_call(functools.partial(backward_kernel, group), out_shape=tuple...  5.46 us
    pallas_call x1, Pallas kernels, forward(): pl.pallas_call(functools.partial(forward_kernel, group), out_shape=(jax.S...  4.13 us
    pallas_call x2, Pallas kernels, assemble(): pl.pallas_call(functools.partial(assemble_kernel, marks, parts, groups),...  2.97 us
    pallas_call x2, Pallas kernels, wgrad_own(): pl.pallas_call(functools.partial(wgrad_own_kernel, offsets), out_shape=(j...  2.74 us
    pallas_call x1, Pallas kernels, wgrad(): pl.pallas_call(functools.partial(wgrad_kernel, sizes), out_shape=(shape,...  2.19 us
  transfers between devices with their start and end apart: 28, of which 9 were waited for; matrix products, arithmetic and copies ran while one was open for 0% of the time, Pallas kernels for 20%

profile of v8, /device:TPU:0, one launch (start us, length us, event | category | flops | bytes accessed | tf_op | source)
XLA Modules:
  0.0 75.5 jit_solution(15646061631794176883)
XLA Ops:
  0.6 2.1 %prep.1 = (bf16[544,256]{1,0:T(8,128)(2,1)}, bf16[64,256]{1,0:T(8,128)(2,1)}, bf16[64,256]{1,0:T(8,128)(2,1)}, bf16[352,256]{1,0:T(8,128)(2,1)}, bf16[352,256]{1,0:T(8,128)(2,1)}, /*index=5*/bf16[352,256]{1,0:T(8,128)(2,1)}) custom-call(bf16[256,256]{1,0:T(8,128)(2,1)} %x_hbm.1, bf16[256,256]{1,0:T(8,128)(2,1)} %dy_hbm.1, s32[27,256]{1,0:T(8,128)} %map_hbm.1, ...), custom_call_target="tpu_custom_call" | custom-call | tf_op jit(solution)/shard_map/prep/pallas_call | solution.py:92
  2.8 3.0 %collective-permute-start.2 = (bf16[352,256]{1,0:T(8,128)(2,1)}, bf16[352,256]{1,0:T(8,128)(2,1)S(1)}, u32[]{:S(2)}, u32[]{:S(2)}) collective-permute-start(bf16[352,256]{1,0:T(8,128)(2,1)} %get-tuple-element.45), channel_id=1, source_target_pairs={{0,8},{4,12},{8,0},{12,4},{16,24},{20,28},{24,16},{28,20},{1,9},{5... | collective-permute-start | bytes 540680 | tf_op jit(solution)/shard_map/ppermute | solution.py:536
  5.8 1.5 %collective-permute-start.3 = (bf16[352,256]{1,0:T(8,128)(2,1)}, bf16[352,256]{1,0:T(8,128)(2,1)S(1)}, u32[]{:S(2)}, u32[]{:S(2)}) collective-permute-start(bf16[352,256]{1,0:T(8,128)(2,1)} %get-tuple-element.46), channel_id=1, source_target_pairs={{0,16},{4,20},{8,24},{12,28},{16,0},{20,4},{24,8},{28,12},{1,17},{... | collective-permute-start | bytes 540680 | tf_op jit(solution)/shard_map/ppermute | solution.py:536
  7.3 2.0 %collective-permute-start = (bf16[64,256]{1,0:T(8,128)(2,1)}, bf16[64,256]{1,0:T(8,128)(2,1)S(1)}, u32[]{:S(2)}, u32[]{:S(2)}) collective-permute-start(bf16[64,256]{1,0:T(8,128)(2,1)} %get-tuple-element.38), channel_id=1, source_target_pairs={{0,1},{2,3},{1,0},{3,2},{4,5},{6,7},{5,4},{7,6},{8,9},{10,11},{9,8... | collective-permute-start | bytes 98312 | tf_op jit(solution)/shard_map/ppermute | solution.py:542
  9.3 0.7 collective-permute-start.1
  10.0 0.9 %copy-done.3 = bf16[544,256]{1,0:T(8,128)(2,1)S(1)} copy-done((bf16[544,256]{1,0:T(8,128)(2,1)S(1)}, bf16[544,256]{1,0:T(8,128)(2,1)}, u32[]{:S(2)}) %copy-start.3) | copy-done | bytes 278552
  11.0 0.1 near_pack.1
  11.0 0.8 %wgrad_own.2 = (bf16[27,64,256]{2,1,0:T(8,128)(2,1)S(1)}, bf16[256,256]{1,0:T(8,128)(2,1)S(1)}, s32[1,32,256]{2,1,0:T(8,128)S(1)}) custom-call(bf16[352,256]{1,0:T(8,128)(2,1)S(1)} %get-tuple-element.40.refs_0_), custom_call_target="tpu_custom_call" | custom-call | flops 100000000 | bytes 100000 | tf_op jit(solution)/shard_map/wgrad_own/pallas_call | solution.py:234
  11.8 0.1 joined.1
  11.9 1.6 %collective-permute-start.5 = (bf16[64,128]{1,0:T(8,128)(2,1)S(1)}, bf16[64,128]{1,0:T(8,128)(2,1)S(1)}, u32[]{:S(2)}, u32[]{:S(2)}) collective-permute-start(bf16[64,128]{1,0:T(8,128)(2,1)S(1)} %get-tuple-element.52), channel_id=1, source_target_pairs={{0,8},{4,12},{8,0},{12,4},{16,24},{20,28},{24,16},{28,20},{1,9},{5... | collective-permute-start | bytes 49160 | tf_op jit(solution)/shard_map/ppermute | solution.py:536
  13.5 1.5 %collective-permute-start.6 = (bf16[64,128]{1,0:T(8,128)(2,1)S(1)}, bf16[64,128]{1,0:T(8,128)(2,1)S(1)}, u32[]{:S(2)}, u32[]{:S(2)}) collective-permute-start(bf16[64,128]{1,0:T(8,128)(2,1)S(1)} %get-tuple-element.53), channel_id=1, source_target_pairs={{0,16},{4,20},{8,24},{12,28},{16,0},{20,4},{24,8},{28,12},{1,17},{... | collective-permute-start | bytes 49160 | tf_op jit(solution)/shard_map/ppermute | solution.py:536
  15.1 0.4 collective-permute-start.7
  15.5 0.4 collective-permute-done.3.refs_1_
  15.9 2.0 %wgrad_own.3 = (bf16[27,64,768]{2,1,0:T(8,128)(2,1)S(1)}, bf16[768,256]{1,0:T(8,128)(2,1)S(1)}, s32[3,32,256]{2,1,0:T(8,128)S(1)}) custom-call(bf16[352,256]{1,0:T(8,128)(2,1)S(1)} %collective-permute-done.2.refs_0_, bf16[352,256]{1,0:T(8,128)(2,1)S(1)} %collective-permute-done.3.refs_1_, bf16[352,256]{1,0:T(8,128)(2,1)S(1)} %collective-permute-done.4.refs_2_), custom_call_target="tpu_custom_call" | custom-call | flops 100000000 | bytes 100000 | tf_op jit(solution)/shard_map/wgrad_own/pallas_call | solution.py:234
  17.9 1.8 %collective-permute-done.7.refs_9_ = bf16[64,128]{1,0:T(8,128)(2,1)S(1)} collective-permute-done((bf16[64,128]{1,0:T(8,128)(2,1)S(1)}, bf16[64,128]{1,0:T(8,128)(2,1)S(1)}, u32[]{:S(2)}, u32[]{:S(2)}) %collective-permute-start.7) | collective-permute-done | bytes 16416 | tf_op jit(solution)/shard_map/ppermute | solution.py:536
  19.7 2.2 %wgrad.1 = (f32[28,32,256]{2,1,0:T(8,128)S(1)}, f32[28,32,256]{2,1,0:T(8,128)S(1)}) custom-call(bf16[27,64,256]{2,1,0:T(8,128)(2,1)S(1)} %get-tuple-element.43.refs_0_, bf16[256,256]{1,0:T(8,128)(2,1)S(1)} %get-tuple-element.41.after_ref.refs_1_, s32[1,32,256]{2,1,0:T(8,128)S(1)} %get-tuple-element.44.refs_2_, ...), custom_call_target="tpu_custom_call" | custom-call | flops 100000000 | bytes 100000 | tf_op jit(solution)/shard_map/wgrad/pallas_call | solution.py:281
  22.0 2.5 %collective-permute-done.8.got_ref = f32[28,32,256]{2,1,0:T(8,128)S(1)} collective-permute-done((f32[28,32,256]{2,1,0:T(8,128)S(1)}, f32[28,32,256]{2,1,0:T(8,128)S(1)}, u32[]{:S(2)}, u32[]{:S(2)}) %collective-permute-start.8) | collective-permute-done | bytes 917536 | tf_op jit(solution)/shard_map/ppermute | solution.py:536
  24.4 0.5 blocks.1
  24.9 4.7 %collective-permute-start.9 = (s16[240,256]{1,0:T(8,128)(2,1)S(1)}, s16[240,256]{1,0:T(8,128)(2,1)S(1)}, u32[]{:S(2)}, u32[]{:S(2)}) collective-permute-start(s16[240,256]{1,0:T(8,128)(2,1)S(1)} %get-tuple-element.58), channel_id=1, source_target_pairs={{0,1},{1,0},{2,3},{3,2},{4,5},{5,4},{6,7},{7,6},{8,9},{9,8},{10,11... | collective-permute-start | bytes 368648 | tf_op jit(solution)/shard_map/ppermute | solution.py:536
  29.6 1.5 %collective-permute-start.10 = (s16[240,256]{1,0:T(8,128)(2,1)S(1)}, s16[240,256]{1,0:T(8,128)(2,1)S(1)}, u32[]{:S(2)}, u32[]{:S(2)}) collective-permute-start(s16[240,256]{1,0:T(8,128)(2,1)S(1)} %get-tuple-element.59), channel_id=1, source_target_pairs={{0,2},{1,3},{2,0},{3,1},{4,6},{5,7},{6,4},{7,5},{8,10},{9,11},{10,... | collective-permute-start | bytes 368648 | tf_op jit(solution)/shard_map/ppermute | solution.py:536
  31.1 1.4 %collective-permute-start.11 = (s16[240,256]{1,0:T(8,128)(2,1)S(1)}, s16[240,256]{1,0:T(8,128)(2,1)S(1)}, u32[]{:S(2)}, u32[]{:S(2)}) collective-permute-start(s16[240,256]{1,0:T(8,128)(2,1)S(1)} %get-tuple-element.60), channel_id=1, source_target_pairs={{0,3},{1,2},{2,1},{3,0},{4,7},{5,6},{6,5},{7,4},{8,11},{9,10},{10,... | collective-permute-start | bytes 368648 | tf_op jit(solution)/shard_map/ppermute | solution.py:536
  32.5 5.5 %backward.1 = (f32[256,256]{1,0:T(8,128)S(1)}, f32[64,256]{1,0:T(8,128)S(1)}, f32[64,256]{1,0:T(8,128)S(1)}, f32[8,128]{1,0:T(8,128)S(1)}) custom-call(bf16[544,256]{1,0:T(8,128)(2,1)S(1)} %get-tuple-element.37.pack_ref, bf16[27,256,256]{2,1,0:T(8,128)(2,1)S(1)} %copy-done, f32[7,32,256]{2,1,0:T(8,128)S(1)} %get-tuple-element.57.after_ref.mine_ref), custom_call_target="tpu_custom_call" | custom-call | flops 100000000 | bytes 100000 | tf_op jit(solution)/shard_map/backward/pallas_call | solution.py:151
  38.0 3.9 %collective-permute-done.10.refs_1_ = s16[240,256]{1,0:T(8,128)(2,1)S(1)} collective-permute-done((s16[240,256]{1,0:T(8,128)(2,1)S(1)}, s16[240,256]{1,0:T(8,128)(2,1)S(1)}, u32[]{:S(2)}, u32[]{:S(2)}) %collective-permute-start.10) | collective-permute-done | bytes 122912 | tf_op jit(solution)/shard_map/ppermute | solution.py:536
  41.9 0.1 total.1.after_ref.refs_0_
  42.0 2.5 %collective-permute-start.16 = (bf16[7,32,256]{2,1,0:T(8,128)(2,1)S(1)}, bf16[7,32,256]{2,1,0:T(8,128)(2,1)S(1)}, u32[]{:S(2)}, u32[]{:S(2)}) collective-permute-start(bf16[7,32,256]{2,1,0:T(8,128)(2,1)S(1)} %total.1.after_ref.refs_0_), channel_id=1, source_target_pairs={{0,3},{1,2},{2,1},{3,0},{4,7},{5,6},{6,5},{7,4},{8,11},{9,10},{10,... | collective-permute-start | bytes 344072 | tf_op jit(solution)/shard_map/ppermute | solution.py:536
  44.6 1.2 %collective-permute-start.15 = (bf16[7,32,256]{2,1,0:T(8,128)(2,1)S(1)}, bf16[7,32,256]{2,1,0:T(8,128)(2,1)S(1)}, u32[]{:S(2)}, u32[]{:S(2)}) collective-permute-start(bf16[7,32,256]{2,1,0:T(8,128)(2,1)S(1)} %total.1.after_ref.refs_0_), channel_id=1, source_target_pairs={{0,2},{1,3},{2,0},{3,1},{4,6},{5,7},{6,4},{7,5},{8,10},{9,11},{10,... | collective-permute-start | bytes 344072 | tf_op jit(solution)/shard_map/ppermute | solution.py:536
  45.8 0.7 collective-permute-start.14
  46.5 0.5 collective-permute-start.19
  47.0 1.5 %collective-permute-start.18 = (bf16[7,32,256]{2,1,0:T(8,128)(2,1)S(1)}, bf16[7,32,256]{2,1,0:T(8,128)(2,1)S(1)}, u32[]{:S(2)}, u32[]{:S(2)}) collective-permute-start(bf16[7,32,256]{2,1,0:T(8,128)(2,1)S(1)} %total.1.after_ref.refs_0_), channel_id=1, source_target_pairs={{0,16},{4,20},{8,24},{12,28},{16,0},{20,4},{24,8},{28,12},{1,17},{... | collective-permute-start | bytes 344072 | tf_op jit(solution)/shard_map/ppermute | solution.py:536
  48.5 0.6 collective-permute-done.16.refs_2_
  49.1 0.9 %collective-permute-start.17 = (bf16[7,32,256]{2,1,0:T(8,128)(2,1)S(1)}, bf16[7,32,256]{2,1,0:T(8,128)(2,1)S(1)}, u32[]{:S(2)}, u32[]{:S(2)}) collective-permute-start(bf16[7,32,256]{2,1,0:T(8,128)(2,1)S(1)} %total.1.after_ref.refs_0_), channel_id=1, source_target_pairs={{0,8},{4,12},{8,0},{12,4},{16,24},{20,28},{24,16},{28,20},{1,9},{5... | collective-permute-start | bytes 344072 | tf_op jit(solution)/shard_map/ppermute | solution.py:536
  50.0 4.1 %forward.1 = (bf16[256,256]{1,0:T(8,128)(2,1)}, f32[8,128]{1,0:T(8,128)S(1)}) custom-call(bf16[544,256]{1,0:T(8,128)(2,1)S(1)} %get-tuple-element.37.pack_ref, bf16[128,256]{1,0:T(8,128)(2,1)S(1)} %get-tuple-element.42.halo_ref, bf16[27,256,256]{2,1,0:T(8,128)(2,1)S(1)} %copy-done, bf16[7,32,256]{2,1,0:T(8,128)(2,1)S(1)} %total.1.after_ref.refs_0_), custom_call_target="tpu_custom_call" | custom-call | flops 100000000 | bytes 100000 | tf_op jit(solution)/shard_map/forward/pallas_call | solution.py:196
  54.1 0.8 %collective-permute-done.15.refs_1_ = bf16[7,32,256]{2,1,0:T(8,128)(2,1)S(1)} collective-permute-done((bf16[7,32,256]{2,1,0:T(8,128)(2,1)S(1)}, bf16[7,32,256]{2,1,0:T(8,128)(2,1)S(1)}, u32[]{:S(2)}, u32[]{:S(2)}) %collective-permute-start.15) | collective-permute-done | bytes 114720 | tf_op jit(solution)/shard_map/ppermute | solution.py:536
  55.0 0.5 collective-permute-start.24
  55.5 1.5 %collective-permute-start.22 = (bf16[3,7,32,256]{3,2,1,0:T(8,128)(2,1)S(1)}, bf16[3,7,32,256]{3,2,1,0:T(8,128)(2,1)S(1)}, u32[]{:S(2)}, u32[]{:S(2)}) collective-permute-start(bf16[3,7,32,256]{3,2,1,0:T(8,128)(2,1)S(1)} %gate.1.after_ref.refs_1_), channel_id=1, source_target_pairs={{0,16},{4,20},{8,24},{12,28},{16,0},{20,4},{24,8},{28,12},{1,17},{... | collective-permute-start | bytes 1032200 | tf_op jit(solution)/shard_map/ppermute | solution.py:536
  57.0 1.5 %collective-permute-start.20 = (bf16[3,7,32,256]{3,2,1,0:T(8,128)(2,1)S(1)}, bf16[3,7,32,256]{3,2,1,0:T(8,128)(2,1)S(1)}, u32[]{:S(2)}, u32[]{:S(2)}) collective-permute-start(bf16[3,7,32,256]{3,2,1,0:T(8,128)(2,1)S(1)} %gate.1.after_ref.refs_1_), channel_id=1, source_target_pairs={{0,8},{4,12},{8,0},{12,4},{16,24},{20,28},{24,16},{28,20},{1,9},{5... | collective-permute-start | bytes 1032200 | tf_op jit(solution)/shard_map/ppermute | solution.py:536
  58.5 4.7 %collective-permute-start.12 = (f32[64,256]{1,0:T(8,128)S(1)}, f32[64,256]{1,0:T(8,128)S(1)}, u32[]{:S(2)}, u32[]{:S(2)}) collective-permute-start(f32[64,256]{1,0:T(8,128)S(1)} %get-tuple-element.64), channel_id=1, source_target_pairs={{0,1},{2,3},{1,0},{3,2},{4,5},{6,7},{5,4},{7,6},{8,9},{10,11},{9,8... | collective-permute-start | bytes 196616 | tf_op jit(solution)/shard_map/ppermute | solution.py:542
  63.2 0.7 collective-permute-start.13
  63.9 1.6 %collective-permute-done.12.first_ref = f32[64,256]{1,0:T(8,128)S(1)} collective-permute-done((f32[64,256]{1,0:T(8,128)S(1)}, f32[64,256]{1,0:T(8,128)S(1)}, u32[]{:S(2)}, u32[]{:S(2)}) %collective-permute-start.12) | collective-permute-done | bytes 65568 | tf_op jit(solution)/shard_map/ppermute | solution.py:542
  65.5 1.0 %final.1 = (bf16[256,256]{1,0:T(8,128)(2,1)}, f32[8,128]{1,0:T(8,128)S(1)}) custom-call(bf16[544,256]{1,0:T(8,128)(2,1)S(1)} %get-tuple-element.37.pack_ref, f32[256,256]{1,0:T(8,128)S(1)} %get-tuple-element.63.own_ref, f32[64,256]{1,0:T(8,128)S(1)} %collective-permute-done.12.first_ref, f32[64,256]{1,0:T(8,128)S(1)} %collective-permute-done.13.second_ref, ...), custom_call_target="tpu_custom_call" | custom-call | tf_op jit(solution)/shard_map/final/pallas_call | solution.py:436
  66.5 0.1 collective-permute-start.26
  66.6 0.6 collective-permute-start.27
  67.2 0.1 collective-permute-start.25
  67.3 4.4 %collective-permute-done.22.refs_2_ = bf16[3,7,32,256]{3,2,1,0:T(8,128)(2,1)S(1)} collective-permute-done((bf16[3,7,32,256]{3,2,1,0:T(8,128)(2,1)S(1)}, bf16[3,7,32,256]{3,2,1,0:T(8,128)(2,1)S(1)}, u32[]{:S(2)}, u32[]{:S(2)}) %collective-permute-start.22) | collective-permute-done | bytes 344096 | tf_op jit(solution)/shard_map/ppermute | solution.py:536
  71.7 0.5 collective-permute-start.21
  72.2 1.4 %assemble.2.refs_7_ = bf16[27,256,256]{2,1,0:T(8,128)(2,1)} custom-call(bf16[4,7,32,256]{3,2,1,0:T(8,128)(2,1)S(1)} %stack.4.refs_0_, bf16[4,7,32,256]{3,2,1,0:T(8,128)(2,1)S(1)} %collective-permute-done.26.refs_1_, bf16[3,7,32,256]{3,2,1,0:T(8,128)(2,1)S(1)} %stack.5.refs_2_, bf16[3,7,32,256]{3,2,1,0:T(8,128)(2,1)S(1)} %collective-permute-done.27.refs_3_), custom_call_target="tpu_custom_call" | custom-call | flops 100000000 | bytes 100000 | tf_op jit(solution)/shard_map/assemble/pallas_call | solution.py:511
  73.6 0.2 collective-permute-done.21.refs_1_
  73.8 1.6 %assemble.3 = bf16[27,256,256]{2,1,0:T(8,128)(2,1)} custom-call(bf16[3,7,32,256]{3,2,1,0:T(8,128)(2,1)S(1)} %collective-permute-done.20.refs_0_, bf16[3,7,32,256]{3,2,1,0:T(8,128)(2,1)S(1)} %collective-permute-done.21.refs_1_, bf16[3,7,32,256]{3,2,1,0:T(8,128)(2,1)S(1)} %collective-permute-done.22.refs_2_, ...), custom_call_target="tpu_custom_call", output_to_operand_aliasing={{}: (7, {})} | custom-call | flops 100000000 | bytes 100000 | tf_op jit(solution)/shard_map/assemble/pallas_call | solution.py:511
  (33 shorter events, 0.3 us)
Async XLA Ops:
  2.8 12.3 %collective-permute-start.2 = (bf16[352,256]{1,0:T(8,128)(2,1)}, bf16[352,256]{1,0:T(8,128)(2,1)S(1)}, u32[]{:S(2)}, u32[]{:S(2)}) collective-permute-start(bf16[352,256]{1,0:T(8,128)(2,1)} %get-tuple-element.45), channel_id=1, source_target_pairs={{0,8},{4,12},{8,0},{12,4},{16,24},{20,28},{24,16},{28,20},{1,9},{5... | collective-permute-start | bytes 540680 | tf_op jit(solution)/shard_map/ppermute | solution.py:536
  5.8 10.2 %collective-permute-start.3 = (bf16[352,256]{1,0:T(8,128)(2,1)}, bf16[352,256]{1,0:T(8,128)(2,1)S(1)}, u32[]{:S(2)}, u32[]{:S(2)}) collective-permute-start(bf16[352,256]{1,0:T(8,128)(2,1)} %get-tuple-element.46), channel_id=1, source_target_pairs={{0,16},{4,20},{8,24},{12,28},{16,0},{20,4},{24,8},{28,12},{1,17},{... | collective-permute-start | bytes 540680 | tf_op jit(solution)/shard_map/ppermute | solution.py:536
  7.3 8.7 %collective-permute-start.4 = (bf16[352,256]{1,0:T(8,128)(2,1)}, bf16[352,256]{1,0:T(8,128)(2,1)S(1)}, u32[]{:S(2)}, u32[]{:S(2)}) collective-permute-start(bf16[352,256]{1,0:T(8,128)(2,1)} %get-tuple-element.47), channel_id=1, source_target_pairs={{0,24},{4,28},{8,16},{12,20},{16,8},{20,12},{24,0},{28,4},{1,25},{... | collective-permute-start | bytes 540680 | tf_op jit(solution)/shard_map/ppermute | solution.py:536
  7.3 4.5 %collective-permute-start = (bf16[64,256]{1,0:T(8,128)(2,1)}, bf16[64,256]{1,0:T(8,128)(2,1)S(1)}, u32[]{:S(2)}, u32[]{:S(2)}) collective-permute-start(bf16[64,256]{1,0:T(8,128)(2,1)} %get-tuple-element.38), channel_id=1, source_target_pairs={{0,1},{2,3},{1,0},{3,2},{4,5},{6,7},{5,4},{7,6},{8,9},{10,11},{9,8... | collective-permute-start | bytes 98312 | tf_op jit(solution)/shard_map/ppermute | solution.py:542
  9.3 2.5 %collective-permute-start.1 = (bf16[64,256]{1,0:T(8,128)(2,1)}, bf16[64,256]{1,0:T(8,128)(2,1)S(1)}, u32[]{:S(2)}, u32[]{:S(2)}) collective-permute-start(bf16[64,256]{1,0:T(8,128)(2,1)} %get-tuple-element.39), channel_id=1, source_target_pairs={{1,2},{2,1},{5,6},{6,5},{9,10},{10,9},{13,14},{14,13},{17,18},{18,... | collective-permute-start | bytes 98312 | tf_op jit(solution)/shard_map/ppermute | solution.py:542
  10.0 1.0 %copy-start.3 = (bf16[544,256]{1,0:T(8,128)(2,1)S(1)}, bf16[544,256]{1,0:T(8,128)(2,1)}, u32[]{:S(2)}) copy-start(bf16[544,256]{1,0:T(8,128)(2,1)} %get-tuple-element.36.pack_ref) | copy-start | bytes 835588
  11.8 20.7 %copy-start = (bf16[27,256,256]{2,1,0:T(8,128)(2,1)S(1)}, bf16[27,256,256]{2,1,0:T(8,128)(2,1)}, u32[]{:S(2)}) copy-start(bf16[27,256,256]{2,1,0:T(8,128)(2,1)} %w_ref.3) | copy-start | bytes 10616836
  11.9 6.0 %collective-permute-start.5 = (bf16[64,128]{1,0:T(8,128)(2,1)S(1)}, bf16[64,128]{1,0:T(8,128)(2,1)S(1)}, u32[]{:S(2)}, u32[]{:S(2)}) collective-permute-start(bf16[64,128]{1,0:T(8,128)(2,1)S(1)} %get-tuple-element.52), channel_id=1, source_target_pairs={{0,8},{4,12},{8,0},{12,4},{16,24},{20,28},{24,16},{28,20},{1,9},{5... | collective-permute-start | bytes 49160 | tf_op jit(solution)/shard_map/ppermute | solution.py:536
  13.5 4.4 %collective-permute-start.6 = (bf16[64,128]{1,0:T(8,128)(2,1)S(1)}, bf16[64,128]{1,0:T(8,128)(2,1)S(1)}, u32[]{:S(2)}, u32[]{:S(2)}) collective-permute-start(bf16[64,128]{1,0:T(8,128)(2,1)S(1)} %get-tuple-element.53), channel_id=1, source_target_pairs={{0,16},{4,20},{8,24},{12,28},{16,0},{20,4},{24,8},{28,12},{1,17},{... | collective-permute-start | bytes 49160 | tf_op jit(solution)/shard_map/ppermute | solution.py:536
  15.1 4.6 %collective-permute-start.7 = (bf16[64,128]{1,0:T(8,128)(2,1)S(1)}, bf16[64,128]{1,0:T(8,128)(2,1)S(1)}, u32[]{:S(2)}, u32[]{:S(2)}) collective-permute-start(bf16[64,128]{1,0:T(8,128)(2,1)S(1)} %get-tuple-element.54), channel_id=1, source_target_pairs={{0,24},{4,28},{8,16},{12,20},{16,8},{20,12},{24,0},{28,4},{1,25},{... | collective-permute-start | bytes 49160 | tf_op jit(solution)/shard_map/ppermute | solution.py:536
  21.9 2.5 %collective-permute-start.8 = (f32[28,32,256]{2,1,0:T(8,128)S(1)}, f32[28,32,256]{2,1,0:T(8,128)S(1)}, u32[]{:S(2)}, u32[]{:S(2)}) collective-permute-start(f32[28,32,256]{2,1,0:T(8,128)S(1)} %get-tuple-element.56), channel_id=1, source_target_pairs={{0,4},{4,0},{8,12},{12,8},{16,20},{20,16},{24,28},{28,24},{1,5},{5... | collective-permute-start | bytes 2752520 | tf_op jit(solution)/shard_map/ppermute | solution.py:536
  24.9 13.1 %collective-permute-start.9 = (s16[240,256]{1,0:T(8,128)(2,1)S(1)}, s16[240,256]{1,0:T(8,128)(2,1)S(1)}, u32[]{:S(2)}, u32[]{:S(2)}) collective-permute-start(s16[240,256]{1,0:T(8,128)(2,1)S(1)} %get-tuple-element.58), channel_id=1, source_target_pairs={{0,1},{1,0},{2,3},{3,2},{4,5},{5,4},{6,7},{7,6},{8,9},{9,8},{10,11... | collective-permute-start | bytes 368648 | tf_op jit(solution)/shard_map/ppermute | solution.py:536
  29.6 12.3 %collective-permute-start.10 = (s16[240,256]{1,0:T(8,128)(2,1)S(1)}, s16[240,256]{1,0:T(8,128)(2,1)S(1)}, u32[]{:S(2)}, u32[]{:S(2)}) collective-permute-start(s16[240,256]{1,0:T(8,128)(2,1)S(1)} %get-tuple-element.59), channel_id=1, source_target_pairs={{0,2},{1,3},{2,0},{3,1},{4,6},{5,7},{6,4},{7,5},{8,10},{9,11},{10,... | collective-permute-start | bytes 368648 | tf_op jit(solution)/shard_map/ppermute | solution.py:536
  31.1 10.8 %collective-permute-start.11 = (s16[240,256]{1,0:T(8,128)(2,1)S(1)}, s16[240,256]{1,0:T(8,128)(2,1)S(1)}, u32[]{:S(2)}, u32[]{:S(2)}) collective-permute-start(s16[240,256]{1,0:T(8,128)(2,1)S(1)} %get-tuple-element.60), channel_id=1, source_target_pairs={{0,3},{1,2},{2,1},{3,0},{4,7},{5,6},{6,5},{7,4},{8,11},{9,10},{10,... | collective-permute-start | bytes 368648 | tf_op jit(solution)/shard_map/ppermute | solution.py:536
  38.0 27.5 %copy-start.1 = (s32[1,64]{1,0:T(1,128)S(1)}, s32[1,64]{1,0:T(1,128)}, u32[]{:S(2)}) copy-start(s32[1,64]{1,0:T(1,128)} %up_ref.1) | copy-start | bytes 772
  38.0 27.5 %copy-start.2 = (s32[1,64]{1,0:T(1,128)S(1)}, s32[1,64]{1,0:T(1,128)}, u32[]{:S(2)}) copy-start(s32[1,64]{1,0:T(1,128)} %down_ref.1) | copy-start | bytes 772
  42.0 7.1 %collective-permute-start.16 = (bf16[7,32,256]{2,1,0:T(8,128)(2,1)S(1)}, bf16[7,32,256]{2,1,0:T(8,128)(2,1)S(1)}, u32[]{:S(2)}, u32[]{:S(2)}) collective-permute-start(bf16[7,32,256]{2,1,0:T(8,128)(2,1)S(1)} %total.1.after_ref.refs_0_), channel_id=1, source_target_pairs={{0,3},{1,2},{2,1},{3,0},{4,7},{5,6},{6,5},{7,4},{8,11},{9,10},{10,... | collective-permute-start | bytes 344072 | tf_op jit(solution)/shard_map/ppermute | solution.py:536
  44.6 10.3 %collective-permute-start.15 = (bf16[7,32,256]{2,1,0:T(8,128)(2,1)S(1)}, bf16[7,32,256]{2,1,0:T(8,128)(2,1)S(1)}, u32[]{:S(2)}, u32[]{:S(2)}) collective-permute-start(bf16[7,32,256]{2,1,0:T(8,128)(2,1)S(1)} %total.1.after_ref.refs_0_), channel_id=1, source_target_pairs={{0,2},{1,3},{2,0},{3,1},{4,6},{5,7},{6,4},{7,5},{8,10},{9,11},{10,... | collective-permute-start | bytes 344072 | tf_op jit(solution)/shard_map/ppermute | solution.py:536
  45.8 9.1 %collective-permute-start.14 = (bf16[7,32,256]{2,1,0:T(8,128)(2,1)S(1)}, bf16[7,32,256]{2,1,0:T(8,128)(2,1)S(1)}, u32[]{:S(2)}, u32[]{:S(2)}) collective-permute-start(bf16[7,32,256]{2,1,0:T(8,128)(2,1)S(1)} %total.1.after_ref.refs_0_), channel_id=1, source_target_pairs={{0,1},{1,0},{2,3},{3,2},{4,5},{5,4},{6,7},{7,6},{8,9},{9,8},{10,11... | collective-permute-start | bytes 344072 | tf_op jit(solution)/shard_map/ppermute | solution.py:536
  46.5 8.4 %collective-permute-start.19 = (bf16[7,32,256]{2,1,0:T(8,128)(2,1)S(1)}, bf16[7,32,256]{2,1,0:T(8,128)(2,1)S(1)}, u32[]{:S(2)}, u32[]{:S(2)}) collective-permute-start(bf16[7,32,256]{2,1,0:T(8,128)(2,1)S(1)} %total.1.after_ref.refs_0_), channel_id=1, source_target_pairs={{0,24},{4,28},{8,16},{12,20},{16,8},{20,12},{24,0},{28,4},{1,25},{... | collective-permute-start | bytes 344072 | tf_op jit(solution)/shard_map/ppermute | solution.py:536
  47.0 8.0 %collective-permute-start.18 = (bf16[7,32,256]{2,1,0:T(8,128)(2,1)S(1)}, bf16[7,32,256]{2,1,0:T(8,128)(2,1)S(1)}, u32[]{:S(2)}, u32[]{:S(2)}) collective-permute-start(bf16[7,32,256]{2,1,0:T(8,128)(2,1)S(1)} %total.1.after_ref.refs_0_), channel_id=1, source_target_pairs={{0,16},{4,20},{8,24},{12,28},{16,0},{20,4},{24,8},{28,12},{1,17},{... | collective-permute-start | bytes 344072 | tf_op jit(solution)/shard_map/ppermute | solution.py:536
  49.1 5.9 %collective-permute-start.17 = (bf16[7,32,256]{2,1,0:T(8,128)(2,1)S(1)}, bf16[7,32,256]{2,1,0:T(8,128)(2,1)S(1)}, u32[]{:S(2)}, u32[]{:S(2)}) collective-permute-start(bf16[7,32,256]{2,1,0:T(8,128)(2,1)S(1)} %total.1.after_ref.refs_0_), channel_id=1, source_target_pairs={{0,8},{4,12},{8,0},{12,4},{16,24},{20,28},{24,16},{28,20},{1,9},{5... | collective-permute-start | bytes 344072 | tf_op jit(solution)/shard_map/ppermute | solution.py:536
  55.0 12.2 %collective-permute-start.24 = (bf16[3,7,32,256]{3,2,1,0:T(8,128)(2,1)S(1)}, bf16[3,7,32,256]{3,2,1,0:T(8,128)(2,1)S(1)}, u32[]{:S(2)}, u32[]{:S(2)}) collective-permute-start(bf16[3,7,32,256]{3,2,1,0:T(8,128)(2,1)S(1)} %gate.1.after_ref.refs_1_), channel_id=1, source_target_pairs={{0,24},{4,28},{8,16},{12,20},{16,8},{20,12},{24,0},{28,4},{1,25},{... | collective-permute-start | bytes 1032200 | tf_op jit(solution)/shard_map/ppermute | solution.py:536
  55.5 16.1 %collective-permute-start.22 = (bf16[3,7,32,256]{3,2,1,0:T(8,128)(2,1)S(1)}, bf16[3,7,32,256]{3,2,1,0:T(8,128)(2,1)S(1)}, u32[]{:S(2)}, u32[]{:S(2)}) collective-permute-start(bf16[3,7,32,256]{3,2,1,0:T(8,128)(2,1)S(1)} %gate.1.after_ref.refs_1_), channel_id=1, source_target_pairs={{0,16},{4,20},{8,24},{12,28},{16,0},{20,4},{24,8},{28,12},{1,17},{... | collective-permute-start | bytes 1032200 | tf_op jit(solution)/shard_map/ppermute | solution.py:536
  57.0 14.6 %collective-permute-start.20 = (bf16[3,7,32,256]{3,2,1,0:T(8,128)(2,1)S(1)}, bf16[3,7,32,256]{3,2,1,0:T(8,128)(2,1)S(1)}, u32[]{:S(2)}, u32[]{:S(2)}) collective-permute-start(bf16[3,7,32,256]{3,2,1,0:T(8,128)(2,1)S(1)} %gate.1.after_ref.refs_1_), channel_id=1, source_target_pairs={{0,8},{4,12},{8,0},{12,4},{16,24},{20,28},{24,16},{28,20},{1,9},{5... | collective-permute-start | bytes 1032200 | tf_op jit(solution)/shard_map/ppermute | solution.py:536
  58.5 6.9 %collective-permute-start.12 = (f32[64,256]{1,0:T(8,128)S(1)}, f32[64,256]{1,0:T(8,128)S(1)}, u32[]{:S(2)}, u32[]{:S(2)}) collective-permute-start(f32[64,256]{1,0:T(8,128)S(1)} %get-tuple-element.64), channel_id=1, source_target_pairs={{0,1},{2,3},{1,0},{3,2},{4,5},{6,7},{5,4},{7,6},{8,9},{10,11},{9,8... | collective-permute-start | bytes 196616 | tf_op jit(solution)/shard_map/ppermute | solution.py:542
  63.2 2.2 %collective-permute-start.13 = (f32[64,256]{1,0:T(8,128)S(1)}, f32[64,256]{1,0:T(8,128)S(1)}, u32[]{:S(2)}, u32[]{:S(2)}) collective-permute-start(f32[64,256]{1,0:T(8,128)S(1)} %get-tuple-element.65), channel_id=1, source_target_pairs={{1,2},{2,1},{5,6},{6,5},{9,10},{10,9},{13,14},{14,13},{17,18},{18,... | collective-permute-start | bytes 196616 | tf_op jit(solution)/shard_map/ppermute | solution.py:542
  66.5 5.7 %collective-permute-start.26 = (bf16[4,7,32,256]{3,2,1,0:T(8,128)(2,1)S(1)}, bf16[4,7,32,256]{3,2,1,0:T(8,128)(2,1)S(1)}, u32[]{:S(2)}, u32[]{:S(2)}) collective-permute-start(bf16[4,7,32,256]{3,2,1,0:T(8,128)(2,1)S(1)} %stack.4.refs_0_), channel_id=1, source_target_pairs={{0,4},{4,0},{8,12},{12,8},{16,20},{20,16},{24,28},{28,24},{1,5},{5... | collective-permute-start | bytes 1376264 | tf_op jit(solution)/shard_map/ppermute | solution.py:536
  66.6 5.6 %collective-permute-start.27 = (bf16[3,7,32,256]{3,2,1,0:T(8,128)(2,1)S(1)}, bf16[3,7,32,256]{3,2,1,0:T(8,128)(2,1)S(1)}, u32[]{:S(2)}, u32[]{:S(2)}) collective-permute-start(bf16[3,7,32,256]{3,2,1,0:T(8,128)(2,1)S(1)} %stack.5.refs_2_), channel_id=1, source_target_pairs={{0,4},{4,0},{8,12},{12,8},{16,20},{20,16},{24,28},{28,24},{1,5},{5... | collective-permute-start | bytes 1032200 | tf_op jit(solution)/shard_map/ppermute | solution.py:536
  67.2 6.4 %collective-permute-start.25 = (bf16[3,7,32,256]{3,2,1,0:T(8,128)(2,1)S(1)}, bf16[3,7,32,256]{3,2,1,0:T(8,128)(2,1)S(1)}, u32[]{:S(2)}, u32[]{:S(2)}) collective-permute-start(bf16[3,7,32,256]{3,2,1,0:T(8,128)(2,1)S(1)} %collective-permute-done.24.refs_4_), channel_id=1, source_target_pairs={{0,4},{4,0},{8,12},{12,8},{16,20},{20,16},{24,28},{28,24},{1,5},{5... | collective-permute-start | bytes 1032200 | tf_op jit(solution)/shard_map/ppermute | solution.py:536
  71.6 1.9 %collective-permute-start.23 = (bf16[3,7,32,256]{3,2,1,0:T(8,128)(2,1)S(1)}, bf16[3,7,32,256]{3,2,1,0:T(8,128)(2,1)S(1)}, u32[]{:S(2)}, u32[]{:S(2)}) collective-permute-start(bf16[3,7,32,256]{3,2,1,0:T(8,128)(2,1)S(1)} %collective-permute-done.22.refs_2_), channel_id=1, source_target_pairs={{0,4},{4,0},{8,12},{12,8},{16,20},{20,16},{24,28},{28,24},{1,5},{5... | collective-permute-start | bytes 1032200 | tf_op jit(solution)/shard_map/ppermute | solution.py:536
  71.7 2.1 %collective-permute-start.21 = (bf16[3,7,32,256]{3,2,1,0:T(8,128)(2,1)S(1)}, bf16[3,7,32,256]{3,2,1,0:T(8,128)(2,1)S(1)}, u32[]{:S(2)}, u32[]{:S(2)}) collective-permute-start(bf16[3,7,32,256]{3,2,1,0:T(8,128)(2,1)S(1)} %collective-permute-done.20.refs_0_), channel_id=1, source_target_pairs={{0,4},{4,0},{8,12},{12,8},{16,20},{20,16},{24,28},{28,24},{1,5},{5... | collective-permute-start | bytes 1032200 | tf_op jit(solution)/shard_map/ppermute | solution.py:536

commit v9 on v8

--- a/solution.py
+++ b/solution.py
@@ -246,48 +246,73 @@
     )(*packs)
 
 
-def wgrad_kernel(sizes, *refs):
-    sets = [refs[3 * n : 3 * n + 3] for n in range(len(sizes))]
-    halos, (keep_ref, send_ref, picked) = refs[3 * len(sizes) : -3], refs[-3:]
-    count, half, width = keep_ref.shape
-    far = halos[0].shape[1]
-    offsets = sets[0][0].shape[0]
-    rows = sets[0][2].shape[2]
+def picked_rows(out_ref, part, j, near_ref, maps, i, halo_ref):
+    rows, half = maps.shape[2], near_ref.shape[1] // 2
+    chosen = chosen_slots(maps, i, j, rows, rows + halo_ref.shape[1], rows)
+    near = near_ref[j, :, i * rows : (i + 1) * rows].astype(F32)
+    value = (dot(halo_ref[...], chosen) + near).astype(BF)
+    for h in range(2):
+        out_ref[h, j * half : (j + 1) * half, part * rows : (part + 1) * rows] = value[h * half : (h + 1) * half]
+
+
+def clear_rest(out_ref, offsets, half):
+    _, size, columns = out_ref.shape
+    if offsets * half < size:
+        out_ref[:, offsets * half :] = jnp.zeros((2, size - offsets * half, columns), BF)
+
+
+def early_kernel(own_ref, own_maps, rest_ref, rest_maps, *refs):
+    halos, out_ref = refs[:-1], refs[-1]
+    offsets, slab, _ = own_ref.shape
+    for j in range(offsets):
+        for s, halo_ref in enumerate(halos):
+            near = (own_ref, own_maps, 0) if s == 0 else (rest_ref, rest_maps, s - 1)
+            picked_rows(out_ref, s, j, *near, halo_ref)
+    clear_rest(out_ref, offsets, slab // 2)
+
+
+def wgrad_early(own_set, rest_set, halos, count):
+    own, _, own_maps = own_set
+    rest, _, rest_maps = rest_set
+    _, slab, rows = own.shape
+    return pl.pallas_call(
+        early_kernel,
+        out_shape=jax.ShapeDtypeStruct((2, count * slab // 2, len(halos) * rows), BF),
+        in_specs=[VMEM] * (4 + len(halos)),
+        out_specs=VMEM,
+        compiler_params=params(),
+        cost_estimate=cost(),
+        name="wgrad_early",
+    )(own, own_maps, rest, rest_maps, *halos)
+
+
+def wgrad_kernel(early_ref, own_dys, rest_ref, rest_dys, rest_maps, halo_ref, keep_ref, send_ref, picked):
+    offsets, slab, _ = rest_ref.shape
+    last, rows = rest_maps.shape[0] - 1, rest_maps.shape[2]
     core = place()[1]
     for j in range(offsets):
-        s = 0
-        for (picked_ref, _, maps), size in zip(sets, sizes):
-            for i in range(size):
-                chosen = chosen_slots(maps, i, j, rows, rows + far, rows)
-                near = picked_ref[j, :, i * rows : (i + 1) * rows].astype(F32)
-                value = (dot(halos[s][...], chosen) + near).astype(BF)
-                for h in range(2):
-                    picked[h, j * half : (j + 1) * half, s * rows : (s + 1) * rows] = value[h * half : (h + 1) * half]
-                s += 1
-    picked[:, offsets * half :] = jnp.zeros((2, (count - offsets) * half, picked.shape[2]), BF)
+        picked_rows(picked, 0, j, rest_ref, rest_maps, last, halo_ref)
+    clear_rest(picked, offsets, slab // 2)
     for out_ref, h in ((send_ref, 1 - core), (keep_ref, core)):
-        total, s = 0.0, 0
-        for (_, dys, _), size in zip(sets, sizes):
-            total = total + dot(picked[h, :, s * rows : (s + size) * rows], dys[...])
-            s += size
+        total = dot(early_ref[h, :, 0:rows], own_dys[...]) + dot(early_ref[h, :, rows:], rest_dys[0 : last * rows])
+        total = total + dot(picked[h], rest_dys[last * rows :])
         out_ref[...] = total.reshape(out_ref.shape)
 
 
-def wgrad(sets, halos, count):
-    sizes = [maps.shape[0] for _, _, maps in sets]
-    _, slab, _ = sets[0][0].shape
-    columns = sum(picked.shape[2] for picked, _, _ in sets)
-    shape = jax.ShapeDtypeStruct((count, slab // 2, sets[0][1].shape[1]), F32)
-    return pl.pallas_call(
-        functools.partial(wgrad_kernel, sizes),
+def wgrad(early, own_set, rest_set, halo, count):
+    rest, rest_dys, rest_maps = rest_set
+    _, slab, _ = rest.shape
+    shape = jax.ShapeDtypeStruct((count, slab // 2, rest_dys.shape[1]), F32)
+    return pl.pallas_call(
+        wgrad_kernel,
         out_shape=(shape, shape),
-        in_specs=[VMEM] * (3 * len(sizes) + len(halos)),
+        in_specs=[VMEM] * 6,
         out_specs=(VMEM, VMEM),
-        scratch_shapes=[pltpu.VMEM((2, count * slab // 2, columns), BF)],
+        scratch_shapes=[pltpu.VMEM((2, count * slab // 2, rest_maps.shape[2]), BF)],
         compiler_params=params(),
         cost_estimate=cost(),
         name="wgrad",
-    )(*[array for one in sets for array in one], *halos)
+    )(early, own_set[1], rest, rest_dys, rest_maps, halo)
 
 
 def power(exponent):
@@ -559,8 +584,9 @@
     own_set = wgrad_own([own_part], offsets, slab, rows)
     halo_rows, own_halo, *halos = joined(met(first_rows, 0), met(second_rows, 1), groups, own_set[1])
     halos = [swap(part, "dp", 2 * m) for m, part in enumerate(halos, 1)]
-    sets = [own_set, wgrad_own(packs, offsets, slab, rows)]
-    keep, send = wgrad(sets, [own_halo, *halos], parts * count)
+    rest_set = wgrad_own(packs, offsets, slab, rows)
+    early = wgrad_early(own_set, rest_set, [own_halo, *halos[:-1]], parts * count)
+    keep, send = wgrad(early, own_set, rest_set, halos[-1], parts * count)
     mine, *coded = blocks(keep, swap(send, "dp", 1), parts)
     own_grad, first_grad, second_grad, token = backward(pack, weights, rows, halo, mine)
     first_back, second_back = met(first_grad, 0), met(second_grad, 1)

time: 76.4 us -> 75.6 us (0.990)
  starting transfers between devices: 35.9 us -> 35.1 us
    pallas_call x1 -> x2, Pallas kernels: 2.19 us -> 2.28 us  [the longest x1 1.38 us: wgrad(): pl.pallas_call(wgrad_kernel, out_shape=(shape, shape), in_specs=[VMEM] *...]
  transfers between devices with their start and end apart: 28 -> 28, of which waited for: 9 -> 10; matrix products, arithmetic and copies ran while one was open for 0% -> 0% of each run, Pallas kernels for 20% -> 21%
where the time goes in v9:
time: 75.6 us; the launch traced here: 75.4 us
  starting transfers between devices  35.1 us (46%)
  Pallas kernels  21.6 us (29%)
  waiting for transfers between devices  16.8 us (22%)
  between operations  1.03 us (1%)
  local copies, waits for them, and re-layouts  0.97 us (1%)
    ppermute x24, starting transfers between devices, swap(): lax.ppermute(value, axis, [(i, i ^ mask) for i in range(lax.axis_size(axi...  27.8 us
    ppermute x24, waiting for transfers between devices, swap(): lax.ppermute(value, axis, [(i, i ^ mask) for i in range(lax.axis_size(axi...  15.2 us
    ppermute x4, starting transfers between devices, met(): lax.ppermute(value, 'space', [(i, i + 1) for i in starts] + [(i + 1, i) f...  7.31 us
    pallas_call x1, Pallas kernels, backward(): pl.pallas_call(functools.partial(backward_kernel, group), out_shape=tuple...  5.46 us
    pallas_call x1, Pallas kernels, forward(): pl.pallas_call(functools.partial(forward_kernel, group), out_shape=(jax.S...  4.1 us
    pallas_call x2, Pallas kernels, assemble(): pl.pallas_call(functools.partial(assemble_kernel, marks, parts, groups),...  2.97 us
    pallas_call x2, Pallas kernels, wgrad_own(): pl.pallas_call(functools.partial(wgrad_own_kernel, offsets), out_shape=(j...  2.74 us
    pallas_call x1, Pallas kernels, prep(): pl.pallas_call(prep_kernel, out_shape=(jax.ShapeDtypeStruct((2 * rows + m...  2.12 us
  transfers between devices with their start and end apart: 28, of which 10 were waited for; matrix products, arithmetic and copies ran while one was open for 0% of the time, Pallas kernels for 21%

profile of v9, /device:TPU:0, one launch (start us, length us, event | category | flops | bytes accessed | tf_op | source)
XLA Modules:
  0.0 75.4 jit_solution(15742667243046565116)
XLA Ops:
  0.6 2.1 %prep.1 = (bf16[544,256]{1,0:T(8,128)(2,1)}, bf16[64,256]{1,0:T(8,128)(2,1)}, bf16[64,256]{1,0:T(8,128)(2,1)}, bf16[352,256]{1,0:T(8,128)(2,1)}, bf16[352,256]{1,0:T(8,128)(2,1)}, /*index=5*/bf16[352,256]{1,0:T(8,128)(2,1)}) custom-call(bf16[256,256]{1,0:T(8,128)(2,1)} %x_hbm.1, bf16[256,256]{1,0:T(8,128)(2,1)} %dy_hbm.1, s32[27,256]{1,0:T(8,128)} %map_hbm.1, ...), custom_call_target="tpu_custom_call" | custom-call | tf_op jit(solution)/shard_map/prep/pallas_call | solution.py:92
  2.8 3.0 %collective-permute-start.2 = (bf16[352,256]{1,0:T(8,128)(2,1)}, bf16[352,256]{1,0:T(8,128)(2,1)S(1)}, u32[]{:S(2)}, u32[]{:S(2)}) collective-permute-start(bf16[352,256]{1,0:T(8,128)(2,1)} %get-tuple-element.45), channel_id=1, source_target_pairs={{0,8},{4,12},{8,0},{12,4},{16,24},{20,28},{24,16},{28,20},{1,9},{5... | collective-permute-start | bytes 540680 | tf_op jit(solution)/shard_map/ppermute | solution.py:561
  5.8 1.5 %collective-permute-start.3 = (bf16[352,256]{1,0:T(8,128)(2,1)}, bf16[352,256]{1,0:T(8,128)(2,1)S(1)}, u32[]{:S(2)}, u32[]{:S(2)}) collective-permute-start(bf16[352,256]{1,0:T(8,128)(2,1)} %get-tuple-element.46), channel_id=1, source_target_pairs={{0,16},{4,20},{8,24},{12,28},{16,0},{20,4},{24,8},{28,12},{1,17},{... | collective-permute-start | bytes 540680 | tf_op jit(solution)/shard_map/ppermute | solution.py:561
  7.3 2.0 %collective-permute-start = (bf16[64,256]{1,0:T(8,128)(2,1)}, bf16[64,256]{1,0:T(8,128)(2,1)S(1)}, u32[]{:S(2)}, u32[]{:S(2)}) collective-permute-start(bf16[64,256]{1,0:T(8,128)(2,1)} %get-tuple-element.38), channel_id=1, source_target_pairs={{0,1},{2,3},{1,0},{3,2},{4,5},{6,7},{5,4},{7,6},{8,9},{10,11},{9,8... | collective-permute-start | bytes 98312 | tf_op jit(solution)/shard_map/ppermute | solution.py:567
  9.3 0.7 collective-permute-start.1
  10.0 0.9 %copy-done.3 = bf16[544,256]{1,0:T(8,128)(2,1)S(1)} copy-done((bf16[544,256]{1,0:T(8,128)(2,1)S(1)}, bf16[544,256]{1,0:T(8,128)(2,1)}, u32[]{:S(2)}) %copy-start.3) | copy-done | bytes 278552
  11.0 0.1 near_pack.1
  11.0 0.8 %wgrad_own.2 = (bf16[27,64,256]{2,1,0:T(8,128)(2,1)S(1)}, bf16[256,256]{1,0:T(8,128)(2,1)S(1)}, s32[1,32,256]{2,1,0:T(8,128)S(1)}) custom-call(bf16[352,256]{1,0:T(8,128)(2,1)S(1)} %get-tuple-element.40.refs_0_), custom_call_target="tpu_custom_call" | custom-call | flops 100000000 | bytes 100000 | tf_op jit(solution)/shard_map/wgrad_own/pallas_call | solution.py:234
  11.8 0.1 joined.1
  11.9 1.6 %collective-permute-start.5 = (bf16[64,128]{1,0:T(8,128)(2,1)S(1)}, bf16[64,128]{1,0:T(8,128)(2,1)S(1)}, u32[]{:S(2)}, u32[]{:S(2)}) collective-permute-start(bf16[64,128]{1,0:T(8,128)(2,1)S(1)} %get-tuple-element.51), channel_id=1, source_target_pairs={{0,8},{4,12},{8,0},{12,4},{16,24},{20,28},{24,16},{28,20},{1,9},{5... | collective-permute-start | bytes 49160 | tf_op jit(solution)/shard_map/ppermute | solution.py:561
  13.5 1.5 %collective-permute-start.6 = (bf16[64,128]{1,0:T(8,128)(2,1)S(1)}, bf16[64,128]{1,0:T(8,128)(2,1)S(1)}, u32[]{:S(2)}, u32[]{:S(2)}) collective-permute-start(bf16[64,128]{1,0:T(8,128)(2,1)S(1)} %get-tuple-element.52), channel_id=1, source_target_pairs={{0,16},{4,20},{8,24},{12,28},{16,0},{20,4},{24,8},{28,12},{1,17},{... | collective-permute-start | bytes 49160 | tf_op jit(solution)/shard_map/ppermute | solution.py:561
  15.1 0.4 collective-permute-start.7
  15.5 0.4 collective-permute-done.3.refs_1_
  15.9 2.0 %wgrad_own.3 = (bf16[27,64,768]{2,1,0:T(8,128)(2,1)S(1)}, bf16[768,256]{1,0:T(8,128)(2,1)S(1)}, s32[3,32,256]{2,1,0:T(8,128)S(1)}) custom-call(bf16[352,256]{1,0:T(8,128)(2,1)S(1)} %collective-permute-done.2.refs_0_, bf16[352,256]{1,0:T(8,128)(2,1)S(1)} %collective-permute-done.3.refs_1_, bf16[352,256]{1,0:T(8,128)(2,1)S(1)} %collective-permute-done.4.refs_2_), custom_call_target="tpu_custom_call" | custom-call | flops 100000000 | bytes 100000 | tf_op jit(solution)/shard_map/wgrad_own/pallas_call | solution.py:234
  17.9 0.9 %wgrad_early.1.early_ref = bf16[2,896,768]{2,1,0:T(8,128)(2,1)S(1)} custom-call(bf16[27,64,256]{2,1,0:T(8,128)(2,1)S(1)} %get-tuple-element.43.own_ref, s32[1,32,256]{2,1,0:T(8,128)S(1)} %get-tuple-element.44.own_maps, bf16[27,64,768]{2,1,0:T(8,128)(2,1)S(1)} %get-tuple-element.48.rest_ref, s32[3,32,256]{2,1,0:T(8,128)S(1)} %get-tuple-element.49.rest_maps, ...), custom_call_target="tpu_custom_call" | custom-call | flops 100000000 | bytes 100000 | tf_op jit(solution)/shard_map/wgrad_early/pallas_call | solution.py:278
  18.8 0.9 %collective-permute-done.7.halo_ref = bf16[64,128]{1,0:T(8,128)(2,1)S(1)} collective-permute-done((bf16[64,128]{1,0:T(8,128)(2,1)S(1)}, bf16[64,128]{1,0:T(8,128)(2,1)S(1)}, u32[]{:S(2)}, u32[]{:S(2)}) %collective-permute-start.7) | collective-permute-done | bytes 16416 | tf_op jit(solution)/shard_map/ppermute | solution.py:561
  19.7 1.4 %wgrad.1 = (f32[28,32,256]{2,1,0:T(8,128)S(1)}, f32[28,32,256]{2,1,0:T(8,128)S(1)}) custom-call(bf16[2,896,768]{2,1,0:T(8,128)(2,1)S(1)} %wgrad_early.1.early_ref, bf16[256,256]{1,0:T(8,128)(2,1)S(1)} %get-tuple-element.41.after_ref.own_dys, bf16[27,64,768]{2,1,0:T(8,128)(2,1)S(1)} %get-tuple-element.48.rest_ref, ...), custom_call_target="tpu_custom_call" | custom-call | flops 100000000 | bytes 100000 | tf_op jit(solution)/shard_map/wgrad/pallas_call | solution.py:306
  21.2 2.5 %collective-permute-done.8.got_ref = f32[28,32,256]{2,1,0:T(8,128)S(1)} collective-permute-done((f32[28,32,256]{2,1,0:T(8,128)S(1)}, f32[28,32,256]{2,1,0:T(8,128)S(1)}, u32[]{:S(2)}, u32[]{:S(2)}) %collective-permute-start.8) | collective-permute-done | bytes 917536 | tf_op jit(solution)/shard_map/ppermute | solution.py:561
  23.6 0.5 blocks.1
  24.1 4.7 %collective-permute-start.9 = (s16[240,256]{1,0:T(8,128)(2,1)S(1)}, s16[240,256]{1,0:T(8,128)(2,1)S(1)}, u32[]{:S(2)}, u32[]{:S(2)}) collective-permute-start(s16[240,256]{1,0:T(8,128)(2,1)S(1)} %get-tuple-element.58), channel_id=1, source_target_pairs={{0,1},{1,0},{2,3},{3,2},{4,5},{5,4},{6,7},{7,6},{8,9},{9,8},{10,11... | collective-permute-start | bytes 368648 | tf_op jit(solution)/shard_map/ppermute | solution.py:561
  28.8 1.5 %collective-permute-start.10 = (s16[240,256]{1,0:T(8,128)(2,1)S(1)}, s16[240,256]{1,0:T(8,128)(2,1)S(1)}, u32[]{:S(2)}, u32[]{:S(2)}) collective-permute-start(s16[240,256]{1,0:T(8,128)(2,1)S(1)} %get-tuple-element.59), channel_id=1, source_target_pairs={{0,2},{1,3},{2,0},{3,1},{4,6},{5,7},{6,4},{7,5},{8,10},{9,11},{10,... | collective-permute-start | bytes 368648 | tf_op jit(solution)/shard_map/ppermute | solution.py:561
  30.3 1.4 %collective-permute-start.11 = (s16[240,256]{1,0:T(8,128)(2,1)S(1)}, s16[240,256]{1,0:T(8,128)(2,1)S(1)}, u32[]{:S(2)}, u32[]{:S(2)}) collective-permute-start(s16[240,256]{1,0:T(8,128)(2,1)S(1)} %get-tuple-element.60), channel_id=1, source_target_pairs={{0,3},{1,2},{2,1},{3,0},{4,7},{5,6},{6,5},{7,4},{8,11},{9,10},{10,... | collective-permute-start | bytes 368648 | tf_op jit(solution)/shard_map/ppermute | solution.py:561
  31.7 5.5 %backward.1 = (f32[256,256]{1,0:T(8,128)S(1)}, f32[64,256]{1,0:T(8,128)S(1)}, f32[64,256]{1,0:T(8,128)S(1)}, f32[8,128]{1,0:T(8,128)S(1)}) custom-call(bf16[544,256]{1,0:T(8,128)(2,1)S(1)} %get-tuple-element.37.pack_ref, bf16[27,256,256]{2,1,0:T(8,128)(2,1)S(1)} %copy-done, f32[7,32,256]{2,1,0:T(8,128)S(1)} %get-tuple-element.57.after_ref.mine_ref), custom_call_target="tpu_custom_call" | custom-call | flops 100000000 | bytes 100000 | tf_op jit(solution)/shard_map/backward/pallas_call | solution.py:151
  37.2 3.9 %collective-permute-done.10.refs_1_ = s16[240,256]{1,0:T(8,128)(2,1)S(1)} collective-permute-done((s16[240,256]{1,0:T(8,128)(2,1)S(1)}, s16[240,256]{1,0:T(8,128)(2,1)S(1)}, u32[]{:S(2)}, u32[]{:S(2)}) %collective-permute-start.10) | collective-permute-done | bytes 122912 | tf_op jit(solution)/shard_map/ppermute | solution.py:561
  41.1 0.1 total.1.after_ref.refs_0_
  41.2 2.5 %collective-permute-start.16 = (bf16[7,32,256]{2,1,0:T(8,128)(2,1)S(1)}, bf16[7,32,256]{2,1,0:T(8,128)(2,1)S(1)}, u32[]{:S(2)}, u32[]{:S(2)}) collective-permute-start(bf16[7,32,256]{2,1,0:T(8,128)(2,1)S(1)} %total.1.after_ref.refs_0_), channel_id=1, source_target_pairs={{0,3},{1,2},{2,1},{3,0},{4,7},{5,6},{6,5},{7,4},{8,11},{9,10},{10,... | collective-permute-start | bytes 344072 | tf_op jit(solution)/shard_map/ppermute | solution.py:561
  43.8 1.2 %collective-permute-start.15 = (bf16[7,32,256]{2,1,0:T(8,128)(2,1)S(1)}, bf16[7,32,256]{2,1,0:T(8,128)(2,1)S(1)}, u32[]{:S(2)}, u32[]{:S(2)}) collective-permute-start(bf16[7,32,256]{2,1,0:T(8,128)(2,1)S(1)} %total.1.after_ref.refs_0_), channel_id=1, source_target_pairs={{0,2},{1,3},{2,0},{3,1},{4,6},{5,7},{6,4},{7,5},{8,10},{9,11},{10,... | collective-permute-start | bytes 344072 | tf_op jit(solution)/shard_map/ppermute | solution.py:561
  45.0 0.7 collective-permute-start.14
  45.7 1.2 %collective-permute-start.19 = (bf16[7,32,256]{2,1,0:T(8,128)(2,1)S(1)}, bf16[7,32,256]{2,1,0:T(8,128)(2,1)S(1)}, u32[]{:S(2)}, u32[]{:S(2)}) collective-permute-start(bf16[7,32,256]{2,1,0:T(8,128)(2,1)S(1)} %total.1.after_ref.refs_0_), channel_id=1, source_target_pairs={{0,24},{4,28},{8,16},{12,20},{16,8},{20,12},{24,0},{28,4},{1,25},{... | collective-permute-start | bytes 344072 | tf_op jit(solution)/shard_map/ppermute | solution.py:561
  46.9 0.8 %collective-permute-start.18 = (bf16[7,32,256]{2,1,0:T(8,128)(2,1)S(1)}, bf16[7,32,256]{2,1,0:T(8,128)(2,1)S(1)}, u32[]{:S(2)}, u32[]{:S(2)}) collective-permute-start(bf16[7,32,256]{2,1,0:T(8,128)(2,1)S(1)} %total.1.after_ref.refs_0_), channel_id=1, source_target_pairs={{0,16},{4,20},{8,24},{12,28},{16,0},{20,4},{24,8},{28,12},{1,17},{... | collective-permute-start | bytes 344072 | tf_op jit(solution)/shard_map/ppermute | solution.py:561
  47.7 0.6 collective-permute-done.16.refs_2_
  48.3 0.9 %collective-permute-start.17 = (bf16[7,32,256]{2,1,0:T(8,128)(2,1)S(1)}, bf16[7,32,256]{2,1,0:T(8,128)(2,1)S(1)}, u32[]{:S(2)}, u32[]{:S(2)}) collective-permute-start(bf16[7,32,256]{2,1,0:T(8,128)(2,1)S(1)} %total.1.after_ref.refs_0_), channel_id=1, source_target_pairs={{0,8},{4,12},{8,0},{12,4},{16,24},{20,28},{24,16},{28,20},{1,9},{5... | collective-permute-start | bytes 344072 | tf_op jit(solution)/shard_map/ppermute | solution.py:561
  49.2 4.1 %forward.1 = (bf16[256,256]{1,0:T(8,128)(2,1)}, f32[8,128]{1,0:T(8,128)S(1)}) custom-call(bf16[544,256]{1,0:T(8,128)(2,1)S(1)} %get-tuple-element.37.pack_ref, bf16[128,256]{1,0:T(8,128)(2,1)S(1)} %get-tuple-element.42.halo_ref, bf16[27,256,256]{2,1,0:T(8,128)(2,1)S(1)} %copy-done, bf16[7,32,256]{2,1,0:T(8,128)(2,1)S(1)} %total.1.after_ref.refs_0_), custom_call_target="tpu_custom_call" | custom-call | flops 100000000 | bytes 100000 | tf_op jit(solution)/shard_map/forward/pallas_call | solution.py:196
  53.3 0.8 %collective-permute-done.15.refs_1_ = bf16[7,32,256]{2,1,0:T(8,128)(2,1)S(1)} collective-permute-done((bf16[7,32,256]{2,1,0:T(8,128)(2,1)S(1)}, bf16[7,32,256]{2,1,0:T(8,128)(2,1)S(1)}, u32[]{:S(2)}, u32[]{:S(2)}) %collective-permute-start.15) | collective-permute-done | bytes 114720 | tf_op jit(solution)/shard_map/ppermute | solution.py:561
  54.2 1.3 %collective-permute-start.24 = (bf16[3,7,32,256]{3,2,1,0:T(8,128)(2,1)S(1)}, bf16[3,7,32,256]{3,2,1,0:T(8,128)(2,1)S(1)}, u32[]{:S(2)}, u32[]{:S(2)}) collective-permute-start(bf16[3,7,32,256]{3,2,1,0:T(8,128)(2,1)S(1)} %gate.1.after_ref.refs_1_), channel_id=1, source_target_pairs={{0,24},{4,28},{8,16},{12,20},{16,8},{20,12},{24,0},{28,4},{1,25},{... | collective-permute-start | bytes 1032200 | tf_op jit(solution)/shard_map/ppermute | solution.py:561
  55.5 0.8 %collective-permute-start.22 = (bf16[3,7,32,256]{3,2,1,0:T(8,128)(2,1)S(1)}, bf16[3,7,32,256]{3,2,1,0:T(8,128)(2,1)S(1)}, u32[]{:S(2)}, u32[]{:S(2)}) collective-permute-start(bf16[3,7,32,256]{3,2,1,0:T(8,128)(2,1)S(1)} %gate.1.after_ref.refs_1_), channel_id=1, source_target_pairs={{0,16},{4,20},{8,24},{12,28},{16,0},{20,4},{24,8},{28,12},{1,17},{... | collective-permute-start | bytes 1032200 | tf_op jit(solution)/shard_map/ppermute | solution.py:561
  56.2 1.5 %collective-permute-start.20 = (bf16[3,7,32,256]{3,2,1,0:T(8,128)(2,1)S(1)}, bf16[3,7,32,256]{3,2,1,0:T(8,128)(2,1)S(1)}, u32[]{:S(2)}, u32[]{:S(2)}) collective-permute-start(bf16[3,7,32,256]{3,2,1,0:T(8,128)(2,1)S(1)} %gate.1.after_ref.refs_1_), channel_id=1, source_target_pairs={{0,8},{4,12},{8,0},{12,4},{16,24},{20,28},{24,16},{28,20},{1,9},{5... | collective-permute-start | bytes 1032200 | tf_op jit(solution)/shard_map/ppermute | solution.py:561
  57.7 4.0 %collective-permute-start.12 = (f32[64,256]{1,0:T(8,128)S(1)}, f32[64,256]{1,0:T(8,128)S(1)}, u32[]{:S(2)}, u32[]{:S(2)}) collective-permute-start(f32[64,256]{1,0:T(8,128)S(1)} %get-tuple-element.64), channel_id=1, source_target_pairs={{0,1},{2,3},{1,0},{3,2},{4,5},{6,7},{5,4},{7,6},{8,9},{10,11},{9,8... | collective-permute-start | bytes 196616 | tf_op jit(solution)/shard_map/ppermute | solution.py:567
  61.7 0.7 collective-permute-start.13
  62.4 1.6 %collective-permute-done.12.first_ref = f32[64,256]{1,0:T(8,128)S(1)} collective-permute-done((f32[64,256]{1,0:T(8,128)S(1)}, f32[64,256]{1,0:T(8,128)S(1)}, u32[]{:S(2)}, u32[]{:S(2)}) %collective-permute-start.12) | collective-permute-done | bytes 65568 | tf_op jit(solution)/shard_map/ppermute | solution.py:567
  64.0 1.0 %final.1 = (bf16[256,256]{1,0:T(8,128)(2,1)}, f32[8,128]{1,0:T(8,128)S(1)}) custom-call(bf16[544,256]{1,0:T(8,128)(2,1)S(1)} %get-tuple-element.37.pack_ref, f32[256,256]{1,0:T(8,128)S(1)} %get-tuple-element.63.own_ref, f32[64,256]{1,0:T(8,128)S(1)} %collective-permute-done.12.first_ref, f32[64,256]{1,0:T(8,128)S(1)} %collective-permute-done.13.second_ref, ...), custom_call_target="tpu_custom_call" | custom-call | tf_op jit(solution)/shard_map/final/pallas_call | solution.py:461
  65.1 0.6 collective-permute-start.27
  65.6 0.5 collective-permute-done.24.refs_4_
  66.1 5.4 %collective-permute-done.22.refs_2_ = bf16[3,7,32,256]{3,2,1,0:T(8,128)(2,1)S(1)} collective-permute-done((bf16[3,7,32,256]{3,2,1,0:T(8,128)(2,1)S(1)}, bf16[3,7,32,256]{3,2,1,0:T(8,128)(2,1)S(1)}, u32[]{:S(2)}, u32[]{:S(2)}) %collective-permute-start.22) | collective-permute-done | bytes 344096 | tf_op jit(solution)/shard_map/ppermute | solution.py:561
  71.6 0.5 collective-permute-start.21
  72.1 1.4 %assemble.2.refs_7_ = bf16[27,256,256]{2,1,0:T(8,128)(2,1)} custom-call(bf16[4,7,32,256]{3,2,1,0:T(8,128)(2,1)S(1)} %stack.4.refs_0_, bf16[4,7,32,256]{3,2,1,0:T(8,128)(2,1)S(1)} %collective-permute-done.26.refs_1_, bf16[3,7,32,256]{3,2,1,0:T(8,128)(2,1)S(1)} %stack.5.refs_2_, bf16[3,7,32,256]{3,2,1,0:T(8,128)(2,1)S(1)} %collective-permute-done.27.refs_3_), custom_call_target="tpu_custom_call" | custom-call | flops 100000000 | bytes 100000 | tf_op jit(solution)/shard_map/assemble/pallas_call | solution.py:536
  73.5 0.2 collective-permute-done.21.refs_1_
  73.7 1.6 %assemble.3 = bf16[27,256,256]{2,1,0:T(8,128)(2,1)} custom-call(bf16[3,7,32,256]{3,2,1,0:T(8,128)(2,1)S(1)} %collective-permute-done.20.refs_0_, bf16[3,7,32,256]{3,2,1,0:T(8,128)(2,1)S(1)} %collective-permute-done.21.refs_1_, bf16[3,7,32,256]{3,2,1,0:T(8,128)(2,1)S(1)} %collective-permute-done.22.refs_2_, ...), custom_call_target="tpu_custom_call", output_to_operand_aliasing={{}: (7, {})} | custom-call | flops 100000000 | bytes 100000 | tf_op jit(solution)/shard_map/assemble/pallas_call | solution.py:536
  (34 shorter events, 0.3 us)
Async XLA Ops:
  2.8 12.3 %collective-permute-start.2 = (bf16[352,256]{1,0:T(8,128)(2,1)}, bf16[352,256]{1,0:T(8,128)(2,1)S(1)}, u32[]{:S(2)}, u32[]{:S(2)}) collective-permute-start(bf16[352,256]{1,0:T(8,128)(2,1)} %get-tuple-element.45), channel_id=1, source_target_pairs={{0,8},{4,12},{8,0},{12,4},{16,24},{20,28},{24,16},{28,20},{1,9},{5... | collective-permute-start | bytes 540680 | tf_op jit(solution)/shard_map/ppermute | solution.py:561
  5.8 10.2 %collective-permute-start.3 = (bf16[352,256]{1,0:T(8,128)(2,1)}, bf16[352,256]{1,0:T(8,128)(2,1)S(1)}, u32[]{:S(2)}, u32[]{:S(2)}) collective-permute-start(bf16[352,256]{1,0:T(8,128)(2,1)} %get-tuple-element.46), channel_id=1, source_target_pairs={{0,16},{4,20},{8,24},{12,28},{16,0},{20,4},{24,8},{28,12},{1,17},{... | collective-permute-start | bytes 540680 | tf_op jit(solution)/shard_map/ppermute | solution.py:561
  7.3 8.7 %collective-permute-start.4 = (bf16[352,256]{1,0:T(8,128)(2,1)}, bf16[352,256]{1,0:T(8,128)(2,1)S(1)}, u32[]{:S(2)}, u32[]{:S(2)}) collective-permute-start(bf16[352,256]{1,0:T(8,128)(2,1)} %get-tuple-element.47), channel_id=1, source_target_pairs={{0,24},{4,28},{8,16},{12,20},{16,8},{20,12},{24,0},{28,4},{1,25},{... | collective-permute-start | bytes 540680 | tf_op jit(solution)/shard_map/ppermute | solution.py:561
  7.3 4.5 %collective-permute-start = (bf16[64,256]{1,0:T(8,128)(2,1)}, bf16[64,256]{1,0:T(8,128)(2,1)S(1)}, u32[]{:S(2)}, u32[]{:S(2)}) collective-permute-start(bf16[64,256]{1,0:T(8,128)(2,1)} %get-tuple-element.38), channel_id=1, source_target_pairs={{0,1},{2,3},{1,0},{3,2},{4,5},{6,7},{5,4},{7,6},{8,9},{10,11},{9,8... | collective-permute-start | bytes 98312 | tf_op jit(solution)/shard_map/ppermute | solution.py:567
  9.3 2.5 %collective-permute-start.1 = (bf16[64,256]{1,0:T(8,128)(2,1)}, bf16[64,256]{1,0:T(8,128)(2,1)S(1)}, u32[]{:S(2)}, u32[]{:S(2)}) collective-permute-start(bf16[64,256]{1,0:T(8,128)(2,1)} %get-tuple-element.39), channel_id=1, source_target_pairs={{1,2},{2,1},{5,6},{6,5},{9,10},{10,9},{13,14},{14,13},{17,18},{18,... | collective-permute-start | bytes 98312 | tf_op jit(solution)/shard_map/ppermute | solution.py:567
  10.0 1.0 %copy-start.3 = (bf16[544,256]{1,0:T(8,128)(2,1)S(1)}, bf16[544,256]{1,0:T(8,128)(2,1)}, u32[]{:S(2)}) copy-start(bf16[544,256]{1,0:T(8,128)(2,1)} %get-tuple-element.36.pack_ref) | copy-start | bytes 835588
  11.9 6.0 %collective-permute-start.5 = (bf16[64,128]{1,0:T(8,128)(2,1)S(1)}, bf16[64,128]{1,0:T(8,128)(2,1)S(1)}, u32[]{:S(2)}, u32[]{:S(2)}) collective-permute-start(bf16[64,128]{1,0:T(8,128)(2,1)S(1)} %get-tuple-element.51), channel_id=1, source_target_pairs={{0,8},{4,12},{8,0},{12,4},{16,24},{20,28},{24,16},{28,20},{1,9},{5... | collective-permute-start | bytes 49160 | tf_op jit(solution)/shard_map/ppermute | solution.py:561
  13.5 4.4 %collective-permute-start.6 = (bf16[64,128]{1,0:T(8,128)(2,1)S(1)}, bf16[64,128]{1,0:T(8,128)(2,1)S(1)}, u32[]{:S(2)}, u32[]{:S(2)}) collective-permute-start(bf16[64,128]{1,0:T(8,128)(2,1)S(1)} %get-tuple-element.52), channel_id=1, source_target_pairs={{0,16},{4,20},{8,24},{12,28},{16,0},{20,4},{24,8},{28,12},{1,17},{... | collective-permute-start | bytes 49160 | tf_op jit(solution)/shard_map/ppermute | solution.py:561
  15.1 4.6 %collective-permute-start.7 = (bf16[64,128]{1,0:T(8,128)(2,1)S(1)}, bf16[64,128]{1,0:T(8,128)(2,1)S(1)}, u32[]{:S(2)}, u32[]{:S(2)}) collective-permute-start(bf16[64,128]{1,0:T(8,128)(2,1)S(1)} %get-tuple-element.54), channel_id=1, source_target_pairs={{0,24},{4,28},{8,16},{12,20},{16,8},{20,12},{24,0},{28,4},{1,25},{... | collective-permute-start | bytes 49160 | tf_op jit(solution)/shard_map/ppermute | solution.py:561
  19.7 12.0 %copy-start = (bf16[27,256,256]{2,1,0:T(8,128)(2,1)S(1)}, bf16[27,256,256]{2,1,0:T(8,128)(2,1)}, u32[]{:S(2)}) copy-start(bf16[27,256,256]{2,1,0:T(8,128)(2,1)} %w_ref.3) | copy-start | bytes 10616836
  21.1 2.5 %collective-permute-start.8 = (f32[28,32,256]{2,1,0:T(8,128)S(1)}, f32[28,32,256]{2,1,0:T(8,128)S(1)}, u32[]{:S(2)}, u32[]{:S(2)}) collective-permute-start(f32[28,32,256]{2,1,0:T(8,128)S(1)} %get-tuple-element.56), channel_id=1, source_target_pairs={{0,4},{4,0},{8,12},{12,8},{16,20},{20,16},{24,28},{28,24},{1,5},{5... | collective-permute-start | bytes 2752520 | tf_op jit(solution)/shard_map/ppermute | solution.py:561
  24.1 13.1 %collective-permute-start.9 = (s16[240,256]{1,0:T(8,128)(2,1)S(1)}, s16[240,256]{1,0:T(8,128)(2,1)S(1)}, u32[]{:S(2)}, u32[]{:S(2)}) collective-permute-start(s16[240,256]{1,0:T(8,128)(2,1)S(1)} %get-tuple-element.58), channel_id=1, source_target_pairs={{0,1},{1,0},{2,3},{3,2},{4,5},{5,4},{6,7},{7,6},{8,9},{9,8},{10,11... | collective-permute-start | bytes 368648 | tf_op jit(solution)/shard_map/ppermute | solution.py:561
  28.8 12.3 %collective-permute-start.10 = (s16[240,256]{1,0:T(8,128)(2,1)S(1)}, s16[240,256]{1,0:T(8,128)(2,1)S(1)}, u32[]{:S(2)}, u32[]{:S(2)}) collective-permute-start(s16[240,256]{1,0:T(8,128)(2,1)S(1)} %get-tuple-element.59), channel_id=1, source_target_pairs={{0,2},{1,3},{2,0},{3,1},{4,6},{5,7},{6,4},{7,5},{8,10},{9,11},{10,... | collective-permute-start | bytes 368648 | tf_op jit(solution)/shard_map/ppermute | solution.py:561
  30.3 10.8 %collective-permute-start.11 = (s16[240,256]{1,0:T(8,128)(2,1)S(1)}, s16[240,256]{1,0:T(8,128)(2,1)S(1)}, u32[]{:S(2)}, u32[]{:S(2)}) collective-permute-start(s16[240,256]{1,0:T(8,128)(2,1)S(1)} %get-tuple-element.60), channel_id=1, source_target_pairs={{0,3},{1,2},{2,1},{3,0},{4,7},{5,6},{6,5},{7,4},{8,11},{9,10},{10,... | collective-permute-start | bytes 368648 | tf_op jit(solution)/shard_map/ppermute | solution.py:561
  37.2 26.8 %copy-start.1 = (s32[1,64]{1,0:T(1,128)S(1)}, s32[1,64]{1,0:T(1,128)}, u32[]{:S(2)}) copy-start(s32[1,64]{1,0:T(1,128)} %up_ref.1) | copy-start | bytes 772
  37.2 26.8 %copy-start.2 = (s32[1,64]{1,0:T(1,128)S(1)}, s32[1,64]{1,0:T(1,128)}, u32[]{:S(2)}) copy-start(s32[1,64]{1,0:T(1,128)} %down_ref.1) | copy-start | bytes 772
  41.2 7.0 %collective-permute-start.16 = (bf16[7,32,256]{2,1,0:T(8,128)(2,1)S(1)}, bf16[7,32,256]{2,1,0:T(8,128)(2,1)S(1)}, u32[]{:S(2)}, u32[]{:S(2)}) collective-permute-start(bf16[7,32,256]{2,1,0:T(8,128)(2,1)S(1)} %total.1.after_ref.refs_0_), channel_id=1, source_target_pairs={{0,3},{1,2},{2,1},{3,0},{4,7},{5,6},{6,5},{7,4},{8,11},{9,10},{10,... | collective-permute-start | bytes 344072 | tf_op jit(solution)/shard_map/ppermute | solution.py:561
  43.8 10.3 %collective-permute-start.15 = (bf16[7,32,256]{2,1,0:T(8,128)(2,1)S(1)}, bf16[7,32,256]{2,1,0:T(8,128)(2,1)S(1)}, u32[]{:S(2)}, u32[]{:S(2)}) collective-permute-start(bf16[7,32,256]{2,1,0:T(8,128)(2,1)S(1)} %total.1.after_ref.refs_0_), channel_id=1, source_target_pairs={{0,2},{1,3},{2,0},{3,1},{4,6},{5,7},{6,4},{7,5},{8,10},{9,11},{10,... | collective-permute-start | bytes 344072 | tf_op jit(solution)/shard_map/ppermute | solution.py:561
  45.0 9.1 %collective-permute-start.14 = (bf16[7,32,256]{2,1,0:T(8,128)(2,1)S(1)}, bf16[7,32,256]{2,1,0:T(8,128)(2,1)S(1)}, u32[]{:S(2)}, u32[]{:S(2)}) collective-permute-start(bf16[7,32,256]{2,1,0:T(8,128)(2,1)S(1)} %total.1.after_ref.refs_0_), channel_id=1, source_target_pairs={{0,1},{1,0},{2,3},{3,2},{4,5},{5,4},{6,7},{7,6},{8,9},{9,8},{10,11... | collective-permute-start | bytes 344072 | tf_op jit(solution)/shard_map/ppermute | solution.py:561
  45.7 8.4 %collective-permute-start.19 = (bf16[7,32,256]{2,1,0:T(8,128)(2,1)S(1)}, bf16[7,32,256]{2,1,0:T(8,128)(2,1)S(1)}, u32[]{:S(2)}, u32[]{:S(2)}) collective-permute-start(bf16[7,32,256]{2,1,0:T(8,128)(2,1)S(1)} %total.1.after_ref.refs_0_), channel_id=1, source_target_pairs={{0,24},{4,28},{8,16},{12,20},{16,8},{20,12},{24,0},{28,4},{1,25},{... | collective-permute-start | bytes 344072 | tf_op jit(solution)/shard_map/ppermute | solution.py:561
  46.9 7.2 %collective-permute-start.18 = (bf16[7,32,256]{2,1,0:T(8,128)(2,1)S(1)}, bf16[7,32,256]{2,1,0:T(8,128)(2,1)S(1)}, u32[]{:S(2)}, u32[]{:S(2)}) collective-permute-start(bf16[7,32,256]{2,1,0:T(8,128)(2,1)S(1)} %total.1.after_ref.refs_0_), channel_id=1, source_target_pairs={{0,16},{4,20},{8,24},{12,28},{16,0},{20,4},{24,8},{28,12},{1,17},{... | collective-permute-start | bytes 344072 | tf_op jit(solution)/shard_map/ppermute | solution.py:561
  48.3 5.9 %collective-permute-start.17 = (bf16[7,32,256]{2,1,0:T(8,128)(2,1)S(1)}, bf16[7,32,256]{2,1,0:T(8,128)(2,1)S(1)}, u32[]{:S(2)}, u32[]{:S(2)}) collective-permute-start(bf16[7,32,256]{2,1,0:T(8,128)(2,1)S(1)} %total.1.after_ref.refs_0_), channel_id=1, source_target_pairs={{0,8},{4,12},{8,0},{12,4},{16,24},{20,28},{24,16},{28,20},{1,9},{5... | collective-permute-start | bytes 344072 | tf_op jit(solution)/shard_map/ppermute | solution.py:561
  54.2 12.0 %collective-permute-start.24 = (bf16[3,7,32,256]{3,2,1,0:T(8,128)(2,1)S(1)}, bf16[3,7,32,256]{3,2,1,0:T(8,128)(2,1)S(1)}, u32[]{:S(2)}, u32[]{:S(2)}) collective-permute-start(bf16[3,7,32,256]{3,2,1,0:T(8,128)(2,1)S(1)} %gate.1.after_ref.refs_1_), channel_id=1, source_target_pairs={{0,24},{4,28},{8,16},{12,20},{16,8},{20,12},{24,0},{28,4},{1,25},{... | collective-permute-start | bytes 1032200 | tf_op jit(solution)/shard_map/ppermute | solution.py:561
  55.5 16.1 %collective-permute-start.22 = (bf16[3,7,32,256]{3,2,1,0:T(8,128)(2,1)S(1)}, bf16[3,7,32,256]{3,2,1,0:T(8,128)(2,1)S(1)}, u32[]{:S(2)}, u32[]{:S(2)}) collective-permute-start(bf16[3,7,32,256]{3,2,1,0:T(8,128)(2,1)S(1)} %gate.1.after_ref.refs_1_), channel_id=1, source_target_pairs={{0,16},{4,20},{8,24},{12,28},{16,0},{20,4},{24,8},{28,12},{1,17},{... | collective-permute-start | bytes 1032200 | tf_op jit(solution)/shard_map/ppermute | solution.py:561
  56.2 15.3 %collective-permute-start.20 = (bf16[3,7,32,256]{3,2,1,0:T(8,128)(2,1)S(1)}, bf16[3,7,32,256]{3,2,1,0:T(8,128)(2,1)S(1)}, u32[]{:S(2)}, u32[]{:S(2)}) collective-permute-start(bf16[3,7,32,256]{3,2,1,0:T(8,128)(2,1)S(1)} %gate.1.after_ref.refs_1_), channel_id=1, source_target_pairs={{0,8},{4,12},{8,0},{12,4},{16,24},{20,28},{24,16},{28,20},{1,9},{5... | collective-permute-start | bytes 1032200 | tf_op jit(solution)/shard_map/ppermute | solution.py:561
  57.7 6.2 %collective-permute-start.12 = (f32[64,256]{1,0:T(8,128)S(1)}, f32[64,256]{1,0:T(8,128)S(1)}, u32[]{:S(2)}, u32[]{:S(2)}) collective-permute-start(f32[64,256]{1,0:T(8,128)S(1)} %get-tuple-element.64), channel_id=1, source_target_pairs={{0,1},{2,3},{1,0},{3,2},{4,5},{6,7},{5,4},{7,6},{8,9},{10,11},{9,8... | collective-permute-start | bytes 196616 | tf_op jit(solution)/shard_map/ppermute | solution.py:567
  61.7 2.2 %collective-permute-start.13 = (f32[64,256]{1,0:T(8,128)S(1)}, f32[64,256]{1,0:T(8,128)S(1)}, u32[]{:S(2)}, u32[]{:S(2)}) collective-permute-start(f32[64,256]{1,0:T(8,128)S(1)} %get-tuple-element.65), channel_id=1, source_target_pairs={{1,2},{2,1},{5,6},{6,5},{9,10},{10,9},{13,14},{14,13},{17,18},{18,... | collective-permute-start | bytes 196616 | tf_op jit(solution)/shard_map/ppermute | solution.py:567
  65.0 7.1 %collective-permute-start.26 = (bf16[4,7,32,256]{3,2,1,0:T(8,128)(2,1)S(1)}, bf16[4,7,32,256]{3,2,1,0:T(8,128)(2,1)S(1)}, u32[]{:S(2)}, u32[]{:S(2)}) collective-permute-start(bf16[4,7,32,256]{3,2,1,0:T(8,128)(2,1)S(1)} %stack.4.refs_0_), channel_id=1, source_target_pairs={{0,4},{4,0},{8,12},{12,8},{16,20},{20,16},{24,28},{28,24},{1,5},{5... | collective-permute-start | bytes 1376264 | tf_op jit(solution)/shard_map/ppermute | solution.py:561
  65.1 7.0 %collective-permute-start.27 = (bf16[3,7,32,256]{3,2,1,0:T(8,128)(2,1)S(1)}, bf16[3,7,32,256]{3,2,1,0:T(8,128)(2,1)S(1)}, u32[]{:S(2)}, u32[]{:S(2)}) collective-permute-start(bf16[3,7,32,256]{3,2,1,0:T(8,128)(2,1)S(1)} %stack.5.refs_2_), channel_id=1, source_target_pairs={{0,4},{4,0},{8,12},{12,8},{16,20},{20,16},{24,28},{28,24},{1,5},{5... | collective-permute-start | bytes 1032200 | tf_op jit(solution)/shard_map/ppermute | solution.py:561
  66.1 7.3 %collective-permute-start.25 = (bf16[3,7,32,256]{3,2,1,0:T(8,128)(2,1)S(1)}, bf16[3,7,32,256]{3,2,1,0:T(8,128)(2,1)S(1)}, u32[]{:S(2)}, u32[]{:S(2)}) collective-permute-start(bf16[3,7,32,256]{3,2,1,0:T(8,128)(2,1)S(1)} %collective-permute-done.24.refs_4_), channel_id=1, source_target_pairs={{0,4},{4,0},{8,12},{12,8},{16,20},{20,16},{24,28},{28,24},{1,5},{5... | collective-permute-start | bytes 1032200 | tf_op jit(solution)/shard_map/ppermute | solution.py:561
  71.6 1.9 %collective-permute-start.23 = (bf16[3,7,32,256]{3,2,1,0:T(8,128)(2,1)S(1)}, bf16[3,7,32,256]{3,2,1,0:T(8,128)(2,1)S(1)}, u32[]{:S(2)}, u32[]{:S(2)}) collective-permute-start(bf16[3,7,32,256]{3,2,1,0:T(8,128)(2,1)S(1)} %collective-permute-done.22.refs_2_), channel_id=1, source_target_pairs={{0,4},{4,0},{8,12},{12,8},{16,20},{20,16},{24,28},{28,24},{1,5},{5... | collective-permute-start | bytes 1032200 | tf_op jit(solution)/shard_map/ppermute | solution.py:561
  71.6 2.1 %collective-permute-start.21 = (bf16[3,7,32,256]{3,2,1,0:T(8,128)(2,1)S(1)}, bf16[3,7,32,256]{3,2,1,0:T(8,128)(2,1)S(1)}, u32[]{:S(2)}, u32[]{:S(2)}) collective-permute-start(bf16[3,7,32,256]{3,2,1,0:T(8,128)(2,1)S(1)} %collective-permute-done.20.refs_0_), channel_id=1, source_target_pairs={{0,4},{4,0},{8,12},{12,8},{16,20},{20,16},{24,28},{28,24},{1,5},{5... | collective-permute-start | bytes 1032200 | tf_op jit(solution)/shard_map/ppermute | solution.py:561

commit v10 on v9

--- a/solution.py
+++ b/solution.py
@@ -286,33 +286,50 @@
     )(own, own_maps, rest, rest_maps, *halos)
 
 
-def wgrad_kernel(early_ref, own_dys, rest_ref, rest_dys, rest_maps, halo_ref, keep_ref, send_ref, picked):
+def half_sum(early_ref, own_dys, rest_dys, picked_ref, h):
+    rows = own_dys.shape[0]
+    last = rest_dys.shape[0] - rows
+    total = dot(early_ref[h, :, 0:rows], own_dys[...]) + dot(early_ref[h, :, rows:], rest_dys[0:last])
+    return total + dot(picked_ref[h], rest_dys[last:])
+
+
+def send_kernel(early_ref, own_dys, rest_ref, rest_dys, rest_maps, halo_ref, send_ref, picked_ref):
     offsets, slab, _ = rest_ref.shape
-    last, rows = rest_maps.shape[0] - 1, rest_maps.shape[2]
-    core = place()[1]
     for j in range(offsets):
-        picked_rows(picked, 0, j, rest_ref, rest_maps, last, halo_ref)
-    clear_rest(picked, offsets, slab // 2)
-    for out_ref, h in ((send_ref, 1 - core), (keep_ref, core)):
-        total = dot(early_ref[h, :, 0:rows], own_dys[...]) + dot(early_ref[h, :, rows:], rest_dys[0 : last * rows])
-        total = total + dot(picked[h], rest_dys[last * rows :])
-        out_ref[...] = total.reshape(out_ref.shape)
+        picked_rows(picked_ref, 0, j, rest_ref, rest_maps, rest_maps.shape[0] - 1, halo_ref)
+    clear_rest(picked_ref, offsets, slab // 2)
+    total = half_sum(early_ref, own_dys, rest_dys, picked_ref, 1 - place()[1])
+    send_ref[...] = total.reshape(send_ref.shape)
+
+
+def keep_kernel(early_ref, own_dys, rest_dys, picked_ref, after_ref, keep_ref):
+    total = half_sum(early_ref, own_dys, rest_dys, picked_ref, place()[1])
+    keep_ref[...] = total.reshape(keep_ref.shape)
 
 
 def wgrad(early, own_set, rest_set, halo, count):
     rest, rest_dys, rest_maps = rest_set
     _, slab, _ = rest.shape
     shape = jax.ShapeDtypeStruct((count, slab // 2, rest_dys.shape[1]), F32)
-    return pl.pallas_call(
-        wgrad_kernel,
-        out_shape=(shape, shape),
+    send, picked = pl.pallas_call(
+        send_kernel,
+        out_shape=(shape, jax.ShapeDtypeStruct((2, count * slab // 2, rest_maps.shape[2]), BF)),
         in_specs=[VMEM] * 6,
         out_specs=(VMEM, VMEM),
-        scratch_shapes=[pltpu.VMEM((2, count * slab // 2, rest_maps.shape[2]), BF)],
-        compiler_params=params(),
-        cost_estimate=cost(),
-        name="wgrad",
+        compiler_params=params(),
+        cost_estimate=cost(),
+        name="wgrad_send",
     )(early, own_set[1], rest, rest_dys, rest_maps, halo)
+    keep = pl.pallas_call(
+        keep_kernel,
+        out_shape=shape,
+        in_specs=[VMEM] * 4 + [ANY],
+        out_specs=VMEM,
+        compiler_params=params(),
+        cost_estimate=cost(),
+        name="wgrad_keep",
+    )(early, own_set[1], rest_dys, picked, send)
+    return keep, send
 
 
 def power(exponent):

time: 75.6 us -> 75.1 us (level)
    pallas_call x1 -> x2, Pallas kernels: 1.38 us -> 1.56 us  [the longest x1 0.91 us: wgrad(): pl.pallas_call(send_kernel, out_shape=(shape, jax.ShapeDtypeStruct((2, co...]
  transfers between devices with their start and end apart: 28 -> 28, of which waited for: 10 -> 10; matrix products, arithmetic and copies ran while one was open for 0% -> 0% of each run, Pallas kernels for 21% -> 22%
where the time goes in v10:
time: 75.1 us; the launch traced here: 74.9 us
  starting transfers between devices  35.1 us (47%)
  Pallas kernels  21.8 us (29%)
  waiting for transfers between devices  16.1 us (21%)
  between operations  1.04 us (1%)
  local copies, waits for them, and re-layouts  0.97 us (1%)
    ppermute x24, starting transfers between devices, swap(): lax.ppermute(value, axis, [(i, i ^ mask) for i in range(lax.axis_size(axi...  27.7 us
    ppermute x24, waiting for transfers between devices, swap(): lax.ppermute(value, axis, [(i, i ^ mask) for i in range(lax.axis_size(axi...  14.5 us
    ppermute x4, starting transfers between devices, met(): lax.ppermute(value, 'space', [(i, i + 1) for i in starts] + [(i + 1, i) f...  7.34 us
    pallas_call x1, Pallas kernels, backward(): pl.pallas_call(functools.partial(backward_kernel, group), out_shape=tuple...  5.47 us
    pallas_call x1, Pallas kernels, forward(): pl.pallas_call(functools.partial(forward_kernel, group), out_shape=(jax.S...  4.11 us
    pallas_call x2, Pallas kernels, assemble(): pl.pallas_call(functools.partial(assemble_kernel, marks, parts, groups),...  2.97 us
    pallas_call x2, Pallas kernels, wgrad_own(): pl.pallas_call(functools.partial(wgrad_own_kernel, offsets), out_shape=(j...  2.74 us
    pallas_call x1, Pallas kernels, prep(): pl.pallas_call(prep_kernel, out_shape=(jax.ShapeDtypeStruct((2 * rows + m...  2.12 us
  transfers between devices with their start and end apart: 28, of which 10 were waited for; matrix products, arithmetic and copies ran while one was open for 0% of the time, Pallas kernels for 22%

profile of v10, /device:TPU:0, one launch (start us, length us, event | category | flops | bytes accessed | tf_op | source)
XLA Modules:
  0.0 74.9 jit_solution(3420071939437554209)
XLA Ops:
  0.6 2.1 %prep.1 = (bf16[544,256]{1,0:T(8,128)(2,1)}, bf16[64,256]{1,0:T(8,128)(2,1)}, bf16[64,256]{1,0:T(8,128)(2,1)}, bf16[352,256]{1,0:T(8,128)(2,1)}, bf16[352,256]{1,0:T(8,128)(2,1)}, /*index=5*/bf16[352,256]{1,0:T(8,128)(2,1)}) custom-call(bf16[256,256]{1,0:T(8,128)(2,1)} %x_hbm.1, bf16[256,256]{1,0:T(8,128)(2,1)} %dy_hbm.1, s32[27,256]{1,0:T(8,128)} %map_hbm.1, ...), custom_call_target="tpu_custom_call" | custom-call | tf_op jit(solution)/shard_map/prep/pallas_call | solution.py:92
  2.8 3.0 %collective-permute-start.2 = (bf16[352,256]{1,0:T(8,128)(2,1)}, bf16[352,256]{1,0:T(8,128)(2,1)S(1)}, u32[]{:S(2)}, u32[]{:S(2)}) collective-permute-start(bf16[352,256]{1,0:T(8,128)(2,1)} %get-tuple-element.45), channel_id=1, source_target_pairs={{0,8},{4,12},{8,0},{12,4},{16,24},{20,28},{24,16},{28,20},{1,9},{5... | collective-permute-start | bytes 540680 | tf_op jit(solution)/shard_map/ppermute | solution.py:578
  5.8 1.5 %collective-permute-start.3 = (bf16[352,256]{1,0:T(8,128)(2,1)}, bf16[352,256]{1,0:T(8,128)(2,1)S(1)}, u32[]{:S(2)}, u32[]{:S(2)}) collective-permute-start(bf16[352,256]{1,0:T(8,128)(2,1)} %get-tuple-element.46), channel_id=1, source_target_pairs={{0,16},{4,20},{8,24},{12,28},{16,0},{20,4},{24,8},{28,12},{1,17},{... | collective-permute-start | bytes 540680 | tf_op jit(solution)/shard_map/ppermute | solution.py:578
  7.3 2.0 %collective-permute-start = (bf16[64,256]{1,0:T(8,128)(2,1)}, bf16[64,256]{1,0:T(8,128)(2,1)S(1)}, u32[]{:S(2)}, u32[]{:S(2)}) collective-permute-start(bf16[64,256]{1,0:T(8,128)(2,1)} %get-tuple-element.38), channel_id=1, source_target_pairs={{0,1},{2,3},{1,0},{3,2},{4,5},{6,7},{5,4},{7,6},{8,9},{10,11},{9,8... | collective-permute-start | bytes 98312 | tf_op jit(solution)/shard_map/ppermute | solution.py:584
  9.3 0.7 collective-permute-start.1
  10.0 0.9 %copy-done.3 = bf16[544,256]{1,0:T(8,128)(2,1)S(1)} copy-done((bf16[544,256]{1,0:T(8,128)(2,1)S(1)}, bf16[544,256]{1,0:T(8,128)(2,1)}, u32[]{:S(2)}) %copy-start.3) | copy-done | bytes 278552
  11.0 0.8 %wgrad_own.2 = (bf16[27,64,256]{2,1,0:T(8,128)(2,1)S(1)}, bf16[256,256]{1,0:T(8,128)(2,1)S(1)}, s32[1,32,256]{2,1,0:T(8,128)S(1)}) custom-call(bf16[352,256]{1,0:T(8,128)(2,1)S(1)} %get-tuple-element.40.refs_0_), custom_call_target="tpu_custom_call" | custom-call | flops 100000000 | bytes 100000 | tf_op jit(solution)/shard_map/wgrad_own/pallas_call | solution.py:234
  11.8 0.1 joined.1
  11.9 1.6 %collective-permute-start.5 = (bf16[64,128]{1,0:T(8,128)(2,1)S(1)}, bf16[64,128]{1,0:T(8,128)(2,1)S(1)}, u32[]{:S(2)}, u32[]{:S(2)}) collective-permute-start(bf16[64,128]{1,0:T(8,128)(2,1)S(1)} %get-tuple-element.51), channel_id=1, source_target_pairs={{0,8},{4,12},{8,0},{12,4},{16,24},{20,28},{24,16},{28,20},{1,9},{5... | collective-permute-start | bytes 49160 | tf_op jit(solution)/shard_map/ppermute | solution.py:578
  13.5 1.5 %collective-permute-start.6 = (bf16[64,128]{1,0:T(8,128)(2,1)S(1)}, bf16[64,128]{1,0:T(8,128)(2,1)S(1)}, u32[]{:S(2)}, u32[]{:S(2)}) collective-permute-start(bf16[64,128]{1,0:T(8,128)(2,1)S(1)} %get-tuple-element.52), channel_id=1, source_target_pairs={{0,16},{4,20},{8,24},{12,28},{16,0},{20,4},{24,8},{28,12},{1,17},{... | collective-permute-start | bytes 49160 | tf_op jit(solution)/shard_map/ppermute | solution.py:578
  15.1 0.4 collective-permute-start.7
  15.5 0.4 collective-permute-done.3.refs_1_
  15.9 2.0 %wgrad_own.3 = (bf16[27,64,768]{2,1,0:T(8,128)(2,1)S(1)}, bf16[768,256]{1,0:T(8,128)(2,1)S(1)}, s32[3,32,256]{2,1,0:T(8,128)S(1)}) custom-call(bf16[352,256]{1,0:T(8,128)(2,1)S(1)} %collective-permute-done.2.refs_0_, bf16[352,256]{1,0:T(8,128)(2,1)S(1)} %collective-permute-done.3.refs_1_, bf16[352,256]{1,0:T(8,128)(2,1)S(1)} %collective-permute-done.4.refs_2_), custom_call_target="tpu_custom_call" | custom-call | flops 100000000 | bytes 100000 | tf_op jit(solution)/shard_map/wgrad_own/pallas_call | solution.py:234
  17.9 0.9 %wgrad_early.1.early_ref = bf16[2,896,768]{2,1,0:T(8,128)(2,1)S(1)} custom-call(bf16[27,64,256]{2,1,0:T(8,128)(2,1)S(1)} %get-tuple-element.43.own_ref, s32[1,32,256]{2,1,0:T(8,128)S(1)} %get-tuple-element.44.own_maps, bf16[27,64,768]{2,1,0:T(8,128)(2,1)S(1)} %get-tuple-element.48.rest_ref, s32[3,32,256]{2,1,0:T(8,128)S(1)} %get-tuple-element.49.rest_maps, ...), custom_call_target="tpu_custom_call" | custom-call | flops 100000000 | bytes 100000 | tf_op jit(solution)/shard_map/wgrad_early/pallas_call | solution.py:278
  18.8 0.9 %collective-permute-done.7.halo_ref = bf16[64,128]{1,0:T(8,128)(2,1)S(1)} collective-permute-done((bf16[64,128]{1,0:T(8,128)(2,1)S(1)}, bf16[64,128]{1,0:T(8,128)(2,1)S(1)}, u32[]{:S(2)}, u32[]{:S(2)}) %collective-permute-start.7) | collective-permute-done | bytes 16416 | tf_op jit(solution)/shard_map/ppermute | solution.py:578
  19.7 0.9 %wgrad_send.1 = (f32[28,32,256]{2,1,0:T(8,128)S(1)}, bf16[2,896,256]{2,1,0:T(8,128)(2,1)S(1)}) custom-call(bf16[2,896,768]{2,1,0:T(8,128)(2,1)S(1)} %wgrad_early.1.early_ref, bf16[256,256]{1,0:T(8,128)(2,1)S(1)} %get-tuple-element.41.after_ref.own_dys, bf16[27,64,768]{2,1,0:T(8,128)(2,1)S(1)} %get-tuple-element.48.rest_ref, ...), custom_call_target="tpu_custom_call" | custom-call | flops 100000000 | bytes 100000 | tf_op jit(solution)/shard_map/wgrad_send/pallas_call | solution.py:314
  20.7 0.6 wgrad_keep.1.keep_ref
  21.4 1.8 %collective-permute-done.8.got_ref = f32[28,32,256]{2,1,0:T(8,128)S(1)} collective-permute-done((f32[28,32,256]{2,1,0:T(8,128)S(1)}, f32[28,32,256]{2,1,0:T(8,128)S(1)}, u32[]{:S(2)}, u32[]{:S(2)}) %collective-permute-start.8) | collective-permute-done | bytes 917536 | tf_op jit(solution)/shard_map/ppermute | solution.py:578
  23.2 0.5 blocks.1
  23.7 4.7 %collective-permute-start.9 = (s16[240,256]{1,0:T(8,128)(2,1)S(1)}, s16[240,256]{1,0:T(8,128)(2,1)S(1)}, u32[]{:S(2)}, u32[]{:S(2)}) collective-permute-start(s16[240,256]{1,0:T(8,128)(2,1)S(1)} %get-tuple-element.58), channel_id=1, source_target_pairs={{0,1},{1,0},{2,3},{3,2},{4,5},{5,4},{6,7},{7,6},{8,9},{9,8},{10,11... | collective-permute-start | bytes 368648 | tf_op jit(solution)/shard_map/ppermute | solution.py:578
  28.3 1.5 %collective-permute-start.10 = (s16[240,256]{1,0:T(8,128)(2,1)S(1)}, s16[240,256]{1,0:T(8,128)(2,1)S(1)}, u32[]{:S(2)}, u32[]{:S(2)}) collective-permute-start(s16[240,256]{1,0:T(8,128)(2,1)S(1)} %get-tuple-element.59), channel_id=1, source_target_pairs={{0,2},{1,3},{2,0},{3,1},{4,6},{5,7},{6,4},{7,5},{8,10},{9,11},{10,... | collective-permute-start | bytes 368648 | tf_op jit(solution)/shard_map/ppermute | solution.py:578
  29.8 1.4 %collective-permute-start.11 = (s16[240,256]{1,0:T(8,128)(2,1)S(1)}, s16[240,256]{1,0:T(8,128)(2,1)S(1)}, u32[]{:S(2)}, u32[]{:S(2)}) collective-permute-start(s16[240,256]{1,0:T(8,128)(2,1)S(1)} %get-tuple-element.60), channel_id=1, source_target_pairs={{0,3},{1,2},{2,1},{3,0},{4,7},{5,6},{6,5},{7,4},{8,11},{9,10},{10,... | collective-permute-start | bytes 368648 | tf_op jit(solution)/shard_map/ppermute | solution.py:578
  31.2 5.5 %backward.1 = (f32[256,256]{1,0:T(8,128)S(1)}, f32[64,256]{1,0:T(8,128)S(1)}, f32[64,256]{1,0:T(8,128)S(1)}, f32[8,128]{1,0:T(8,128)S(1)}) custom-call(bf16[544,256]{1,0:T(8,128)(2,1)S(1)} %get-tuple-element.37.pack_ref, bf16[27,256,256]{2,1,0:T(8,128)(2,1)S(1)} %copy-done, f32[7,32,256]{2,1,0:T(8,128)S(1)} %get-tuple-element.57.after_ref.mine_ref), custom_call_target="tpu_custom_call" | custom-call | flops 100000000 | bytes 100000 | tf_op jit(solution)/shard_map/backward/pallas_call | solution.py:151
  36.7 3.9 %collective-permute-done.10.refs_1_ = s16[240,256]{1,0:T(8,128)(2,1)S(1)} collective-permute-done((s16[240,256]{1,0:T(8,128)(2,1)S(1)}, s16[240,256]{1,0:T(8,128)(2,1)S(1)}, u32[]{:S(2)}, u32[]{:S(2)}) %collective-permute-start.10) | collective-permute-done | bytes 122912 | tf_op jit(solution)/shard_map/ppermute | solution.py:578
  40.6 0.1 total.1.after_ref.refs_0_
  40.8 2.5 %collective-permute-start.16 = (bf16[7,32,256]{2,1,0:T(8,128)(2,1)S(1)}, bf16[7,32,256]{2,1,0:T(8,128)(2,1)S(1)}, u32[]{:S(2)}, u32[]{:S(2)}) collective-permute-start(bf16[7,32,256]{2,1,0:T(8,128)(2,1)S(1)} %total.1.after_ref.refs_0_), channel_id=1, source_target_pairs={{0,3},{1,2},{2,1},{3,0},{4,7},{5,6},{6,5},{7,4},{8,11},{9,10},{10,... | collective-permute-start | bytes 344072 | tf_op jit(solution)/shard_map/ppermute | solution.py:578
  43.3 1.2 %collective-permute-start.15 = (bf16[7,32,256]{2,1,0:T(8,128)(2,1)S(1)}, bf16[7,32,256]{2,1,0:T(8,128)(2,1)S(1)}, u32[]{:S(2)}, u32[]{:S(2)}) collective-permute-start(bf16[7,32,256]{2,1,0:T(8,128)(2,1)S(1)} %total.1.after_ref.refs_0_), channel_id=1, source_target_pairs={{0,2},{1,3},{2,0},{3,1},{4,6},{5,7},{6,4},{7,5},{8,10},{9,11},{10,... | collective-permute-start | bytes 344072 | tf_op jit(solution)/shard_map/ppermute | solution.py:578
  44.5 0.7 collective-permute-start.14
  45.2 1.2 %collective-permute-start.19 = (bf16[7,32,256]{2,1,0:T(8,128)(2,1)S(1)}, bf16[7,32,256]{2,1,0:T(8,128)(2,1)S(1)}, u32[]{:S(2)}, u32[]{:S(2)}) collective-permute-start(bf16[7,32,256]{2,1,0:T(8,128)(2,1)S(1)} %total.1.after_ref.refs_0_), channel_id=1, source_target_pairs={{0,24},{4,28},{8,16},{12,20},{16,8},{20,12},{24,0},{28,4},{1,25},{... | collective-permute-start | bytes 344072 | tf_op jit(solution)/shard_map/ppermute | solution.py:578
  46.4 0.8 %collective-permute-start.18 = (bf16[7,32,256]{2,1,0:T(8,128)(2,1)S(1)}, bf16[7,32,256]{2,1,0:T(8,128)(2,1)S(1)}, u32[]{:S(2)}, u32[]{:S(2)}) collective-permute-start(bf16[7,32,256]{2,1,0:T(8,128)(2,1)S(1)} %total.1.after_ref.refs_0_), channel_id=1, source_target_pairs={{0,16},{4,20},{8,24},{12,28},{16,0},{20,4},{24,8},{28,12},{1,17},{... | collective-permute-start | bytes 344072 | tf_op jit(solution)/shard_map/ppermute | solution.py:578
  47.2 0.7 collective-permute-done.16.refs_2_
  47.9 0.9 %collective-permute-start.17 = (bf16[7,32,256]{2,1,0:T(8,128)(2,1)S(1)}, bf16[7,32,256]{2,1,0:T(8,128)(2,1)S(1)}, u32[]{:S(2)}, u32[]{:S(2)}) collective-permute-start(bf16[7,32,256]{2,1,0:T(8,128)(2,1)S(1)} %total.1.after_ref.refs_0_), channel_id=1, source_target_pairs={{0,8},{4,12},{8,0},{12,4},{16,24},{20,28},{24,16},{28,20},{1,9},{5... | collective-permute-start | bytes 344072 | tf_op jit(solution)/shard_map/ppermute | solution.py:578
  48.7 4.1 %forward.1 = (bf16[256,256]{1,0:T(8,128)(2,1)}, f32[8,128]{1,0:T(8,128)S(1)}) custom-call(bf16[544,256]{1,0:T(8,128)(2,1)S(1)} %get-tuple-element.37.pack_ref, bf16[128,256]{1,0:T(8,128)(2,1)S(1)} %get-tuple-element.42.halo_ref, bf16[27,256,256]{2,1,0:T(8,128)(2,1)S(1)} %copy-done, bf16[7,32,256]{2,1,0:T(8,128)(2,1)S(1)} %total.1.after_ref.refs_0_), custom_call_target="tpu_custom_call" | custom-call | flops 100000000 | bytes 100000 | tf_op jit(solution)/shard_map/forward/pallas_call | solution.py:196
  52.8 0.8 %collective-permute-done.15.refs_1_ = bf16[7,32,256]{2,1,0:T(8,128)(2,1)S(1)} collective-permute-done((bf16[7,32,256]{2,1,0:T(8,128)(2,1)S(1)}, bf16[7,32,256]{2,1,0:T(8,128)(2,1)S(1)}, u32[]{:S(2)}, u32[]{:S(2)}) %collective-permute-start.15) | collective-permute-done | bytes 114720 | tf_op jit(solution)/shard_map/ppermute | solution.py:578
  53.7 1.3 %collective-permute-start.24 = (bf16[3,7,32,256]{3,2,1,0:T(8,128)(2,1)S(1)}, bf16[3,7,32,256]{3,2,1,0:T(8,128)(2,1)S(1)}, u32[]{:S(2)}, u32[]{:S(2)}) collective-permute-start(bf16[3,7,32,256]{3,2,1,0:T(8,128)(2,1)S(1)} %gate.1.after_ref.refs_1_), channel_id=1, source_target_pairs={{0,24},{4,28},{8,16},{12,20},{16,8},{20,12},{24,0},{28,4},{1,25},{... | collective-permute-start | bytes 1032200 | tf_op jit(solution)/shard_map/ppermute | solution.py:578
  55.0 0.8 %collective-permute-start.22 = (bf16[3,7,32,256]{3,2,1,0:T(8,128)(2,1)S(1)}, bf16[3,7,32,256]{3,2,1,0:T(8,128)(2,1)S(1)}, u32[]{:S(2)}, u32[]{:S(2)}) collective-permute-start(bf16[3,7,32,256]{3,2,1,0:T(8,128)(2,1)S(1)} %gate.1.after_ref.refs_1_), channel_id=1, source_target_pairs={{0,16},{4,20},{8,24},{12,28},{16,0},{20,4},{24,8},{28,12},{1,17},{... | collective-permute-start | bytes 1032200 | tf_op jit(solution)/shard_map/ppermute | solution.py:578
  55.8 1.5 %collective-permute-start.20 = (bf16[3,7,32,256]{3,2,1,0:T(8,128)(2,1)S(1)}, bf16[3,7,32,256]{3,2,1,0:T(8,128)(2,1)S(1)}, u32[]{:S(2)}, u32[]{:S(2)}) collective-permute-start(bf16[3,7,32,256]{3,2,1,0:T(8,128)(2,1)S(1)} %gate.1.after_ref.refs_1_), channel_id=1, source_target_pairs={{0,8},{4,12},{8,0},{12,4},{16,24},{20,28},{24,16},{28,20},{1,9},{5... | collective-permute-start | bytes 1032200 | tf_op jit(solution)/shard_map/ppermute | solution.py:578
  57.2 4.0 %collective-permute-start.12 = (f32[64,256]{1,0:T(8,128)S(1)}, f32[64,256]{1,0:T(8,128)S(1)}, u32[]{:S(2)}, u32[]{:S(2)}) collective-permute-start(f32[64,256]{1,0:T(8,128)S(1)} %get-tuple-element.64), channel_id=1, source_target_pairs={{0,1},{2,3},{1,0},{3,2},{4,5},{6,7},{5,4},{7,6},{8,9},{10,11},{9,8... | collective-permute-start | bytes 196616 | tf_op jit(solution)/shard_map/ppermute | solution.py:584
  61.3 0.7 collective-permute-start.13
  61.9 1.6 %collective-permute-done.12.first_ref = f32[64,256]{1,0:T(8,128)S(1)} collective-permute-done((f32[64,256]{1,0:T(8,128)S(1)}, f32[64,256]{1,0:T(8,128)S(1)}, u32[]{:S(2)}, u32[]{:S(2)}) %collective-permute-start.12) | collective-permute-done | bytes 65568 | tf_op jit(solution)/shard_map/ppermute | solution.py:584
  63.5 1.0 %final.1 = (bf16[256,256]{1,0:T(8,128)(2,1)}, f32[8,128]{1,0:T(8,128)S(1)}) custom-call(bf16[544,256]{1,0:T(8,128)(2,1)S(1)} %get-tuple-element.37.pack_ref, f32[256,256]{1,0:T(8,128)S(1)} %get-tuple-element.63.own_ref, f32[64,256]{1,0:T(8,128)S(1)} %collective-permute-done.12.first_ref, f32[64,256]{1,0:T(8,128)S(1)} %collective-permute-done.13.second_ref, ...), custom_call_target="tpu_custom_call" | custom-call | tf_op jit(solution)/shard_map/final/pallas_call | solution.py:478
  64.6 0.6 collective-permute-start.27
  65.2 0.5 collective-permute-done.24.refs_4_
  65.7 5.4 %collective-permute-done.22.refs_2_ = bf16[3,7,32,256]{3,2,1,0:T(8,128)(2,1)S(1)} collective-permute-done((bf16[3,7,32,256]{3,2,1,0:T(8,128)(2,1)S(1)}, bf16[3,7,32,256]{3,2,1,0:T(8,128)(2,1)S(1)}, u32[]{:S(2)}, u32[]{:S(2)}) %collective-permute-start.22) | collective-permute-done | bytes 344096 | tf_op jit(solution)/shard_map/ppermute | solution.py:578
  71.1 0.5 collective-permute-start.21
  71.6 1.4 %assemble.2.refs_7_ = bf16[27,256,256]{2,1,0:T(8,128)(2,1)} custom-call(bf16[4,7,32,256]{3,2,1,0:T(8,128)(2,1)S(1)} %stack.4.refs_0_, bf16[4,7,32,256]{3,2,1,0:T(8,128)(2,1)S(1)} %collective-permute-done.26.refs_1_, bf16[3,7,32,256]{3,2,1,0:T(8,128)(2,1)S(1)} %stack.5.refs_2_, bf16[3,7,32,256]{3,2,1,0:T(8,128)(2,1)S(1)} %collective-permute-done.27.refs_3_), custom_call_target="tpu_custom_call" | custom-call | flops 100000000 | bytes 100000 | tf_op jit(solution)/shard_map/assemble/pallas_call | solution.py:553
  73.0 0.2 collective-permute-done.21.refs_1_
  73.2 1.6 %assemble.3 = bf16[27,256,256]{2,1,0:T(8,128)(2,1)} custom-call(bf16[3,7,32,256]{3,2,1,0:T(8,128)(2,1)S(1)} %collective-permute-done.20.refs_0_, bf16[3,7,32,256]{3,2,1,0:T(8,128)(2,1)S(1)} %collective-permute-done.21.refs_1_, bf16[3,7,32,256]{3,2,1,0:T(8,128)(2,1)S(1)} %collective-permute-done.22.refs_2_, ...), custom_call_target="tpu_custom_call", output_to_operand_aliasing={{}: (7, {})} | custom-call | flops 100000000 | bytes 100000 | tf_op jit(solution)/shard_map/assemble/pallas_call | solution.py:553
  (35 shorter events, 0.4 us)
Async XLA Ops:
  2.8 12.3 %collective-permute-start.2 = (bf16[352,256]{1,0:T(8,128)(2,1)}, bf16[352,256]{1,0:T(8,128)(2,1)S(1)}, u32[]{:S(2)}, u32[]{:S(2)}) collective-permute-start(bf16[352,256]{1,0:T(8,128)(2,1)} %get-tuple-element.45), channel_id=1, source_target_pairs={{0,8},{4,12},{8,0},{12,4},{16,24},{20,28},{24,16},{28,20},{1,9},{5... | collective-permute-start | bytes 540680 | tf_op jit(solution)/shard_map/ppermute | solution.py:578
  5.8 10.2 %collective-permute-start.3 = (bf16[352,256]{1,0:T(8,128)(2,1)}, bf16[352,256]{1,0:T(8,128)(2,1)S(1)}, u32[]{:S(2)}, u32[]{:S(2)}) collective-permute-start(bf16[352,256]{1,0:T(8,128)(2,1)} %get-tuple-element.46), channel_id=1, source_target_pairs={{0,16},{4,20},{8,24},{12,28},{16,0},{20,4},{24,8},{28,12},{1,17},{... | collective-permute-start | bytes 540680 | tf_op jit(solution)/shard_map/ppermute | solution.py:578
  7.3 8.7 %collective-permute-start.4 = (bf16[352,256]{1,0:T(8,128)(2,1)}, bf16[352,256]{1,0:T(8,128)(2,1)S(1)}, u32[]{:S(2)}, u32[]{:S(2)}) collective-permute-start(bf16[352,256]{1,0:T(8,128)(2,1)} %get-tuple-element.47), channel_id=1, source_target_pairs={{0,24},{4,28},{8,16},{12,20},{16,8},{20,12},{24,0},{28,4},{1,25},{... | collective-permute-start | bytes 540680 | tf_op jit(solution)/shard_map/ppermute | solution.py:578
  7.3 4.5 %collective-permute-start = (bf16[64,256]{1,0:T(8,128)(2,1)}, bf16[64,256]{1,0:T(8,128)(2,1)S(1)}, u32[]{:S(2)}, u32[]{:S(2)}) collective-permute-start(bf16[64,256]{1,0:T(8,128)(2,1)} %get-tuple-element.38), channel_id=1, source_target_pairs={{0,1},{2,3},{1,0},{3,2},{4,5},{6,7},{5,4},{7,6},{8,9},{10,11},{9,8... | collective-permute-start | bytes 98312 | tf_op jit(solution)/shard_map/ppermute | solution.py:584
  9.3 2.5 %collective-permute-start.1 = (bf16[64,256]{1,0:T(8,128)(2,1)}, bf16[64,256]{1,0:T(8,128)(2,1)S(1)}, u32[]{:S(2)}, u32[]{:S(2)}) collective-permute-start(bf16[64,256]{1,0:T(8,128)(2,1)} %get-tuple-element.39), channel_id=1, source_target_pairs={{1,2},{2,1},{5,6},{6,5},{9,10},{10,9},{13,14},{14,13},{17,18},{18,... | collective-permute-start | bytes 98312 | tf_op jit(solution)/shard_map/ppermute | solution.py:584
  10.0 1.0 %copy-start.3 = (bf16[544,256]{1,0:T(8,128)(2,1)S(1)}, bf16[544,256]{1,0:T(8,128)(2,1)}, u32[]{:S(2)}) copy-start(bf16[544,256]{1,0:T(8,128)(2,1)} %get-tuple-element.36.pack_ref) | copy-start | bytes 835588
  11.9 6.0 %collective-permute-start.5 = (bf16[64,128]{1,0:T(8,128)(2,1)S(1)}, bf16[64,128]{1,0:T(8,128)(2,1)S(1)}, u32[]{:S(2)}, u32[]{:S(2)}) collective-permute-start(bf16[64,128]{1,0:T(8,128)(2,1)S(1)} %get-tuple-element.51), channel_id=1, source_target_pairs={{0,8},{4,12},{8,0},{12,4},{16,24},{20,28},{24,16},{28,20},{1,9},{5... | collective-permute-start | bytes 49160 | tf_op jit(solution)/shard_map/ppermute | solution.py:578
  13.5 4.4 %collective-permute-start.6 = (bf16[64,128]{1,0:T(8,128)(2,1)S(1)}, bf16[64,128]{1,0:T(8,128)(2,1)S(1)}, u32[]{:S(2)}, u32[]{:S(2)}) collective-permute-start(bf16[64,128]{1,0:T(8,128)(2,1)S(1)} %get-tuple-element.52), channel_id=1, source_target_pairs={{0,16},{4,20},{8,24},{12,28},{16,0},{20,4},{24,8},{28,12},{1,17},{... | collective-permute-start | bytes 49160 | tf_op jit(solution)/shard_map/ppermute | solution.py:578
  15.1 4.6 %collective-permute-start.7 = (bf16[64,128]{1,0:T(8,128)(2,1)S(1)}, bf16[64,128]{1,0:T(8,128)(2,1)S(1)}, u32[]{:S(2)}, u32[]{:S(2)}) collective-permute-start(bf16[64,128]{1,0:T(8,128)(2,1)S(1)} %get-tuple-element.54), channel_id=1, source_target_pairs={{0,24},{4,28},{8,16},{12,20},{16,8},{20,12},{24,0},{28,4},{1,25},{... | collective-permute-start | bytes 49160 | tf_op jit(solution)/shard_map/ppermute | solution.py:578
  20.6 2.5 %collective-permute-start.8 = (f32[28,32,256]{2,1,0:T(8,128)S(1)}, f32[28,32,256]{2,1,0:T(8,128)S(1)}, u32[]{:S(2)}, u32[]{:S(2)}) collective-permute-start(f32[28,32,256]{2,1,0:T(8,128)S(1)} %get-tuple-element.56.after_ref), channel_id=1, source_target_pairs={{0,4},{4,0},{8,12},{12,8},{16,20},{20,16},{24,28},{28,24},{1,5},{5... | collective-permute-start | bytes 2752520 | tf_op jit(solution)/shard_map/ppermute | solution.py:578
  20.7 10.5 %copy-start = (bf16[27,256,256]{2,1,0:T(8,128)(2,1)S(1)}, bf16[27,256,256]{2,1,0:T(8,128)(2,1)}, u32[]{:S(2)}) copy-start(bf16[27,256,256]{2,1,0:T(8,128)(2,1)} %w_ref.3) | copy-start | bytes 10616836
  23.7 13.1 %collective-permute-start.9 = (s16[240,256]{1,0:T(8,128)(2,1)S(1)}, s16[240,256]{1,0:T(8,128)(2,1)S(1)}, u32[]{:S(2)}, u32[]{:S(2)}) collective-permute-start(s16[240,256]{1,0:T(8,128)(2,1)S(1)} %get-tuple-element.58), channel_id=1, source_target_pairs={{0,1},{1,0},{2,3},{3,2},{4,5},{5,4},{6,7},{7,6},{8,9},{9,8},{10,11... | collective-permute-start | bytes 368648 | tf_op jit(solution)/shard_map/ppermute | solution.py:578
  28.3 12.3 %collective-permute-start.10 = (s16[240,256]{1,0:T(8,128)(2,1)S(1)}, s16[240,256]{1,0:T(8,128)(2,1)S(1)}, u32[]{:S(2)}, u32[]{:S(2)}) collective-permute-start(s16[240,256]{1,0:T(8,128)(2,1)S(1)} %get-tuple-element.59), channel_id=1, source_target_pairs={{0,2},{1,3},{2,0},{3,1},{4,6},{5,7},{6,4},{7,5},{8,10},{9,11},{10,... | collective-permute-start | bytes 368648 | tf_op jit(solution)/shard_map/ppermute | solution.py:578
  29.8 10.8 %collective-permute-start.11 = (s16[240,256]{1,0:T(8,128)(2,1)S(1)}, s16[240,256]{1,0:T(8,128)(2,1)S(1)}, u32[]{:S(2)}, u32[]{:S(2)}) collective-permute-start(s16[240,256]{1,0:T(8,128)(2,1)S(1)} %get-tuple-element.60), channel_id=1, source_target_pairs={{0,3},{1,2},{2,1},{3,0},{4,7},{5,6},{6,5},{7,4},{8,11},{9,10},{10,... | collective-permute-start | bytes 368648 | tf_op jit(solution)/shard_map/ppermute | solution.py:578
  36.7 26.8 %copy-start.1 = (s32[1,64]{1,0:T(1,128)S(1)}, s32[1,64]{1,0:T(1,128)}, u32[]{:S(2)}) copy-start(s32[1,64]{1,0:T(1,128)} %up_ref.1) | copy-start | bytes 772
  36.7 26.8 %copy-start.2 = (s32[1,64]{1,0:T(1,128)S(1)}, s32[1,64]{1,0:T(1,128)}, u32[]{:S(2)}) copy-start(s32[1,64]{1,0:T(1,128)} %down_ref.1) | copy-start | bytes 772
  40.8 7.1 %collective-permute-start.16 = (bf16[7,32,256]{2,1,0:T(8,128)(2,1)S(1)}, bf16[7,32,256]{2,1,0:T(8,128)(2,1)S(1)}, u32[]{:S(2)}, u32[]{:S(2)}) collective-permute-start(bf16[7,32,256]{2,1,0:T(8,128)(2,1)S(1)} %total.1.after_ref.refs_0_), channel_id=1, source_target_pairs={{0,3},{1,2},{2,1},{3,0},{4,7},{5,6},{6,5},{7,4},{8,11},{9,10},{10,... | collective-permute-start | bytes 344072 | tf_op jit(solution)/shard_map/ppermute | solution.py:578
  43.3 10.3 %collective-permute-start.15 = (bf16[7,32,256]{2,1,0:T(8,128)(2,1)S(1)}, bf16[7,32,256]{2,1,0:T(8,128)(2,1)S(1)}, u32[]{:S(2)}, u32[]{:S(2)}) collective-permute-start(bf16[7,32,256]{2,1,0:T(8,128)(2,1)S(1)} %total.1.after_ref.refs_0_), channel_id=1, source_target_pairs={{0,2},{1,3},{2,0},{3,1},{4,6},{5,7},{6,4},{7,5},{8,10},{9,11},{10,... | collective-permute-start | bytes 344072 | tf_op jit(solution)/shard_map/ppermute | solution.py:578
  44.5 9.1 %collective-permute-start.14 = (bf16[7,32,256]{2,1,0:T(8,128)(2,1)S(1)}, bf16[7,32,256]{2,1,0:T(8,128)(2,1)S(1)}, u32[]{:S(2)}, u32[]{:S(2)}) collective-permute-start(bf16[7,32,256]{2,1,0:T(8,128)(2,1)S(1)} %total.1.after_ref.refs_0_), channel_id=1, source_target_pairs={{0,1},{1,0},{2,3},{3,2},{4,5},{5,4},{6,7},{7,6},{8,9},{9,8},{10,11... | collective-permute-start | bytes 344072 | tf_op jit(solution)/shard_map/ppermute | solution.py:578
  45.2 8.4 %collective-permute-start.19 = (bf16[7,32,256]{2,1,0:T(8,128)(2,1)S(1)}, bf16[7,32,256]{2,1,0:T(8,128)(2,1)S(1)}, u32[]{:S(2)}, u32[]{:S(2)}) collective-permute-start(bf16[7,32,256]{2,1,0:T(8,128)(2,1)S(1)} %total.1.after_ref.refs_0_), channel_id=1, source_target_pairs={{0,24},{4,28},{8,16},{12,20},{16,8},{20,12},{24,0},{28,4},{1,25},{... | collective-permute-start | bytes 344072 | tf_op jit(solution)/shard_map/ppermute | solution.py:578
  46.4 7.2 %collective-permute-start.18 = (bf16[7,32,256]{2,1,0:T(8,128)(2,1)S(1)}, bf16[7,32,256]{2,1,0:T(8,128)(2,1)S(1)}, u32[]{:S(2)}, u32[]{:S(2)}) collective-permute-start(bf16[7,32,256]{2,1,0:T(8,128)(2,1)S(1)} %total.1.after_ref.refs_0_), channel_id=1, source_target_pairs={{0,16},{4,20},{8,24},{12,28},{16,0},{20,4},{24,8},{28,12},{1,17},{... | collective-permute-start | bytes 344072 | tf_op jit(solution)/shard_map/ppermute | solution.py:578
  47.9 5.8 %collective-permute-start.17 = (bf16[7,32,256]{2,1,0:T(8,128)(2,1)S(1)}, bf16[7,32,256]{2,1,0:T(8,128)(2,1)S(1)}, u32[]{:S(2)}, u32[]{:S(2)}) collective-permute-start(bf16[7,32,256]{2,1,0:T(8,128)(2,1)S(1)} %total.1.after_ref.refs_0_), channel_id=1, source_target_pairs={{0,8},{4,12},{8,0},{12,4},{16,24},{20,28},{24,16},{28,20},{1,9},{5... | collective-permute-start | bytes 344072 | tf_op jit(solution)/shard_map/ppermute | solution.py:578
  53.7 12.0 %collective-permute-start.24 = (bf16[3,7,32,256]{3,2,1,0:T(8,128)(2,1)S(1)}, bf16[3,7,32,256]{3,2,1,0:T(8,128)(2,1)S(1)}, u32[]{:S(2)}, u32[]{:S(2)}) collective-permute-start(bf16[3,7,32,256]{3,2,1,0:T(8,128)(2,1)S(1)} %gate.1.after_ref.refs_1_), channel_id=1, source_target_pairs={{0,24},{4,28},{8,16},{12,20},{16,8},{20,12},{24,0},{28,4},{1,25},{... | collective-permute-start | bytes 1032200 | tf_op jit(solution)/shard_map/ppermute | solution.py:578
  55.0 16.1 %collective-permute-start.22 = (bf16[3,7,32,256]{3,2,1,0:T(8,128)(2,1)S(1)}, bf16[3,7,32,256]{3,2,1,0:T(8,128)(2,1)S(1)}, u32[]{:S(2)}, u32[]{:S(2)}) collective-permute-start(bf16[3,7,32,256]{3,2,1,0:T(8,128)(2,1)S(1)} %gate.1.after_ref.refs_1_), channel_id=1, source_target_pairs={{0,16},{4,20},{8,24},{12,28},{16,0},{20,4},{24,8},{28,12},{1,17},{... | collective-permute-start | bytes 1032200 | tf_op jit(solution)/shard_map/ppermute | solution.py:578
  55.8 15.3 %collective-permute-start.20 = (bf16[3,7,32,256]{3,2,1,0:T(8,128)(2,1)S(1)}, bf16[3,7,32,256]{3,2,1,0:T(8,128)(2,1)S(1)}, u32[]{:S(2)}, u32[]{:S(2)}) collective-permute-start(bf16[3,7,32,256]{3,2,1,0:T(8,128)(2,1)S(1)} %gate.1.after_ref.refs_1_), channel_id=1, source_target_pairs={{0,8},{4,12},{8,0},{12,4},{16,24},{20,28},{24,16},{28,20},{1,9},{5... | collective-permute-start | bytes 1032200 | tf_op jit(solution)/shard_map/ppermute | solution.py:578
  57.2 6.2 %collective-permute-start.12 = (f32[64,256]{1,0:T(8,128)S(1)}, f32[64,256]{1,0:T(8,128)S(1)}, u32[]{:S(2)}, u32[]{:S(2)}) collective-permute-start(f32[64,256]{1,0:T(8,128)S(1)} %get-tuple-element.64), channel_id=1, source_target_pairs={{0,1},{2,3},{1,0},{3,2},{4,5},{6,7},{5,4},{7,6},{8,9},{10,11},{9,8... | collective-permute-start | bytes 196616 | tf_op jit(solution)/shard_map/ppermute | solution.py:584
  61.3 2.2 %collective-permute-start.13 = (f32[64,256]{1,0:T(8,128)S(1)}, f32[64,256]{1,0:T(8,128)S(1)}, u32[]{:S(2)}, u32[]{:S(2)}) collective-permute-start(f32[64,256]{1,0:T(8,128)S(1)} %get-tuple-element.65), channel_id=1, source_target_pairs={{1,2},{2,1},{5,6},{6,5},{9,10},{10,9},{13,14},{14,13},{17,18},{18,... | collective-permute-start | bytes 196616 | tf_op jit(solution)/shard_map/ppermute | solution.py:584
  64.5 7.1 %collective-permute-start.26 = (bf16[4,7,32,256]{3,2,1,0:T(8,128)(2,1)S(1)}, bf16[4,7,32,256]{3,2,1,0:T(8,128)(2,1)S(1)}, u32[]{:S(2)}, u32[]{:S(2)}) collective-permute-start(bf16[4,7,32,256]{3,2,1,0:T(8,128)(2,1)S(1)} %stack.4.refs_0_), channel_id=1, source_target_pairs={{0,4},{4,0},{8,12},{12,8},{16,20},{20,16},{24,28},{28,24},{1,5},{5... | collective-permute-start | bytes 1376264 | tf_op jit(solution)/shard_map/ppermute | solution.py:578
  64.6 7.0 %collective-permute-start.27 = (bf16[3,7,32,256]{3,2,1,0:T(8,128)(2,1)S(1)}, bf16[3,7,32,256]{3,2,1,0:T(8,128)(2,1)S(1)}, u32[]{:S(2)}, u32[]{:S(2)}) collective-permute-start(bf16[3,7,32,256]{3,2,1,0:T(8,128)(2,1)S(1)} %stack.5.refs_2_), channel_id=1, source_target_pairs={{0,4},{4,0},{8,12},{12,8},{16,20},{20,16},{24,28},{28,24},{1,5},{5... | collective-permute-start | bytes 1032200 | tf_op jit(solution)/shard_map/ppermute | solution.py:578
  65.7 7.3 %collective-permute-start.25 = (bf16[3,7,32,256]{3,2,1,0:T(8,128)(2,1)S(1)}, bf16[3,7,32,256]{3,2,1,0:T(8,128)(2,1)S(1)}, u32[]{:S(2)}, u32[]{:S(2)}) collective-permute-start(bf16[3,7,32,256]{3,2,1,0:T(8,128)(2,1)S(1)} %collective-permute-done.24.refs_4_), channel_id=1, source_target_pairs={{0,4},{4,0},{8,12},{12,8},{16,20},{20,16},{24,28},{28,24},{1,5},{5... | collective-permute-start | bytes 1032200 | tf_op jit(solution)/shard_map/ppermute | solution.py:578
  71.1 1.9 %collective-permute-start.23 = (bf16[3,7,32,256]{3,2,1,0:T(8,128)(2,1)S(1)}, bf16[3,7,32,256]{3,2,1,0:T(8,128)(2,1)S(1)}, u32[]{:S(2)}, u32[]{:S(2)}) collective-permute-start(bf16[3,7,32,256]{3,2,1,0:T(8,128)(2,1)S(1)} %collective-permute-done.22.refs_2_), channel_id=1, source_target_pairs={{0,4},{4,0},{8,12},{12,8},{16,20},{20,16},{24,28},{28,24},{1,5},{5... | collective-permute-start | bytes 1032200 | tf_op jit(solution)/shard_map/ppermute | solution.py:578
  71.1 2.1 %collective-permute-start.21 = (bf16[3,7,32,256]{3,2,1,0:T(8,128)(2,1)S(1)}, bf16[3,7,32,256]{3,2,1,0:T(8,128)(2,1)S(1)}, u32[]{:S(2)}, u32[]{:S(2)}) collective-permute-start(bf16[3,7,32,256]{3,2,1,0:T(8,128)(2,1)S(1)} %collective-permute-done.20.refs_0_), channel_id=1, source_target_pairs={{0,4},{4,0},{8,12},{12,8},{16,20},{20,16},{24,28},{28,24},{1,5},{5... | collective-permute-start | bytes 1032200 | tf_op jit(solution)/shard_map/ppermute | solution.py:578
